TPU v7x, 32 devices: a whole 2x2x4 slice. The times are simulated.
32 devices in a mesh: groups: 2 (over y), team: 4 (over z), rep: 4 (over x, core).
Axes of the slice: x: 2, y: 2, z: 4, core: 2. Of those that a mesh axis runs over, the one named last changes fastest.
Arguments:
- omega_rows: float32 [128, 32768], P(('groups', 'team'), 'rep'), parts along dimension 0, as said below
- covariance_columns: float32 [32768, 2048], P('rep', ('groups', 'team')), parts along dimension 1, may hold values from -0.03125 to 0.03125
- tile_offsets: int32 [8], P(('groups', 'team')), parts along dimension 0, may hold values from 0 to 32512, as said below
Outputs:
- new_omega: float32 [64, 2048], P('rep', ('groups', 'team')), parts along dimension 1
There are 2 independent parts, one for each index of `groups`. A program takes and returns all parts, laid end to end along the dimension named above; each array names one. Nothing has to cross between parts.
Inputs may be any that keep to these rules, and one draw needn't show every extreme that they name: `tile_offsets`: distinct multiples of 256; both 0 and 32512 occur. `omega_rows`: entries with column equal to row lie in 1 to 2.
All inputs are finite; a program needn't handle non-finite values.
Results may differ from a plain program's by a relative error of at most 0.0003.
Values sent between devices are 32-bit elements; how exact they have to be, the bound alone decides.
No kernel may reach another device: no remote copies, remote signals or barrier semaphores. Data moves between devices by JAX's collectives and lax.ppermute only.
A program may use at most 64 MiB of HBM per device.

v0:
```python
import jax
import jax.numpy as jnp
from jax import lax
from jax.sharding import PartitionSpec as P

step_size = 0.5
penalty = 0.1


def shifted(array, axis, by):
    devices = lax.axis_size(axis)
    return lax.ppermute(array, axis, [(i, (i + by) % devices) for i in range(devices)])


def from_root(array, axis, root):
    mine = lax.axis_index(axis) == root
    return lax.psum(jnp.where(mine, array, jnp.zeros_like(array)), axis)


def per_device(omega_rows, covariance_columns, tile_offsets):
    team_count = lax.axis_size("team")
    rep_count = lax.axis_size("rep")
    team_index = lax.axis_index("team")
    rep_index = lax.axis_index("rep")
    block_rows, part_width = omega_rows.shape
    tile_width = covariance_columns.shape[1]
    all_rows = block_rows * team_count
    rows_share = all_rows // rep_count
    offset = tile_offsets[0]
    owner = offset // part_width
    inside = jnp.clip(offset - rep_index * part_width, 0, part_width - tile_width)

    def place(collected, block, source):
        first = source * block_rows
        return lax.dynamic_update_slice_in_dim(collected, block, first, 0)

    empty = jnp.zeros((all_rows, part_width), jnp.float32)

    def advance(shift_count, carry):
        block, collected = carry
        block = shifted(block, "team", 1)
        source = (team_index - shift_count) % team_count
        return (block, place(collected, block, source))

    final = lax.fori_loop(
        1, team_count, advance, (omega_rows, place(empty, omega_rows, team_index))
    )
    collected = final[1]
    partial_value = jnp.dot(
        collected,
        covariance_columns,
        preferred_element_type=jnp.float32,
        precision=lax.Precision.HIGHEST,
    )
    values = lax.dynamic_slice_in_dim(collected, inside, tile_width, 1)
    summed = lax.psum_scatter(partial_value, "rep", scatter_dimension=0, tiled=True)
    everyone = from_root(values, "rep", owner)
    current = lax.dynamic_slice_in_dim(everyone, rep_index * rows_share, rows_share, 0)
    global_rows = rep_index * rows_share + jnp.arange(rows_share, dtype=jnp.int32)
    global_cols = offset + jnp.arange(tile_width, dtype=jnp.int32)
    diagonal = global_rows[:, None] == global_cols[None, :]
    safe = jnp.where(diagonal, current, jnp.float32(1.0))
    gradient = summed - jnp.where(diagonal, 1.0 / safe, jnp.float32(0.0))
    moved = current - step_size * gradient
    shrunk = jnp.sign(moved) * jnp.maximum(jnp.abs(moved) - step_size * penalty, 0.0)
    return jnp.where(diagonal, moved, shrunk)


def solution(mesh):
    in_specs = (P(("groups", "team"), "rep"), P("rep", ("groups", "team")), P(("groups", "team")))
    out_specs = P("rep", ("groups", "team"))
    return jax.shard_map(
        per_device, mesh=mesh, in_specs=in_specs, out_specs=out_specs, check_vma=False
    )
```

profile of v0, /device:TPU:0, one launch (start us, length us, event | category | flops | bytes accessed | tf_op | source)
XLA Modules:
  0.0 114.8 jit_solution(6271310564918737601)
XLA Ops:
  6.5 0.0 all-reduce.2.cloned.1.call-start
  6.5 1.0 copy.18
  8.3 0.1 broadcast_in_dim.13
  8.5 46.3 %while.17 = (s32[]{:T(128)}, f32[16,8192]{1,0:T(8,128)S(1)}, f32[64,8192]{1,0:T(8,128)S(1)}, s32[]{:T(128)}, s32[]{:T(128)}, /*index=5*/s32[]{:T(128)}, s32[]{:T(128)}, s32[]{:T(128)}, s32[]{:T(128)}, s32[]{:T(128)}) while((s32[]{:T(128)}, f32[16,8192]{1,0:T(8,128)S(1)}, f32[64,8192]{1,0:T(8,128)S(1)}, s32[]{:T(128)}, s32[]{:T(128)}, ...), condition=%wide.region_1.2_spmd, body=%wide.region_0.1_spmd.sunk | while | flops 18 | bytes 4194616 | solution.py:45
  8.5 3.1 %collective-permute-start = (f32[16,8192]{1,0:T(8,128)S(1)}, f32[16,8192]{1,0:T(8,128)S(1)}, u32[]{:S(2)}, u32[]{:S(2)}) collective-permute-start(f32[16,8192]{1,0:T(8,128)S(1)} %get-tuple-element.161), channel_id=1, source_target_pairs={{0,4},{4,8},{8,12},{12,0},{1,5},{5,9},{9,13},{13,1},{2,6},{6,10},{... | collective-permute-start | bytes 1572872 | tf_op jit(solution)/shard_map/while/body/eval_jaxpr/ppermute | solution.py:12
  11.5 13.9 %collective-permute-done = f32[16,8192]{1,0:T(8,128)S(1)} collective-permute-done((f32[16,8192]{1,0:T(8,128)S(1)}, f32[16,8192]{1,0:T(8,128)S(1)}, u32[]{:S(2)}, u32[]{:S(2)}) %collective-permute-start) | collective-permute-done | bytes 524320 | tf_op jit(solution)/shard_map/while/body/eval_jaxpr/ppermute | solution.py:12
  25.6 0.1 collective-permute-start
  25.7 14.9 %collective-permute-done = f32[16,8192]{1,0:T(8,128)S(1)} collective-permute-done((f32[16,8192]{1,0:T(8,128)S(1)}, f32[16,8192]{1,0:T(8,128)S(1)}, u32[]{:S(2)}, u32[]{:S(2)}) %collective-permute-start) | collective-permute-done | bytes 524320 | tf_op jit(solution)/shard_map/while/body/eval_jaxpr/ppermute | solution.py:12
  40.7 0.1 collective-permute-start
  40.7 13.9 %collective-permute-done = f32[16,8192]{1,0:T(8,128)S(1)} collective-permute-done((f32[16,8192]{1,0:T(8,128)S(1)}, f32[16,8192]{1,0:T(8,128)S(1)}, u32[]{:S(2)}, u32[]{:S(2)}) %collective-permute-start) | collective-permute-done | bytes 524320 | tf_op jit(solution)/shard_map/while/body/eval_jaxpr/ppermute | solution.py:12
  54.8 0.7 dynamic-slice_select_fusion
  55.5 0.0 all-reduce.2.cloned.1.call-update
  55.5 0.0 reduce-scatter.2.cloned.1.call-start
  55.6 7.3 %fusion.4 = f32[64,256]{1,0:T(8,128)} fusion(f32[64,8192]{1,0:T(8,128)S(1)} %get-tuple-element.116, f32[8192,256]{1,0:T(8,128)} %param.6), kind=kOutput, calls=%fused_computation.12 | convolution fusion | flops 1610612736 | bytes 10551296 | tf_op jit(solution)/shard_map/dot_general | solution.py:49
  62.9 0.0 reduce-scatter.2.cloned.1.call-update
  63.0 21.5 %all-reduce.2.cloned.1.call-done = f32[64,256]{1,0:T(8,128)} async-done(((f32[64,256]{1,0:T(8,128)}), f32[64,256]{1,0:T(8,128)}) %all-reduce.2.cloned.1.call-update) | async-done | bytes 65552 | tf_op jit(solution)/shard_map/psum | solution.py:17
  84.5 22.0 %reduce-scatter.2.cloned.1.call-done = f32[16,256]{1,0:T(8,128)} async-done(((f32[64,256]{1,0:T(8,128)}), f32[16,256]{1,0:T(8,128)}) %reduce-scatter.2.cloned.1.call-update) | async-done | bytes 16400 | tf_op jit(solution)/shard_map/reduce_scatter | solution.py:56
  106.5 1.4 %compare_select_fusion = f32[16,256]{1,0:T(8,128)} fusion(f32[16,256]{1,0:T(8,128)} %reduce-scatter.2.cloned.1.call-done, f32[64,256]{1,0:T(8,128)} %all-reduce.2.cloned.1.call-done, s32[]{:T(128)S(6)} %select_n.64, s32[256]{0:T(256)S(1)} %iota_add_fusion, s32[16]{0:T(128)S(1)} %iota_add_fusion.1), kind=kLoop, calls=%fused_computation.2 | loop fusion | flops 53248 | bytes 50244 | tf_op jit(solution)/shard_map/jit(_where)/select_n | solution.py:66
  (9 shorter events, 0.3 us)
Async XLA Ops:
  6.5 78.0 %all-reduce.2.cloned.1.call-start = ((), (), s32[]{:S(2)}) async-start(), calls=%async_computation.1 | async-start | bytes 131072 | tf_op jit(solution)/shard_map/psum | solution.py:17
  8.5 17.0 %collective-permute-start = (f32[16,8192]{1,0:T(8,128)S(1)}, f32[16,8192]{1,0:T(8,128)S(1)}, u32[]{:S(2)}, u32[]{:S(2)}) collective-permute-start(f32[16,8192]{1,0:T(8,128)S(1)} %get-tuple-element.161), channel_id=1, source_target_pairs={{0,4},{4,8},{8,12},{12,0},{1,5},{5,9},{9,13},{13,1},{2,6},{6,10},{... | collective-permute-start | bytes 1572872 | tf_op jit(solution)/shard_map/while/body/eval_jaxpr/ppermute | solution.py:12
  25.6 15.0 %collective-permute-start = (f32[16,8192]{1,0:T(8,128)S(1)}, f32[16,8192]{1,0:T(8,128)S(1)}, u32[]{:S(2)}, u32[]{:S(2)}) collective-permute-start(f32[16,8192]{1,0:T(8,128)S(1)} %get-tuple-element.161), channel_id=1, source_target_pairs={{0,4},{4,8},{8,12},{12,0},{1,5},{5,9},{9,13},{13,1},{2,6},{6,10},{... | collective-permute-start | bytes 1572872 | tf_op jit(solution)/shard_map/while/body/eval_jaxpr/ppermute | solution.py:12
  40.7 14.0 %collective-permute-start = (f32[16,8192]{1,0:T(8,128)S(1)}, f32[16,8192]{1,0:T(8,128)S(1)}, u32[]{:S(2)}, u32[]{:S(2)}) collective-permute-start(f32[16,8192]{1,0:T(8,128)S(1)} %get-tuple-element.161), channel_id=1, source_target_pairs={{0,4},{4,8},{8,12},{12,0},{1,5},{5,9},{9,13},{13,1},{2,6},{6,10},{... | collective-permute-start | bytes 1572872 | tf_op jit(solution)/shard_map/while/body/eval_jaxpr/ppermute | solution.py:12
  55.5 51.0 %reduce-scatter.2.cloned.1.call-start = ((), (), s32[]{:S(2)}) async-start(), calls=%async_computation.2 | async-start | bytes 81920 | tf_op jit(solution)/shard_map/reduce_scatter | solution.py:56
Sparse Core Ops, SparseCore 0:
  55.7 28.7 all-reduce.1
  87.0 19.4 reduce-scatter.1
where the time goes:
time: 115 us
  waiting for transfers between devices  86.4 us (75%)
  between operations  14.1 us (12%)
  matrix products  7.33 us (6%)
  starting transfers between devices  3.24 us (3%)
  other arithmetic  2.16 us (2%)
  local copies, waits for them, and re-layouts  1.45 us (1%)
    ppermute x3, waiting for transfers between devices, shifted(): lax.ppermute(array, axis, [(i, (i + by) % devices) for i in range(devices)])  42.8 us
    reduce_scatter x1, waiting for transfers between devices, per_device(): lax.psum_scatter(partial_value, 'rep', scatter_dimension=0, tiled=True)  22 us
    psum x1, waiting for transfers between devices, from_root(): return lax.psum(jnp.where(mine, array, jnp.zeros_like(array)), axis)  21.5 us
    dot_general x1, matrix products, per_device(): jnp.dot(collected, covariance_columns, preferred_element_type=jnp.float32...  7.33 us
    ppermute x3, starting transfers between devices, shifted(): lax.ppermute(array, axis, [(i, (i + by) % devices) for i in range(devices)])  3.19 us
  transfers between devices with their start and end apart: 5, of which 5 were waited for; matrix products, arithmetic and copies ran while one was open for 6% of the time, Pallas kernels for 0%

commit v1 on v0

v1 whole, which is shorter than its diff:
```python
import jax
import jax.numpy as jnp
from jax import lax
from jax.sharding import PartitionSpec as P

step_size = 0.5
penalty = 0.1
largest_bf16 = 3.3895313892515355e38


def halves(array):
    high = lax.reduce_precision(jnp.clip(array, -largest_bf16, largest_bf16), 8, 7)
    return high.astype(jnp.bfloat16), (array - high).astype(jnp.bfloat16)


def product_of(block, weights):
    high, low = halves(block)
    rows = block.shape[0]
    both = jnp.dot(
        jnp.concatenate([high, low], 0), weights[0], preferred_element_type=jnp.float32
    )
    cross = jnp.dot(high, weights[1], preferred_element_type=jnp.float32)
    return both[:rows] + both[rows:] + cross


def sum_of(terms):
    total = terms[0]
    for term in terms[1:]:
        total = total + term
    return total


def per_device(omega_rows, covariance_columns, tile_offsets):
    team_count = lax.axis_size("team")
    rep_count = lax.axis_size("rep")
    team_index = lax.axis_index("team")
    rep_index = lax.axis_index("rep")
    block_rows, part_width = omega_rows.shape
    tile_width = covariance_columns.shape[1]
    all_rows = block_rows * team_count
    rows_share = all_rows // rep_count
    offset = tile_offsets[0]
    chunks = 2 if team_count <= 4 else 1
    width = part_width // chunks
    assert all_rows <= width and width % tile_width == 0

    weights = []
    for c in range(chunks):
        columns = covariance_columns[c * width : (c + 1) * width]
        k_ids = rep_index * part_width + c * width + jnp.arange(width, dtype=jnp.int32)
        c_ids = offset + jnp.arange(tile_width, dtype=jnp.int32)
        chosen = (k_ids[:, None] == c_ids[None, :]).astype(jnp.float32)
        weights.append(halves(chosen - step_size * columns))

    def inverse_diagonal(first_chunk, source):
        start = jnp.clip(offset, 0, width - tile_width)
        values = lax.dynamic_slice_in_dim(first_chunk, start, tile_width, 1)
        row_ids = source * block_rows + jnp.arange(block_rows, dtype=jnp.int32)
        c_ids = offset + jnp.arange(tile_width, dtype=jnp.int32)
        mask = (row_ids[:, None] == c_ids[None, :]) & (rep_index == 0)
        return jnp.where(mask, step_size / jnp.where(mask, values, 1.0), 0.0)

    own = [omega_rows[:, c * width : (c + 1) * width] for c in range(chunks)]
    slots = []

    def add_slot(parts, source, valid):
        terms = [product_of(parts[c], weights[c]) for c in range(chunks)]
        terms.append(inverse_diagonal(parts[0], source))
        slots.append((sum_of(terms), jnp.where(valid, source, -1)))

    add_slot(own, team_index, True)
    right, left = own, own
    for step in range(1, team_count):
        to_right = [(d, d + 1) for d in range(step - 1, team_count - 1)]
        to_left = [(d, d - 1) for d in range(1, team_count - step + 1)]
        right, left = (
            [lax.ppermute(part, "team", to_right) for part in right],
            [lax.ppermute(part, "team", to_left) for part in left],
        )
        from_left = team_index >= step
        if 2 * step < team_count:
            add_slot(right, team_index - step, from_left)
            add_slot(left, team_index + step, team_index + step < team_count)
        else:
            merged = [jnp.where(from_left, r, l) for r, l in zip(right, left)]
            source = jnp.where(from_left, team_index - step, team_index + step)
            add_slot(merged, source, from_left | (source < team_count))

    blocks = []
    for b in range(team_count):
        value = jnp.zeros((block_rows, tile_width), jnp.float32)
        for slot, source in slots:
            value = jnp.where(source == b, slot, value)
        blocks.append(value)
    partial_moved = jnp.concatenate(blocks, 0)

    terms = []
    for by in range(rep_count):
        target = (rep_index + by) % rep_count
        part = lax.dynamic_slice_in_dim(partial_moved, target * rows_share, rows_share, 0)
        if by:
            pairs = [(d, (d + by) % rep_count) for d in range(rep_count)]
            part = lax.ppermute(part, "rep", pairs)
        terms.append(part)
    moved = sum_of(terms)

    global_rows = rep_index * rows_share + jnp.arange(rows_share, dtype=jnp.int32)
    global_cols = offset + jnp.arange(tile_width, dtype=jnp.int32)
    diagonal = global_rows[:, None] == global_cols[None, :]
    shrunk = jnp.sign(moved) * jnp.maximum(jnp.abs(moved) - step_size * penalty, 0.0)
    return jnp.where(diagonal, moved, shrunk)


def solution(mesh):
    in_specs = (P(("groups", "team"), "rep"), P("rep", ("groups", "team")), P(("groups", "team")))
    out_specs = P("rep", ("groups", "team"))
    return jax.shard_map(
        per_device, mesh=mesh, in_specs=in_specs, out_specs=out_specs, check_vma=False
    )
```

time: 115 us -> 73.3 us (0.64)
  waiting for transfers between devices: 86.4 us -> 23.4 us
  starting transfers between devices: 3.24 us -> 23.7 us
  between operations: 14.1 us -> 1.09 us
  other arithmetic: 2.16 us -> 11.9 us
  matrix products: 7.33 us -> 10.2 us
    reduce_scatter x1 -> x0, waiting for transfers between devices: 22 us -> none  [per_device(): lax.psum_scatter(partial_value, 'rep', scatter_dimension=0, tiled=True)]
    psum x1 -> x0, waiting for transfers between devices: 21.5 us -> none  [from_root(): return lax.psum(jnp.where(mine, array, jnp.zeros_like(array)), axis)]
    ppermute x3 -> x15, starting transfers between devices: 3.19 us -> 23.7 us  [the longest x6 12.9 us: per_device(): lax.ppermute(part, 'team', to_right)]
    ppermute x3 -> x15, waiting for transfers between devices: 42.8 us -> 23.4 us  [the longest x6 21.9 us: per_device(): lax.ppermute(part, 'team', to_left)]
    convert_element_type x0 -> x12, other arithmetic: none -> 11.2 us  [halves(): return (high.astype(jnp.bfloat16), (array - high).astype(jnp.bfloat16))]
    dot_general x1 -> x20, matrix products: 7.33 us -> 10.2 us  [the longest x10 6.34 us: product_of(): jnp.dot(jnp.concatenate([high, low], 0), weights[0], preferred_element_ty...]
    unnamed x1 -> x10, local copies, waits for them, and re-layouts: 1.04 us -> 2.22 us
  transfers between devices with their start and end apart: 5 -> 15, of which waited for: 5 -> 7; matrix products, arithmetic and copies ran while one was open for 6% -> 25% of each run, Pallas kernels for 0% -> 0%
where the time goes in v1:
time: 73.3 us; the launch traced here: 72.5 us
  starting transfers between devices  23.7 us (32%)
  waiting for transfers between devices  23.4 us (32%)
  other arithmetic  11.9 us (16%)
  matrix products  10.2 us (14%)
  local copies, waits for them, and re-layouts  2.23 us (3%)
  between operations  1.09 us (1%)
    ppermute x6, waiting for transfers between devices, per_device(): lax.ppermute(part, 'team', to_left)  21.9 us
    ppermute x6, starting transfers between devices, per_device(): lax.ppermute(part, 'team', to_right)  12.9 us
    convert_element_type x12, other arithmetic, halves(): return (high.astype(jnp.bfloat16), (array - high).astype(jnp.bfloat16))  11.2 us
    ppermute x6, starting transfers between devices, per_device(): lax.ppermute(part, 'team', to_left)  7.74 us
    dot_general x10, matrix products, product_of(): jnp.dot(jnp.concatenate([high, low], 0), weights[0], preferred_element_ty...  6.34 us
    dot_general x10, matrix products, product_of(): cross = jnp.dot(high, weights[1], preferred_element_type=jnp.float32)  3.9 us
    ppermute x3, starting transfers between devices, per_device(): part = lax.ppermute(part, 'rep', pairs)  3 us
    unnamed x10, local copies, waits for them, and re-layouts  2.22 us
  transfers between devices with their start and end apart: 15, of which 7 were waited for; matrix products, arithmetic and copies ran while one was open for 25% of the time, Pallas kernels for 0%

profile of v1, /device:TPU:0, one launch (start us, length us, event | category | flops | bytes accessed | tf_op | source)
XLA Modules:
  0.0 72.5 jit_solution(16457546246810985580)
XLA Ops:
  0.0 1.8 %subtract_convert_fusion.2 = (bf16[16,4096]{1,0:T(8,128)(2,1)S(1)}, bf16[16,4096]{1,0:T(8,128)(2,1)S(1)}, bf16[16,4096]{1,0:T(8,128)(2,1)S(1)}, bf16[16,4096]{1,...) fusion(f32[16,8192]{1,0:T(8,128)} %param.3), kind=kLoop, calls=%fused_computation.68 | loop fusion | flops 655360 | bytes 1572864 | tf_op jit(solution)/shard_map/convert_element_type | solution.py:13
  1.8 5.6 %collective-permute-start.6 = (f32[16,4096]{1,0:T(8,128)}, f32[16,4096]{1,0:T(8,128)}, u32[]{:S(2)}, u32[]{:S(2)}) collective-permute-start(f32[16,4096]{1,0:T(8,128)} %get-tuple-element.19), channel_id=1, source_target_pairs={{0,4},{4,8},{8,12},{1,5},{5,9},{9,13},{2,6},{6,10},{10,14},{3,7},{... | collective-permute-start | bytes 786440 | tf_op jit(solution)/shard_map/ppermute | solution.py:77
  7.4 1.3 %collective-permute-start.9 = (f32[16,4096]{1,0:T(8,128)}, f32[16,4096]{1,0:T(8,128)}, u32[]{:S(2)}, u32[]{:S(2)}) collective-permute-start(f32[16,4096]{1,0:T(8,128)} %get-tuple-element.19), channel_id=1, source_target_pairs={{4,0},{8,4},{12,8},{5,1},{9,5},{13,9},{6,2},{10,6},{14,10},{7,3},{... | collective-permute-start | bytes 786440 | tf_op jit(solution)/shard_map/ppermute | solution.py:78
  8.7 4.6 %collective-permute-start = (f32[16,4096]{1,0:T(8,128)S(1)}, f32[16,4096]{1,0:T(8,128)S(1)}, u32[]{:S(2)}, u32[]{:S(2)}) collective-permute-start(f32[16,4096]{1,0:T(8,128)S(1)} %get-tuple-element.20), channel_id=1, source_target_pairs={{0,4},{4,8},{8,12},{1,5},{5,9},{9,13},{2,6},{6,10},{10,14},{3,7},{... | collective-permute-start | bytes 786440 | tf_op jit(solution)/shard_map/ppermute | solution.py:77
  13.3 1.3 %collective-permute-start.3 = (f32[16,4096]{1,0:T(8,128)S(1)}, f32[16,4096]{1,0:T(8,128)S(1)}, u32[]{:S(2)}, u32[]{:S(2)}) collective-permute-start(f32[16,4096]{1,0:T(8,128)S(1)} %get-tuple-element.20), channel_id=1, source_target_pairs={{4,0},{8,4},{12,8},{5,1},{9,5},{13,9},{6,2},{10,6},{14,10},{7,3},{... | collective-permute-start | bytes 786440 | tf_op jit(solution)/shard_map/ppermute | solution.py:78
  15.5 7.1 %fusion = (bf16[4096,256]{1,0:T(8,128)(2,1)}, bf16[4096,256]{1,0:T(8,128)(2,1)S(1)}, bf16[4096,256]{1,0:T(8,128)(2,1)S(1)}, bf16[4096,256]{1,0:T(8,128)(2,1)S(1)}) fusion(f32[8192,256]{1,0:T(8,128)} %param.4, s32[256]{0:T(256)S(1)} %iota_add_fusion.2, s32[4096]{0:T(1024)S(1)} %get-tuple-element.41, s32[4096]{0:T(1024)S(1)} %get-tuple-element.42), kind=kLoop, calls=%fused_computation.2 | loop fusion | flops 18874368 | bytes 16811008 | tf_op jit(solution)/shard_map/convert_element_type | solution.py:13
  22.6 0.0 copy-start.3
  22.6 0.0 copy-start.1
  22.6 1.3 %copy-done.3 = bf16[4096,256]{1,0:T(8,128)(2,1)} copy-done((bf16[4096,256]{1,0:T(8,128)(2,1)}, bf16[4096,256]{1,0:T(8,128)(2,1)S(1)}, u32[]{:S(2)}) %copy-start.3) | copy-done | bytes 2097176
  23.9 0.5 fusion.44
  24.4 0.2 copy-done.1
  24.6 0.4 convolution_add_fusion.1
  25.0 0.0 copy-start
  25.0 2.2 %fusion.48 = f32[32,256]{1,0:T(8,128)S(1)} fusion(bf16[4096,256]{1,0:T(8,128)(2,1)} %get-tuple-element.9, bf16[16,4096]{1,0:T(8,128)(2,1)S(1)} %get-tuple-element.15, bf16[16,4096]{1,0:T(8,128)(2,1)S(1)} %get-tuple-element.18), kind=kOutput, calls=%fused_computation.64 | convolution fusion | flops 67633152 | bytes 2392064 | tf_op jit(solution)/shard_map/dot_general | solution.py:19
  27.2 0.4 fusion.3
  27.6 0.0 collective-permute-done.6
  27.6 1.0 %subtract_convert_fusion.4 = (bf16[16,4096]{1,0:T(8,128)(2,1)S(1)}, bf16[16,4096]{1,0:T(8,128)(2,1)S(1)}) fusion(f32[16,4096]{1,0:T(8,128)} %collective-permute-done.6), kind=kLoop, calls=%fused_computation.74 | loop fusion | flops 327680 | bytes 524288 | tf_op jit(solution)/shard_map/convert_element_type | solution.py:13
  28.6 0.0 copy-done
  28.6 0.5 fusion.40
  29.0 0.4 convolution_add_fusion.2
  29.4 0.0 collective-permute-done.9
  29.4 1.0 %subtract_convert_fusion.6 = (bf16[16,4096]{1,0:T(8,128)(2,1)S(1)}, bf16[16,4096]{1,0:T(8,128)(2,1)S(1)}) fusion(f32[16,4096]{1,0:T(8,128)} %collective-permute-done.9), kind=kLoop, calls=%fused_computation.80 | loop fusion | flops 327680 | bytes 524288 | tf_op jit(solution)/shard_map/convert_element_type | solution.py:13
  30.4 0.0 copy-start.4
  30.4 0.5 fusion.32
  30.9 0.4 convolution_add_fusion.4
  31.3 0.0 collective-permute-done
  31.4 0.7 copy-done.4
  32.0 0.5 fusion.36
  32.5 0.0 collective-permute-done.3
  32.6 0.5 fusion.28
  33.0 0.7 collective-permute-start.1
  33.7 1.3 %collective-permute-start.4 = (f32[16,4096]{1,0:T(8,128)S(1)}, f32[16,4096]{1,0:T(8,128)S(1)}, u32[]{:S(2)}, u32[]{:S(2)}) collective-permute-start(f32[16,4096]{1,0:T(8,128)S(1)} %collective-permute-done.3), channel_id=1, source_target_pairs={{4,0},{8,4},{5,1},{9,5},{6,2},{10,6},{7,3},{11,7},{20,16},{24,20},... | collective-permute-start | bytes 786440 | tf_op jit(solution)/shard_map/ppermute | solution.py:78
  35.0 1.3 %collective-permute-start.10 = (f32[16,4096]{1,0:T(8,128)}, f32[16,4096]{1,0:T(8,128)S(1)}, u32[]{:S(2)}, u32[]{:S(2)}) collective-permute-start(f32[16,4096]{1,0:T(8,128)} %collective-permute-done.9), channel_id=1, source_target_pairs={{4,0},{8,4},{5,1},{9,5},{6,2},{10,6},{7,3},{11,7},{20,16},{24,20},... | collective-permute-start | bytes 786440 | tf_op jit(solution)/shard_map/ppermute | solution.py:78
  36.3 0.7 collective-permute-start.7
  37.0 0.0 copy-done.2
  37.0 0.4 fusion.5
  37.4 0.4 fusion.7
  37.8 0.0 collective-permute-done.1
  37.8 10.1 %collective-permute-done.4 = f32[16,4096]{1,0:T(8,128)S(1)} collective-permute-done((f32[16,4096]{1,0:T(8,128)S(1)}, f32[16,4096]{1,0:T(8,128)S(1)}, u32[]{:S(2)}, u32[]{:S(2)}) %collective-permute-start.4) | collective-permute-done | bytes 262176 | tf_op jit(solution)/shard_map/ppermute | solution.py:78
  47.9 0.5 fusion.20
  48.4 0.4 convolution_add_fusion.7
  48.8 2.7 %collective-permute-done.10 = f32[16,4096]{1,0:T(8,128)S(1)} collective-permute-done((f32[16,4096]{1,0:T(8,128)}, f32[16,4096]{1,0:T(8,128)S(1)}, u32[]{:S(2)}, u32[]{:S(2)}) %collective-permute-start.10) | collective-permute-done | bytes 262176 | tf_op jit(solution)/shard_map/ppermute | solution.py:78
  51.4 0.0 collective-permute-done.7
  51.5 0.5 fusion.24
  51.9 0.7 collective-permute-start.2
  52.6 1.3 %collective-permute-start.5 = (f32[16,4096]{1,0:T(8,128)S(1)}, f32[16,4096]{1,0:T(8,128)S(1)}, u32[]{:S(2)}, u32[]{:S(2)}) collective-permute-start(f32[16,4096]{1,0:T(8,128)S(1)} %collective-permute-done.4), channel_id=1, source_target_pairs={{4,0},{5,1},{6,2},{7,3},{20,16},{21,17},{22,18},{23,19}} | collective-permute-start | bytes 786440 | tf_op jit(solution)/shard_map/ppermute | solution.py:78
  53.9 1.3 %collective-permute-start.11 = (f32[16,4096]{1,0:T(8,128)S(1)}, f32[16,4096]{1,0:T(8,128)S(1)}, u32[]{:S(2)}, u32[]{:S(2)}) collective-permute-start(f32[16,4096]{1,0:T(8,128)S(1)} %collective-permute-done.10), channel_id=1, source_target_pairs={{4,0},{5,1},{6,2},{7,3},{20,16},{21,17},{22,18},{23,19}} | collective-permute-start | bytes 786440 | tf_op jit(solution)/shard_map/ppermute | solution.py:78
  55.2 0.7 collective-permute-start.8
  55.9 0.4 fusion.9
  56.3 0.0 collective-permute-done.2
  56.3 7.3 %collective-permute-done.5 = f32[16,4096]{1,0:T(8,128)S(1)} collective-permute-done((f32[16,4096]{1,0:T(8,128)S(1)}, f32[16,4096]{1,0:T(8,128)S(1)}, u32[]{:S(2)}, u32[]{:S(2)}) %collective-permute-start.5) | collective-permute-done | bytes 262176 | tf_op jit(solution)/shard_map/ppermute | solution.py:78
  63.7 0.5 fusion.12
  64.1 0.4 convolution_add_fusion.9
  64.5 1.9 %collective-permute-done.11 = f32[16,4096]{1,0:T(8,128)S(1)} collective-permute-done((f32[16,4096]{1,0:T(8,128)S(1)}, f32[16,4096]{1,0:T(8,128)S(1)}, u32[]{:S(2)}, u32[]{:S(2)}) %collective-permute-start.11) | collective-permute-done | bytes 262176 | tf_op jit(solution)/shard_map/ppermute | solution.py:78
  66.4 0.0 collective-permute-done.8
  66.5 0.5 fusion.16
  66.9 0.4 select_select_fusion.3
  67.4 0.1 collective-permute-start.12
  67.4 1.6 %collective-permute-start.13 = (f32[16,256]{1,0:T(8,128)S(1)}, f32[16,256]{1,0:T(8,128)S(1)}, u32[]{:S(2)}, u32[]{:S(2)}) collective-permute-start(f32[16,256]{1,0:T(8,128)S(1)} %get-tuple-element.39), channel_id=1, source_target_pairs={{0,2},{1,3},{2,0},{3,1},{4,6},{5,7},{6,4},{7,5},{8,10},{9,11},{10,... | collective-permute-start | bytes 49160 | tf_op jit(solution)/shard_map/ppermute | solution.py:103
  69.0 1.4 %collective-permute-start.14 = (f32[16,256]{1,0:T(8,128)S(1)}, f32[16,256]{1,0:T(8,128)S(1)}, u32[]{:S(2)}, u32[]{:S(2)}) collective-permute-start(f32[16,256]{1,0:T(8,128)S(1)} %get-tuple-element.38), channel_id=1, source_target_pairs={{0,3},{1,0},{2,1},{3,2},{4,7},{5,4},{6,5},{7,6},{8,11},{9,8},{10,9... | collective-permute-start | bytes 49160 | tf_op jit(solution)/shard_map/ppermute | solution.py:103
  70.4 0.2 collective-permute-done.12
  70.6 0.7 collective-permute-done.13
  71.3 0.6 collective-permute-done.14
  71.8 0.7 multiply_select_fusion
  (20 shorter events, 0.4 us)
Async XLA Ops:
  1.8 25.8 %collective-permute-start.6 = (f32[16,4096]{1,0:T(8,128)}, f32[16,4096]{1,0:T(8,128)}, u32[]{:S(2)}, u32[]{:S(2)}) collective-permute-start(f32[16,4096]{1,0:T(8,128)} %get-tuple-element.19), channel_id=1, source_target_pairs={{0,4},{4,8},{8,12},{1,5},{5,9},{9,13},{2,6},{6,10},{10,14},{3,7},{... | collective-permute-start | bytes 786440 | tf_op jit(solution)/shard_map/ppermute | solution.py:77
  7.4 22.0 %collective-permute-start.9 = (f32[16,4096]{1,0:T(8,128)}, f32[16,4096]{1,0:T(8,128)}, u32[]{:S(2)}, u32[]{:S(2)}) collective-permute-start(f32[16,4096]{1,0:T(8,128)} %get-tuple-element.19), channel_id=1, source_target_pairs={{4,0},{8,4},{12,8},{5,1},{9,5},{13,9},{6,2},{10,6},{14,10},{7,3},{... | collective-permute-start | bytes 786440 | tf_op jit(solution)/shard_map/ppermute | solution.py:78
  8.7 22.6 %collective-permute-start = (f32[16,4096]{1,0:T(8,128)S(1)}, f32[16,4096]{1,0:T(8,128)S(1)}, u32[]{:S(2)}, u32[]{:S(2)}) collective-permute-start(f32[16,4096]{1,0:T(8,128)S(1)} %get-tuple-element.20), channel_id=1, source_target_pairs={{0,4},{4,8},{8,12},{1,5},{5,9},{9,13},{2,6},{6,10},{10,14},{3,7},{... | collective-permute-start | bytes 786440 | tf_op jit(solution)/shard_map/ppermute | solution.py:77
  13.3 19.2 %collective-permute-start.3 = (f32[16,4096]{1,0:T(8,128)S(1)}, f32[16,4096]{1,0:T(8,128)S(1)}, u32[]{:S(2)}, u32[]{:S(2)}) collective-permute-start(f32[16,4096]{1,0:T(8,128)S(1)} %get-tuple-element.20), channel_id=1, source_target_pairs={{4,0},{8,4},{12,8},{5,1},{9,5},{13,9},{6,2},{10,6},{14,10},{7,3},{... | collective-permute-start | bytes 786440 | tf_op jit(solution)/shard_map/ppermute | solution.py:78
  22.6 1.3 %copy-start.3 = (bf16[4096,256]{1,0:T(8,128)(2,1)}, bf16[4096,256]{1,0:T(8,128)(2,1)S(1)}, u32[]{:S(2)}) copy-start(bf16[4096,256]{1,0:T(8,128)(2,1)S(1)} %get-tuple-element.14) | copy-start | bytes 6291460
  22.6 2.0 %copy-start.1 = (bf16[4096,256]{1,0:T(8,128)(2,1)}, bf16[4096,256]{1,0:T(8,128)(2,1)S(1)}, u32[]{:S(2)}) copy-start(bf16[4096,256]{1,0:T(8,128)(2,1)S(1)} %get-tuple-element.13) | copy-start | bytes 6291460
  25.0 3.6 %copy-start = (bf16[4096,256]{1,0:T(8,128)(2,1)S(1)}, bf16[4096,256]{1,0:T(8,128)(2,1)}, u32[]{:S(2)}) copy-start(bf16[4096,256]{1,0:T(8,128)(2,1)} %get-tuple-element.9) | copy-start | bytes 6291460
  30.4 1.6 %copy-start.4 = (bf16[4096,256]{1,0:T(8,128)(2,1)S(1)}, bf16[4096,256]{1,0:T(8,128)(2,1)}, u32[]{:S(2)}) copy-start(bf16[4096,256]{1,0:T(8,128)(2,1)} %copy-done.3) | copy-start | bytes 6291460
  32.0 5.0 %copy-start.2 = (bf16[4096,256]{1,0:T(8,128)(2,1)S(1)}, bf16[4096,256]{1,0:T(8,128)(2,1)}, u32[]{:S(2)}) copy-start(bf16[4096,256]{1,0:T(8,128)(2,1)} %copy-done.1) | copy-start | bytes 6291460
  33.0 4.8 %collective-permute-start.1 = (f32[16,4096]{1,0:T(8,128)S(1)}, f32[16,4096]{1,0:T(8,128)S(1)}, u32[]{:S(2)}, u32[]{:S(2)}) collective-permute-start(f32[16,4096]{1,0:T(8,128)S(1)} %collective-permute-done), channel_id=1, source_target_pairs={{4,8},{8,12},{5,9},{9,13},{6,10},{10,14},{7,11},{11,15},{20,24},{2... | collective-permute-start | bytes 786440 | tf_op jit(solution)/shard_map/ppermute | solution.py:77
  33.7 14.1 %collective-permute-start.4 = (f32[16,4096]{1,0:T(8,128)S(1)}, f32[16,4096]{1,0:T(8,128)S(1)}, u32[]{:S(2)}, u32[]{:S(2)}) collective-permute-start(f32[16,4096]{1,0:T(8,128)S(1)} %collective-permute-done.3), channel_id=1, source_target_pairs={{4,0},{8,4},{5,1},{9,5},{6,2},{10,6},{7,3},{11,7},{20,16},{24,20},... | collective-permute-start | bytes 786440 | tf_op jit(solution)/shard_map/ppermute | solution.py:78
  35.0 16.4 %collective-permute-start.10 = (f32[16,4096]{1,0:T(8,128)}, f32[16,4096]{1,0:T(8,128)S(1)}, u32[]{:S(2)}, u32[]{:S(2)}) collective-permute-start(f32[16,4096]{1,0:T(8,128)} %collective-permute-done.9), channel_id=1, source_target_pairs={{4,0},{8,4},{5,1},{9,5},{6,2},{10,6},{7,3},{11,7},{20,16},{24,20},... | collective-permute-start | bytes 786440 | tf_op jit(solution)/shard_map/ppermute | solution.py:78
  36.3 15.1 %collective-permute-start.7 = (f32[16,4096]{1,0:T(8,128)}, f32[16,4096]{1,0:T(8,128)S(1)}, u32[]{:S(2)}, u32[]{:S(2)}) collective-permute-start(f32[16,4096]{1,0:T(8,128)} %collective-permute-done.6), channel_id=1, source_target_pairs={{4,8},{8,12},{5,9},{9,13},{6,10},{10,14},{7,11},{11,15},{20,24},{2... | collective-permute-start | bytes 786440 | tf_op jit(solution)/shard_map/ppermute | solution.py:77
  51.9 4.4 %collective-permute-start.2 = (f32[16,4096]{1,0:T(8,128)S(1)}, f32[16,4096]{1,0:T(8,128)S(1)}, u32[]{:S(2)}, u32[]{:S(2)}) collective-permute-start(f32[16,4096]{1,0:T(8,128)S(1)} %collective-permute-done.1), channel_id=1, source_target_pairs={{8,12},{9,13},{10,14},{11,15},{24,28},{25,29},{26,30},{27,31}} | collective-permute-start | bytes 786440 | tf_op jit(solution)/shard_map/ppermute | solution.py:77
  52.6 11.0 %collective-permute-start.5 = (f32[16,4096]{1,0:T(8,128)S(1)}, f32[16,4096]{1,0:T(8,128)S(1)}, u32[]{:S(2)}, u32[]{:S(2)}) collective-permute-start(f32[16,4096]{1,0:T(8,128)S(1)} %collective-permute-done.4), channel_id=1, source_target_pairs={{4,0},{5,1},{6,2},{7,3},{20,16},{21,17},{22,18},{23,19}} | collective-permute-start | bytes 786440 | tf_op jit(solution)/shard_map/ppermute | solution.py:78
  53.9 12.5 %collective-permute-start.11 = (f32[16,4096]{1,0:T(8,128)S(1)}, f32[16,4096]{1,0:T(8,128)S(1)}, u32[]{:S(2)}, u32[]{:S(2)}) collective-permute-start(f32[16,4096]{1,0:T(8,128)S(1)} %collective-permute-done.10), channel_id=1, source_target_pairs={{4,0},{5,1},{6,2},{7,3},{20,16},{21,17},{22,18},{23,19}} | collective-permute-start | bytes 786440 | tf_op jit(solution)/shard_map/ppermute | solution.py:78
  55.2 11.2 %collective-permute-start.8 = (f32[16,4096]{1,0:T(8,128)S(1)}, f32[16,4096]{1,0:T(8,128)S(1)}, u32[]{:S(2)}, u32[]{:S(2)}) collective-permute-start(f32[16,4096]{1,0:T(8,128)S(1)} %collective-permute-done.7), channel_id=1, source_target_pairs={{8,12},{9,13},{10,14},{11,15},{24,28},{25,29},{26,30},{27,31}} | collective-permute-start | bytes 786440 | tf_op jit(solution)/shard_map/ppermute | solution.py:77
  67.4 3.2 %collective-permute-start.12 = (f32[16,256]{1,0:T(8,128)S(1)}, f32[16,256]{1,0:T(8,128)S(1)}, u32[]{:S(2)}, u32[]{:S(2)}) collective-permute-start(f32[16,256]{1,0:T(8,128)S(1)} %get-tuple-element.37), channel_id=1, source_target_pairs={{0,1},{1,2},{2,3},{3,0},{4,5},{5,6},{6,7},{7,4},{8,9},{9,10},{10,1... | collective-permute-start | bytes 49160 | tf_op jit(solution)/shard_map/ppermute | solution.py:103
  67.4 3.8 %collective-permute-start.13 = (f32[16,256]{1,0:T(8,128)S(1)}, f32[16,256]{1,0:T(8,128)S(1)}, u32[]{:S(2)}, u32[]{:S(2)}) collective-permute-start(f32[16,256]{1,0:T(8,128)S(1)} %get-tuple-element.39), channel_id=1, source_target_pairs={{0,2},{1,3},{2,0},{3,1},{4,6},{5,7},{6,4},{7,5},{8,10},{9,11},{10,... | collective-permute-start | bytes 49160 | tf_op jit(solution)/shard_map/ppermute | solution.py:103
  69.0 2.8 %collective-permute-start.14 = (f32[16,256]{1,0:T(8,128)S(1)}, f32[16,256]{1,0:T(8,128)S(1)}, u32[]{:S(2)}, u32[]{:S(2)}) collective-permute-start(f32[16,256]{1,0:T(8,128)S(1)} %get-tuple-element.38), channel_id=1, source_target_pairs={{0,3},{1,0},{2,1},{3,2},{4,7},{5,4},{6,5},{7,6},{8,11},{9,8},{10,9... | collective-permute-start | bytes 49160 | tf_op jit(solution)/shard_map/ppermute | solution.py:103

commit v2 on v1

--- a/solution.py
+++ b/solution.py
@@ -40,51 +40,53 @@
     all_rows = block_rows * team_count
     rows_share = all_rows // rep_count
     offset = tile_offsets[0]
-    chunks = 2 if team_count <= 4 else 1
-    width = part_width // chunks
-    assert all_rows <= width and width % tile_width == 0
+    assert all_rows <= part_width and part_width % tile_width == 0
 
-    weights = []
-    for c in range(chunks):
-        columns = covariance_columns[c * width : (c + 1) * width]
-        k_ids = rep_index * part_width + c * width + jnp.arange(width, dtype=jnp.int32)
-        c_ids = offset + jnp.arange(tile_width, dtype=jnp.int32)
-        chosen = (k_ids[:, None] == c_ids[None, :]).astype(jnp.float32)
-        weights.append(halves(chosen - step_size * columns))
+    k_ids = rep_index * part_width + jnp.arange(part_width, dtype=jnp.int32)
+    c_ids = offset + jnp.arange(tile_width, dtype=jnp.int32)
+    chosen = (k_ids[:, None] == c_ids[None, :]).astype(jnp.float32)
+    weights = halves(chosen - step_size * covariance_columns)
 
-    def inverse_diagonal(first_chunk, source):
-        start = jnp.clip(offset, 0, width - tile_width)
-        values = lax.dynamic_slice_in_dim(first_chunk, start, tile_width, 1)
+    def inverse_diagonal(block, source):
+        start = jnp.clip(offset, 0, part_width - tile_width)
+        values = lax.dynamic_slice_in_dim(block, start, tile_width, 1)
         row_ids = source * block_rows + jnp.arange(block_rows, dtype=jnp.int32)
-        c_ids = offset + jnp.arange(tile_width, dtype=jnp.int32)
         mask = (row_ids[:, None] == c_ids[None, :]) & (rep_index == 0)
         return jnp.where(mask, step_size / jnp.where(mask, values, 1.0), 0.0)
 
-    own = [omega_rows[:, c * width : (c + 1) * width] for c in range(chunks)]
     slots = []
 
-    def add_slot(parts, source, valid):
-        terms = [product_of(parts[c], weights[c]) for c in range(chunks)]
-        terms.append(inverse_diagonal(parts[0], source))
-        slots.append((sum_of(terms), jnp.where(valid, source, -1)))
+    def add_slot(block, source, valid=True):
+        moved_part = product_of(block, weights) + inverse_diagonal(block, source)
+        slots.append((moved_part, jnp.where(valid, source, -1)))
 
-    add_slot(own, team_index, True)
-    right, left = own, own
-    for step in range(1, team_count):
-        to_right = [(d, d + 1) for d in range(step - 1, team_count - 1)]
-        to_left = [(d, d - 1) for d in range(1, team_count - step + 1)]
-        right, left = (
-            [lax.ppermute(part, "team", to_right) for part in right],
-            [lax.ppermute(part, "team", to_left) for part in left],
-        )
-        from_left = team_index >= step
-        if 2 * step < team_count:
-            add_slot(right, team_index - step, from_left)
-            add_slot(left, team_index + step, team_index + step < team_count)
-        else:
-            merged = [jnp.where(from_left, r, l) for r, l in zip(right, left)]
-            source = jnp.where(from_left, team_index - step, team_index + step)
-            add_slot(merged, source, from_left | (source < team_count))
+    add_slot(omega_rows, team_index)
+    if team_count == 4:
+        across = lax.ppermute(omega_rows, "team", [(0, 2), (1, 3), (2, 0), (3, 1)])
+        pair = lax.ppermute(omega_rows, "team", [(0, 1), (1, 0), (2, 3), (3, 2)])
+        passed = lax.ppermute(across, "team", [(1, 0), (2, 3)])
+        own_later, _ = lax.optimization_barrier((omega_rows, across))
+        middle = lax.ppermute(own_later, "team", [(1, 2), (2, 1)])
+        add_slot(across, (team_index + 2) % 4)
+        add_slot(pair, team_index ^ 1)
+        is_end = (team_index == 0) | (team_index == 3)
+        add_slot(jnp.where(is_end, passed, middle), 3 - team_index)
+    else:
+        right, left = omega_rows, omega_rows
+        for step in range(1, team_count):
+            to_right = [(d, d + 1) for d in range(step - 1, team_count - 1)]
+            to_left = [(d, d - 1) for d in range(1, team_count - step + 1)]
+            right = lax.ppermute(right, "team", to_right)
+            left = lax.ppermute(left, "team", to_left)
+            from_left = team_index >= step
+            from_right = team_index + step < team_count
+            if 2 * step < team_count:
+                add_slot(right, team_index - step, from_left)
+                add_slot(left, team_index + step, from_right)
+            else:
+                merged = jnp.where(from_left, right, left)
+                source = jnp.where(from_left, team_index - step, team_index + step)
+                add_slot(merged, source, from_left | from_right)
 
     blocks = []
     for b in range(team_count):

time: 73.3 us -> 50.9 us (0.69)
  starting transfers between devices: 23.7 us -> 10.6 us
  matrix products: 10.2 us -> 5.96 us
  other arithmetic: 11.9 us -> 8.7 us
  local copies, waits for them, and re-layouts: 2.23 us -> 0.19 us
    ppermute x12 -> x4, starting transfers between devices: 20.7 us -> 7.59 us  [the longest x1 4.04 us: per_device(): across = lax.ppermute(omega_rows, 'team', [(0, 2), (1, 3), (2, 0), (3, 1)])]
    convert_element_type x12 -> x6, other arithmetic: 11.2 us -> 7.97 us  [halves(): return (high.astype(jnp.bfloat16), (array - high).astype(jnp.bfloat16))]
    dot_general x10 -> x4, matrix products: 6.34 us -> 3.31 us  [product_of(): jnp.dot(jnp.concatenate([high, low], 0), weights[0], preferred_element_ty...]
    unnamed x10 -> x2, local copies, waits for them, and re-layouts: 2.22 us -> 0.17 us
    dot_general x10 -> x4, matrix products: 3.9 us -> 2.65 us  [product_of(): cross = jnp.dot(high, weights[1], preferred_element_type=jnp.float32)]
    ppermute x12 -> x4, waiting for transfers between devices: 21.9 us -> 22.6 us  [the longest x1 11.6 us: per_device(): across = lax.ppermute(omega_rows, 'team', [(0, 2), (1, 3), (2, 0), (3, 1)])]
  transfers between devices with their start and end apart: 15 -> 7, of which waited for: 7 -> 5; matrix products, arithmetic and copies ran while one was open for 25% -> 25% of each run, Pallas kernels for 0% -> 0%
where the time goes in v2:
time: 50.9 us; the launch traced here: 50.4 us
  waiting for transfers between devices  24 us (47%)
  starting transfers between devices  10.6 us (21%)
  other arithmetic  8.7 us (17%)
  matrix products  5.96 us (12%)
  between operations  0.93 us (2%)
    ppermute x1, waiting for transfers between devices, per_device(): across = lax.ppermute(omega_rows, 'team', [(0, 2), (1, 3), (2, 0), (3, 1)])  11.6 us
    ppermute x1, waiting for transfers between devices, per_device(): passed = lax.ppermute(across, 'team', [(1, 0), (2, 3)])  10.9 us
    convert_element_type x6, other arithmetic, halves(): return (high.astype(jnp.bfloat16), (array - high).astype(jnp.bfloat16))  7.97 us
    ppermute x1, starting transfers between devices, per_device(): across = lax.ppermute(omega_rows, 'team', [(0, 2), (1, 3), (2, 0), (3, 1)])  4.04 us
    dot_general x4, matrix products, product_of(): jnp.dot(jnp.concatenate([high, low], 0), weights[0], preferred_element_ty...  3.31 us
    ppermute x3, starting transfers between devices, per_device(): part = lax.ppermute(part, 'rep', pairs)  3 us
    dot_general x4, matrix products, product_of(): cross = jnp.dot(high, weights[1], preferred_element_type=jnp.float32)  2.65 us
    ppermute x1, starting transfers between devices, per_device(): pair = lax.ppermute(omega_rows, 'team', [(0, 1), (1, 0), (2, 3), (3, 2)])  1.58 us
  transfers between devices with their start and end apart: 7, of which 5 were waited for; matrix products, arithmetic and copies ran while one was open for 25% of the time, Pallas kernels for 0%

profile of v2, /device:TPU:0, one launch (start us, length us, event | category | flops | bytes accessed | tf_op | source)
XLA Modules:
  0.0 50.4 jit_solution(10203711108040533631)
XLA Ops:
  0.0 4.0 %collective-permute-start = (f32[16,8192]{1,0:T(8,128)}, f32[16,8192]{1,0:T(8,128)S(1)}, u32[]{:S(2)}, u32[]{:S(2)}) collective-permute-start(f32[16,8192]{1,0:T(8,128)} %param.3), channel_id=1, source_target_pairs={{0,8},{4,12},{8,0},{12,4},{1,9},{5,13},{9,1},{13,5},{2,10},{6,14},... | collective-permute-start | bytes 1572872 | tf_op jit(solution)/shard_map/ppermute | solution.py:65
  4.0 1.6 %collective-permute-start.3 = (f32[16,8192]{1,0:T(8,128)}, f32[16,8192]{1,0:T(8,128)S(1)}, u32[]{:S(2)}, u32[]{:S(2)}) collective-permute-start(f32[16,8192]{1,0:T(8,128)} %param.3), channel_id=1, source_target_pairs={{0,4},{4,0},{8,12},{12,8},{1,5},{5,1},{9,13},{13,9},{2,6},{6,2},{1... | collective-permute-start | bytes 1572872 | tf_op jit(solution)/shard_map/ppermute | solution.py:66
  5.6 1.1 %subtract_convert_fusion.1 = (bf16[16,8192]{1,0:T(8,128)(2,1)S(1)}, bf16[16,8192]{1,0:T(8,128)(2,1)S(1)}) fusion(f32[16,8192]{1,0:T(8,128)} %param.3), kind=kLoop, calls=%fused_computation.28 | loop fusion | flops 655360 | bytes 1048576 | tf_op jit(solution)/shard_map/convert_element_type | solution.py:13
  7.6 6.6 %fusion = (bf16[8192,256]{1,0:T(8,128)(2,1)S(1)}, bf16[8192,256]{1,0:T(8,128)(2,1)S(1)}) fusion(f32[8192,256]{1,0:T(8,128)} %param.4, s32[256]{0:T(256)S(1)} %iota_add_fusion.1, s32[8192]{0:T(1024)S(1)} %iota_add_fusion), kind=kLoop, calls=%fused_computation.2 | loop fusion | flops 18874368 | bytes 16811008 | tf_op jit(solution)/shard_map/convert_element_type | solution.py:13
  14.2 0.0 copy-start
  14.2 0.8 %fusion.17 = f32[32,256]{1,0:T(8,128)S(1)} fusion(bf16[8192,256]{1,0:T(8,128)(2,1)S(1)} %get-tuple-element.9, bf16[16,8192]{1,0:T(8,128)(2,1)S(1)} %get-tuple-element.11, bf16[16,8192]{1,0:T(8,128)(2,1)S(1)} %get-tuple-element.12), kind=kOutput, calls=%fused_computation.24 | convolution fusion | flops 135266304 | bytes 4751360 | tf_op jit(solution)/shard_map/dot_general | solution.py:19
  15.0 0.2 copy-done
  15.2 0.7 %fusion.1 = f32[16,256]{1,0:T(8,128)S(1)} fusion(bf16[16,8192]{1,0:T(8,128)(2,1)S(1)} %get-tuple-element.12, bf16[8192,256]{1,0:T(8,128)(2,1)S(1)} %get-tuple-element.10, f32[32,256]{1,0:T(8,128)S(1)} %fusion.17, f32[16,8192]{1,0:T(8,128)S(1)} %copy-done, s32[]{:T(128)S(6)} %min.39, s32[256]{0:T(256)S(1)} %iota_add_fusion.1, s32[16]{0:T(128)S(1)} %iota_add_fusion.2, ...), kind=kOutput, calls=%fused_computation.5 | convolution fusion | flops 67141632 | bytes 4523077 | tf_op jit(solution)/shard_map/dot_general | solution.py:22
  15.9 11.6 %collective-permute-done = f32[16,8192]{1,0:T(8,128)S(1)} collective-permute-done((f32[16,8192]{1,0:T(8,128)}, f32[16,8192]{1,0:T(8,128)S(1)}, u32[]{:S(2)}, u32[]{:S(2)}) %collective-permute-start) | collective-permute-done | bytes 524320 | tf_op jit(solution)/shard_map/ppermute | solution.py:65
  27.5 0.7 %collective-permute-start.2 = (f32[16,8192]{1,0:T(8,128)S(1)}, f32[16,8192]{1,0:T(8,128)S(1)}, u32[]{:S(2)}, u32[]{:S(2)}) collective-permute-start(f32[16,8192]{1,0:T(8,128)S(1)} %copy-done), channel_id=1, source_target_pairs={{4,8},{8,4},{5,9},{9,5},{6,10},{10,6},{7,11},{11,7},{20,24},{24,20... | collective-permute-start | bytes 1572872 | tf_op jit(solution)/shard_map/ppermute | solution.py:69
  28.2 0.1 subtract_convert_fusion.2
  28.3 1.3 %collective-permute-start.1 = (f32[16,8192]{1,0:T(8,128)S(1)}, f32[16,8192]{1,0:T(8,128)S(1)}, u32[]{:S(2)}, u32[]{:S(2)}) collective-permute-start(f32[16,8192]{1,0:T(8,128)S(1)} %collective-permute-done), channel_id=1, source_target_pairs={{4,0},{8,12},{5,1},{9,13},{6,2},{10,14},{7,3},{11,15},{20,16},{24,... | collective-permute-start | bytes 1572872 | tf_op jit(solution)/shard_map/ppermute | solution.py:67
  29.6 0.8 %fusion.13 = f32[32,256]{1,0:T(8,128)S(1)} fusion(bf16[8192,256]{1,0:T(8,128)(2,1)S(1)} %get-tuple-element.9, bf16[16,8192]{1,0:T(8,128)(2,1)S(1)} %get-tuple-element.13, bf16[16,8192]{1,0:T(8,128)(2,1)S(1)} %get-tuple-element.14), kind=kOutput, calls=%fused_computation.20 | convolution fusion | flops 135266304 | bytes 4751360 | tf_op jit(solution)/shard_map/dot_general | solution.py:19
  30.4 0.0 collective-permute-done.3
  30.4 0.1 subtract_convert_fusion.3
  30.5 0.7 %fusion.2 = f32[16,256]{1,0:T(8,128)S(1)} fusion(bf16[16,8192]{1,0:T(8,128)(2,1)S(1)} %get-tuple-element.14, bf16[8192,256]{1,0:T(8,128)(2,1)S(1)} %get-tuple-element.10, f32[32,256]{1,0:T(8,128)S(1)} %fusion.13, f32[16,8192]{1,0:T(8,128)S(1)} %collective-permute-done, s32[]{:T(128)S(6)} %min.39, s32[256]{0:T(256)S(1)} %iota_add_fusion.1, ...), kind=kOutput, calls=%fused_computation.7 | convolution fusion | flops 67141632 | bytes 4523077 | tf_op jit(solution)/shard_map/dot_general | solution.py:22
  31.2 0.8 %fusion.9 = f32[32,256]{1,0:T(8,128)S(1)} fusion(bf16[8192,256]{1,0:T(8,128)(2,1)S(1)} %get-tuple-element.9, bf16[16,8192]{1,0:T(8,128)(2,1)S(1)} %get-tuple-element.15, bf16[16,8192]{1,0:T(8,128)(2,1)S(1)} %get-tuple-element.16), kind=kOutput, calls=%fused_computation.16 | convolution fusion | flops 135266304 | bytes 4751360 | tf_op jit(solution)/shard_map/dot_general | solution.py:19
  32.0 0.7 %fusion.3 = f32[16,256]{1,0:T(8,128)S(1)} fusion(bf16[16,8192]{1,0:T(8,128)(2,1)S(1)} %get-tuple-element.16, bf16[8192,256]{1,0:T(8,128)(2,1)S(1)} %get-tuple-element.10, f32[32,256]{1,0:T(8,128)S(1)} %fusion.9, f32[16,8192]{1,0:T(8,128)S(1)} %collective-permute-done.3, s32[]{:T(128)S(6)} %min.39, s32[256]{0:T(256)S(1)} %iota_add_fusion.1, ...), kind=kOutput, calls=%fused_computation.9 | convolution fusion | flops 67141632 | bytes 4523077 | tf_op jit(solution)/shard_map/dot_general | solution.py:22
  32.7 0.0 collective-permute-done.2
  32.7 10.9 %collective-permute-done.1 = f32[16,8192]{1,0:T(8,128)S(1)} collective-permute-done((f32[16,8192]{1,0:T(8,128)S(1)}, f32[16,8192]{1,0:T(8,128)S(1)}, u32[]{:S(2)}, u32[]{:S(2)}) %collective-permute-start.1) | collective-permute-done | bytes 524320 | tf_op jit(solution)/shard_map/ppermute | solution.py:67
  43.6 0.1 subtract_convert_fusion.4
  43.7 0.8 %fusion.5 = f32[32,256]{1,0:T(8,128)S(1)} fusion(bf16[8192,256]{1,0:T(8,128)(2,1)S(1)} %get-tuple-element.9, bf16[16,8192]{1,0:T(8,128)(2,1)S(1)} %get-tuple-element.7, bf16[16,8192]{1,0:T(8,128)(2,1)S(1)} %fusion.24), kind=kOutput, calls=%fused_computation.12 | convolution fusion | flops 135266304 | bytes 4751360 | tf_op jit(solution)/shard_map/dot_general | solution.py:19
  44.6 0.7 %select_select_fusion.3 = (f32[16,256]{1,0:T(8,128)S(1)}, f32[16,256]{1,0:T(8,128)S(1)}, f32[16,256]{1,0:T(8,128)S(1)}, f32[16,256]{1,0:T(8,128)S(1)}) fusion(f32[16,256]{1,0:T(8,128)S(1)} %fusion.3, f32[16,256]{1,0:T(8,128)S(1)} %fusion.2, f32[16,256]{1,0:T(8,128)S(1)} %fusion.1, pred[]{:T(512)S(6)} %eq.136, pred[]{:T(512)S(6)} %eq.147, pred[]{:T(512)S(6)} %eq.144, ...), kind=kOutput, calls=%fused_computation.51 | convolution fusion | flops 67190784 | bytes 4621393 | tf_op jit(solution)/shard_map/dot_general | solution.py:22
  45.3 0.1 collective-permute-start.4
  45.3 1.6 %collective-permute-start.5 = (f32[16,256]{1,0:T(8,128)S(1)}, f32[16,256]{1,0:T(8,128)S(1)}, u32[]{:S(2)}, u32[]{:S(2)}) collective-permute-start(f32[16,256]{1,0:T(8,128)S(1)} %get-tuple-element.19), channel_id=1, source_target_pairs={{0,2},{1,3},{2,0},{3,1},{4,6},{5,7},{6,4},{7,5},{8,10},{9,11},{10,... | collective-permute-start | bytes 49160 | tf_op jit(solution)/shard_map/ppermute | solution.py:105
  46.9 1.4 %collective-permute-start.6 = (f32[16,256]{1,0:T(8,128)S(1)}, f32[16,256]{1,0:T(8,128)S(1)}, u32[]{:S(2)}, u32[]{:S(2)}) collective-permute-start(f32[16,256]{1,0:T(8,128)S(1)} %get-tuple-element.18), channel_id=1, source_target_pairs={{0,3},{1,0},{2,1},{3,2},{4,7},{5,4},{6,5},{7,6},{8,11},{9,8},{10,9... | collective-permute-start | bytes 49160 | tf_op jit(solution)/shard_map/ppermute | solution.py:105
  48.3 0.2 collective-permute-done.4
  48.5 0.7 %collective-permute-done.5 = f32[16,256]{1,0:T(8,128)S(1)} collective-permute-done((f32[16,256]{1,0:T(8,128)S(1)}, f32[16,256]{1,0:T(8,128)S(1)}, u32[]{:S(2)}, u32[]{:S(2)}) %collective-permute-start.5) | collective-permute-done | bytes 16416 | tf_op jit(solution)/shard_map/ppermute | solution.py:105
  49.2 0.6 %collective-permute-done.6 = f32[16,256]{1,0:T(8,128)S(1)} collective-permute-done((f32[16,256]{1,0:T(8,128)S(1)}, f32[16,256]{1,0:T(8,128)S(1)}, u32[]{:S(2)}, u32[]{:S(2)}) %collective-permute-start.6) | collective-permute-done | bytes 16416 | tf_op jit(solution)/shard_map/ppermute | solution.py:105
  49.7 0.7 %multiply_select_fusion = f32[16,256]{1,0:T(8,128)} fusion(f32[16,256]{1,0:T(8,128)S(1)} %collective-permute-done.6, f32[16,256]{1,0:T(8,128)S(1)} %collective-permute-done.5, f32[16,256]{1,0:T(8,128)S(1)} %collective-permute-done.4, f32[64,256]{1,0:T(8,128)S(1)} %pad_maximum_fusion, s32[]{:T(128)S(6)} %select_n.223, s32[256]{0:T(256)S(1)} %iota_add_fusion.1, ...), kind=kLoop, calls=%fused_computation.47 | loop fusion | flops 40960 | bytes 83012 | tf_op jit(solution)/shard_map/jit(_where)/select_n | solution.py:113
  (11 shorter events, 0.1 us)
Async XLA Ops:
  0.0 27.5 %collective-permute-start = (f32[16,8192]{1,0:T(8,128)}, f32[16,8192]{1,0:T(8,128)S(1)}, u32[]{:S(2)}, u32[]{:S(2)}) collective-permute-start(f32[16,8192]{1,0:T(8,128)} %param.3), channel_id=1, source_target_pairs={{0,8},{4,12},{8,0},{12,4},{1,9},{5,13},{9,1},{13,5},{2,10},{6,14},... | collective-permute-start | bytes 1572872 | tf_op jit(solution)/shard_map/ppermute | solution.py:65
  4.0 26.4 %collective-permute-start.3 = (f32[16,8192]{1,0:T(8,128)}, f32[16,8192]{1,0:T(8,128)S(1)}, u32[]{:S(2)}, u32[]{:S(2)}) collective-permute-start(f32[16,8192]{1,0:T(8,128)} %param.3), channel_id=1, source_target_pairs={{0,4},{4,0},{8,12},{12,8},{1,5},{5,1},{9,13},{13,9},{2,6},{6,2},{1... | collective-permute-start | bytes 1572872 | tf_op jit(solution)/shard_map/ppermute | solution.py:66
  14.2 1.0 %copy-start = (f32[16,8192]{1,0:T(8,128)S(1)}, f32[16,8192]{1,0:T(8,128)}, u32[]{:S(2)}) copy-start(f32[16,8192]{1,0:T(8,128)} %param.3) | copy-start | bytes 1572868
  27.5 5.1 %collective-permute-start.2 = (f32[16,8192]{1,0:T(8,128)S(1)}, f32[16,8192]{1,0:T(8,128)S(1)}, u32[]{:S(2)}, u32[]{:S(2)}) collective-permute-start(f32[16,8192]{1,0:T(8,128)S(1)} %copy-done), channel_id=1, source_target_pairs={{4,8},{8,4},{5,9},{9,5},{6,10},{10,6},{7,11},{11,7},{20,24},{24,20... | collective-permute-start | bytes 1572872 | tf_op jit(solution)/shard_map/ppermute | solution.py:69
  28.3 15.3 %collective-permute-start.1 = (f32[16,8192]{1,0:T(8,128)S(1)}, f32[16,8192]{1,0:T(8,128)S(1)}, u32[]{:S(2)}, u32[]{:S(2)}) collective-permute-start(f32[16,8192]{1,0:T(8,128)S(1)} %collective-permute-done), channel_id=1, source_target_pairs={{4,0},{8,12},{5,1},{9,13},{6,2},{10,14},{7,3},{11,15},{20,16},{24,... | collective-permute-start | bytes 1572872 | tf_op jit(solution)/shard_map/ppermute | solution.py:67
  45.3 3.2 %collective-permute-start.4 = (f32[16,256]{1,0:T(8,128)S(1)}, f32[16,256]{1,0:T(8,128)S(1)}, u32[]{:S(2)}, u32[]{:S(2)}) collective-permute-start(f32[16,256]{1,0:T(8,128)S(1)} %get-tuple-element.17), channel_id=1, source_target_pairs={{0,1},{1,2},{2,3},{3,0},{4,5},{5,6},{6,7},{7,4},{8,9},{9,10},{10,1... | collective-permute-start | bytes 49160 | tf_op jit(solution)/shard_map/ppermute | solution.py:105
  45.3 3.8 %collective-permute-start.5 = (f32[16,256]{1,0:T(8,128)S(1)}, f32[16,256]{1,0:T(8,128)S(1)}, u32[]{:S(2)}, u32[]{:S(2)}) collective-permute-start(f32[16,256]{1,0:T(8,128)S(1)} %get-tuple-element.19), channel_id=1, source_target_pairs={{0,2},{1,3},{2,0},{3,1},{4,6},{5,7},{6,4},{7,5},{8,10},{9,11},{10,... | collective-permute-start | bytes 49160 | tf_op jit(solution)/shard_map/ppermute | solution.py:105
  46.9 2.8 %collective-permute-start.6 = (f32[16,256]{1,0:T(8,128)S(1)}, f32[16,256]{1,0:T(8,128)S(1)}, u32[]{:S(2)}, u32[]{:S(2)}) collective-permute-start(f32[16,256]{1,0:T(8,128)S(1)} %get-tuple-element.18), channel_id=1, source_target_pairs={{0,3},{1,0},{2,1},{3,2},{4,7},{5,4},{6,5},{7,6},{8,11},{9,8},{10,9... | collective-permute-start | bytes 49160 | tf_op jit(solution)/shard_map/ppermute | solution.py:105

commit v3 on v2

--- a/solution.py
+++ b/solution.py
@@ -56,37 +56,34 @@
 
     slots = []
 
-    def add_slot(block, source, valid=True):
+    def add_slot(block, source):
         moved_part = product_of(block, weights) + inverse_diagonal(block, source)
-        slots.append((moved_part, jnp.where(valid, source, -1)))
+        slots.append((moved_part, source))
 
-    add_slot(omega_rows, team_index)
-    if team_count == 4:
-        across = lax.ppermute(omega_rows, "team", [(0, 2), (1, 3), (2, 0), (3, 1)])
-        pair = lax.ppermute(omega_rows, "team", [(0, 1), (1, 0), (2, 3), (3, 2)])
-        passed = lax.ppermute(across, "team", [(1, 0), (2, 3)])
-        own_later, _ = lax.optimization_barrier((omega_rows, across))
-        middle = lax.ppermute(own_later, "team", [(1, 2), (2, 1)])
-        add_slot(across, (team_index + 2) % 4)
-        add_slot(pair, team_index ^ 1)
-        is_end = (team_index == 0) | (team_index == 3)
-        add_slot(jnp.where(is_end, passed, middle), 3 - team_index)
-    else:
-        right, left = omega_rows, omega_rows
-        for step in range(1, team_count):
-            to_right = [(d, d + 1) for d in range(step - 1, team_count - 1)]
-            to_left = [(d, d - 1) for d in range(1, team_count - step + 1)]
-            right = lax.ppermute(right, "team", to_right)
-            left = lax.ppermute(left, "team", to_left)
-            from_left = team_index >= step
-            from_right = team_index + step < team_count
-            if 2 * step < team_count:
-                add_slot(right, team_index - step, from_left)
-                add_slot(left, team_index + step, from_right)
-            else:
-                merged = jnp.where(from_left, right, left)
-                source = jnp.where(from_left, team_index - step, team_index + step)
-                add_slot(merged, source, from_left | from_right)
+    ring = list(range(0, team_count, 2)) + list(range(1, team_count, 2))[::-1]
+    onward = [(ring[k], ring[(k + 1) % team_count]) for k in range(team_count)]
+    backward = [(to, source) for source, to in onward]
+    half = team_index // 2
+    place = jnp.where(team_index % 2 == 0, half, team_count - 1 - half)
+
+    def device_at(spot):
+        spot = spot % team_count
+        up = 2 * spot
+        return jnp.where(up < team_count, up, 2 * team_count - 1 - up)
+
+    first = lax.ppermute(omega_rows, "team", onward)
+    own, *weights = lax.optimization_barrier((omega_rows, *weights))
+    gathered = [(own, 0), (first, 1)]
+    held = first
+    for step in range(2, team_count // 2 + 1):
+        held = lax.ppermute(held, "team", onward)
+        gathered.append((held, step))
+    held = own
+    for step in range(1, team_count - team_count // 2):
+        held = lax.ppermute(held, "team", backward)
+        gathered.append((held, -step))
+    for block, step in gathered:
+        add_slot(block, device_at(place - step))
 
     blocks = []
     for b in range(team_count):

time: 50.9 us -> 47.4 us (0.931)
  waiting for transfers between devices: 24 us -> 18.7 us
  matrix products: 5.96 us -> 8.25 us
  starting transfers between devices: 10.6 us -> 9.94 us
    ppermute x4 -> x3, waiting for transfers between devices: 22.6 us -> 17.2 us  [the longest x1 8.75 us: per_device(): held = lax.ppermute(held, 'team', backward)]
    dot_general x4, matrix products: 3.31 us -> 5.61 us  [product_of(): jnp.dot(jnp.concatenate([high, low], 0), weights[0], preferred_element_ty...]
    ppermute x4 -> x3, starting transfers between devices: 7.59 us -> 6.93 us  [the longest x1 4.04 us: per_device(): first = lax.ppermute(omega_rows, 'team', onward)]
    convert_element_type x6 -> x5, other arithmetic: 7.97 us -> 8.25 us  [halves(): return (high.astype(jnp.bfloat16), (array - high).astype(jnp.bfloat16))]
  transfers between devices with their start and end apart: 7 -> 6, of which waited for: 5 -> 5; matrix products, arithmetic and copies ran while one was open for 25% -> 30% of each run, Pallas kernels for 0% -> 0%
where the time goes in v3:
time: 47.4 us; the launch traced here: 47.1 us
  waiting for transfers between devices  18.7 us (39%)
  starting transfers between devices  9.94 us (21%)
  other arithmetic  8.98 us (19%)
  matrix products  8.25 us (17%)
  between operations  1 us (2%)
    ppermute x1, waiting for transfers between devices, per_device(): held = lax.ppermute(held, 'team', backward)  8.75 us
    ppermute x1, waiting for transfers between devices, per_device(): held = lax.ppermute(held, 'team', onward)  8.48 us
    convert_element_type x5, other arithmetic, halves(): return (high.astype(jnp.bfloat16), (array - high).astype(jnp.bfloat16))  8.25 us
    dot_general x4, matrix products, product_of(): jnp.dot(jnp.concatenate([high, low], 0), weights[0], preferred_element_ty...  5.61 us
    ppermute x1, starting transfers between devices, per_device(): first = lax.ppermute(omega_rows, 'team', onward)  4.04 us
    ppermute x3, starting transfers between devices, per_device(): part = lax.ppermute(part, 'rep', pairs)  3.01 us
    ppermute x1, starting transfers between devices, per_device(): held = lax.ppermute(held, 'team', onward)  2.89 us
    dot_general x4, matrix products, product_of(): cross = jnp.dot(high, weights[1], preferred_element_type=jnp.float32)  2.64 us
  transfers between devices with their start and end apart: 6, of which 5 were waited for; matrix products, arithmetic and copies ran while one was open for 30% of the time, Pallas kernels for 0%

profile of v3, /device:TPU:0, one launch (start us, length us, event | category | flops | bytes accessed | tf_op | source)
XLA Modules:
  0.0 47.1 jit_solution(5274744486002305513)
XLA Ops:
  0.0 4.0 %collective-permute-start.1 = (f32[16,8192]{1,0:T(8,128)}, f32[16,8192]{1,0:T(8,128)S(1)}, u32[]{:S(2)}, u32[]{:S(2)}) collective-permute-start(f32[16,8192]{1,0:T(8,128)} %param.3), channel_id=1, source_target_pairs={{0,8},{8,12},{12,4},{4,0},{1,9},{9,13},{13,5},{5,1},{2,10},{10,14}... | collective-permute-start | bytes 1572872 | tf_op jit(solution)/shard_map/ppermute | solution.py:74
  4.7 0.0 copy-start.2
  4.7 8.0 %subtract_convert_fusion = (bf16[8192,256]{1,0:T(8,128)(2,1)}, bf16[8192,256]{1,0:T(8,128)(2,1)}) fusion(f32[8192,256]{1,0:T(8,128)} %param.4, s32[256]{0:T(256)S(1)} %iota_add_fusion.1, s32[8192]{0:T(1024)S(1)} %iota_add_fusion), kind=kLoop, calls=%fused_computation | loop fusion | flops 18874368 | bytes 16811008 | tf_op jit(solution)/shard_map/convert_element_type | solution.py:13
  12.7 0.0 copy-done.2
  12.7 0.0 collective-permute-start
  12.8 0.1 subtract_convert_fusion.1
  13.0 0.0 copy-start
  13.0 0.0 copy-start.1
  13.0 3.2 %fusion.17 = f32[32,256]{1,0:T(8,128)S(1)} fusion(bf16[8192,256]{1,0:T(8,128)(2,1)} %get-tuple-element.9, bf16[16,8192]{1,0:T(8,128)(2,1)S(1)} %get-tuple-element.13, bf16[16,8192]{1,0:T(8,128)(2,1)S(1)} %get-tuple-element.14), kind=kOutput, calls=%fused_computation.24 | convolution fusion | flops 135266304 | bytes 4751360 | tf_op jit(solution)/shard_map/dot_general | solution.py:19
  16.2 0.2 copy-done
  16.5 0.7 %fusion.1 = f32[16,256]{1,0:T(8,128)S(1)} fusion(bf16[16,8192]{1,0:T(8,128)(2,1)S(1)} %get-tuple-element.14, bf16[8192,256]{1,0:T(8,128)(2,1)S(1)} %copy-done, f32[32,256]{1,0:T(8,128)S(1)} %fusion.17, f32[16,8192]{1,0:T(8,128)S(1)} %copy-done.2, s32[]{:T(128)S(6)} %min.39, s32[256]{0:T(256)S(1)} %iota_add_fusion.1, s32[16]{0:T(128)S(1)} %iota_add_fusion.2, ...), kind=kOutput, calls=%fused_computation.5 | convolution fusion | flops 67141632 | bytes 4523077 | tf_op jit(solution)/shard_map/dot_general | solution.py:22
  17.1 0.0 collective-permute-done.1
  17.1 0.1 subtract_convert_fusion.2
  17.2 2.9 %collective-permute-start.2 = (f32[16,8192]{1,0:T(8,128)S(1)}, f32[16,8192]{1,0:T(8,128)S(1)}, u32[]{:S(2)}, u32[]{:S(2)}) collective-permute-start(f32[16,8192]{1,0:T(8,128)S(1)} %collective-permute-done.1), channel_id=1, source_target_pairs={{0,8},{8,12},{12,4},{4,0},{1,9},{9,13},{13,5},{5,1},{2,10},{10,14}... | collective-permute-start | bytes 1572872 | tf_op jit(solution)/shard_map/ppermute | solution.py:79
  20.1 0.0 copy-done.1
  20.1 0.8 %fusion.13 = f32[32,256]{1,0:T(8,128)S(1)} fusion(bf16[8192,256]{1,0:T(8,128)(2,1)S(1)} %copy-done.1, bf16[16,8192]{1,0:T(8,128)(2,1)S(1)} %get-tuple-element.15, bf16[16,8192]{1,0:T(8,128)(2,1)S(1)} %get-tuple-element.16), kind=kOutput, calls=%fused_computation.20 | convolution fusion | flops 135266304 | bytes 4751360 | tf_op jit(solution)/shard_map/dot_general | solution.py:19
  20.9 8.7 %collective-permute-done = f32[16,8192]{1,0:T(8,128)S(1)} collective-permute-done((f32[16,8192]{1,0:T(8,128)S(1)}, f32[16,8192]{1,0:T(8,128)S(1)}, u32[]{:S(2)}, u32[]{:S(2)}) %collective-permute-start) | collective-permute-done | bytes 524320 | tf_op jit(solution)/shard_map/ppermute | solution.py:83
  29.7 0.1 subtract_convert_fusion.4
  29.7 0.8 %fusion.5 = f32[32,256]{1,0:T(8,128)S(1)} fusion(bf16[8192,256]{1,0:T(8,128)(2,1)S(1)} %copy-done.1, bf16[16,8192]{1,0:T(8,128)(2,1)S(1)} %get-tuple-element.19, bf16[16,8192]{1,0:T(8,128)(2,1)S(1)} %get-tuple-element.20), kind=kOutput, calls=%fused_computation.12 | convolution fusion | flops 135266304 | bytes 4751360 | tf_op jit(solution)/shard_map/dot_general | solution.py:19
  30.6 0.7 %fusion.2 = f32[16,256]{1,0:T(8,128)S(1)} fusion(bf16[16,8192]{1,0:T(8,128)(2,1)S(1)} %get-tuple-element.16, bf16[8192,256]{1,0:T(8,128)(2,1)S(1)} %copy-done, f32[32,256]{1,0:T(8,128)S(1)} %fusion.13, f32[16,8192]{1,0:T(8,128)S(1)} %collective-permute-done.1, s32[]{:T(128)S(6)} %min.39, s32[256]{0:T(256)S(1)} %iota_add_fusion.1, s32[16]{0:T(128)S(1)} %iota_add_fusion.3, ...), kind=kOutput, calls=%fused_computation.7 | convolution fusion | flops 67141632 | bytes 4523077 | tf_op jit(solution)/shard_map/dot_general | solution.py:22
  31.2 8.5 %collective-permute-done.2 = f32[16,8192]{1,0:T(8,128)S(1)} collective-permute-done((f32[16,8192]{1,0:T(8,128)S(1)}, f32[16,8192]{1,0:T(8,128)S(1)}, u32[]{:S(2)}, u32[]{:S(2)}) %collective-permute-start.2) | collective-permute-done | bytes 524320 | tf_op jit(solution)/shard_map/ppermute | solution.py:79
  39.7 0.1 subtract_convert_fusion.3
  39.8 0.8 %fusion.9 = f32[32,256]{1,0:T(8,128)S(1)} fusion(bf16[8192,256]{1,0:T(8,128)(2,1)S(1)} %copy-done.1, bf16[16,8192]{1,0:T(8,128)(2,1)S(1)} %get-tuple-element.17, bf16[16,8192]{1,0:T(8,128)(2,1)S(1)} %get-tuple-element.18), kind=kOutput, calls=%fused_computation.16 | convolution fusion | flops 135266304 | bytes 4751360 | tf_op jit(solution)/shard_map/dot_general | solution.py:19
  40.6 0.7 %fusion.3 = f32[16,256]{1,0:T(8,128)S(1)} fusion(bf16[16,8192]{1,0:T(8,128)(2,1)S(1)} %get-tuple-element.18, bf16[8192,256]{1,0:T(8,128)(2,1)S(1)} %copy-done, f32[32,256]{1,0:T(8,128)S(1)} %fusion.9, f32[16,8192]{1,0:T(8,128)S(1)} %collective-permute-done.2, s32[]{:T(128)S(6)} %min.39, s32[256]{0:T(256)S(1)} %iota_add_fusion.1, s32[16]{0:T(128)S(1)} %iota_add_fusion.4, ...), kind=kOutput, calls=%fused_computation.9 | convolution fusion | flops 67141632 | bytes 4523077 | tf_op jit(solution)/shard_map/dot_general | solution.py:22
  41.3 0.7 %select_select_fusion.3 = (f32[16,256]{1,0:T(8,128)S(1)}, f32[16,256]{1,0:T(8,128)S(1)}, f32[16,256]{1,0:T(8,128)S(1)}, f32[16,256]{1,0:T(8,128)S(1)}) fusion(f32[16,256]{1,0:T(8,128)S(1)} %fusion.3, f32[16,256]{1,0:T(8,128)S(1)} %fusion.2, f32[16,256]{1,0:T(8,128)S(1)} %fusion.1, pred[]{:T(512)S(6)} %eq.154, pred[]{:T(512)S(6)} %eq.151, pred[]{:T(512)S(6)} %eq.148, ...), kind=kOutput, calls=%fused_computation.50 | convolution fusion | flops 67190784 | bytes 4621393 | tf_op jit(solution)/shard_map/dot_general | solution.py:22
  42.0 0.1 collective-permute-start.3
  42.0 1.6 %collective-permute-start.4 = (f32[16,256]{1,0:T(8,128)S(1)}, f32[16,256]{1,0:T(8,128)S(1)}, u32[]{:S(2)}, u32[]{:S(2)}) collective-permute-start(f32[16,256]{1,0:T(8,128)S(1)} %get-tuple-element.23), channel_id=1, source_target_pairs={{0,2},{1,3},{2,0},{3,1},{4,6},{5,7},{6,4},{7,5},{8,10},{9,11},{10,... | collective-permute-start | bytes 49160 | tf_op jit(solution)/shard_map/ppermute | solution.py:102
  43.6 1.4 %collective-permute-start.5 = (f32[16,256]{1,0:T(8,128)S(1)}, f32[16,256]{1,0:T(8,128)S(1)}, u32[]{:S(2)}, u32[]{:S(2)}) collective-permute-start(f32[16,256]{1,0:T(8,128)S(1)} %get-tuple-element.22), channel_id=1, source_target_pairs={{0,3},{1,0},{2,1},{3,2},{4,7},{5,4},{6,5},{7,6},{8,11},{9,8},{10,9... | collective-permute-start | bytes 49160 | tf_op jit(solution)/shard_map/ppermute | solution.py:102
  45.0 0.2 collective-permute-done.3
  45.2 0.7 %collective-permute-done.4 = f32[16,256]{1,0:T(8,128)S(1)} collective-permute-done((f32[16,256]{1,0:T(8,128)S(1)}, f32[16,256]{1,0:T(8,128)S(1)}, u32[]{:S(2)}, u32[]{:S(2)}) %collective-permute-start.4) | collective-permute-done | bytes 16416 | tf_op jit(solution)/shard_map/ppermute | solution.py:102
  45.8 0.6 %collective-permute-done.5 = f32[16,256]{1,0:T(8,128)S(1)} collective-permute-done((f32[16,256]{1,0:T(8,128)S(1)}, f32[16,256]{1,0:T(8,128)S(1)}, u32[]{:S(2)}, u32[]{:S(2)}) %collective-permute-start.5) | collective-permute-done | bytes 16416 | tf_op jit(solution)/shard_map/ppermute | solution.py:102
  46.4 0.7 %multiply_select_fusion = f32[16,256]{1,0:T(8,128)} fusion(f32[16,256]{1,0:T(8,128)S(1)} %collective-permute-done.5, f32[16,256]{1,0:T(8,128)S(1)} %collective-permute-done.4, f32[16,256]{1,0:T(8,128)S(1)} %collective-permute-done.3, f32[64,256]{1,0:T(8,128)S(1)} %pad_maximum_fusion, s32[]{:T(128)S(6)} %select_n.253, s32[256]{0:T(256)S(1)} %iota_add_fusion.1, ...), kind=kLoop, calls=%fused_computation.46 | loop fusion | flops 40960 | bytes 83012 | tf_op jit(solution)/shard_map/jit(_where)/select_n | solution.py:110
  (10 shorter events, 0.1 us)
Async XLA Ops:
  0.0 17.1 %collective-permute-start.1 = (f32[16,8192]{1,0:T(8,128)}, f32[16,8192]{1,0:T(8,128)S(1)}, u32[]{:S(2)}, u32[]{:S(2)}) collective-permute-start(f32[16,8192]{1,0:T(8,128)} %param.3), channel_id=1, source_target_pairs={{0,8},{8,12},{12,4},{4,0},{1,9},{9,13},{13,5},{5,1},{2,10},{10,14}... | collective-permute-start | bytes 1572872 | tf_op jit(solution)/shard_map/ppermute | solution.py:74
  4.7 8.0 %copy-start.2 = (f32[16,8192]{1,0:T(8,128)S(1)}, f32[16,8192]{1,0:T(8,128)}, u32[]{:S(2)}) copy-start(f32[16,8192]{1,0:T(8,128)} %param.3) | copy-start | bytes 1572868
  12.7 17.0 %collective-permute-start = (f32[16,8192]{1,0:T(8,128)S(1)}, f32[16,8192]{1,0:T(8,128)S(1)}, u32[]{:S(2)}, u32[]{:S(2)}) collective-permute-start(f32[16,8192]{1,0:T(8,128)S(1)} %copy-done.2), channel_id=1, source_target_pairs={{8,0},{12,8},{4,12},{0,4},{9,1},{13,9},{5,13},{1,5},{10,2},{14,10}... | collective-permute-start | bytes 1572872 | tf_op jit(solution)/shard_map/ppermute | solution.py:83
  13.0 3.5 %copy-start = (bf16[8192,256]{1,0:T(8,128)(2,1)S(1)}, bf16[8192,256]{1,0:T(8,128)(2,1)}, u32[]{:S(2)}) copy-start(bf16[8192,256]{1,0:T(8,128)(2,1)} %get-tuple-element.10) | copy-start | bytes 12582916
  13.0 7.1 %copy-start.1 = (bf16[8192,256]{1,0:T(8,128)(2,1)S(1)}, bf16[8192,256]{1,0:T(8,128)(2,1)}, u32[]{:S(2)}) copy-start(bf16[8192,256]{1,0:T(8,128)(2,1)} %get-tuple-element.9) | copy-start | bytes 12582916
  17.2 22.5 %collective-permute-start.2 = (f32[16,8192]{1,0:T(8,128)S(1)}, f32[16,8192]{1,0:T(8,128)S(1)}, u32[]{:S(2)}, u32[]{:S(2)}) collective-permute-start(f32[16,8192]{1,0:T(8,128)S(1)} %collective-permute-done.1), channel_id=1, source_target_pairs={{0,8},{8,12},{12,4},{4,0},{1,9},{9,13},{13,5},{5,1},{2,10},{10,14}... | collective-permute-start | bytes 1572872 | tf_op jit(solution)/shard_map/ppermute | solution.py:79
  42.0 3.2 %collective-permute-start.3 = (f32[16,256]{1,0:T(8,128)S(1)}, f32[16,256]{1,0:T(8,128)S(1)}, u32[]{:S(2)}, u32[]{:S(2)}) collective-permute-start(f32[16,256]{1,0:T(8,128)S(1)} %get-tuple-element.21), channel_id=1, source_target_pairs={{0,1},{1,2},{2,3},{3,0},{4,5},{5,6},{6,7},{7,4},{8,9},{9,10},{10,1... | collective-permute-start | bytes 49160 | tf_op jit(solution)/shard_map/ppermute | solution.py:102
  42.0 3.8 %collective-permute-start.4 = (f32[16,256]{1,0:T(8,128)S(1)}, f32[16,256]{1,0:T(8,128)S(1)}, u32[]{:S(2)}, u32[]{:S(2)}) collective-permute-start(f32[16,256]{1,0:T(8,128)S(1)} %get-tuple-element.23), channel_id=1, source_target_pairs={{0,2},{1,3},{2,0},{3,1},{4,6},{5,7},{6,4},{7,5},{8,10},{9,11},{10,... | collective-permute-start | bytes 49160 | tf_op jit(solution)/shard_map/ppermute | solution.py:102
  43.6 2.8 %collective-permute-start.5 = (f32[16,256]{1,0:T(8,128)S(1)}, f32[16,256]{1,0:T(8,128)S(1)}, u32[]{:S(2)}, u32[]{:S(2)}) collective-permute-start(f32[16,256]{1,0:T(8,128)S(1)} %get-tuple-element.22), channel_id=1, source_target_pairs={{0,3},{1,0},{2,1},{3,2},{4,7},{5,4},{6,5},{7,6},{8,11},{9,8},{10,9... | collective-permute-start | bytes 49160 | tf_op jit(solution)/shard_map/ppermute | solution.py:102

commit v4 on v3

--- a/solution.py
+++ b/solution.py
@@ -1,6 +1,10 @@
+import math
+
 import jax
 import jax.numpy as jnp
 from jax import lax
+from jax.experimental import pallas as pl
+from jax.experimental.pallas import tpu as pltpu
 from jax.sharding import PartitionSpec as P
 
 step_size = 0.5
@@ -13,14 +17,36 @@
     return high.astype(jnp.bfloat16), (array - high).astype(jnp.bfloat16)
 
 
-def product_of(block, weights):
-    high, low = halves(block)
-    rows = block.shape[0]
-    both = jnp.dot(
-        jnp.concatenate([high, low], 0), weights[0], preferred_element_type=jnp.float32
-    )
-    cross = jnp.dot(high, weights[1], preferred_element_type=jnp.float32)
-    return both[:rows] + both[rows:] + cross
+def slot_kernel(places, block, high, low, out):
+    rows, depth = block.shape
+    columns = high.shape[1]
+    step = math.gcd(depth, 2048)
+    total = jnp.zeros((rows, columns), jnp.float32)
+    for k in range(0, depth, step):
+        values = block[:, k : k + step]
+        upper = jnp.clip(values, -largest_bf16, largest_bf16).astype(jnp.bfloat16)
+        lower = (values - upper.astype(jnp.float32)).astype(jnp.bfloat16)
+        both = jnp.concatenate([upper, lower], 0)
+        main = jnp.dot(both, high[k : k + step], preferred_element_type=jnp.float32)
+        cross = jnp.dot(upper, low[k : k + step], preferred_element_type=jnp.float32)
+        total += main[:rows] + main[rows:] + cross
+    current = block[:, pl.ds(pl.multiple_of(places[0], columns), columns)]
+    row_ids = lax.broadcasted_iota(jnp.int32, (rows, columns), 0) + places[1]
+    mask = row_ids == lax.broadcasted_iota(jnp.int32, (rows, columns), 1)
+    out[...] = total + jnp.where(mask, step_size / jnp.where(mask, current, 1.0), 0.0)
+
+
+def slot_product(places, block, weights):
+    rows, columns = block.shape[0], weights[0].shape[1]
+    return pl.pallas_call(
+        slot_kernel,
+        out_shape=jax.ShapeDtypeStruct((rows, columns), jnp.float32),
+        in_specs=[pl.BlockSpec(memory_space=pltpu.SMEM)]
+        + [pl.BlockSpec(memory_space=pltpu.VMEM)] * 3,
+        out_specs=pl.BlockSpec(memory_space=pltpu.VMEM),
+        compiler_params=pltpu.CompilerParams(vmem_limit_bytes=32 * 1024 * 1024),
+        cost_estimate=pl.CostEstimate(flops=0, bytes_accessed=block.size * 4, transcendentals=0),
+    )(places, block, *weights)
 
 
 def sum_of(terms):
@@ -41,24 +67,19 @@
     rows_share = all_rows // rep_count
     offset = tile_offsets[0]
     assert all_rows <= part_width and part_width % tile_width == 0
+    assert rows_share % block_rows == 0
 
     k_ids = rep_index * part_width + jnp.arange(part_width, dtype=jnp.int32)
     c_ids = offset + jnp.arange(tile_width, dtype=jnp.int32)
     chosen = (k_ids[:, None] == c_ids[None, :]).astype(jnp.float32)
     weights = halves(chosen - step_size * covariance_columns)
 
-    def inverse_diagonal(block, source):
+    def part_of(block, source):
         start = jnp.clip(offset, 0, part_width - tile_width)
-        values = lax.dynamic_slice_in_dim(block, start, tile_width, 1)
-        row_ids = source * block_rows + jnp.arange(block_rows, dtype=jnp.int32)
-        mask = (row_ids[:, None] == c_ids[None, :]) & (rep_index == 0)
-        return jnp.where(mask, step_size / jnp.where(mask, values, 1.0), 0.0)
+        shift = jnp.where(rep_index == 0, source * block_rows - offset, 1 << 20)
+        return slot_product(jnp.stack([start, shift]).astype(jnp.int32), block, weights)
 
     slots = []
-
-    def add_slot(block, source):
-        moved_part = product_of(block, weights) + inverse_diagonal(block, source)
-        slots.append((moved_part, source))
 
     ring = list(range(0, team_count, 2)) + list(range(1, team_count, 2))[::-1]
     onward = [(ring[k], ring[(k + 1) % team_count]) for k in range(team_count)]
@@ -73,17 +94,21 @@
 
     first = lax.ppermute(omega_rows, "team", onward)
     own, *weights = lax.optimization_barrier((omega_rows, *weights))
+    last_step = team_count // 2
     gathered = [(own, 0), (first, 1)]
     held = first
-    for step in range(2, team_count // 2 + 1):
+    for step in range(2, last_step + 1):
         held = lax.ppermute(held, "team", onward)
         gathered.append((held, step))
+    last = held
     held = own
-    for step in range(1, team_count - team_count // 2):
+    for step in range(1, team_count - last_step):
         held = lax.ppermute(held, "team", backward)
         gathered.append((held, -step))
     for block, step in gathered:
-        add_slot(block, device_at(place - step))
+        if step != last_step:
+            source = device_at(place - step)
+            slots.append((part_of(block, source), source))
 
     blocks = []
     for b in range(team_count):
@@ -101,7 +126,25 @@
             pairs = [(d, (d + by) % rep_count) for d in range(rep_count)]
             part = lax.ppermute(part, "rep", pairs)
         terms.append(part)
-    moved = sum_of(terms)
+
+    last_source = device_at(place - last_step)
+    last_part = part_of(last, last_source)
+    share_blocks = rows_share // block_rows
+    roots = [
+        ring[(ring.index(d) - last_step) % team_count] // share_blocks for d in range(team_count)
+    ]
+    late = last_part
+    for by in range(1, rep_count):
+        pairs = [
+            (d * rep_count + (roots[d] + by) % rep_count, d * rep_count + roots[d])
+            for d in range(team_count)
+        ]
+        late = late + lax.ppermute(last_part, ("team", "rep"), pairs)
+    late_place = jnp.where(
+        last_source // share_blocks == rep_index, last_source % share_blocks, -1
+    )
+    late_blocks = [jnp.where(late_place == b, late, 0.0) for b in range(share_blocks)]
+    moved = sum_of(terms) + jnp.concatenate(late_blocks, 0)
 
     global_rows = rep_index * rows_share + jnp.arange(rows_share, dtype=jnp.int32)
     global_cols = offset + jnp.arange(tile_width, dtype=jnp.int32)

time: 47.4 us -> 54 us (1.14)
  local copies, waits for them, and re-layouts: 0.27 us -> 8.77 us
  matrix products: 8.25 us -> 0 us
  Pallas kernels: 0 us -> 7.41 us
  waiting for transfers between devices: 18.7 us -> 11.9 us
  starting transfers between devices: 9.94 us -> 15.6 us
    unnamed x6 -> x10, local copies, waits for them, and re-layouts: 0.26 us -> 8.76 us
    dot_general x8 -> x0, matrix products: 8.25 us -> none  [the longest x4 5.61 us: product_of(): jnp.dot(jnp.concatenate([high, low], 0), weights[0], preferred_element_ty...]
    pallas_call x0 -> x4, Pallas kernels: none -> 7.41 us  [slot_product(): pl.pallas_call(slot_kernel, out_shape=jax.ShapeDtypeStruct((rows, columns...]
    ppermute x0 -> x3, starting transfers between devices: none -> 5.6 us  [per_device(): late = late + lax.ppermute(last_part, ('team', 'rep'), pairs)]
    ppermute x1, waiting for transfers between devices: 8.48 us -> 4.75 us  [per_device(): held = lax.ppermute(held, 'team', onward)]
    ppermute x1, waiting for transfers between devices: 8.75 us -> 5.78 us  [per_device(): held = lax.ppermute(held, 'team', backward)]
    ppermute x3, waiting for transfers between devices: 1.44 us -> 0.01 us  [per_device(): part = lax.ppermute(part, 'rep', pairs)]
    ppermute x0 -> x3, waiting for transfers between devices: none -> 1.35 us  [per_device(): late = late + lax.ppermute(last_part, ('team', 'rep'), pairs)]
  transfers between devices with their start and end apart: 6 -> 9, of which waited for: 5 -> 3; matrix products, arithmetic and copies ran while one was open for 30% -> 15% of each run, Pallas kernels for 0% -> 14%
where the time goes in v4:
time: 54 us; the launch traced here: 53.7 us
  starting transfers between devices  15.6 us (29%)
  waiting for transfers between devices  11.9 us (22%)
  other arithmetic  8.94 us (17%)
  local copies, waits for them, and re-layouts  8.77 us (16%)
  Pallas kernels  7.41 us (14%)
  between operations  1.02 us (2%)
    unnamed x10, local copies, waits for them, and re-layouts  8.76 us
    convert_element_type x1, other arithmetic, halves(): return (high.astype(jnp.bfloat16), (array - high).astype(jnp.bfloat16))  7.98 us
    pallas_call x4, Pallas kernels, slot_product(): pl.pallas_call(slot_kernel, out_shape=jax.ShapeDtypeStruct((rows, columns...  7.41 us
    ppermute x1, waiting for transfers between devices, per_device(): held = lax.ppermute(held, 'team', backward)  5.78 us
    ppermute x3, starting transfers between devices, per_device(): late = late + lax.ppermute(last_part, ('team', 'rep'), pairs)  5.6 us
    ppermute x1, waiting for transfers between devices, per_device(): held = lax.ppermute(held, 'team', onward)  4.75 us
    ppermute x1, starting transfers between devices, per_device(): first = lax.ppermute(omega_rows, 'team', onward)  4.04 us
    ppermute x3, starting transfers between devices, per_device(): part = lax.ppermute(part, 'rep', pairs)  3.28 us
  transfers between devices with their start and end apart: 9, of which 3 were waited for; matrix products, arithmetic and copies ran while one was open for 15% of the time, Pallas kernels for 14%

profile of v4, /device:TPU:0, one launch (start us, length us, event | category | flops | bytes accessed | tf_op | source)
XLA Modules:
  0.0 53.7 jit_solution(9772061048124043401)
XLA Ops:
  0.0 4.0 %collective-permute-start.1 = (f32[16,8192]{1,0:T(8,128)}, f32[16,8192]{1,0:T(8,128)S(1)}, u32[]{:S(2)}, u32[]{:S(2)}) collective-permute-start(f32[16,8192]{1,0:T(8,128)} %block), channel_id=1, source_target_pairs={{0,8},{8,12},{12,4},{4,0},{1,9},{9,13},{13,5},{5,1},{2,10},{10,14}... | collective-permute-start | bytes 1572872 | tf_op jit(solution)/shard_map/ppermute | solution.py:95
  4.7 0.0 copy-start.4
  4.7 8.0 %subtract_convert_fusion = (bf16[8192,256]{1,0:T(8,128)(2,1)}, bf16[8192,256]{1,0:T(8,128)(2,1)}) fusion(f32[8192,256]{1,0:T(8,128)} %param.4, s32[256]{0:T(256)S(1)} %iota_add_fusion.1, s32[8192]{0:T(1024)S(1)} %iota_add_fusion), kind=kLoop, calls=%fused_computation | loop fusion | flops 18874368 | bytes 16811008 | tf_op jit(solution)/shard_map/convert_element_type | solution.py:17
  12.7 0.0 copy-done.4
  12.7 0.0 collective-permute-start
  12.9 0.1 pad_add_fusion.2.places
  13.0 0.0 copy-start
  13.0 2.2 %copy-done = bf16[8192,256]{1,0:T(8,128)(2,1)S(1)} copy-done((bf16[8192,256]{1,0:T(8,128)(2,1)S(1)}, bf16[8192,256]{1,0:T(8,128)(2,1)}, u32[]{:S(2)}) %copy-start) | copy-done | bytes 4194328
  15.2 0.0 copy-start.2
  15.2 2.2 %copy-done.2 = bf16[8192,256]{1,0:T(8,128)(2,1)S(1)} copy-done((bf16[8192,256]{1,0:T(8,128)(2,1)S(1)}, bf16[8192,256]{1,0:T(8,128)(2,1)}, u32[]{:S(2)}) %copy-start.2) | copy-done | bytes 4194328
  17.4 1.9 %shard_map.39 = f32[16,256]{1,0:T(8,128)S(1)} custom-call(s32[2]{0:T(128)S(1)} %pad_add_fusion.2.places, f32[16,8192]{1,0:T(8,128)S(1)} %copy-done.4, bf16[8192,256]{1,0:T(8,128)(2,1)S(1)} %copy-done.2, bf16[8192,256]{1,0:T(8,128)(2,1)S(1)} %copy-done), custom_call_target="tpu_custom_call" | custom-call | bytes 524288 | tf_op jit(solution)/shard_map/pallas_call | solution.py:41
  19.2 0.1 pad_add_fusion
  19.3 0.0 collective-permute-done.1.block
  19.3 2.7 %collective-permute-start.5 = (f32[16,8192]{1,0:T(8,128)S(1)}, f32[16,8192]{1,0:T(8,128)S(1)}, u32[]{:S(2)}, u32[]{:S(2)}) collective-permute-start(f32[16,8192]{1,0:T(8,128)S(1)} %collective-permute-done.1.block), channel_id=1, source_target_pairs={{0,8},{8,12},{12,4},{4,0},{1,9},{9,13},{13,5},{5,1},{2,10},{10,14}... | collective-permute-start | bytes 1572872 | tf_op jit(solution)/shard_map/ppermute | solution.py:101
  22.0 1.9 %shard_map.38 = f32[16,256]{1,0:T(8,128)S(1)} custom-call(s32[2]{0:T(128)S(1)} %get-tuple-element.21.places, f32[16,8192]{1,0:T(8,128)S(1)} %collective-permute-done.1.block, bf16[8192,256]{1,0:T(8,128)(2,1)S(1)} %copy-done.2, bf16[8192,256]{1,0:T(8,128)(2,1)S(1)} %copy-done), custom_call_target="tpu_custom_call" | custom-call | bytes 524288 | tf_op jit(solution)/shard_map/pallas_call | solution.py:41
  23.9 5.8 %collective-permute-done.block = f32[16,8192]{1,0:T(8,128)S(1)} collective-permute-done((f32[16,8192]{1,0:T(8,128)S(1)}, f32[16,8192]{1,0:T(8,128)S(1)}, u32[]{:S(2)}, u32[]{:S(2)}) %collective-permute-start) | collective-permute-done | bytes 524320 | tf_op jit(solution)/shard_map/ppermute | solution.py:106
  29.7 1.9 %shard_map.37 = f32[16,256]{1,0:T(8,128)S(1)} custom-call(s32[2]{0:T(128)S(1)} %get-tuple-element.20.places, f32[16,8192]{1,0:T(8,128)S(1)} %collective-permute-done.block, bf16[8192,256]{1,0:T(8,128)(2,1)S(1)} %copy-done.2, bf16[8192,256]{1,0:T(8,128)(2,1)S(1)} %copy-done), custom_call_target="tpu_custom_call" | custom-call | bytes 524288 | tf_op jit(solution)/shard_map/pallas_call | solution.py:41
  31.6 0.1 collective-permute-start.2
  31.7 0.1 pad_add_fusion.3.places
  31.7 1.7 %collective-permute-start.4 = (f32[16,256]{1,0:T(8,128)S(1)}, f32[16,256]{1,0:T(8,128)S(1)}, u32[]{:S(2)}, u32[]{:S(2)}) collective-permute-start(f32[16,256]{1,0:T(8,128)S(1)} %get-tuple-element.14), channel_id=1, source_target_pairs={{0,3},{1,0},{2,1},{3,2},{4,7},{5,4},{6,5},{7,6},{8,11},{9,8},{10,9... | collective-permute-start | bytes 49160 | tf_op jit(solution)/shard_map/ppermute | solution.py:127
  33.5 1.5 %collective-permute-start.3 = (f32[16,256]{1,0:T(8,128)S(1)}, f32[16,256]{1,0:T(8,128)S(1)}, u32[]{:S(2)}, u32[]{:S(2)}) collective-permute-start(f32[16,256]{1,0:T(8,128)S(1)} %get-tuple-element.15), channel_id=1, source_target_pairs={{0,2},{1,3},{2,0},{3,1},{4,6},{5,7},{6,4},{7,5},{8,10},{9,11},{10,... | collective-permute-start | bytes 49160 | tf_op jit(solution)/shard_map/ppermute | solution.py:127
  35.0 4.8 %collective-permute-done.5.block = f32[16,8192]{1,0:T(8,128)S(1)} collective-permute-done((f32[16,8192]{1,0:T(8,128)S(1)}, f32[16,8192]{1,0:T(8,128)S(1)}, u32[]{:S(2)}, u32[]{:S(2)}) %collective-permute-start.5) | collective-permute-done | bytes 524320 | tf_op jit(solution)/shard_map/ppermute | solution.py:101
  39.7 0.0 copy-start.1
  39.7 2.2 %copy-done.1 = bf16[8192,256]{1,0:T(8,128)(2,1)S(1)} copy-done((bf16[8192,256]{1,0:T(8,128)(2,1)S(1)}, bf16[8192,256]{1,0:T(8,128)(2,1)}, u32[]{:S(2)}) %copy-start.1) | copy-done | bytes 4194328
  41.9 0.0 copy-start.3
  41.9 2.2 %copy-done.3 = bf16[8192,256]{1,0:T(8,128)(2,1)S(1)} copy-done((bf16[8192,256]{1,0:T(8,128)(2,1)S(1)}, bf16[8192,256]{1,0:T(8,128)(2,1)}, u32[]{:S(2)}) %copy-start.3) | copy-done | bytes 4194328
  44.1 1.9 %shard_map.40 = f32[16,256]{1,0:T(8,128)S(1)} custom-call(s32[2]{0:T(128)S(1)} %pad_add_fusion.3.places, f32[16,8192]{1,0:T(8,128)S(1)} %collective-permute-done.5.block, bf16[8192,256]{1,0:T(8,128)(2,1)S(1)} %copy-done.3, bf16[8192,256]{1,0:T(8,128)(2,1)S(1)} %copy-done.1), custom_call_target="tpu_custom_call" | custom-call | bytes 524288 | tf_op jit(solution)/shard_map/pallas_call | solution.py:41
  45.9 0.7 %collective-permute-start.8 = (f32[16,256]{1,0:T(8,128)S(1)}, f32[16,256]{1,0:T(8,128)S(1)}, u32[]{:S(2)}, u32[]{:S(2)}) collective-permute-start(f32[16,256]{1,0:T(8,128)S(1)} %shard_map.40), channel_id=1, source_target_pairs={{2,3},{5,6},{8,9},{15,12},{18,19},{21,22},{24,25},{31,28}} | collective-permute-start | bytes 49160 | tf_op jit(solution)/shard_map/ppermute | solution.py:142
  46.6 0.7 %collective-permute-start.7 = (f32[16,256]{1,0:T(8,128)S(1)}, f32[16,256]{1,0:T(8,128)S(1)}, u32[]{:S(2)}, u32[]{:S(2)}) collective-permute-start(f32[16,256]{1,0:T(8,128)S(1)} %shard_map.40), channel_id=1, source_target_pairs={{1,3},{4,6},{11,9},{14,12},{17,19},{20,22},{27,25},{30,28}} | collective-permute-start | bytes 49160 | tf_op jit(solution)/shard_map/ppermute | solution.py:142
  47.3 0.0 collective-permute-done.2
  47.3 4.3 %collective-permute-start.6 = (f32[16,256]{1,0:T(8,128)S(1)}, f32[16,256]{1,0:T(8,128)S(1)}, u32[]{:S(2)}, u32[]{:S(2)}) collective-permute-start(f32[16,256]{1,0:T(8,128)S(1)} %shard_map.40), channel_id=1, source_target_pairs={{0,3},{7,6},{10,9},{13,12},{16,19},{23,22},{26,25},{29,28}} | collective-permute-start | bytes 49160 | tf_op jit(solution)/shard_map/ppermute | solution.py:142
  51.6 0.0 collective-permute-done.4
  51.6 0.0 collective-permute-done.3
  51.6 0.0 collective-permute-done.8
  51.6 0.0 collective-permute-done.7
  51.6 1.3 %collective-permute-done.6 = f32[16,256]{1,0:T(8,128)S(1)} collective-permute-done((f32[16,256]{1,0:T(8,128)S(1)}, f32[16,256]{1,0:T(8,128)S(1)}, u32[]{:S(2)}, u32[]{:S(2)}) %collective-permute-start.6) | collective-permute-done | bytes 16416 | tf_op jit(solution)/shard_map/ppermute | solution.py:142
  53.0 0.7 %multiply_select_fusion = f32[16,256]{1,0:T(8,128)} fusion(f32[16,256]{1,0:T(8,128)S(1)} %collective-permute-done.8, f32[16,256]{1,0:T(8,128)S(1)} %collective-permute-done.7, f32[16,256]{1,0:T(8,128)S(1)} %shard_map.40, f32[16,256]{1,0:T(8,128)S(1)} %collective-permute-done.6, f32[16,256]{1,0:T(8,128)S(1)} %collective-permute-done.4, ...), kind=kLoop, calls=%fused_computation.6 | loop fusion | flops 61440 | bytes 148549 | tf_op jit(solution)/shard_map/jit(_where)/select_n | solution.py:153
  (6 shorter events, 0.1 us)
Async XLA Ops:
  0.0 19.3 %collective-permute-start.1 = (f32[16,8192]{1,0:T(8,128)}, f32[16,8192]{1,0:T(8,128)S(1)}, u32[]{:S(2)}, u32[]{:S(2)}) collective-permute-start(f32[16,8192]{1,0:T(8,128)} %block), channel_id=1, source_target_pairs={{0,8},{8,12},{12,4},{4,0},{1,9},{9,13},{13,5},{5,1},{2,10},{10,14}... | collective-permute-start | bytes 1572872 | tf_op jit(solution)/shard_map/ppermute | solution.py:95
  4.7 8.0 %copy-start.4 = (f32[16,8192]{1,0:T(8,128)S(1)}, f32[16,8192]{1,0:T(8,128)}, u32[]{:S(2)}) copy-start(f32[16,8192]{1,0:T(8,128)} %block) | copy-start | bytes 1572868
  12.7 17.0 %collective-permute-start = (f32[16,8192]{1,0:T(8,128)S(1)}, f32[16,8192]{1,0:T(8,128)S(1)}, u32[]{:S(2)}, u32[]{:S(2)}) collective-permute-start(f32[16,8192]{1,0:T(8,128)S(1)} %copy-done.4), channel_id=1, source_target_pairs={{8,0},{12,8},{4,12},{0,4},{9,1},{13,9},{5,13},{1,5},{10,2},{14,10}... | collective-permute-start | bytes 1572872 | tf_op jit(solution)/shard_map/ppermute | solution.py:106
  13.0 2.2 %copy-start = (bf16[8192,256]{1,0:T(8,128)(2,1)S(1)}, bf16[8192,256]{1,0:T(8,128)(2,1)}, u32[]{:S(2)}) copy-start(bf16[8192,256]{1,0:T(8,128)(2,1)} %get-tuple-element.10.low) | copy-start | bytes 12582916
  15.2 2.2 %copy-start.2 = (bf16[8192,256]{1,0:T(8,128)(2,1)S(1)}, bf16[8192,256]{1,0:T(8,128)(2,1)}, u32[]{:S(2)}) copy-start(bf16[8192,256]{1,0:T(8,128)(2,1)} %get-tuple-element.9.high) | copy-start | bytes 12582916
  19.3 20.4 %collective-permute-start.5 = (f32[16,8192]{1,0:T(8,128)S(1)}, f32[16,8192]{1,0:T(8,128)S(1)}, u32[]{:S(2)}, u32[]{:S(2)}) collective-permute-start(f32[16,8192]{1,0:T(8,128)S(1)} %collective-permute-done.1.block), channel_id=1, source_target_pairs={{0,8},{8,12},{12,4},{4,0},{1,9},{9,13},{13,5},{5,1},{2,10},{10,14}... | collective-permute-start | bytes 1572872 | tf_op jit(solution)/shard_map/ppermute | solution.py:101
  31.6 15.7 %collective-permute-start.2 = (f32[16,256]{1,0:T(8,128)S(1)}, f32[16,256]{1,0:T(8,128)S(1)}, u32[]{:S(2)}, u32[]{:S(2)}) collective-permute-start(f32[16,256]{1,0:T(8,128)S(1)} %get-tuple-element.13), channel_id=1, source_target_pairs={{0,1},{1,2},{2,3},{3,0},{4,5},{5,6},{6,7},{7,4},{8,9},{9,10},{10,1... | collective-permute-start | bytes 49160 | tf_op jit(solution)/shard_map/ppermute | solution.py:127
  31.7 19.9 %collective-permute-start.4 = (f32[16,256]{1,0:T(8,128)S(1)}, f32[16,256]{1,0:T(8,128)S(1)}, u32[]{:S(2)}, u32[]{:S(2)}) collective-permute-start(f32[16,256]{1,0:T(8,128)S(1)} %get-tuple-element.14), channel_id=1, source_target_pairs={{0,3},{1,0},{2,1},{3,2},{4,7},{5,4},{6,5},{7,6},{8,11},{9,8},{10,9... | collective-permute-start | bytes 49160 | tf_op jit(solution)/shard_map/ppermute | solution.py:127
  33.5 18.2 %collective-permute-start.3 = (f32[16,256]{1,0:T(8,128)S(1)}, f32[16,256]{1,0:T(8,128)S(1)}, u32[]{:S(2)}, u32[]{:S(2)}) collective-permute-start(f32[16,256]{1,0:T(8,128)S(1)} %get-tuple-element.15), channel_id=1, source_target_pairs={{0,2},{1,3},{2,0},{3,1},{4,6},{5,7},{6,4},{7,5},{8,10},{9,11},{10,... | collective-permute-start | bytes 49160 | tf_op jit(solution)/shard_map/ppermute | solution.py:127
  39.7 2.2 %copy-start.1 = (bf16[8192,256]{1,0:T(8,128)(2,1)S(1)}, bf16[8192,256]{1,0:T(8,128)(2,1)}, u32[]{:S(2)}) copy-start(bf16[8192,256]{1,0:T(8,128)(2,1)} %get-tuple-element.10.low) | copy-start | bytes 12582916
  41.9 2.2 %copy-start.3 = (bf16[8192,256]{1,0:T(8,128)(2,1)S(1)}, bf16[8192,256]{1,0:T(8,128)(2,1)}, u32[]{:S(2)}) copy-start(bf16[8192,256]{1,0:T(8,128)(2,1)} %get-tuple-element.9.high) | copy-start | bytes 12582916
  45.9 5.7 %collective-permute-start.8 = (f32[16,256]{1,0:T(8,128)S(1)}, f32[16,256]{1,0:T(8,128)S(1)}, u32[]{:S(2)}, u32[]{:S(2)}) collective-permute-start(f32[16,256]{1,0:T(8,128)S(1)} %shard_map.40), channel_id=1, source_target_pairs={{2,3},{5,6},{8,9},{15,12},{18,19},{21,22},{24,25},{31,28}} | collective-permute-start | bytes 49160 | tf_op jit(solution)/shard_map/ppermute | solution.py:142
  46.6 5.0 %collective-permute-start.7 = (f32[16,256]{1,0:T(8,128)S(1)}, f32[16,256]{1,0:T(8,128)S(1)}, u32[]{:S(2)}, u32[]{:S(2)}) collective-permute-start(f32[16,256]{1,0:T(8,128)S(1)} %shard_map.40), channel_id=1, source_target_pairs={{1,3},{4,6},{11,9},{14,12},{17,19},{20,22},{27,25},{30,28}} | collective-permute-start | bytes 49160 | tf_op jit(solution)/shard_map/ppermute | solution.py:142
  47.3 5.7 %collective-permute-start.6 = (f32[16,256]{1,0:T(8,128)S(1)}, f32[16,256]{1,0:T(8,128)S(1)}, u32[]{:S(2)}, u32[]{:S(2)}) collective-permute-start(f32[16,256]{1,0:T(8,128)S(1)} %shard_map.40), channel_id=1, source_target_pairs={{0,3},{7,6},{10,9},{13,12},{16,19},{23,22},{26,25},{29,28}} | collective-permute-start | bytes 49160 | tf_op jit(solution)/shard_map/ppermute | solution.py:142

commit v5 on v4

--- a/solution.py
+++ b/solution.py
@@ -17,7 +17,8 @@
     return high.astype(jnp.bfloat16), (array - high).astype(jnp.bfloat16)
 
 
-def slot_kernel(places, block, high, low, out):
+def slot_kernel(places, block, high, low, *rest):
+    *others, out = rest
     rows, depth = block.shape
     columns = high.shape[1]
     step = math.gcd(depth, 2048)
@@ -33,20 +34,27 @@
     current = block[:, pl.ds(pl.multiple_of(places[0], columns), columns)]
     row_ids = lax.broadcasted_iota(jnp.int32, (rows, columns), 0) + places[1]
     mask = row_ids == lax.broadcasted_iota(jnp.int32, (rows, columns), 1)
-    out[...] = total + jnp.where(mask, step_size / jnp.where(mask, current, 1.0), 0.0)
+    total += jnp.where(mask, step_size / jnp.where(mask, current, 1.0), 0.0)
+    if not others:
+        out[...] = total
+        return
+    for position, part in enumerate(others):
+        out[places[2 + position]] = part[...]
+    out[places[2 + len(others)]] = total
 
 
-def slot_product(places, block, weights):
+def slot_product(places, block, weights, others=()):
     rows, columns = block.shape[0], weights[0].shape[1]
+    shape = (len(others) + 1, rows, columns) if others else (rows, columns)
     return pl.pallas_call(
         slot_kernel,
-        out_shape=jax.ShapeDtypeStruct((rows, columns), jnp.float32),
+        out_shape=jax.ShapeDtypeStruct(shape, jnp.float32),
         in_specs=[pl.BlockSpec(memory_space=pltpu.SMEM)]
-        + [pl.BlockSpec(memory_space=pltpu.VMEM)] * 3,
+        + [pl.BlockSpec(memory_space=pltpu.VMEM)] * (3 + len(others)),
         out_specs=pl.BlockSpec(memory_space=pltpu.VMEM),
-        compiler_params=pltpu.CompilerParams(vmem_limit_bytes=32 * 1024 * 1024),
+        compiler_params=pltpu.CompilerParams(vmem_limit_bytes=2 * 1024 * 1024),
         cost_estimate=pl.CostEstimate(flops=0, bytes_accessed=block.size * 4, transcendentals=0),
-    )(places, block, *weights)
+    )(places, block, *weights, *others)
 
 
 def sum_of(terms):
@@ -74,12 +82,11 @@
     chosen = (k_ids[:, None] == c_ids[None, :]).astype(jnp.float32)
     weights = halves(chosen - step_size * covariance_columns)
 
-    def part_of(block, source):
+    def part_of(block, source, others=(), sources=()):
         start = jnp.clip(offset, 0, part_width - tile_width)
         shift = jnp.where(rep_index == 0, source * block_rows - offset, 1 << 20)
-        return slot_product(jnp.stack([start, shift]).astype(jnp.int32), block, weights)
-
-    slots = []
+        places = jnp.stack([start, shift, *sources]).astype(jnp.int32)
+        return slot_product(places, block, weights, others)
 
     ring = list(range(0, team_count, 2)) + list(range(1, team_count, 2))[::-1]
     onward = [(ring[k], ring[(k + 1) % team_count]) for k in range(team_count)]
@@ -105,46 +112,18 @@
     for step in range(1, team_count - last_step):
         held = lax.ppermute(held, "team", backward)
         gathered.append((held, -step))
+    others, sources = [], []
     for block, step in gathered:
         if step != last_step:
             source = device_at(place - step)
-            slots.append((part_of(block, source), source))
+            others.append(part_of(block, source))
+            sources.append(source)
+    source = device_at(place - last_step)
+    partial_moved = part_of(last, source, others, sources + [source])
 
-    blocks = []
-    for b in range(team_count):
-        value = jnp.zeros((block_rows, tile_width), jnp.float32)
-        for slot, source in slots:
-            value = jnp.where(source == b, slot, value)
-        blocks.append(value)
-    partial_moved = jnp.concatenate(blocks, 0)
-
-    terms = []
-    for by in range(rep_count):
-        target = (rep_index + by) % rep_count
-        part = lax.dynamic_slice_in_dim(partial_moved, target * rows_share, rows_share, 0)
-        if by:
-            pairs = [(d, (d + by) % rep_count) for d in range(rep_count)]
-            part = lax.ppermute(part, "rep", pairs)
-        terms.append(part)
-
-    last_source = device_at(place - last_step)
-    last_part = part_of(last, last_source)
-    share_blocks = rows_share // block_rows
-    roots = [
-        ring[(ring.index(d) - last_step) % team_count] // share_blocks for d in range(team_count)
-    ]
-    late = last_part
-    for by in range(1, rep_count):
-        pairs = [
-            (d * rep_count + (roots[d] + by) % rep_count, d * rep_count + roots[d])
-            for d in range(team_count)
-        ]
-        late = late + lax.ppermute(last_part, ("team", "rep"), pairs)
-    late_place = jnp.where(
-        last_source // share_blocks == rep_index, last_source % share_blocks, -1
-    )
-    late_blocks = [jnp.where(late_place == b, late, 0.0) for b in range(share_blocks)]
-    moved = sum_of(terms) + jnp.concatenate(late_blocks, 0)
+    shares = partial_moved.reshape(rep_count, rows_share, tile_width)
+    shares = lax.all_to_all(shares, "rep", 0, 0)
+    moved = sum_of([shares[r] for r in range(rep_count)])
 
     global_rows = rep_index * rows_share + jnp.arange(rows_share, dtype=jnp.int32)
     global_cols = offset + jnp.arange(tile_width, dtype=jnp.int32)

time: 54 us -> 50.2 us (0.930)
  starting transfers between devices: 15.6 us -> 10.6 us
  waiting for transfers between devices: 11.9 us -> 12.8 us
  Pallas kernels: 7.41 us -> 8.05 us
    ppermute x6 -> x0, starting transfers between devices: 8.88 us -> none  [the longest x3 5.6 us: per_device(): late = late + lax.ppermute(last_part, ('team', 'rep'), pairs)]
    ppermute x1, waiting for transfers between devices: 5.78 us -> 0.01 us  [per_device(): held = lax.ppermute(held, 'team', backward)]
    all_to_all x0 -> x1, waiting for transfers between devices: none -> 4.07 us  [per_device(): shares = lax.all_to_all(shares, 'rep', 0, 0)]
    ppermute x1, waiting for transfers between devices: 0.01 us -> 3.96 us  [per_device(): first = lax.ppermute(omega_rows, 'team', onward)]
    all_to_all x0 -> x1, starting transfers between devices: none -> 3.28 us  [per_device(): shares = lax.all_to_all(shares, 'rep', 0, 0)]
    ppermute x6 -> x0, waiting for transfers between devices: 1.36 us -> none  [the longest x3 1.35 us: per_device(): late = late + lax.ppermute(last_part, ('team', 'rep'), pairs)]
    pallas_call x4, Pallas kernels: 7.41 us -> 8.05 us  [slot_product(): pl.pallas_call(slot_kernel, out_shape=jax.ShapeDtypeStruct(shape, jnp.flo...]
    ppermute x1, starting transfers between devices: 2.72 us -> 3.27 us  [per_device(): held = lax.ppermute(held, 'team', onward)]
  transfers between devices with their start and end apart: 9 -> 4, of which waited for: 3 -> 3; matrix products, arithmetic and copies ran while one was open for 15% -> 17% of each run, Pallas kernels for 14% -> 11%
where the time goes in v5:
time: 50.2 us; the launch traced here: 49.9 us
  waiting for transfers between devices  12.8 us (25%)
  starting transfers between devices  10.6 us (21%)
  local copies, waits for them, and re-layouts  8.85 us (18%)
  other arithmetic  8.82 us (18%)
  Pallas kernels  8.05 us (16%)
  between operations  0.71 us (1%)
    unnamed x10, local copies, waits for them, and re-layouts  8.77 us
    pallas_call x4, Pallas kernels, slot_product(): pl.pallas_call(slot_kernel, out_shape=jax.ShapeDtypeStruct(shape, jnp.flo...  8.05 us
    convert_element_type x1, other arithmetic, halves(): return (high.astype(jnp.bfloat16), (array - high).astype(jnp.bfloat16))  7.98 us
    ppermute x1, waiting for transfers between devices, per_device(): held = lax.ppermute(held, 'team', onward)  4.79 us
    all_to_all x1, waiting for transfers between devices, per_device(): shares = lax.all_to_all(shares, 'rep', 0, 0)  4.07 us
    ppermute x1, starting transfers between devices, per_device(): first = lax.ppermute(omega_rows, 'team', onward)  4.04 us
    ppermute x1, waiting for transfers between devices, per_device(): first = lax.ppermute(omega_rows, 'team', onward)  3.96 us
    all_to_all x1, starting transfers between devices, per_device(): shares = lax.all_to_all(shares, 'rep', 0, 0)  3.28 us
  transfers between devices with their start and end apart: 4, of which 3 were waited for; matrix products, arithmetic and copies ran while one was open for 17% of the time, Pallas kernels for 11%

profile of v5, /device:TPU:0, one launch (start us, length us, event | category | flops | bytes accessed | tf_op | source)
XLA Modules:
  0.0 49.9 jit_solution(6080701420886205191)
XLA Ops:
  0.0 4.0 %collective-permute-start = (f32[16,8192]{1,0:T(8,128)}, f32[16,8192]{1,0:T(8,128)S(1)}, u32[]{:S(2)}, u32[]{:S(2)}) collective-permute-start(f32[16,8192]{1,0:T(8,128)} %block), channel_id=1, source_target_pairs={{0,8},{8,12},{12,4},{4,0},{1,9},{9,13},{13,5},{5,1},{2,10},{10,14}... | collective-permute-start | bytes 1572872 | tf_op jit(solution)/shard_map/ppermute | solution.py:102
  4.7 0.0 copy-start.4
  4.7 8.0 %subtract_convert_fusion = (bf16[8192,256]{1,0:T(8,128)(2,1)}, bf16[8192,256]{1,0:T(8,128)(2,1)}) fusion(f32[8192,256]{1,0:T(8,128)} %param.4, s32[256]{0:T(256)S(1)} %iota_add_fusion.1, s32[8192]{0:T(1024)S(1)} %iota_add_fusion), kind=kLoop, calls=%fused_computation | loop fusion | flops 18874368 | bytes 16811008 | tf_op jit(solution)/shard_map/convert_element_type | solution.py:17
  12.7 0.0 copy-done.4
  12.7 0.0 collective-permute-start.2
  12.7 4.0 %collective-permute-done.block = f32[16,8192]{1,0:T(8,128)S(1)} collective-permute-done((f32[16,8192]{1,0:T(8,128)}, f32[16,8192]{1,0:T(8,128)S(1)}, u32[]{:S(2)}, u32[]{:S(2)}) %collective-permute-start) | collective-permute-done | bytes 524320 | tf_op jit(solution)/shard_map/ppermute | solution.py:102
  16.7 3.3 %collective-permute-start.1 = (f32[16,8192]{1,0:T(8,128)S(1)}, f32[16,8192]{1,0:T(8,128)S(1)}, u32[]{:S(2)}, u32[]{:S(2)}) collective-permute-start(f32[16,8192]{1,0:T(8,128)S(1)} %collective-permute-done.block), channel_id=1, source_target_pairs={{0,8},{8,12},{12,4},{4,0},{1,9},{9,13},{13,5},{5,1},{2,10},{10,14}... | collective-permute-start | bytes 1572872 | tf_op jit(solution)/shard_map/ppermute | solution.py:108
  20.0 0.1 pad_add_fusion
  20.0 0.0 copy-start
  20.0 2.2 %copy-done = bf16[8192,256]{1,0:T(8,128)(2,1)S(1)} copy-done((bf16[8192,256]{1,0:T(8,128)(2,1)S(1)}, bf16[8192,256]{1,0:T(8,128)(2,1)}, u32[]{:S(2)}) %copy-start) | copy-done | bytes 4194328
  22.2 0.0 copy-start.2
  22.2 2.2 %copy-done.2 = bf16[8192,256]{1,0:T(8,128)(2,1)S(1)} copy-done((bf16[8192,256]{1,0:T(8,128)(2,1)S(1)}, bf16[8192,256]{1,0:T(8,128)(2,1)}, u32[]{:S(2)}) %copy-start.2) | copy-done | bytes 4194328
  24.4 1.9 %shard_map.37.rest_0_ = f32[16,256]{1,0:T(8,128)S(1)} custom-call(s32[2]{0:T(128)S(1)} %get-tuple-element.13.places, f32[16,8192]{1,0:T(8,128)S(1)} %copy-done.4, bf16[8192,256]{1,0:T(8,128)(2,1)S(1)} %copy-done.2, bf16[8192,256]{1,0:T(8,128)(2,1)S(1)} %copy-done), custom_call_target="tpu_custom_call" | custom-call | bytes 524288 | tf_op jit(solution)/shard_map/pallas_call | solution.py:49
  26.3 0.1 stack.48.places
  26.4 0.1 pad_add_fusion.2.places
  26.4 0.0 copy-start.1
  26.4 2.2 %copy-done.1 = bf16[8192,256]{1,0:T(8,128)(2,1)S(1)} copy-done((bf16[8192,256]{1,0:T(8,128)(2,1)S(1)}, bf16[8192,256]{1,0:T(8,128)(2,1)}, u32[]{:S(2)}) %copy-start.1) | copy-done | bytes 4194328
  28.6 0.0 copy-start.3
  28.6 2.2 %copy-done.3 = bf16[8192,256]{1,0:T(8,128)(2,1)S(1)} copy-done((bf16[8192,256]{1,0:T(8,128)(2,1)S(1)}, bf16[8192,256]{1,0:T(8,128)(2,1)}, u32[]{:S(2)}) %copy-start.3) | copy-done | bytes 4194328
  30.8 1.9 %shard_map.38.rest_1_ = f32[16,256]{1,0:T(8,128)S(1)} custom-call(s32[2]{0:T(128)S(1)} %get-tuple-element.14.places, f32[16,8192]{1,0:T(8,128)S(1)} %collective-permute-done.block, bf16[8192,256]{1,0:T(8,128)(2,1)S(1)} %copy-done.3, bf16[8192,256]{1,0:T(8,128)(2,1)S(1)} %copy-done.1), custom_call_target="tpu_custom_call" | custom-call | bytes 524288 | tf_op jit(solution)/shard_map/pallas_call | solution.py:49
  32.7 0.0 collective-permute-done.2.block
  32.7 1.9 %shard_map.39.rest_2_ = f32[16,256]{1,0:T(8,128)S(1)} custom-call(s32[2]{0:T(128)S(1)} %pad_add_fusion.2.places, f32[16,8192]{1,0:T(8,128)S(1)} %collective-permute-done.2.block, bf16[8192,256]{1,0:T(8,128)(2,1)S(1)} %copy-done.3, bf16[8192,256]{1,0:T(8,128)(2,1)S(1)} %copy-done.1), custom_call_target="tpu_custom_call" | custom-call | bytes 524288 | tf_op jit(solution)/shard_map/pallas_call | solution.py:49
  34.5 4.8 %collective-permute-done.1.block = f32[16,8192]{1,0:T(8,128)S(1)} collective-permute-done((f32[16,8192]{1,0:T(8,128)S(1)}, f32[16,8192]{1,0:T(8,128)S(1)}, u32[]{:S(2)}, u32[]{:S(2)}) %collective-permute-start.1) | collective-permute-done | bytes 524320 | tf_op jit(solution)/shard_map/ppermute | solution.py:108
  39.3 2.5 %shard_map.40 = f32[4,16,256]{2,1,0:T(8,128)} custom-call(s32[6]{0:T(128)S(1)} %stack.48.places, f32[16,8192]{1,0:T(8,128)S(1)} %collective-permute-done.1.block, bf16[8192,256]{1,0:T(8,128)(2,1)S(1)} %copy-done.3, bf16[8192,256]{1,0:T(8,128)(2,1)S(1)} %copy-done.1, f32[16,256]{1,0:T(8,128)S(1)} %shard_map.37.rest_0_, f32[16,256]{1,0:T(8,128)S(1)} %shard_map.38.rest_1_, ...), custom_call_target="tpu_custom_call" | custom-call | bytes 524288 | tf_op jit(solution)/shard_map/pallas_call | solution.py:49
  41.8 3.3 %all-to-all-start = ((f32[4,16,256]{2,1,0:T(8,128)}), f32[4,16,256]{2,1,0:T(8,128)S(1)}, u32[]{:S(2)}, u32[]{:S(2)}) async-start(f32[4,16,256]{2,1,0:T(8,128)} %shard_map.40), calls=%async_computation | async-start | bytes 131072 | tf_op jit(solution)/shard_map/all_to_all | solution.py:125
  45.1 4.1 %all-to-all-done = f32[4,16,256]{2,1,0:T(8,128)S(1)} async-done(((f32[4,16,256]{2,1,0:T(8,128)}), f32[4,16,256]{2,1,0:T(8,128)S(1)}, u32[]{:S(2)}, u32[]{:S(2)}) %all-to-all-start) | async-done | bytes 65568 | tf_op jit(solution)/shard_map/all_to_all | solution.py:125
  49.2 0.7 %multiply_select_fusion = f32[16,256]{1,0:T(8,128)} fusion(f32[4,16,256]{2,1,0:T(8,128)S(1)} %all-to-all-done, s32[256]{0:T(256)S(1)} %iota_add_fusion.1, s32[16]{0:T(128)S(1)} %iota_add_fusion.2), kind=kLoop, calls=%fused_computation.9 | loop fusion | flops 40960 | bytes 83008 | tf_op jit(solution)/shard_map/jit(_where)/select_n | solution.py:132
  (3 shorter events, 0.0 us)
Async XLA Ops:
  0.0 16.7 %collective-permute-start = (f32[16,8192]{1,0:T(8,128)}, f32[16,8192]{1,0:T(8,128)S(1)}, u32[]{:S(2)}, u32[]{:S(2)}) collective-permute-start(f32[16,8192]{1,0:T(8,128)} %block), channel_id=1, source_target_pairs={{0,8},{8,12},{12,4},{4,0},{1,9},{9,13},{13,5},{5,1},{2,10},{10,14}... | collective-permute-start | bytes 1572872 | tf_op jit(solution)/shard_map/ppermute | solution.py:102
  4.7 8.0 %copy-start.4 = (f32[16,8192]{1,0:T(8,128)S(1)}, f32[16,8192]{1,0:T(8,128)}, u32[]{:S(2)}) copy-start(f32[16,8192]{1,0:T(8,128)} %block) | copy-start | bytes 1572868
  12.7 20.0 %collective-permute-start.2 = (f32[16,8192]{1,0:T(8,128)S(1)}, f32[16,8192]{1,0:T(8,128)S(1)}, u32[]{:S(2)}, u32[]{:S(2)}) collective-permute-start(f32[16,8192]{1,0:T(8,128)S(1)} %copy-done.4), channel_id=1, source_target_pairs={{8,0},{12,8},{4,12},{0,4},{9,1},{13,9},{5,13},{1,5},{10,2},{14,10}... | collective-permute-start | bytes 1572872 | tf_op jit(solution)/shard_map/ppermute | solution.py:113
  16.7 22.6 %collective-permute-start.1 = (f32[16,8192]{1,0:T(8,128)S(1)}, f32[16,8192]{1,0:T(8,128)S(1)}, u32[]{:S(2)}, u32[]{:S(2)}) collective-permute-start(f32[16,8192]{1,0:T(8,128)S(1)} %collective-permute-done.block), channel_id=1, source_target_pairs={{0,8},{8,12},{12,4},{4,0},{1,9},{9,13},{13,5},{5,1},{2,10},{10,14}... | collective-permute-start | bytes 1572872 | tf_op jit(solution)/shard_map/ppermute | solution.py:108
  20.0 2.2 %copy-start = (bf16[8192,256]{1,0:T(8,128)(2,1)S(1)}, bf16[8192,256]{1,0:T(8,128)(2,1)}, u32[]{:S(2)}) copy-start(bf16[8192,256]{1,0:T(8,128)(2,1)} %get-tuple-element.9.low) | copy-start | bytes 12582916
  22.2 2.2 %copy-start.2 = (bf16[8192,256]{1,0:T(8,128)(2,1)S(1)}, bf16[8192,256]{1,0:T(8,128)(2,1)}, u32[]{:S(2)}) copy-start(bf16[8192,256]{1,0:T(8,128)(2,1)} %get-tuple-element.8.high) | copy-start | bytes 12582916
  26.4 2.2 %copy-start.1 = (bf16[8192,256]{1,0:T(8,128)(2,1)S(1)}, bf16[8192,256]{1,0:T(8,128)(2,1)}, u32[]{:S(2)}) copy-start(bf16[8192,256]{1,0:T(8,128)(2,1)} %get-tuple-element.9.low) | copy-start | bytes 12582916
  28.6 2.2 %copy-start.3 = (bf16[8192,256]{1,0:T(8,128)(2,1)S(1)}, bf16[8192,256]{1,0:T(8,128)(2,1)}, u32[]{:S(2)}) copy-start(bf16[8192,256]{1,0:T(8,128)(2,1)} %get-tuple-element.8.high) | copy-start | bytes 12582916
  41.8 7.4 %all-to-all-start = ((f32[4,16,256]{2,1,0:T(8,128)}), f32[4,16,256]{2,1,0:T(8,128)S(1)}, u32[]{:S(2)}, u32[]{:S(2)}) async-start(f32[4,16,256]{2,1,0:T(8,128)} %shard_map.40), calls=%async_computation | async-start | bytes 131072 | tf_op jit(solution)/shard_map/all_to_all | solution.py:125

commit v6 on v5

v6 whole, which is shorter than its diff:
```python
import functools
import math

import jax
import jax.numpy as jnp
from jax import lax
from jax.experimental import pallas as pl
from jax.experimental.pallas import tpu as pltpu
from jax.sharding import PartitionSpec as P

step_size = 0.5
penalty = 0.1
largest_bf16 = 3.3895313892515355e38


def halves(array):
    high = lax.reduce_precision(jnp.clip(array, -largest_bf16, largest_bf16), 8, 7)
    return high.astype(jnp.bfloat16), (array - high).astype(jnp.bfloat16)


def slot_kernel(first_k, parts, places, block, high, low, *rest):
    others, outs = rest[:parts], rest[parts:]
    rows, depth = block.shape
    columns = high.shape[1]
    step = math.gcd(depth, 4096)
    total = jnp.zeros((rows, columns), jnp.float32)
    for k in range(0, depth, step):
        values = block[:, k : k + step]
        upper = jnp.clip(values, -largest_bf16, largest_bf16).astype(jnp.bfloat16)
        lower = (values - upper.astype(jnp.float32)).astype(jnp.bfloat16)
        both = jnp.concatenate([upper, lower], 0)
        span = slice(first_k + k, first_k + k + step)
        main = jnp.dot(both, high[span], preferred_element_type=jnp.float32)
        cross = jnp.dot(upper, low[span], preferred_element_type=jnp.float32)
        total += main[:rows] + main[rows:] + cross
    if first_k == 0:
        current = block[:, pl.ds(pl.multiple_of(places[0], columns), columns)]
        row_ids = lax.broadcasted_iota(jnp.int32, (rows, columns), 0) + places[1]
        mask = row_ids == lax.broadcasted_iota(jnp.int32, (rows, columns), 1)
        total += jnp.where(mask, step_size / jnp.where(mask, current, 1.0), 0.0)
    if not parts:
        outs[0][...] = total
        return
    values = [part[...] for part in others]
    values[-1] += total
    per_share = outs[0].shape[0] // rows
    for share, out in enumerate(outs):
        for b in range(per_share):
            found = jnp.zeros((rows, columns), jnp.float32)
            for part, value in enumerate(values):
                found = jnp.where(places[2 + part] == share * per_share + b, value, found)
            out[b * rows : (b + 1) * rows] = found


def slot_product(places, block, weights, first_k=0, others=(), shares=1):
    rows, columns = block.shape[0], weights[0].shape[1]
    shape = (rows * max(len(others), 1) // shares, columns)
    return pl.pallas_call(
        functools.partial(slot_kernel, first_k, len(others)),
        out_shape=[jax.ShapeDtypeStruct(shape, jnp.float32)] * shares,
        in_specs=[pl.BlockSpec(memory_space=pltpu.SMEM)]
        + [pl.BlockSpec(memory_space=pltpu.VMEM)] * (3 + len(others)),
        out_specs=[pl.BlockSpec(memory_space=pltpu.VMEM)] * shares,
        compiler_params=pltpu.CompilerParams(vmem_limit_bytes=(2 + len(others) // 4) * 1024 * 1024),
        cost_estimate=pl.CostEstimate(flops=0, bytes_accessed=block.size * 4, transcendentals=0),
    )(places, block, *weights, *others)


def sum_of(terms):
    total = terms[0]
    for term in terms[1:]:
        total = total + term
    return total


def per_device(omega_rows, covariance_columns, tile_offsets):
    team_count = lax.axis_size("team")
    rep_count = lax.axis_size("rep")
    team_index = lax.axis_index("team")
    rep_index = lax.axis_index("rep")
    block_rows, part_width = omega_rows.shape
    tile_width = covariance_columns.shape[1]
    all_rows = block_rows * team_count
    rows_share = all_rows // rep_count
    offset = tile_offsets[0]
    assert all_rows <= part_width and part_width % tile_width == 0
    assert rows_share % block_rows == 0

    k_ids = rep_index * part_width + jnp.arange(part_width, dtype=jnp.int32)
    c_ids = offset + jnp.arange(tile_width, dtype=jnp.int32)
    chosen = (k_ids[:, None] == c_ids[None, :]).astype(jnp.float32)
    weights = halves(chosen - step_size * covariance_columns)

    half = part_width // 2
    assert all_rows <= half and half % tile_width == 0

    def places_of(source, *more):
        start = jnp.clip(offset, 0, half - tile_width)
        shift = jnp.where(rep_index == 0, source * block_rows - offset, 1 << 20)
        return jnp.stack([start, shift, *more]).astype(jnp.int32)

    ring = list(range(0, team_count, 2)) + list(range(1, team_count, 2))[::-1]
    onward = [(ring[k], ring[(k + 1) % team_count]) for k in range(team_count)]
    backward = [(to, source) for source, to in onward]
    rank = team_index // 2
    place = jnp.where(team_index % 2 == 0, rank, team_count - 1 - rank)

    def device_at(spot):
        spot = spot % team_count
        up = 2 * spot
        return jnp.where(up < team_count, up, 2 * team_count - 1 - up)

    first = lax.ppermute(omega_rows, "team", onward)
    own, *weights = lax.optimization_barrier((omega_rows, *weights))
    last_step = team_count // 2
    gathered = [(own, 0), (first, 1)]
    held = first
    for step in range(2, last_step):
        held = lax.ppermute(held, "team", onward)
        gathered.append((held, step))
    last_held = held
    held = own
    for step in range(1, team_count - last_step):
        held = lax.ppermute(held, "team", backward)
        gathered.append((held, -step))

    last_left = lax.ppermute(last_held[:, :half], "team", onward)
    others, sources = [], []
    for block, step in gathered:
        source = device_at(place - step)
        others += slot_product(places_of(source), block, weights)
        sources.append(source)
        if step == 1:
            last_held, others[-1] = lax.optimization_barrier((last_held, others[-1]))
    last_right = lax.ppermute(last_held[:, half:], "team", onward)
    source = device_at(place - last_step)
    others += slot_product(places_of(source), last_left, weights)
    sources.append(source)

    share_blocks = rows_share // block_rows
    spots = [(source - rep_index * share_blocks) % team_count for source in sources]
    shares = slot_product(
        places_of(source, *spots), last_right, weights, half, others, rep_count
    )
    terms = [shares[0]]
    for by in range(1, rep_count):
        pairs = [(d, (d + by) % rep_count) for d in range(rep_count)]
        terms.append(lax.ppermute(shares[by], "rep", pairs))
    moved = sum_of(terms)

    global_rows = rep_index * rows_share + jnp.arange(rows_share, dtype=jnp.int32)
    global_cols = offset + jnp.arange(tile_width, dtype=jnp.int32)
    diagonal = global_rows[:, None] == global_cols[None, :]
    shrunk = jnp.sign(moved) * jnp.maximum(jnp.abs(moved) - step_size * penalty, 0.0)
    return jnp.where(diagonal, moved, shrunk)


def solution(mesh):
    in_specs = (P(("groups", "team"), "rep"), P("rep", ("groups", "team")), P(("groups", "team")))
    out_specs = P("rep", ("groups", "team"))
    return jax.shard_map(
        per_device, mesh=mesh, in_specs=in_specs, out_specs=out_specs, check_vma=False
    )
```

time: 50.2 us -> 47.7 us (0.950)
  waiting for transfers between devices: 12.8 us -> 5.25 us
  local copies, waits for them, and re-layouts: 8.85 us -> 13.6 us
    unnamed x10 -> x18, local copies, waits for them, and re-layouts: 8.77 us -> 13.5 us
    all_to_all x1 -> x0, waiting for transfers between devices: 4.07 us -> none  [per_device(): shares = lax.all_to_all(shares, 'rep', 0, 0)]
    ppermute x1 -> x5, waiting for transfers between devices: 4.79 us -> 1.44 us  [the longest x3 1.44 us: per_device(): terms.append(lax.ppermute(shares[by], 'rep', pairs))]
    all_to_all x1 -> x0, starting transfers between devices: 3.28 us -> none  [per_device(): shares = lax.all_to_all(shares, 'rep', 0, 0)]
    ppermute x1 -> x5, starting transfers between devices: 3.27 us -> 6.39 us  [the longest x1 3.33 us: per_device(): last_left = lax.ppermute(last_held[:, :half], 'team', onward)]
    pallas_call x4 -> x5, Pallas kernels: 8.05 us -> 8.01 us  [slot_product(): pl.pallas_call(functools.partial(slot_kernel, first_k, len(others)), out_...]
  transfers between devices with their start and end apart: 4 -> 7, of which waited for: 3 -> 4; matrix products, arithmetic and copies ran while one was open for 17% -> 18% of each run, Pallas kernels for 11% -> 14%
where the time goes in v6:
time: 47.7 us; the launch traced here: 47.2 us
  local copies, waits for them, and re-layouts  13.6 us (29%)
  starting transfers between devices  10.4 us (22%)
  other arithmetic  8.91 us (19%)
  Pallas kernels  8.01 us (17%)
  waiting for transfers between devices  5.25 us (11%)
  between operations  0.94 us (2%)
    unnamed x18, local copies, waits for them, and re-layouts  13.5 us
    pallas_call x5, Pallas kernels, slot_product(): pl.pallas_call(functools.partial(slot_kernel, first_k, len(others)), out_...  8.01 us
    convert_element_type x1, other arithmetic, halves(): return (high.astype(jnp.bfloat16), (array - high).astype(jnp.bfloat16))  8 us
    ppermute x1, starting transfers between devices, per_device(): first = lax.ppermute(omega_rows, 'team', onward)  4.04 us
    ppermute x1, waiting for transfers between devices, per_device(): first = lax.ppermute(omega_rows, 'team', onward)  3.8 us
    ppermute x1, starting transfers between devices, per_device(): last_left = lax.ppermute(last_held[:, :half], 'team', onward)  3.33 us
    ppermute x3, starting transfers between devices, per_device(): terms.append(lax.ppermute(shares[by], 'rep', pairs))  3 us
    ppermute x3, waiting for transfers between devices, per_device(): terms.append(lax.ppermute(shares[by], 'rep', pairs))  1.44 us
  transfers between devices with their start and end apart: 7, of which 4 were waited for; matrix products, arithmetic and copies ran while one was open for 18% of the time, Pallas kernels for 14%

profile of v6, /device:TPU:0, one launch (start us, length us, event | category | flops | bytes accessed | tf_op | source)
XLA Modules:
  0.0 47.2 jit_solution(10705682575408290461)
XLA Ops:
  0.0 4.0 %collective-permute-start = (f32[16,8192]{1,0:T(8,128)}, f32[16,8192]{1,0:T(8,128)S(1)}, u32[]{:S(2)}, u32[]{:S(2)}) collective-permute-start(f32[16,8192]{1,0:T(8,128)} %block), channel_id=1, source_target_pairs={{0,8},{8,12},{12,4},{4,0},{1,9},{9,13},{13,5},{5,1},{2,10},{10,14}... | collective-permute-start | bytes 1572872 | tf_op jit(solution)/shard_map/ppermute | solution.py:113
  4.7 0.0 copy-start.8
  4.7 8.0 %subtract_convert_fusion = (bf16[8192,256]{1,0:T(8,128)(2,1)}, bf16[8192,256]{1,0:T(8,128)(2,1)}) fusion(f32[8192,256]{1,0:T(8,128)} %param.4, s32[256]{0:T(256)S(1)} %iota_add_fusion.1, s32[8192]{0:T(1024)S(1)} %iota_add_fusion), kind=kLoop, calls=%fused_computation | loop fusion | flops 18874368 | bytes 16811008 | tf_op jit(solution)/shard_map/convert_element_type | solution.py:18
  12.7 0.0 copy-done.8
  12.7 0.0 collective-permute-start.2
  12.8 0.1 pad_add_fusion.places
  12.9 3.8 %collective-permute-done.block = f32[16,8192]{1,0:T(8,128)S(1)} collective-permute-done((f32[16,8192]{1,0:T(8,128)}, f32[16,8192]{1,0:T(8,128)S(1)}, u32[]{:S(2)}, u32[]{:S(2)}) %collective-permute-start) | collective-permute-done | bytes 524320 | tf_op jit(solution)/shard_map/ppermute | solution.py:113
  16.7 3.3 %collective-permute-start.3 = (f32[16,4096]{1,0:T(8,128)S(1)}, f32[16,4096]{1,0:T(8,128)S(1)}, u32[]{:S(2)}, u32[]{:S(2)}) collective-permute-start(f32[16,4096]{1,0:T(8,128)S(1)} %slice.8), channel_id=1, source_target_pairs={{0,8},{8,12},{12,4},{4,0},{1,9},{9,13},{13,5},{5,1},{2,10},{10,14}... | collective-permute-start | bytes 786440 | tf_op jit(solution)/shard_map/ppermute | solution.py:127
  20.0 0.0 copy-start
  20.0 2.2 %copy-done = bf16[8192,256]{1,0:T(8,128)(2,1)S(1)} copy-done((bf16[8192,256]{1,0:T(8,128)(2,1)S(1)}, bf16[8192,256]{1,0:T(8,128)(2,1)}, u32[]{:S(2)}) %copy-start) | copy-done | bytes 4194328
  22.2 0.0 copy-start.4
  22.2 2.2 %copy-done.4 = bf16[8192,256]{1,0:T(8,128)(2,1)S(1)} copy-done((bf16[8192,256]{1,0:T(8,128)(2,1)S(1)}, bf16[8192,256]{1,0:T(8,128)(2,1)}, u32[]{:S(2)}) %copy-start.4) | copy-done | bytes 4194328
  24.4 1.9 %shard_map.37.rest_1_ = f32[16,256]{1,0:T(8,128)S(1)} custom-call(s32[2]{0:T(128)S(1)} %pad_add_fusion.places, f32[16,8192]{1,0:T(8,128)S(1)} %collective-permute-done.block, bf16[8192,256]{1,0:T(8,128)(2,1)S(1)} %copy-done.4, bf16[8192,256]{1,0:T(8,128)(2,1)S(1)} %copy-done), custom_call_target="tpu_custom_call" | custom-call | bytes 524288 | tf_op jit(solution)/shard_map/pallas_call | solution.py:58
  26.3 0.1 collective-permute-start.1
  26.5 0.1 pad_add_fusion.1
  26.6 0.0 copy-start.1
  26.6 2.2 %copy-done.1 = bf16[8192,256]{1,0:T(8,128)(2,1)S(1)} copy-done((bf16[8192,256]{1,0:T(8,128)(2,1)S(1)}, bf16[8192,256]{1,0:T(8,128)(2,1)}, u32[]{:S(2)}) %copy-start.1) | copy-done | bytes 4194328
  28.8 0.0 copy-start.5
  28.8 2.2 %copy-done.5 = bf16[8192,256]{1,0:T(8,128)(2,1)S(1)} copy-done((bf16[8192,256]{1,0:T(8,128)(2,1)S(1)}, bf16[8192,256]{1,0:T(8,128)(2,1)}, u32[]{:S(2)}) %copy-start.5) | copy-done | bytes 4194328
  31.0 1.9 %shard_map.38.rest_0_ = f32[16,256]{1,0:T(8,128)S(1)} custom-call(s32[2]{0:T(128)S(1)} %get-tuple-element.25.places, f32[16,8192]{1,0:T(8,128)S(1)} %copy-done.8, bf16[8192,256]{1,0:T(8,128)(2,1)S(1)} %copy-done.5, bf16[8192,256]{1,0:T(8,128)(2,1)S(1)} %copy-done.1), custom_call_target="tpu_custom_call" | custom-call | bytes 524288 | tf_op jit(solution)/shard_map/pallas_call | solution.py:58
  32.8 0.1 stack.53.places
  32.9 0.1 pad_add_fusion.3.places
  33.0 0.0 collective-permute-done.2.block
  33.0 0.0 copy-start.2
  33.0 2.2 %copy-done.2 = bf16[8192,256]{1,0:T(8,128)(2,1)S(1)} copy-done((bf16[8192,256]{1,0:T(8,128)(2,1)S(1)}, bf16[8192,256]{1,0:T(8,128)(2,1)}, u32[]{:S(2)}) %copy-start.2) | copy-done | bytes 4194328
  35.2 0.0 copy-start.6
  35.2 2.2 %copy-done.6 = bf16[8192,256]{1,0:T(8,128)(2,1)S(1)} copy-done((bf16[8192,256]{1,0:T(8,128)(2,1)S(1)}, bf16[8192,256]{1,0:T(8,128)(2,1)}, u32[]{:S(2)}) %copy-start.6) | copy-done | bytes 4194328
  37.4 0.0 copy-start.3
  37.4 0.0 copy-start.7
  37.4 1.9 %shard_map.39.rest_2_ = f32[16,256]{1,0:T(8,128)S(1)} custom-call(s32[2]{0:T(128)S(1)} %get-tuple-element.26.places, f32[16,8192]{1,0:T(8,128)S(1)} %collective-permute-done.2.block, bf16[8192,256]{1,0:T(8,128)(2,1)S(1)} %copy-done.6, bf16[8192,256]{1,0:T(8,128)(2,1)S(1)} %copy-done.2), custom_call_target="tpu_custom_call" | custom-call | bytes 524288 | tf_op jit(solution)/shard_map/pallas_call | solution.py:58
  39.2 0.0 collective-permute-done.3.block
  39.2 1.2 %shard_map.40.rest_3_ = f32[16,256]{1,0:T(8,128)S(1)} custom-call(s32[2]{0:T(128)S(1)} %pad_add_fusion.3.places, f32[16,4096]{1,0:T(8,128)S(1)} %collective-permute-done.3.block, bf16[8192,256]{1,0:T(8,128)(2,1)S(1)} %copy-done.6, bf16[8192,256]{1,0:T(8,128)(2,1)S(1)} %copy-done.2), custom_call_target="tpu_custom_call" | custom-call | bytes 262144 | tf_op jit(solution)/shard_map/pallas_call | solution.py:58
  40.5 0.0 collective-permute-done.1.block
  40.5 0.0 copy-done.3
  40.5 0.3 copy-done.7
  40.8 1.2 %shard_map.41 = (f32[16,256]{1,0:T(8,128)S(1)}, f32[16,256]{1,0:T(8,128)S(1)}, f32[16,256]{1,0:T(8,128)S(1)}, f32[16,256]{1,0:T(8,128)S(1)}) custom-call(s32[6]{0:T(128)S(1)} %stack.53.places, f32[16,4096]{1,0:T(8,128)S(1)} %collective-permute-done.1.block, bf16[8192,256]{1,0:T(8,128)(2,1)S(1)} %copy-done.7, bf16[8192,256]{1,0:T(8,128)(2,1)S(1)} %copy-done.3, ...), custom_call_target="tpu_custom_call" | custom-call | bytes 262144 | tf_op jit(solution)/shard_map/pallas_call | solution.py:58
  42.1 0.1 collective-permute-start.4
  42.1 1.6 %collective-permute-start.5 = (f32[16,256]{1,0:T(8,128)S(1)}, f32[16,256]{1,0:T(8,128)S(1)}, u32[]{:S(2)}, u32[]{:S(2)}) collective-permute-start(f32[16,256]{1,0:T(8,128)S(1)} %get-tuple-element.21), channel_id=1, source_target_pairs={{0,2},{1,3},{2,0},{3,1},{4,6},{5,7},{6,4},{7,5},{8,10},{9,11},{10,... | collective-permute-start | bytes 49160 | tf_op jit(solution)/shard_map/ppermute | solution.py:148
  43.7 1.4 %collective-permute-start.6 = (f32[16,256]{1,0:T(8,128)S(1)}, f32[16,256]{1,0:T(8,128)S(1)}, u32[]{:S(2)}, u32[]{:S(2)}) collective-permute-start(f32[16,256]{1,0:T(8,128)S(1)} %get-tuple-element.22), channel_id=1, source_target_pairs={{0,3},{1,0},{2,1},{3,2},{4,7},{5,4},{6,5},{7,6},{8,11},{9,8},{10,9... | collective-permute-start | bytes 49160 | tf_op jit(solution)/shard_map/ppermute | solution.py:148
  45.1 0.2 collective-permute-done.4
  45.3 0.7 %collective-permute-done.5 = f32[16,256]{1,0:T(8,128)S(1)} collective-permute-done((f32[16,256]{1,0:T(8,128)S(1)}, f32[16,256]{1,0:T(8,128)S(1)}, u32[]{:S(2)}, u32[]{:S(2)}) %collective-permute-start.5) | collective-permute-done | bytes 16416 | tf_op jit(solution)/shard_map/ppermute | solution.py:148
  45.9 0.6 %collective-permute-done.6 = f32[16,256]{1,0:T(8,128)S(1)} collective-permute-done((f32[16,256]{1,0:T(8,128)S(1)}, f32[16,256]{1,0:T(8,128)S(1)}, u32[]{:S(2)}, u32[]{:S(2)}) %collective-permute-start.6) | collective-permute-done | bytes 16416 | tf_op jit(solution)/shard_map/ppermute | solution.py:148
  46.5 0.7 %multiply_select_fusion = f32[16,256]{1,0:T(8,128)} fusion(f32[16,256]{1,0:T(8,128)S(1)} %collective-permute-done.6, f32[16,256]{1,0:T(8,128)S(1)} %collective-permute-done.5, f32[16,256]{1,0:T(8,128)S(1)} %get-tuple-element.19, f32[16,256]{1,0:T(8,128)S(1)} %collective-permute-done.4, s32[256]{0:T(256)S(1)} %iota_add_fusion.1, s32[16]{0:T(128)S(1)} %iota_add_fusion.2), kind=kLoop, calls=%fused_computation.5 | loop fusion | flops 40960 | bytes 83008 | tf_op jit(solution)/shard_map/jit(_where)/select_n | solution.py:155
  (5 shorter events, 0.1 us)
Async XLA Ops:
  0.0 16.7 %collective-permute-start = (f32[16,8192]{1,0:T(8,128)}, f32[16,8192]{1,0:T(8,128)S(1)}, u32[]{:S(2)}, u32[]{:S(2)}) collective-permute-start(f32[16,8192]{1,0:T(8,128)} %block), channel_id=1, source_target_pairs={{0,8},{8,12},{12,4},{4,0},{1,9},{9,13},{13,5},{5,1},{2,10},{10,14}... | collective-permute-start | bytes 1572872 | tf_op jit(solution)/shard_map/ppermute | solution.py:113
  4.7 8.0 %copy-start.8 = (f32[16,8192]{1,0:T(8,128)S(1)}, f32[16,8192]{1,0:T(8,128)}, u32[]{:S(2)}) copy-start(f32[16,8192]{1,0:T(8,128)} %block) | copy-start | bytes 1572868
  12.7 20.2 %collective-permute-start.2 = (f32[16,8192]{1,0:T(8,128)S(1)}, f32[16,8192]{1,0:T(8,128)S(1)}, u32[]{:S(2)}, u32[]{:S(2)}) collective-permute-start(f32[16,8192]{1,0:T(8,128)S(1)} %copy-done.8), channel_id=1, source_target_pairs={{8,0},{12,8},{4,12},{0,4},{9,1},{13,9},{5,13},{1,5},{10,2},{14,10}... | collective-permute-start | bytes 1572872 | tf_op jit(solution)/shard_map/ppermute | solution.py:124
  16.7 22.5 %collective-permute-start.3 = (f32[16,4096]{1,0:T(8,128)S(1)}, f32[16,4096]{1,0:T(8,128)S(1)}, u32[]{:S(2)}, u32[]{:S(2)}) collective-permute-start(f32[16,4096]{1,0:T(8,128)S(1)} %slice.8), channel_id=1, source_target_pairs={{0,8},{8,12},{12,4},{4,0},{1,9},{9,13},{13,5},{5,1},{2,10},{10,14}... | collective-permute-start | bytes 786440 | tf_op jit(solution)/shard_map/ppermute | solution.py:127
  20.0 2.2 %copy-start = (bf16[8192,256]{1,0:T(8,128)(2,1)S(1)}, bf16[8192,256]{1,0:T(8,128)(2,1)}, u32[]{:S(2)}) copy-start(bf16[8192,256]{1,0:T(8,128)(2,1)} %get-tuple-element.15.low) | copy-start | bytes 12582916
  22.2 2.2 %copy-start.4 = (bf16[8192,256]{1,0:T(8,128)(2,1)S(1)}, bf16[8192,256]{1,0:T(8,128)(2,1)}, u32[]{:S(2)}) copy-start(bf16[8192,256]{1,0:T(8,128)(2,1)} %get-tuple-element.14.high) | copy-start | bytes 12582916
  26.3 14.2 %collective-permute-start.1 = (f32[16,4096]{1,0:T(8,128)S(1)}, f32[16,4096]{1,0:T(8,128)S(1)}, u32[]{:S(2)}, u32[]{:S(2)}) collective-permute-start(f32[16,4096]{1,0:T(8,128)S(1)} %slice.6), channel_id=1, source_target_pairs={{0,8},{8,12},{12,4},{4,0},{1,9},{9,13},{13,5},{5,1},{2,10},{10,14}... | collective-permute-start | bytes 786440 | tf_op jit(solution)/shard_map/ppermute | solution.py:135
  26.6 2.2 %copy-start.1 = (bf16[8192,256]{1,0:T(8,128)(2,1)S(1)}, bf16[8192,256]{1,0:T(8,128)(2,1)}, u32[]{:S(2)}) copy-start(bf16[8192,256]{1,0:T(8,128)(2,1)} %get-tuple-element.15.low) | copy-start | bytes 12582916
  28.8 2.2 %copy-start.5 = (bf16[8192,256]{1,0:T(8,128)(2,1)S(1)}, bf16[8192,256]{1,0:T(8,128)(2,1)}, u32[]{:S(2)}) copy-start(bf16[8192,256]{1,0:T(8,128)(2,1)} %get-tuple-element.14.high) | copy-start | bytes 12582916
  33.0 2.2 %copy-start.2 = (bf16[8192,256]{1,0:T(8,128)(2,1)S(1)}, bf16[8192,256]{1,0:T(8,128)(2,1)}, u32[]{:S(2)}) copy-start(bf16[8192,256]{1,0:T(8,128)(2,1)} %get-tuple-element.15.low) | copy-start | bytes 12582916
  35.2 2.2 %copy-start.6 = (bf16[8192,256]{1,0:T(8,128)(2,1)S(1)}, bf16[8192,256]{1,0:T(8,128)(2,1)}, u32[]{:S(2)}) copy-start(bf16[8192,256]{1,0:T(8,128)(2,1)} %get-tuple-element.14.high) | copy-start | bytes 12582916
  37.4 3.1 %copy-start.3 = (bf16[8192,256]{1,0:T(8,128)(2,1)S(1)}, bf16[8192,256]{1,0:T(8,128)(2,1)}, u32[]{:S(2)}) copy-start(bf16[8192,256]{1,0:T(8,128)(2,1)} %get-tuple-element.15.low) | copy-start | bytes 12582916
  37.4 3.5 %copy-start.7 = (bf16[8192,256]{1,0:T(8,128)(2,1)S(1)}, bf16[8192,256]{1,0:T(8,128)(2,1)}, u32[]{:S(2)}) copy-start(bf16[8192,256]{1,0:T(8,128)(2,1)} %get-tuple-element.14.high) | copy-start | bytes 12582916
  42.1 3.2 %collective-permute-start.4 = (f32[16,256]{1,0:T(8,128)S(1)}, f32[16,256]{1,0:T(8,128)S(1)}, u32[]{:S(2)}, u32[]{:S(2)}) collective-permute-start(f32[16,256]{1,0:T(8,128)S(1)} %get-tuple-element.20), channel_id=1, source_target_pairs={{0,1},{1,2},{2,3},{3,0},{4,5},{5,6},{6,7},{7,4},{8,9},{9,10},{10,1... | collective-permute-start | bytes 49160 | tf_op jit(solution)/shard_map/ppermute | solution.py:148
  42.1 3.8 %collective-permute-start.5 = (f32[16,256]{1,0:T(8,128)S(1)}, f32[16,256]{1,0:T(8,128)S(1)}, u32[]{:S(2)}, u32[]{:S(2)}) collective-permute-start(f32[16,256]{1,0:T(8,128)S(1)} %get-tuple-element.21), channel_id=1, source_target_pairs={{0,2},{1,3},{2,0},{3,1},{4,6},{5,7},{6,4},{7,5},{8,10},{9,11},{10,... | collective-permute-start | bytes 49160 | tf_op jit(solution)/shard_map/ppermute | solution.py:148
  43.7 2.8 %collective-permute-start.6 = (f32[16,256]{1,0:T(8,128)S(1)}, f32[16,256]{1,0:T(8,128)S(1)}, u32[]{:S(2)}, u32[]{:S(2)}) collective-permute-start(f32[16,256]{1,0:T(8,128)S(1)} %get-tuple-element.22), channel_id=1, source_target_pairs={{0,3},{1,0},{2,1},{3,2},{4,7},{5,4},{6,5},{7,6},{8,11},{9,8},{10,9... | collective-permute-start | bytes 49160 | tf_op jit(solution)/shard_map/ppermute | solution.py:148

commit v7 on v6

--- a/solution.py
+++ b/solution.py
@@ -13,9 +13,52 @@
 largest_bf16 = 3.3895313892515355e38
 
 
-def halves(array):
-    high = lax.reduce_precision(jnp.clip(array, -largest_bf16, largest_bf16), 8, 7)
-    return high.astype(jnp.bfloat16), (array - high).astype(jnp.bfloat16)
+def weights_kernel(shift, covariance, high, low, held, arrived):
+    depth, columns = covariance.shape
+    step = held.shape[1]
+    pieces = depth // step
+
+    def copy(piece):
+        return pltpu.make_async_copy(
+            covariance.at[pl.ds(piece * step, step)], held.at[piece % 4], arrived.at[piece % 4]
+        )
+
+    for piece in range(min(3, pieces)):
+        copy(piece).start()
+    ahead = lax.broadcasted_iota(jnp.int32, (step, columns), 0)
+    ahead -= lax.broadcasted_iota(jnp.int32, (step, columns), 1)
+    for piece in range(pieces):
+        if piece + 3 < pieces:
+            copy(piece + 3).start()
+        copy(piece).wait()
+        scaled = -step_size * held[piece % 4]
+        values = jnp.where(ahead == shift[0] - piece * step, scaled + 1.0, scaled)
+        upper = values.astype(jnp.bfloat16)
+        rows = slice(piece * step, (piece + 1) * step)
+        high[rows] = upper
+        low[rows] = (values - upper.astype(jnp.float32)).astype(jnp.bfloat16)
+
+
+def weights_of(covariance, shift):
+    depth, columns = covariance.shape
+    step = math.gcd(depth, 512)
+    return pl.pallas_call(
+        weights_kernel,
+        out_shape=[pltpu.VMEM((depth, columns), jnp.bfloat16)] * 2,
+        in_specs=[
+            pl.BlockSpec(memory_space=pltpu.SMEM),
+            pl.BlockSpec(memory_space=pltpu.HBM),
+        ],
+        out_specs=[pl.BlockSpec(memory_space=pltpu.VMEM)] * 2,
+        scratch_shapes=[
+            pltpu.VMEM((4, step, columns), jnp.float32),
+            pltpu.SemaphoreType.DMA((4,)),
+        ],
+        compiler_params=pltpu.CompilerParams(vmem_limit_bytes=8 * 1024 * 1024),
+        cost_estimate=pl.CostEstimate(
+            flops=0, bytes_accessed=covariance.size * 4, transcendentals=0
+        ),
+    )(shift, pltpu.with_memory_space_constraint(covariance, pltpu.HBM))
 
 
 def slot_kernel(first_k, parts, places, block, high, low, *rest):
@@ -63,7 +106,7 @@
         out_specs=[pl.BlockSpec(memory_space=pltpu.VMEM)] * shares,
         compiler_params=pltpu.CompilerParams(vmem_limit_bytes=(2 + len(others) // 4) * 1024 * 1024),
         cost_estimate=pl.CostEstimate(flops=0, bytes_accessed=block.size * 4, transcendentals=0),
-    )(places, block, *weights, *others)
+    )(places, block, *[pltpu.with_memory_space_constraint(w, pltpu.VMEM) for w in weights], *others)
 
 
 def sum_of(terms):
@@ -86,10 +129,8 @@
     assert all_rows <= part_width and part_width % tile_width == 0
     assert rows_share % block_rows == 0
 
-    k_ids = rep_index * part_width + jnp.arange(part_width, dtype=jnp.int32)
-    c_ids = offset + jnp.arange(tile_width, dtype=jnp.int32)
-    chosen = (k_ids[:, None] == c_ids[None, :]).astype(jnp.float32)
-    weights = halves(chosen - step_size * covariance_columns)
+    shift = jnp.reshape(offset - rep_index * part_width, (1,)).astype(jnp.int32)
+    weights = weights_of(covariance_columns, shift)
 
     half = part_width // 2
     assert all_rows <= half and half % tile_width == 0
@@ -111,9 +152,10 @@
         return jnp.where(up < team_count, up, 2 * team_count - 1 - up)
 
     first = lax.ppermute(omega_rows, "team", onward)
-    own, *weights = lax.optimization_barrier((omega_rows, *weights))
+    own_part = slot_product(places_of(team_index), omega_rows, weights)
+    own, *own_part = lax.optimization_barrier((omega_rows, *own_part))
     last_step = team_count // 2
-    gathered = [(own, 0), (first, 1)]
+    gathered = [(first, 1)]
     held = first
     for step in range(2, last_step):
         held = lax.ppermute(held, "team", onward)
@@ -125,7 +167,7 @@
         gathered.append((held, -step))
 
     last_left = lax.ppermute(last_held[:, :half], "team", onward)
-    others, sources = [], []
+    others, sources = own_part, [team_index]
     for block, step in gathered:
         source = device_at(place - step)
         others += slot_product(places_of(source), block, weights)

time: 47.7 us -> 58.2 us (1.22)
  the two profiles are of different devices: /device:TPU:0 before, /device:TPU:25 now
where the time goes in v7:
time: 58.2 us; the launch traced here: 57.7 us
  local copies, waits for them, and re-layouts  17.2 us (30%)
  starting transfers between devices  13.4 us (23%)
  Pallas kernels  13.3 us (23%)
  waiting for transfers between devices  12.2 us (21%)
  other arithmetic  0.91 us (2%)
  between operations  0.72 us (1%)
    unnamed x20, local copies, waits for them, and re-layouts  17.1 us
    ppermute x3, starting transfers between devices, per_device(): terms.append(lax.ppermute(shares[by], 'rep', pairs))  10.7 us
    pallas_call x5, Pallas kernels, slot_product(): pl.pallas_call(functools.partial(slot_kernel, first_k, len(others)), out_...  7.97 us
    pallas_call x1, Pallas kernels, weights_of(): pl.pallas_call(weights_kernel, out_shape=[pltpu.VMEM((depth, columns), jn...  5.34 us
    ppermute x1, waiting for transfers between devices, per_device(): last_right = lax.ppermute(last_held[:, half:], 'team', onward)  4.42 us
    ppermute x1, waiting for transfers between devices, per_device(): held = lax.ppermute(held, 'team', backward)  4.27 us
    ppermute x3, waiting for transfers between devices, per_device(): terms.append(lax.ppermute(shares[by], 'rep', pairs))  2.94 us
    ppermute x1, starting transfers between devices, per_device(): held = lax.ppermute(held, 'team', backward)  1.42 us
  transfers between devices with their start and end apart: 7, of which 6 were waited for; matrix products, arithmetic and copies ran while one was open for 1% of the time, Pallas kernels for 21%

profile of v7, /device:TPU:25, one launch (start us, length us, event | category | flops | bytes accessed | tf_op | source)
XLA Modules:
  0.0 57.7 jit_solution(8280053022836923230)
XLA Ops:
  0.0 0.1 collective-permute-start
  0.7 0.0 copy-start.9
  0.7 5.3 %shard_map.37 = (bf16[8192,256]{1,0:T(8,128)(2,1)S(1)}, bf16[8192,256]{1,0:T(8,128)(2,1)S(1)}) custom-call(s32[1]{0:T(128)} %bitcast.8.shift, f32[8192,256]{1,0:T(8,128)} %covariance.1), custom_call_target="tpu_custom_call" | custom-call | bytes 8388608 | tf_op jit(solution)/shard_map/pallas_call | solution.py:45
  6.1 0.0 copy-start
  6.1 1.9 %copy-done = bf16[8192,256]{1,0:T(8,128)(2,1)} copy-done((bf16[8192,256]{1,0:T(8,128)(2,1)}, bf16[8192,256]{1,0:T(8,128)(2,1)S(1)}, u32[]{:S(2)}) %copy-start) | copy-done | bytes 4194328
  8.0 0.0 copy-start.5
  8.0 2.0 %copy-done.5 = bf16[8192,256]{1,0:T(8,128)(2,1)} copy-done((bf16[8192,256]{1,0:T(8,128)(2,1)}, bf16[8192,256]{1,0:T(8,128)(2,1)S(1)}, u32[]{:S(2)}) %copy-start.5) | copy-done | bytes 4194328
  10.0 0.1 pad_add_fusion.1.places
  10.1 0.0 copy-done.9
  10.1 0.0 copy-start.1
  10.1 2.2 %copy-done.1 = bf16[8192,256]{1,0:T(8,128)(2,1)S(1)} copy-done((bf16[8192,256]{1,0:T(8,128)(2,1)S(1)}, bf16[8192,256]{1,0:T(8,128)(2,1)}, u32[]{:S(2)}) %copy-start.1) | copy-done | bytes 4194328
  12.3 0.0 copy-start.6
  12.3 2.2 %copy-done.6 = bf16[8192,256]{1,0:T(8,128)(2,1)S(1)} copy-done((bf16[8192,256]{1,0:T(8,128)(2,1)S(1)}, bf16[8192,256]{1,0:T(8,128)(2,1)}, u32[]{:S(2)}) %copy-start.6) | copy-done | bytes 4194328
  14.5 1.9 %shard_map.39.rest_0_ = f32[16,256]{1,0:T(8,128)S(1)} custom-call(s32[2]{0:T(128)S(1)} %pad_add_fusion.1.places, f32[16,8192]{1,0:T(8,128)S(1)} %copy-done.9, bf16[8192,256]{1,0:T(8,128)(2,1)S(1)} %copy-done.1, bf16[8192,256]{1,0:T(8,128)(2,1)S(1)} %copy-done.6), custom_call_target="tpu_custom_call" | custom-call | bytes 524288 | tf_op jit(solution)/shard_map/pallas_call | solution.py:101
  16.3 1.4 %collective-permute-start.2 = (f32[16,8192]{1,0:T(8,128)S(1)}, f32[16,8192]{1,0:T(8,128)S(1)}, u32[]{:S(2)}, u32[]{:S(2)}) collective-permute-start(f32[16,8192]{1,0:T(8,128)S(1)} %copy-done.9), channel_id=1, source_target_pairs={{8,0},{12,8},{4,12},{0,4},{9,1},{13,9},{5,13},{1,5},{10,2},{14,10}... | collective-permute-start | bytes 1572872 | tf_op jit(solution)/shard_map/ppermute | solution.py:166
  17.7 0.1 pad_add_fusion.places
  17.8 0.0 collective-permute-done.block
  17.8 1.0 %collective-permute-start.3 = (f32[16,4096]{1,0:T(8,128)S(1)}, f32[16,4096]{1,0:T(8,128)S(1)}, u32[]{:S(2)}, u32[]{:S(2)}) collective-permute-start(f32[16,4096]{1,0:T(8,128)S(1)} %slice.8), channel_id=1, source_target_pairs={{0,8},{8,12},{12,4},{4,0},{1,9},{9,13},{13,5},{5,1},{2,10},{10,14}... | collective-permute-start | bytes 786440 | tf_op jit(solution)/shard_map/ppermute | solution.py:169
  18.8 0.0 copy-start.2
  18.9 2.2 %copy-done.2 = bf16[8192,256]{1,0:T(8,128)(2,1)S(1)} copy-done((bf16[8192,256]{1,0:T(8,128)(2,1)S(1)}, bf16[8192,256]{1,0:T(8,128)(2,1)}, u32[]{:S(2)}) %copy-start.2) | copy-done | bytes 4194328
  21.0 0.0 copy-start.7
  21.0 2.2 %copy-done.7 = bf16[8192,256]{1,0:T(8,128)(2,1)S(1)} copy-done((bf16[8192,256]{1,0:T(8,128)(2,1)S(1)}, bf16[8192,256]{1,0:T(8,128)(2,1)}, u32[]{:S(2)}) %copy-start.7) | copy-done | bytes 4194328
  23.2 1.9 %shard_map.38.rest_1_ = f32[16,256]{1,0:T(8,128)S(1)} custom-call(s32[2]{0:T(128)S(1)} %pad_add_fusion.places, f32[16,8192]{1,0:T(8,128)S(1)} %collective-permute-done.block, bf16[8192,256]{1,0:T(8,128)(2,1)S(1)} %copy-done.2, bf16[8192,256]{1,0:T(8,128)(2,1)S(1)} %copy-done.7), custom_call_target="tpu_custom_call" | custom-call | bytes 524288 | tf_op jit(solution)/shard_map/pallas_call | solution.py:101
  25.1 0.2 collective-permute-start.1
  25.3 0.1 stack.53.places
  25.4 0.1 pad_add_fusion.2
  25.5 4.3 %collective-permute-done.2.block = f32[16,8192]{1,0:T(8,128)S(1)} collective-permute-done((f32[16,8192]{1,0:T(8,128)S(1)}, f32[16,8192]{1,0:T(8,128)S(1)}, u32[]{:S(2)}, u32[]{:S(2)}) %collective-permute-start.2) | collective-permute-done | bytes 524320 | tf_op jit(solution)/shard_map/ppermute | solution.py:166
  29.7 0.0 copy-start.3
  29.7 2.2 %copy-done.3 = bf16[8192,256]{1,0:T(8,128)(2,1)S(1)} copy-done((bf16[8192,256]{1,0:T(8,128)(2,1)S(1)}, bf16[8192,256]{1,0:T(8,128)(2,1)}, u32[]{:S(2)}) %copy-start.3) | copy-done | bytes 4194328
  31.9 0.0 copy-start.8
  31.9 2.2 %copy-done.8 = bf16[8192,256]{1,0:T(8,128)(2,1)S(1)} copy-done((bf16[8192,256]{1,0:T(8,128)(2,1)S(1)}, bf16[8192,256]{1,0:T(8,128)(2,1)}, u32[]{:S(2)}) %copy-start.8) | copy-done | bytes 4194328
  34.1 1.9 %shard_map.40.rest_2_ = f32[16,256]{1,0:T(8,128)S(1)} custom-call(s32[2]{0:T(128)S(1)} %get-tuple-element.25.places, f32[16,8192]{1,0:T(8,128)S(1)} %collective-permute-done.2.block, bf16[8192,256]{1,0:T(8,128)(2,1)S(1)} %copy-done.3, bf16[8192,256]{1,0:T(8,128)(2,1)S(1)} %copy-done.8), custom_call_target="tpu_custom_call" | custom-call | bytes 524288 | tf_op jit(solution)/shard_map/pallas_call | solution.py:101
  36.0 0.6 %collective-permute-done.3.block = f32[16,4096]{1,0:T(8,128)S(1)} collective-permute-done((f32[16,4096]{1,0:T(8,128)S(1)}, f32[16,4096]{1,0:T(8,128)S(1)}, u32[]{:S(2)}, u32[]{:S(2)}) %collective-permute-start.3) | collective-permute-done | bytes 262176 | tf_op jit(solution)/shard_map/ppermute | solution.py:169
  36.6 0.0 copy-start.4
  36.6 1.2 %shard_map.41.rest_3_ = f32[16,256]{1,0:T(8,128)S(1)} custom-call(s32[2]{0:T(128)S(1)} %get-tuple-element.26.places, f32[16,4096]{1,0:T(8,128)S(1)} %collective-permute-done.3.block, bf16[8192,256]{1,0:T(8,128)(2,1)S(1)} %copy-done.3, bf16[8192,256]{1,0:T(8,128)(2,1)S(1)} %copy-done.8), custom_call_target="tpu_custom_call" | custom-call | bytes 262144 | tf_op jit(solution)/shard_map/pallas_call | solution.py:101
  37.8 4.4 %collective-permute-done.1.block = f32[16,4096]{1,0:T(8,128)S(1)} collective-permute-done((f32[16,4096]{1,0:T(8,128)S(1)}, f32[16,4096]{1,0:T(8,128)S(1)}, u32[]{:S(2)}, u32[]{:S(2)}) %collective-permute-start.1) | collective-permute-done | bytes 262176 | tf_op jit(solution)/shard_map/ppermute | solution.py:177
  42.2 0.0 copy-done.4
  42.2 1.2 %shard_map.42 = (f32[16,256]{1,0:T(8,128)S(1)}, f32[16,256]{1,0:T(8,128)S(1)}, f32[16,256]{1,0:T(8,128)S(1)}, f32[16,256]{1,0:T(8,128)S(1)}) custom-call(s32[6]{0:T(128)S(1)} %stack.53.places, f32[16,4096]{1,0:T(8,128)S(1)} %collective-permute-done.1.block, bf16[8192,256]{1,0:T(8,128)(2,1)S(1)} %copy-done.4, bf16[8192,256]{1,0:T(8,128)(2,1)S(1)} %copy-done.8, ...), custom_call_target="tpu_custom_call" | custom-call | bytes 262144 | tf_op jit(solution)/shard_map/pallas_call | solution.py:101
  43.4 10.2 %collective-permute-start.4 = (f32[16,256]{1,0:T(8,128)S(1)}, f32[16,256]{1,0:T(8,128)S(1)}, u32[]{:S(2)}, u32[]{:S(2)}) collective-permute-start(f32[16,256]{1,0:T(8,128)S(1)} %get-tuple-element.22), channel_id=1, source_target_pairs={{0,1},{1,2},{2,3},{3,0},{4,5},{5,6},{6,7},{7,4},{8,9},{9,10},{10,1... | collective-permute-start | bytes 49160 | tf_op jit(solution)/shard_map/ppermute | solution.py:190
  53.6 0.3 collective-permute-start.5
  53.9 0.2 collective-permute-start.6
  54.1 0.4 collective-permute-done.4
  54.5 1.7 %collective-permute-done.5 = f32[16,256]{1,0:T(8,128)S(1)} collective-permute-done((f32[16,256]{1,0:T(8,128)S(1)}, f32[16,256]{1,0:T(8,128)S(1)}, u32[]{:S(2)}, u32[]{:S(2)}) %collective-permute-start.5) | collective-permute-done | bytes 16416 | tf_op jit(solution)/shard_map/ppermute | solution.py:190
  56.2 0.8 %collective-permute-done.6 = f32[16,256]{1,0:T(8,128)S(1)} collective-permute-done((f32[16,256]{1,0:T(8,128)S(1)}, f32[16,256]{1,0:T(8,128)S(1)}, u32[]{:S(2)}, u32[]{:S(2)}) %collective-permute-start.6) | collective-permute-done | bytes 16416 | tf_op jit(solution)/shard_map/ppermute | solution.py:190
  57.1 0.7 %multiply_select_fusion = f32[16,256]{1,0:T(8,128)} fusion(f32[16,256]{1,0:T(8,128)S(1)} %collective-permute-done.6, f32[16,256]{1,0:T(8,128)S(1)} %collective-permute-done.5, f32[16,256]{1,0:T(8,128)S(1)} %get-tuple-element.21, f32[16,256]{1,0:T(8,128)S(1)} %collective-permute-done.4, s32[256]{0:T(256)S(1)} %iota_add_fusion, s32[16]{0:T(128)S(1)} %iota_add_fusion.1), kind=kLoop, calls=%fused_computation | loop fusion | flops 40960 | bytes 83008 | tf_op jit(solution)/shard_map/jit(_where)/select_n | solution.py:197
  (4 shorter events, 0.0 us)
Async XLA Ops:
  0.0 17.8 %collective-permute-start = (f32[16,8192]{1,0:T(8,128)}, f32[16,8192]{1,0:T(8,128)S(1)}, u32[]{:S(2)}, u32[]{:S(2)}) collective-permute-start(f32[16,8192]{1,0:T(8,128)} %block.1), channel_id=1, source_target_pairs={{0,8},{8,12},{12,4},{4,0},{1,9},{9,13},{13,5},{5,1},{2,10},{10,14}... | collective-permute-start | bytes 1572872 | tf_op jit(solution)/shard_map/ppermute | solution.py:154
  0.7 9.4 %copy-start.9 = (f32[16,8192]{1,0:T(8,128)S(1)}, f32[16,8192]{1,0:T(8,128)}, u32[]{:S(2)}) copy-start(f32[16,8192]{1,0:T(8,128)} %block.1) | copy-start | bytes 1572868
  6.1 2.0 %copy-start = (bf16[8192,256]{1,0:T(8,128)(2,1)}, bf16[8192,256]{1,0:T(8,128)(2,1)S(1)}, u32[]{:S(2)}) copy-start(bf16[8192,256]{1,0:T(8,128)(2,1)S(1)} %get-tuple-element.15.high) | copy-start | bytes 12582916
  8.0 2.0 %copy-start.5 = (bf16[8192,256]{1,0:T(8,128)(2,1)}, bf16[8192,256]{1,0:T(8,128)(2,1)S(1)}, u32[]{:S(2)}) copy-start(bf16[8192,256]{1,0:T(8,128)(2,1)S(1)} %get-tuple-element.16.low) | copy-start | bytes 12582916
  10.1 2.2 %copy-start.1 = (bf16[8192,256]{1,0:T(8,128)(2,1)S(1)}, bf16[8192,256]{1,0:T(8,128)(2,1)}, u32[]{:S(2)}) copy-start(bf16[8192,256]{1,0:T(8,128)(2,1)} %copy-done) | copy-start | bytes 12582916
  12.3 2.2 %copy-start.6 = (bf16[8192,256]{1,0:T(8,128)(2,1)S(1)}, bf16[8192,256]{1,0:T(8,128)(2,1)}, u32[]{:S(2)}) copy-start(bf16[8192,256]{1,0:T(8,128)(2,1)} %copy-done.5) | copy-start | bytes 12582916
  16.3 13.4 %collective-permute-start.2 = (f32[16,8192]{1,0:T(8,128)S(1)}, f32[16,8192]{1,0:T(8,128)S(1)}, u32[]{:S(2)}, u32[]{:S(2)}) collective-permute-start(f32[16,8192]{1,0:T(8,128)S(1)} %copy-done.9), channel_id=1, source_target_pairs={{8,0},{12,8},{4,12},{0,4},{9,1},{13,9},{5,13},{1,5},{10,2},{14,10}... | collective-permute-start | bytes 1572872 | tf_op jit(solution)/shard_map/ppermute | solution.py:166
  17.8 18.7 %collective-permute-start.3 = (f32[16,4096]{1,0:T(8,128)S(1)}, f32[16,4096]{1,0:T(8,128)S(1)}, u32[]{:S(2)}, u32[]{:S(2)}) collective-permute-start(f32[16,4096]{1,0:T(8,128)S(1)} %slice.8), channel_id=1, source_target_pairs={{0,8},{8,12},{12,4},{4,0},{1,9},{9,13},{13,5},{5,1},{2,10},{10,14}... | collective-permute-start | bytes 786440 | tf_op jit(solution)/shard_map/ppermute | solution.py:169
  18.8 2.2 %copy-start.2 = (bf16[8192,256]{1,0:T(8,128)(2,1)S(1)}, bf16[8192,256]{1,0:T(8,128)(2,1)}, u32[]{:S(2)}) copy-start(bf16[8192,256]{1,0:T(8,128)(2,1)} %copy-done) | copy-start | bytes 12582916
  21.0 2.2 %copy-start.7 = (bf16[8192,256]{1,0:T(8,128)(2,1)S(1)}, bf16[8192,256]{1,0:T(8,128)(2,1)}, u32[]{:S(2)}) copy-start(bf16[8192,256]{1,0:T(8,128)(2,1)} %copy-done.5) | copy-start | bytes 12582916
  25.1 17.1 %collective-permute-start.1 = (f32[16,4096]{1,0:T(8,128)S(1)}, f32[16,4096]{1,0:T(8,128)S(1)}, u32[]{:S(2)}, u32[]{:S(2)}) collective-permute-start(f32[16,4096]{1,0:T(8,128)S(1)} %slice.6), channel_id=1, source_target_pairs={{0,8},{8,12},{12,4},{4,0},{1,9},{9,13},{13,5},{5,1},{2,10},{10,14}... | collective-permute-start | bytes 786440 | tf_op jit(solution)/shard_map/ppermute | solution.py:177
  29.7 2.2 %copy-start.3 = (bf16[8192,256]{1,0:T(8,128)(2,1)S(1)}, bf16[8192,256]{1,0:T(8,128)(2,1)}, u32[]{:S(2)}) copy-start(bf16[8192,256]{1,0:T(8,128)(2,1)} %copy-done) | copy-start | bytes 12582916
  31.9 2.2 %copy-start.8 = (bf16[8192,256]{1,0:T(8,128)(2,1)S(1)}, bf16[8192,256]{1,0:T(8,128)(2,1)}, u32[]{:S(2)}) copy-start(bf16[8192,256]{1,0:T(8,128)(2,1)} %copy-done.5) | copy-start | bytes 12582916
  36.6 5.6 %copy-start.4 = (bf16[8192,256]{1,0:T(8,128)(2,1)S(1)}, bf16[8192,256]{1,0:T(8,128)(2,1)}, u32[]{:S(2)}) copy-start(bf16[8192,256]{1,0:T(8,128)(2,1)} %copy-done) | copy-start | bytes 12582916
  43.4 11.1 %collective-permute-start.4 = (f32[16,256]{1,0:T(8,128)S(1)}, f32[16,256]{1,0:T(8,128)S(1)}, u32[]{:S(2)}, u32[]{:S(2)}) collective-permute-start(f32[16,256]{1,0:T(8,128)S(1)} %get-tuple-element.22), channel_id=1, source_target_pairs={{0,1},{1,2},{2,3},{3,0},{4,5},{5,6},{6,7},{7,4},{8,9},{9,10},{10,1... | collective-permute-start | bytes 49160 | tf_op jit(solution)/shard_map/ppermute | solution.py:190
  53.6 2.6 %collective-permute-start.5 = (f32[16,256]{1,0:T(8,128)S(1)}, f32[16,256]{1,0:T(8,128)S(1)}, u32[]{:S(2)}, u32[]{:S(2)}) collective-permute-start(f32[16,256]{1,0:T(8,128)S(1)} %get-tuple-element.23), channel_id=1, source_target_pairs={{0,2},{1,3},{2,0},{3,1},{4,6},{5,7},{6,4},{7,5},{8,10},{9,11},{10,... | collective-permute-start | bytes 49160 | tf_op jit(solution)/shard_map/ppermute | solution.py:190
  53.9 3.2 %collective-permute-start.6 = (f32[16,256]{1,0:T(8,128)S(1)}, f32[16,256]{1,0:T(8,128)S(1)}, u32[]{:S(2)}, u32[]{:S(2)}) collective-permute-start(f32[16,256]{1,0:T(8,128)S(1)} %get-tuple-element.24), channel_id=1, source_target_pairs={{0,3},{1,0},{2,1},{3,2},{4,7},{5,4},{6,5},{7,6},{8,11},{9,8},{10,9... | collective-permute-start | bytes 49160 | tf_op jit(solution)/shard_map/ppermute | solution.py:190

commit v8 on v6

v8 whole, which is shorter than its diff:
```python
import functools
import math

import jax
import jax.numpy as jnp
from jax import lax
from jax.experimental import pallas as pl
from jax.experimental.pallas import tpu as pltpu
from jax.sharding import PartitionSpec as P

step_size = 0.5
penalty = 0.1
largest_bf16 = 3.3895313892515355e38


def halves(array):
    high = lax.reduce_precision(jnp.clip(array, -largest_bf16, largest_bf16), 8, 7)
    return high.astype(jnp.bfloat16), (array - high).astype(jnp.bfloat16)


def slots_kernel(first_k, blocks_count, parts_count, places, *refs):
    blocks, refs = refs[:blocks_count], refs[blocks_count:]
    high, low, *refs = refs
    parts, outs = refs[:parts_count], refs[parts_count:]
    rows, depth = blocks[0].shape
    columns = high.shape[1]
    step = math.gcd(depth, 4096)
    all_rows = rows * blocks_count
    total = jnp.zeros((all_rows, columns), jnp.float32)
    for k in range(0, depth, step):
        values = jnp.concatenate([block[:, k : k + step] for block in blocks], 0)
        upper = jnp.clip(values, -largest_bf16, largest_bf16).astype(jnp.bfloat16)
        lower = (values - upper.astype(jnp.float32)).astype(jnp.bfloat16)
        both = jnp.concatenate([upper, lower], 0)
        span = slice(first_k + k, first_k + k + step)
        main = jnp.dot(both, high[span], preferred_element_type=jnp.float32)
        cross = jnp.dot(upper, low[span], preferred_element_type=jnp.float32)
        total += main[:all_rows] + main[all_rows:] + cross
    totals = [total[b * rows : (b + 1) * rows] for b in range(blocks_count)]
    if first_k == 0:
        start = pl.multiple_of(places[0], columns)
        ahead = lax.broadcasted_iota(jnp.int32, (rows, columns), 1)
        ahead -= lax.broadcasted_iota(jnp.int32, (rows, columns), 0)
        for b, block in enumerate(blocks):
            current = block[:, pl.ds(start, columns)]
            mask = ahead == places[1 + b]
            inverse = step_size / jnp.where(mask, current, 1.0)
            totals[b] += jnp.where(mask, inverse, 0.0)
    if not parts_count:
        for out, value in zip(outs, totals):
            out[...] = value
        return
    values = [part[...] for part in parts]
    values[-1] += totals[0]
    per_out = outs[0].shape[0] // rows
    for o, out in enumerate(outs):
        for b in range(per_out):
            found = jnp.zeros((rows, columns), jnp.float32)
            for part, value in enumerate(values):
                found = jnp.where(places[part] == o * per_out + b, value, found)
            out[b * rows : (b + 1) * rows] = found


def slot_products(places, blocks, weights, first_k=0, parts=()):
    rows, columns = blocks[0].shape[0], weights[0].shape[1]
    outs = 2 if parts else len(blocks)
    shape = (rows * len(parts) // 2 if parts else rows, columns)
    return pl.pallas_call(
        functools.partial(slots_kernel, first_k, len(blocks), len(parts)),
        out_shape=[jax.ShapeDtypeStruct(shape, jnp.float32)] * outs,
        in_specs=[pl.BlockSpec(memory_space=pltpu.SMEM)]
        + [pl.BlockSpec(memory_space=pltpu.VMEM)] * (len(blocks) + 2 + len(parts)),
        out_specs=[pl.BlockSpec(memory_space=pltpu.VMEM)] * outs,
        compiler_params=pltpu.CompilerParams(
            vmem_limit_bytes=(4 + len(parts) // 4) * 1024 * 1024
        ),
        cost_estimate=pl.CostEstimate(
            flops=0, bytes_accessed=blocks[0].size * 4, transcendentals=0
        ),
    )(places, *blocks, *weights, *parts)


def sum_of(terms):
    total = terms[0]
    for term in terms[1:]:
        total = total + term
    return total


def per_device(omega_rows, covariance_columns, tile_offsets):
    team_count = lax.axis_size("team")
    rep_count = lax.axis_size("rep")
    team_index = lax.axis_index("team")
    rep_index = lax.axis_index("rep")
    block_rows, part_width = omega_rows.shape
    tile_width = covariance_columns.shape[1]
    all_rows = block_rows * team_count
    rows_share = all_rows // rep_count
    offset = tile_offsets[0]
    assert all_rows <= part_width and part_width % tile_width == 0
    assert rows_share % block_rows == 0 and rep_count & (rep_count - 1) == 0 and rep_count > 1

    k_ids = rep_index * part_width + jnp.arange(part_width, dtype=jnp.int32)
    c_ids = offset + jnp.arange(tile_width, dtype=jnp.int32)
    chosen = (k_ids[:, None] == c_ids[None, :]).astype(jnp.float32)
    weights = halves(chosen - step_size * covariance_columns)

    half = part_width // 2
    assert all_rows <= half and half % tile_width == 0

    def products_of(blocks, sources):
        start = jnp.clip(offset, 0, half - tile_width)
        shifts = [
            jnp.where(rep_index == 0, source * block_rows - offset, 1 << 20) for source in sources
        ]
        places = jnp.stack([start, *shifts]).astype(jnp.int32)
        return slot_products(places, blocks, weights)

    ring = list(range(0, team_count, 2)) + list(range(1, team_count, 2))[::-1]
    onward = [(ring[k], ring[(k + 1) % team_count]) for k in range(team_count)]
    backward = [(to, source) for source, to in onward]
    rank = team_index // 2
    place = jnp.where(team_index % 2 == 0, rank, team_count - 1 - rank)

    def device_at(spot):
        spot = spot % team_count
        up = 2 * spot
        return jnp.where(up < team_count, up, 2 * team_count - 1 - up)

    first = lax.ppermute(omega_rows, "team", onward)
    own, *weights = lax.optimization_barrier((omega_rows, *weights))
    last_step = team_count // 2
    gathered = []
    held = first
    for step in range(2, last_step):
        held = lax.ppermute(held, "team", onward)
        gathered.append((held, step))
    last_held = held
    held = own
    for step in range(1, team_count - last_step):
        held = lax.ppermute(held, "team", backward)
        gathered.append((held, -step))

    last_left = lax.ppermute(last_held[:, :half], "team", onward)
    sources = [team_index, device_at(place - 1)]
    parts = products_of([own, first], sources)
    last_held, *parts = lax.optimization_barrier((last_held, *parts))
    last_right = lax.ppermute(last_held[:, half:], "team", onward)
    for block, step in gathered:
        sources.append(device_at(place - step))
        parts += products_of([block], sources[-1:])
    sources.append(device_at(place - last_step))
    parts += products_of([last_left], sources[-1:])

    share_blocks = rows_share // block_rows
    spots = [
        ((source // share_blocks) ^ rep_index) * share_blocks + source % share_blocks
        for source in sources
    ]
    kept, sent = slot_products(
        jnp.stack(spots).astype(jnp.int32), [last_right], weights, half, parts
    )
    flip = rep_count // 2
    while True:
        pairs = [(d, d ^ flip) for d in range(rep_count)]
        kept = kept + lax.ppermute(sent, "rep", pairs)
        flip //= 2
        if not flip:
            break
        kept, sent = kept[: flip * rows_share], kept[flip * rows_share :]
    moved = kept

    global_rows = rep_index * rows_share + jnp.arange(rows_share, dtype=jnp.int32)
    global_cols = offset + jnp.arange(tile_width, dtype=jnp.int32)
    diagonal = global_rows[:, None] == global_cols[None, :]
    shrunk = jnp.sign(moved) * jnp.maximum(jnp.abs(moved) - step_size * penalty, 0.0)
    return jnp.where(diagonal, moved, shrunk)


def solution(mesh):
    in_specs = (P(("groups", "team"), "rep"), P("rep", ("groups", "team")), P(("groups", "team")))
    out_specs = P("rep", ("groups", "team"))
    return jax.shard_map(
        per_device, mesh=mesh, in_specs=in_specs, out_specs=out_specs, check_vma=False
    )
```

time: 47.7 us -> 46.8 us (0.981)
  waiting for transfers between devices: 5.25 us -> 12.5 us
  local copies, waits for them, and re-layouts: 13.6 us -> 8.81 us
  Pallas kernels: 8.01 us -> 6.37 us
  starting transfers between devices: 10.4 us -> 9.06 us
    unnamed x18 -> x14, local copies, waits for them, and re-layouts: 13.5 us -> 8.76 us
    ppermute x1, waiting for transfers between devices: 0.01 us -> 2.84 us  [per_device(): held = lax.ppermute(held, 'team', backward)]
    ppermute x1, waiting for transfers between devices: 0.01 us -> 2.24 us  [per_device(): last_right = lax.ppermute(last_held[:, half:], 'team', onward)]
    ppermute x3 -> x2, waiting for transfers between devices: 1.44 us -> 3.58 us  [per_device(): kept = kept + lax.ppermute(sent, 'rep', pairs)]
    pallas_call x5 -> x4, Pallas kernels: 8.01 us -> 6.37 us  [slot_products(): pl.pallas_call(functools.partial(slots_kernel, first_k, len(blocks), len(...]
    ppermute x3 -> x2, starting transfers between devices: 3 us -> 1.62 us  [per_device(): kept = kept + lax.ppermute(sent, 'rep', pairs)]
  transfers between devices with their start and end apart: 7 -> 6, of which waited for: 4 -> 5; matrix products, arithmetic and copies ran while one was open for 18% -> 18% of each run, Pallas kernels for 14% -> 11%
where the time goes in v8:
time: 46.8 us; the launch traced here: 46.5 us
  waiting for transfers between devices  12.5 us (27%)
  starting transfers between devices  9.06 us (19%)
  other arithmetic  8.9 us (19%)
  local copies, waits for them, and re-layouts  8.81 us (19%)
  Pallas kernels  6.37 us (14%)
  between operations  0.87 us (2%)
    unnamed x14, local copies, waits for them, and re-layouts  8.76 us
    convert_element_type x1, other arithmetic, halves(): return (high.astype(jnp.bfloat16), (array - high).astype(jnp.bfloat16))  7.97 us
    pallas_call x4, Pallas kernels, slot_products(): pl.pallas_call(functools.partial(slots_kernel, first_k, len(blocks), len(...  6.37 us
    ppermute x1, starting transfers between devices, per_device(): first = lax.ppermute(omega_rows, 'team', onward)  4.04 us
    ppermute x1, waiting for transfers between devices, per_device(): first = lax.ppermute(omega_rows, 'team', onward)  3.83 us
    ppermute x2, waiting for transfers between devices, per_device(): kept = kept + lax.ppermute(sent, 'rep', pairs)  3.58 us
    ppermute x1, starting transfers between devices, per_device(): last_left = lax.ppermute(last_held[:, :half], 'team', onward)  3.33 us
    ppermute x1, waiting for transfers between devices, per_device(): held = lax.ppermute(held, 'team', backward)  2.84 us
  transfers between devices with their start and end apart: 6, of which 5 were waited for; matrix products, arithmetic and copies ran while one was open for 18% of the time, Pallas kernels for 11%

profile of v8, /device:TPU:0, one launch (start us, length us, event | category | flops | bytes accessed | tf_op | source)
XLA Modules:
  0.0 46.5 jit_solution(4002130835426901498)
XLA Ops:
  0.0 4.0 %collective-permute-start = (f32[16,8192]{1,0:T(8,128)}, f32[16,8192]{1,0:T(8,128)S(1)}, u32[]{:S(2)}, u32[]{:S(2)}) collective-permute-start(f32[16,8192]{1,0:T(8,128)} %refs_0_), channel_id=1, source_target_pairs={{0,8},{8,12},{12,4},{4,0},{1,9},{9,13},{13,5},{5,1},{2,10},{10,14}... | collective-permute-start | bytes 1572872 | tf_op jit(solution)/shard_map/ppermute | solution.py:130
  4.7 0.0 copy-start.6
  4.7 8.0 %subtract_convert_fusion = (bf16[8192,256]{1,0:T(8,128)(2,1)}, bf16[8192,256]{1,0:T(8,128)(2,1)}) fusion(f32[8192,256]{1,0:T(8,128)} %param.4, s32[256]{0:T(256)S(1)} %iota_add_fusion.1, s32[8192]{0:T(1024)S(1)} %iota_add_fusion), kind=kLoop, calls=%fused_computation | loop fusion | flops 18874368 | bytes 16811008 | tf_op jit(solution)/shard_map/convert_element_type | solution.py:18
  12.7 0.0 copy-done.6
  12.7 0.0 collective-permute-start.2
  12.8 0.1 pad_add_fusion.1.places
  12.9 3.8 %collective-permute-done.refs_1_ = f32[16,8192]{1,0:T(8,128)S(1)} collective-permute-done((f32[16,8192]{1,0:T(8,128)}, f32[16,8192]{1,0:T(8,128)S(1)}, u32[]{:S(2)}, u32[]{:S(2)}) %collective-permute-start) | collective-permute-done | bytes 524320 | tf_op jit(solution)/shard_map/ppermute | solution.py:130
  16.7 3.3 %collective-permute-start.3 = (f32[16,4096]{1,0:T(8,128)S(1)}, f32[16,4096]{1,0:T(8,128)S(1)}, u32[]{:S(2)}, u32[]{:S(2)}) collective-permute-start(f32[16,4096]{1,0:T(8,128)S(1)} %slice.16), channel_id=1, source_target_pairs={{0,8},{8,12},{12,4},{4,0},{1,9},{9,13},{13,5},{5,1},{2,10},{10,14}... | collective-permute-start | bytes 786440 | tf_op jit(solution)/shard_map/ppermute | solution.py:144
  20.0 0.0 copy-start
  20.0 2.2 %copy-done = bf16[8192,256]{1,0:T(8,128)(2,1)S(1)} copy-done((bf16[8192,256]{1,0:T(8,128)(2,1)S(1)}, bf16[8192,256]{1,0:T(8,128)(2,1)}, u32[]{:S(2)}) %copy-start) | copy-done | bytes 4194328
  22.2 0.0 copy-start.3
  22.2 2.2 %copy-done.3 = bf16[8192,256]{1,0:T(8,128)(2,1)S(1)} copy-done((bf16[8192,256]{1,0:T(8,128)(2,1)S(1)}, bf16[8192,256]{1,0:T(8,128)(2,1)}, u32[]{:S(2)}) %copy-start.3) | copy-done | bytes 4194328
  24.4 2.1 %shard_map.37 = (f32[16,256]{1,0:T(8,128)S(1)}, f32[16,256]{1,0:T(8,128)S(1)}) custom-call(s32[3]{0:T(128)S(1)} %pad_add_fusion.1.places, f32[16,8192]{1,0:T(8,128)S(1)} %copy-done.6, f32[16,8192]{1,0:T(8,128)S(1)} %collective-permute-done.refs_1_, bf16[8192,256]{1,0:T(8,128)(2,1)S(1)} %copy-done.3, bf16[8192,256]{1,0:T(8,128)(2,1)S(1)} %copy-done), custom_call_target="tpu_custom_call" | custom-call | bytes 524288 | tf_op jit(solution)/shard_map/pallas_call | solution.py:68
  26.5 0.1 collective-permute-start.1
  26.7 0.1 pad_add_fusion.places
  26.8 0.1 pad_add_fusion.2
  26.8 2.8 %collective-permute-done.2.refs_0_ = f32[16,8192]{1,0:T(8,128)S(1)} collective-permute-done((f32[16,8192]{1,0:T(8,128)S(1)}, f32[16,8192]{1,0:T(8,128)S(1)}, u32[]{:S(2)}, u32[]{:S(2)}) %collective-permute-start.2) | collective-permute-done | bytes 524320 | tf_op jit(solution)/shard_map/ppermute | solution.py:141
  29.7 0.0 copy-start.1
  29.7 2.2 %copy-done.1 = bf16[8192,256]{1,0:T(8,128)(2,1)S(1)} copy-done((bf16[8192,256]{1,0:T(8,128)(2,1)S(1)}, bf16[8192,256]{1,0:T(8,128)(2,1)}, u32[]{:S(2)}) %copy-start.1) | copy-done | bytes 4194328
  31.9 0.0 copy-start.4
  31.9 2.2 %copy-done.4 = bf16[8192,256]{1,0:T(8,128)(2,1)S(1)} copy-done((bf16[8192,256]{1,0:T(8,128)(2,1)S(1)}, bf16[8192,256]{1,0:T(8,128)(2,1)}, u32[]{:S(2)}) %copy-start.4) | copy-done | bytes 4194328
  34.1 0.0 copy-start.2
  34.1 0.0 copy-start.5
  34.1 1.8 %shard_map.38.refs_5_ = f32[16,256]{1,0:T(8,128)S(1)} custom-call(s32[2]{0:T(128)S(1)} %get-tuple-element.27.places, f32[16,8192]{1,0:T(8,128)S(1)} %collective-permute-done.2.refs_0_, bf16[8192,256]{1,0:T(8,128)(2,1)S(1)} %copy-done.4, bf16[8192,256]{1,0:T(8,128)(2,1)S(1)} %copy-done.1), custom_call_target="tpu_custom_call" | custom-call | bytes 524288 | tf_op jit(solution)/shard_map/pallas_call | solution.py:68
  35.9 0.0 collective-permute-done.3.refs_0_
  35.9 1.2 %shard_map.39.refs_6_ = f32[16,256]{1,0:T(8,128)S(1)} custom-call(s32[2]{0:T(128)S(1)} %get-tuple-element.28.places, f32[16,4096]{1,0:T(8,128)S(1)} %collective-permute-done.3.refs_0_, bf16[8192,256]{1,0:T(8,128)(2,1)S(1)} %copy-done.4, bf16[8192,256]{1,0:T(8,128)(2,1)S(1)} %copy-done.1), custom_call_target="tpu_custom_call" | custom-call | bytes 262144 | tf_op jit(solution)/shard_map/pallas_call | solution.py:68
  37.1 2.2 %collective-permute-done.1.refs_0_ = f32[16,4096]{1,0:T(8,128)S(1)} collective-permute-done((f32[16,4096]{1,0:T(8,128)S(1)}, f32[16,4096]{1,0:T(8,128)S(1)}, u32[]{:S(2)}, u32[]{:S(2)}) %collective-permute-start.1) | collective-permute-done | bytes 262176 | tf_op jit(solution)/shard_map/ppermute | solution.py:148
  39.4 0.0 copy-done.2
  39.4 0.0 copy-done.5
  39.4 1.2 %shard_map.40 = (f32[32,256]{1,0:T(8,128)S(1)}, f32[32,256]{1,0:T(8,128)S(1)}) custom-call(s32[4]{0:T(128)S(1)} %pad_add_fusion.places, f32[16,4096]{1,0:T(8,128)S(1)} %collective-permute-done.1.refs_0_, bf16[8192,256]{1,0:T(8,128)(2,1)S(1)} %copy-done.5, bf16[8192,256]{1,0:T(8,128)(2,1)S(1)} %copy-done.2, f32[16,256]{1,0:T(8,128)S(1)} %get-tuple-element.21.refs_3_, ...), custom_call_target="tpu_custom_call" | custom-call | bytes 262144 | tf_op jit(solution)/shard_map/pallas_call | solution.py:68
  40.6 1.6 %collective-permute-start.4 = (f32[32,256]{1,0:T(8,128)S(1)}, f32[32,256]{1,0:T(8,128)S(1)}, u32[]{:S(2)}, u32[]{:S(2)}) collective-permute-start(f32[32,256]{1,0:T(8,128)S(1)} %get-tuple-element.24), channel_id=1, source_target_pairs={{0,2},{1,3},{2,0},{3,1},{4,6},{5,7},{6,4},{7,5},{8,10},{9,11},{10,... | collective-permute-start | bytes 98312 | tf_op jit(solution)/shard_map/ppermute | solution.py:166
  42.1 2.4 %collective-permute-done.4 = f32[32,256]{1,0:T(8,128)S(1)} collective-permute-done((f32[32,256]{1,0:T(8,128)S(1)}, f32[32,256]{1,0:T(8,128)S(1)}, u32[]{:S(2)}, u32[]{:S(2)}) %collective-permute-start.4) | collective-permute-done | bytes 32800 | tf_op jit(solution)/shard_map/ppermute | solution.py:166
  44.6 0.1 collective-permute-start.5
  44.6 1.2 %collective-permute-done.5 = f32[16,256]{1,0:T(8,128)S(1)} collective-permute-done((f32[16,256]{1,0:T(8,128)S(1)}, f32[16,256]{1,0:T(8,128)S(1)}, u32[]{:S(2)}, u32[]{:S(2)}) %collective-permute-start.5) | collective-permute-done | bytes 16416 | tf_op jit(solution)/shard_map/ppermute | solution.py:166
  45.8 0.7 %multiply_select_fusion = f32[16,256]{1,0:T(8,128)} fusion(f32[16,256]{1,0:T(8,128)S(1)} %collective-permute-done.5, f32[32,256]{1,0:T(8,128)S(1)} %add.78, s32[256]{0:T(256)S(1)} %iota_add_fusion.1, s32[16]{0:T(128)S(1)} %iota_add_fusion.2), kind=kLoop, calls=%fused_computation.6 | loop fusion | flops 32768 | bytes 50240 | tf_op jit(solution)/shard_map/jit(_where)/select_n | solution.py:177
  (7 shorter events, 0.1 us)
Async XLA Ops:
  0.0 16.7 %collective-permute-start = (f32[16,8192]{1,0:T(8,128)}, f32[16,8192]{1,0:T(8,128)S(1)}, u32[]{:S(2)}, u32[]{:S(2)}) collective-permute-start(f32[16,8192]{1,0:T(8,128)} %refs_0_), channel_id=1, source_target_pairs={{0,8},{8,12},{12,4},{4,0},{1,9},{9,13},{13,5},{5,1},{2,10},{10,14}... | collective-permute-start | bytes 1572872 | tf_op jit(solution)/shard_map/ppermute | solution.py:130
  4.7 8.0 %copy-start.6 = (f32[16,8192]{1,0:T(8,128)S(1)}, f32[16,8192]{1,0:T(8,128)}, u32[]{:S(2)}) copy-start(f32[16,8192]{1,0:T(8,128)} %refs_0_) | copy-start | bytes 1572868
  12.7 17.0 %collective-permute-start.2 = (f32[16,8192]{1,0:T(8,128)S(1)}, f32[16,8192]{1,0:T(8,128)S(1)}, u32[]{:S(2)}, u32[]{:S(2)}) collective-permute-start(f32[16,8192]{1,0:T(8,128)S(1)} %copy-done.6), channel_id=1, source_target_pairs={{8,0},{12,8},{4,12},{0,4},{9,1},{13,9},{5,13},{1,5},{10,2},{14,10}... | collective-permute-start | bytes 1572872 | tf_op jit(solution)/shard_map/ppermute | solution.py:141
  16.7 19.2 %collective-permute-start.3 = (f32[16,4096]{1,0:T(8,128)S(1)}, f32[16,4096]{1,0:T(8,128)S(1)}, u32[]{:S(2)}, u32[]{:S(2)}) collective-permute-start(f32[16,4096]{1,0:T(8,128)S(1)} %slice.16), channel_id=1, source_target_pairs={{0,8},{8,12},{12,4},{4,0},{1,9},{9,13},{13,5},{5,1},{2,10},{10,14}... | collective-permute-start | bytes 786440 | tf_op jit(solution)/shard_map/ppermute | solution.py:144
  20.0 2.2 %copy-start = (bf16[8192,256]{1,0:T(8,128)(2,1)S(1)}, bf16[8192,256]{1,0:T(8,128)(2,1)}, u32[]{:S(2)}) copy-start(bf16[8192,256]{1,0:T(8,128)(2,1)} %get-tuple-element.17.refs_3_.refs_2_) | copy-start | bytes 12582916
  22.2 2.2 %copy-start.3 = (bf16[8192,256]{1,0:T(8,128)(2,1)S(1)}, bf16[8192,256]{1,0:T(8,128)(2,1)}, u32[]{:S(2)}) copy-start(bf16[8192,256]{1,0:T(8,128)(2,1)} %get-tuple-element.16.refs_2_.refs_1_) | copy-start | bytes 12582916
  26.5 12.8 %collective-permute-start.1 = (f32[16,4096]{1,0:T(8,128)S(1)}, f32[16,4096]{1,0:T(8,128)S(1)}, u32[]{:S(2)}, u32[]{:S(2)}) collective-permute-start(f32[16,4096]{1,0:T(8,128)S(1)} %slice.12), channel_id=1, source_target_pairs={{0,8},{8,12},{12,4},{4,0},{1,9},{9,13},{13,5},{5,1},{2,10},{10,14}... | collective-permute-start | bytes 786440 | tf_op jit(solution)/shard_map/ppermute | solution.py:148
  29.7 2.2 %copy-start.1 = (bf16[8192,256]{1,0:T(8,128)(2,1)S(1)}, bf16[8192,256]{1,0:T(8,128)(2,1)}, u32[]{:S(2)}) copy-start(bf16[8192,256]{1,0:T(8,128)(2,1)} %get-tuple-element.17.refs_3_.refs_2_) | copy-start | bytes 12582916
  31.9 2.2 %copy-start.4 = (bf16[8192,256]{1,0:T(8,128)(2,1)S(1)}, bf16[8192,256]{1,0:T(8,128)(2,1)}, u32[]{:S(2)}) copy-start(bf16[8192,256]{1,0:T(8,128)(2,1)} %get-tuple-element.16.refs_2_.refs_1_) | copy-start | bytes 12582916
  34.1 5.3 %copy-start.2 = (bf16[8192,256]{1,0:T(8,128)(2,1)S(1)}, bf16[8192,256]{1,0:T(8,128)(2,1)}, u32[]{:S(2)}) copy-start(bf16[8192,256]{1,0:T(8,128)(2,1)} %get-tuple-element.17.refs_3_.refs_2_) | copy-start | bytes 12582916
  34.1 5.3 %copy-start.5 = (bf16[8192,256]{1,0:T(8,128)(2,1)S(1)}, bf16[8192,256]{1,0:T(8,128)(2,1)}, u32[]{:S(2)}) copy-start(bf16[8192,256]{1,0:T(8,128)(2,1)} %get-tuple-element.16.refs_2_.refs_1_) | copy-start | bytes 12582916
  40.6 4.0 %collective-permute-start.4 = (f32[32,256]{1,0:T(8,128)S(1)}, f32[32,256]{1,0:T(8,128)S(1)}, u32[]{:S(2)}, u32[]{:S(2)}) collective-permute-start(f32[32,256]{1,0:T(8,128)S(1)} %get-tuple-element.24), channel_id=1, source_target_pairs={{0,2},{1,3},{2,0},{3,1},{4,6},{5,7},{6,4},{7,5},{8,10},{9,11},{10,... | collective-permute-start | bytes 98312 | tf_op jit(solution)/shard_map/ppermute | solution.py:166
  44.6 1.2 %collective-permute-start.5 = (f32[16,256]{1,0:T(8,128)S(1)}, f32[16,256]{1,0:T(8,128)S(1)}, u32[]{:S(2)}, u32[]{:S(2)}) collective-permute-start(f32[16,256]{1,0:T(8,128)S(1)} %slice.18), channel_id=1, source_target_pairs={{0,1},{1,0},{2,3},{3,2},{4,5},{5,4},{6,7},{7,6},{8,9},{9,8},{10,11... | collective-permute-start | bytes 49160 | tf_op jit(solution)/shard_map/ppermute | solution.py:166

commit v9 on v8

--- a/solution.py
+++ b/solution.py
@@ -61,10 +61,10 @@
             out[b * rows : (b + 1) * rows] = found
 
 
-def slot_products(places, blocks, weights, first_k=0, parts=()):
+def slot_products(places, blocks, weights, first_k=0, parts=(), shares=0):
     rows, columns = blocks[0].shape[0], weights[0].shape[1]
-    outs = 2 if parts else len(blocks)
-    shape = (rows * len(parts) // 2 if parts else rows, columns)
+    outs = shares or len(blocks)
+    shape = (rows * len(parts) // shares if shares else rows, columns)
     return pl.pallas_call(
         functools.partial(slots_kernel, first_k, len(blocks), len(parts)),
         out_shape=[jax.ShapeDtypeStruct(shape, jnp.float32)] * outs,
@@ -157,18 +157,14 @@
         ((source // share_blocks) ^ rep_index) * share_blocks + source % share_blocks
         for source in sources
     ]
-    kept, sent = slot_products(
-        jnp.stack(spots).astype(jnp.int32), [last_right], weights, half, parts
+    shares = slot_products(
+        jnp.stack(spots).astype(jnp.int32), [last_right], weights, half, parts, rep_count
     )
-    flip = rep_count // 2
-    while True:
+    terms = [shares[0]]
+    for flip in range(rep_count - 1, 0, -1):
         pairs = [(d, d ^ flip) for d in range(rep_count)]
-        kept = kept + lax.ppermute(sent, "rep", pairs)
-        flip //= 2
-        if not flip:
-            break
-        kept, sent = kept[: flip * rows_share], kept[flip * rows_share :]
-    moved = kept
+        terms.append(lax.ppermute(shares[flip], "rep", pairs))
+    moved = sum_of(terms)
 
     global_rows = rep_index * rows_share + jnp.arange(rows_share, dtype=jnp.int32)
     global_cols = offset + jnp.arange(tile_width, dtype=jnp.int32)

time: 46.8 us -> 46.2 us (0.987)
  waiting for transfers between devices: 12.5 us -> 11.6 us
    ppermute x2 -> x3, waiting for transfers between devices: 3.58 us -> 2.69 us  [per_device(): terms.append(lax.ppermute(shares[flip], 'rep', pairs))]
    ppermute x2 -> x3, starting transfers between devices: 1.62 us -> 1.92 us  [per_device(): terms.append(lax.ppermute(shares[flip], 'rep', pairs))]
  transfers between devices with their start and end apart: 6 -> 7, of which waited for: 5 -> 5; matrix products, arithmetic and copies ran while one was open for 18% -> 18% of each run, Pallas kernels for 11% -> 11%
where the time goes in v9:
time: 46.2 us; the launch traced here: 45.9 us
  waiting for transfers between devices  11.6 us (25%)
  starting transfers between devices  9.36 us (20%)
  other arithmetic  8.9 us (19%)
  local copies, waits for them, and re-layouts  8.8 us (19%)
  Pallas kernels  6.37 us (14%)
  between operations  0.86 us (2%)
    unnamed x14, local copies, waits for them, and re-layouts  8.76 us
    convert_element_type x1, other arithmetic, halves(): return (high.astype(jnp.bfloat16), (array - high).astype(jnp.bfloat16))  7.98 us
    pallas_call x4, Pallas kernels, slot_products(): pl.pallas_call(functools.partial(slots_kernel, first_k, len(blocks), len(...  6.37 us
    ppermute x1, starting transfers between devices, per_device(): first = lax.ppermute(omega_rows, 'team', onward)  4.04 us
    ppermute x1, waiting for transfers between devices, per_device(): first = lax.ppermute(omega_rows, 'team', onward)  3.81 us
    ppermute x1, starting transfers between devices, per_device(): last_left = lax.ppermute(last_held[:, :half], 'team', onward)  3.33 us
    ppermute x1, waiting for transfers between devices, per_device(): held = lax.ppermute(held, 'team', backward)  2.84 us
    ppermute x3, waiting for transfers between devices, per_device(): terms.append(lax.ppermute(shares[flip], 'rep', pairs))  2.69 us
  transfers between devices with their start and end apart: 7, of which 5 were waited for; matrix products, arithmetic and copies ran while one was open for 18% of the time, Pallas kernels for 11%

profile of v9, /device:TPU:0, one launch (start us, length us, event | category | flops | bytes accessed | tf_op | source)
XLA Modules:
  0.0 45.9 jit_solution(9922347847691074033)
XLA Ops:
  0.0 4.0 %collective-permute-start = (f32[16,8192]{1,0:T(8,128)}, f32[16,8192]{1,0:T(8,128)S(1)}, u32[]{:S(2)}, u32[]{:S(2)}) collective-permute-start(f32[16,8192]{1,0:T(8,128)} %refs_0_), channel_id=1, source_target_pairs={{0,8},{8,12},{12,4},{4,0},{1,9},{9,13},{13,5},{5,1},{2,10},{10,14}... | collective-permute-start | bytes 1572872 | tf_op jit(solution)/shard_map/ppermute | solution.py:130
  4.7 0.0 copy-start.6
  4.7 8.0 %subtract_convert_fusion = (bf16[8192,256]{1,0:T(8,128)(2,1)}, bf16[8192,256]{1,0:T(8,128)(2,1)}) fusion(f32[8192,256]{1,0:T(8,128)} %param.4, s32[256]{0:T(256)S(1)} %iota_add_fusion.1, s32[8192]{0:T(1024)S(1)} %iota_add_fusion), kind=kLoop, calls=%fused_computation | loop fusion | flops 18874368 | bytes 16811008 | tf_op jit(solution)/shard_map/convert_element_type | solution.py:18
  12.7 0.0 copy-done.6
  12.7 0.0 collective-permute-start.2
  12.8 0.1 pad_add_fusion.1.places
  12.9 3.8 %collective-permute-done.refs_1_ = f32[16,8192]{1,0:T(8,128)S(1)} collective-permute-done((f32[16,8192]{1,0:T(8,128)}, f32[16,8192]{1,0:T(8,128)S(1)}, u32[]{:S(2)}, u32[]{:S(2)}) %collective-permute-start) | collective-permute-done | bytes 524320 | tf_op jit(solution)/shard_map/ppermute | solution.py:130
  16.7 3.3 %collective-permute-start.3 = (f32[16,4096]{1,0:T(8,128)S(1)}, f32[16,4096]{1,0:T(8,128)S(1)}, u32[]{:S(2)}, u32[]{:S(2)}) collective-permute-start(f32[16,4096]{1,0:T(8,128)S(1)} %slice.8), channel_id=1, source_target_pairs={{0,8},{8,12},{12,4},{4,0},{1,9},{9,13},{13,5},{5,1},{2,10},{10,14}... | collective-permute-start | bytes 786440 | tf_op jit(solution)/shard_map/ppermute | solution.py:144
  20.0 0.0 copy-start
  20.0 2.2 %copy-done = bf16[8192,256]{1,0:T(8,128)(2,1)S(1)} copy-done((bf16[8192,256]{1,0:T(8,128)(2,1)S(1)}, bf16[8192,256]{1,0:T(8,128)(2,1)}, u32[]{:S(2)}) %copy-start) | copy-done | bytes 4194328
  22.2 0.0 copy-start.3
  22.2 2.2 %copy-done.3 = bf16[8192,256]{1,0:T(8,128)(2,1)S(1)} copy-done((bf16[8192,256]{1,0:T(8,128)(2,1)S(1)}, bf16[8192,256]{1,0:T(8,128)(2,1)}, u32[]{:S(2)}) %copy-start.3) | copy-done | bytes 4194328
  24.4 2.1 %shard_map.37 = (f32[16,256]{1,0:T(8,128)S(1)}, f32[16,256]{1,0:T(8,128)S(1)}) custom-call(s32[3]{0:T(128)S(1)} %pad_add_fusion.1.places, f32[16,8192]{1,0:T(8,128)S(1)} %copy-done.6, f32[16,8192]{1,0:T(8,128)S(1)} %collective-permute-done.refs_1_, bf16[8192,256]{1,0:T(8,128)(2,1)S(1)} %copy-done.3, bf16[8192,256]{1,0:T(8,128)(2,1)S(1)} %copy-done), custom_call_target="tpu_custom_call" | custom-call | bytes 524288 | tf_op jit(solution)/shard_map/pallas_call | solution.py:68
  26.5 0.1 collective-permute-start.1
  26.7 0.1 pad_add_fusion.places
  26.8 0.1 pad_add_fusion.2
  26.8 2.8 %collective-permute-done.2.refs_0_ = f32[16,8192]{1,0:T(8,128)S(1)} collective-permute-done((f32[16,8192]{1,0:T(8,128)S(1)}, f32[16,8192]{1,0:T(8,128)S(1)}, u32[]{:S(2)}, u32[]{:S(2)}) %collective-permute-start.2) | collective-permute-done | bytes 524320 | tf_op jit(solution)/shard_map/ppermute | solution.py:141
  29.7 0.0 copy-start.1
  29.7 2.2 %copy-done.1 = bf16[8192,256]{1,0:T(8,128)(2,1)S(1)} copy-done((bf16[8192,256]{1,0:T(8,128)(2,1)S(1)}, bf16[8192,256]{1,0:T(8,128)(2,1)}, u32[]{:S(2)}) %copy-start.1) | copy-done | bytes 4194328
  31.9 0.0 copy-start.4
  31.9 2.2 %copy-done.4 = bf16[8192,256]{1,0:T(8,128)(2,1)S(1)} copy-done((bf16[8192,256]{1,0:T(8,128)(2,1)S(1)}, bf16[8192,256]{1,0:T(8,128)(2,1)}, u32[]{:S(2)}) %copy-start.4) | copy-done | bytes 4194328
  34.1 0.0 copy-start.2
  34.1 0.0 copy-start.5
  34.1 1.8 %shard_map.38.refs_5_ = f32[16,256]{1,0:T(8,128)S(1)} custom-call(s32[2]{0:T(128)S(1)} %get-tuple-element.31.places, f32[16,8192]{1,0:T(8,128)S(1)} %collective-permute-done.2.refs_0_, bf16[8192,256]{1,0:T(8,128)(2,1)S(1)} %copy-done.4, bf16[8192,256]{1,0:T(8,128)(2,1)S(1)} %copy-done.1), custom_call_target="tpu_custom_call" | custom-call | bytes 524288 | tf_op jit(solution)/shard_map/pallas_call | solution.py:68
  35.9 0.0 collective-permute-done.3.refs_0_
  35.9 1.2 %shard_map.39.refs_6_ = f32[16,256]{1,0:T(8,128)S(1)} custom-call(s32[2]{0:T(128)S(1)} %get-tuple-element.32.places, f32[16,4096]{1,0:T(8,128)S(1)} %collective-permute-done.3.refs_0_, bf16[8192,256]{1,0:T(8,128)(2,1)S(1)} %copy-done.4, bf16[8192,256]{1,0:T(8,128)(2,1)S(1)} %copy-done.1), custom_call_target="tpu_custom_call" | custom-call | bytes 262144 | tf_op jit(solution)/shard_map/pallas_call | solution.py:68
  37.1 2.2 %collective-permute-done.1.refs_0_ = f32[16,4096]{1,0:T(8,128)S(1)} collective-permute-done((f32[16,4096]{1,0:T(8,128)S(1)}, f32[16,4096]{1,0:T(8,128)S(1)}, u32[]{:S(2)}, u32[]{:S(2)}) %collective-permute-start.1) | collective-permute-done | bytes 262176 | tf_op jit(solution)/shard_map/ppermute | solution.py:148
  39.4 0.0 copy-done.2
  39.4 0.0 copy-done.5
  39.4 1.2 %shard_map.40 = (f32[16,256]{1,0:T(8,128)S(1)}, f32[16,256]{1,0:T(8,128)S(1)}, f32[16,256]{1,0:T(8,128)S(1)}, f32[16,256]{1,0:T(8,128)S(1)}) custom-call(s32[4]{0:T(128)S(1)} %pad_add_fusion.places, f32[16,4096]{1,0:T(8,128)S(1)} %collective-permute-done.1.refs_0_, bf16[8192,256]{1,0:T(8,128)(2,1)S(1)} %copy-done.5, bf16[8192,256]{1,0:T(8,128)(2,1)S(1)} %copy-done.2, ...), custom_call_target="tpu_custom_call" | custom-call | bytes 262144 | tf_op jit(solution)/shard_map/pallas_call | solution.py:68
  40.6 0.8 %collective-permute-start.4 = (f32[16,256]{1,0:T(8,128)S(1)}, f32[16,256]{1,0:T(8,128)S(1)}, u32[]{:S(2)}, u32[]{:S(2)}) collective-permute-start(f32[16,256]{1,0:T(8,128)S(1)} %get-tuple-element.26), channel_id=1, source_target_pairs={{0,3},{1,2},{2,1},{3,0},{4,7},{5,6},{6,5},{7,4},{8,11},{9,10},{10,... | collective-permute-start | bytes 49160 | tf_op jit(solution)/shard_map/ppermute | solution.py:166
  41.3 0.9 %collective-permute-start.5 = (f32[16,256]{1,0:T(8,128)S(1)}, f32[16,256]{1,0:T(8,128)S(1)}, u32[]{:S(2)}, u32[]{:S(2)}) collective-permute-start(f32[16,256]{1,0:T(8,128)S(1)} %get-tuple-element.27), channel_id=1, source_target_pairs={{0,2},{1,3},{2,0},{3,1},{4,6},{5,7},{6,4},{7,5},{8,10},{9,11},{10,... | collective-permute-start | bytes 49160 | tf_op jit(solution)/shard_map/ppermute | solution.py:166
  42.2 0.3 collective-permute-start.6
  42.5 1.4 %collective-permute-done.4 = f32[16,256]{1,0:T(8,128)S(1)} collective-permute-done((f32[16,256]{1,0:T(8,128)S(1)}, f32[16,256]{1,0:T(8,128)S(1)}, u32[]{:S(2)}, u32[]{:S(2)}) %collective-permute-start.4) | collective-permute-done | bytes 16416 | tf_op jit(solution)/shard_map/ppermute | solution.py:166
  43.9 1.3 %collective-permute-done.5 = f32[16,256]{1,0:T(8,128)S(1)} collective-permute-done((f32[16,256]{1,0:T(8,128)S(1)}, f32[16,256]{1,0:T(8,128)S(1)}, u32[]{:S(2)}, u32[]{:S(2)}) %collective-permute-start.5) | collective-permute-done | bytes 16416 | tf_op jit(solution)/shard_map/ppermute | solution.py:166
  45.2 0.0 collective-permute-done.6
  45.2 0.7 %multiply_select_fusion = f32[16,256]{1,0:T(8,128)} fusion(f32[16,256]{1,0:T(8,128)S(1)} %collective-permute-done.6, f32[16,256]{1,0:T(8,128)S(1)} %collective-permute-done.5, f32[16,256]{1,0:T(8,128)S(1)} %get-tuple-element.25, f32[16,256]{1,0:T(8,128)S(1)} %collective-permute-done.4, s32[256]{0:T(256)S(1)} %iota_add_fusion.1, s32[16]{0:T(128)S(1)} %iota_add_fusion.2), kind=kLoop, calls=%fused_computation.5 | loop fusion | flops 40960 | bytes 83008 | tf_op jit(solution)/shard_map/jit(_where)/select_n | solution.py:173
  (5 shorter events, 0.0 us)
Async XLA Ops:
  0.0 16.7 %collective-permute-start = (f32[16,8192]{1,0:T(8,128)}, f32[16,8192]{1,0:T(8,128)S(1)}, u32[]{:S(2)}, u32[]{:S(2)}) collective-permute-start(f32[16,8192]{1,0:T(8,128)} %refs_0_), channel_id=1, source_target_pairs={{0,8},{8,12},{12,4},{4,0},{1,9},{9,13},{13,5},{5,1},{2,10},{10,14}... | collective-permute-start | bytes 1572872 | tf_op jit(solution)/shard_map/ppermute | solution.py:130
  4.7 8.0 %copy-start.6 = (f32[16,8192]{1,0:T(8,128)S(1)}, f32[16,8192]{1,0:T(8,128)}, u32[]{:S(2)}) copy-start(f32[16,8192]{1,0:T(8,128)} %refs_0_) | copy-start | bytes 1572868
  12.7 17.0 %collective-permute-start.2 = (f32[16,8192]{1,0:T(8,128)S(1)}, f32[16,8192]{1,0:T(8,128)S(1)}, u32[]{:S(2)}, u32[]{:S(2)}) collective-permute-start(f32[16,8192]{1,0:T(8,128)S(1)} %copy-done.6), channel_id=1, source_target_pairs={{8,0},{12,8},{4,12},{0,4},{9,1},{13,9},{5,13},{1,5},{10,2},{14,10}... | collective-permute-start | bytes 1572872 | tf_op jit(solution)/shard_map/ppermute | solution.py:141
  16.7 19.2 %collective-permute-start.3 = (f32[16,4096]{1,0:T(8,128)S(1)}, f32[16,4096]{1,0:T(8,128)S(1)}, u32[]{:S(2)}, u32[]{:S(2)}) collective-permute-start(f32[16,4096]{1,0:T(8,128)S(1)} %slice.8), channel_id=1, source_target_pairs={{0,8},{8,12},{12,4},{4,0},{1,9},{9,13},{13,5},{5,1},{2,10},{10,14}... | collective-permute-start | bytes 786440 | tf_op jit(solution)/shard_map/ppermute | solution.py:144
  20.0 2.2 %copy-start = (bf16[8192,256]{1,0:T(8,128)(2,1)S(1)}, bf16[8192,256]{1,0:T(8,128)(2,1)}, u32[]{:S(2)}) copy-start(bf16[8192,256]{1,0:T(8,128)(2,1)} %get-tuple-element.19.refs_3_.refs_2_) | copy-start | bytes 12582916
  22.2 2.2 %copy-start.3 = (bf16[8192,256]{1,0:T(8,128)(2,1)S(1)}, bf16[8192,256]{1,0:T(8,128)(2,1)}, u32[]{:S(2)}) copy-start(bf16[8192,256]{1,0:T(8,128)(2,1)} %get-tuple-element.18.refs_2_.refs_1_) | copy-start | bytes 12582916
  26.5 12.8 %collective-permute-start.1 = (f32[16,4096]{1,0:T(8,128)S(1)}, f32[16,4096]{1,0:T(8,128)S(1)}, u32[]{:S(2)}, u32[]{:S(2)}) collective-permute-start(f32[16,4096]{1,0:T(8,128)S(1)} %slice.6), channel_id=1, source_target_pairs={{0,8},{8,12},{12,4},{4,0},{1,9},{9,13},{13,5},{5,1},{2,10},{10,14}... | collective-permute-start | bytes 786440 | tf_op jit(solution)/shard_map/ppermute | solution.py:148
  29.7 2.2 %copy-start.1 = (bf16[8192,256]{1,0:T(8,128)(2,1)S(1)}, bf16[8192,256]{1,0:T(8,128)(2,1)}, u32[]{:S(2)}) copy-start(bf16[8192,256]{1,0:T(8,128)(2,1)} %get-tuple-element.19.refs_3_.refs_2_) | copy-start | bytes 12582916
  31.9 2.2 %copy-start.4 = (bf16[8192,256]{1,0:T(8,128)(2,1)S(1)}, bf16[8192,256]{1,0:T(8,128)(2,1)}, u32[]{:S(2)}) copy-start(bf16[8192,256]{1,0:T(8,128)(2,1)} %get-tuple-element.18.refs_2_.refs_1_) | copy-start | bytes 12582916
  34.1 5.3 %copy-start.2 = (bf16[8192,256]{1,0:T(8,128)(2,1)S(1)}, bf16[8192,256]{1,0:T(8,128)(2,1)}, u32[]{:S(2)}) copy-start(bf16[8192,256]{1,0:T(8,128)(2,1)} %get-tuple-element.19.refs_3_.refs_2_) | copy-start | bytes 12582916
  34.1 5.3 %copy-start.5 = (bf16[8192,256]{1,0:T(8,128)(2,1)S(1)}, bf16[8192,256]{1,0:T(8,128)(2,1)}, u32[]{:S(2)}) copy-start(bf16[8192,256]{1,0:T(8,128)(2,1)} %get-tuple-element.18.refs_2_.refs_1_) | copy-start | bytes 12582916
  40.6 3.4 %collective-permute-start.4 = (f32[16,256]{1,0:T(8,128)S(1)}, f32[16,256]{1,0:T(8,128)S(1)}, u32[]{:S(2)}, u32[]{:S(2)}) collective-permute-start(f32[16,256]{1,0:T(8,128)S(1)} %get-tuple-element.26), channel_id=1, source_target_pairs={{0,3},{1,2},{2,1},{3,0},{4,7},{5,6},{6,5},{7,4},{8,11},{9,10},{10,... | collective-permute-start | bytes 49160 | tf_op jit(solution)/shard_map/ppermute | solution.py:166
  41.3 3.9 %collective-permute-start.5 = (f32[16,256]{1,0:T(8,128)S(1)}, f32[16,256]{1,0:T(8,128)S(1)}, u32[]{:S(2)}, u32[]{:S(2)}) collective-permute-start(f32[16,256]{1,0:T(8,128)S(1)} %get-tuple-element.27), channel_id=1, source_target_pairs={{0,2},{1,3},{2,0},{3,1},{4,6},{5,7},{6,4},{7,5},{8,10},{9,11},{10,... | collective-permute-start | bytes 49160 | tf_op jit(solution)/shard_map/ppermute | solution.py:166
  42.2 3.0 %collective-permute-start.6 = (f32[16,256]{1,0:T(8,128)S(1)}, f32[16,256]{1,0:T(8,128)S(1)}, u32[]{:S(2)}, u32[]{:S(2)}) collective-permute-start(f32[16,256]{1,0:T(8,128)S(1)} %get-tuple-element.28), channel_id=1, source_target_pairs={{0,1},{1,0},{2,3},{3,2},{4,5},{5,4},{6,7},{7,6},{8,9},{9,8},{10,11... | collective-permute-start | bytes 49160 | tf_op jit(solution)/shard_map/ppermute | solution.py:166

commit v10 on v9

--- a/solution.py
+++ b/solution.py
@@ -24,7 +24,7 @@
     parts, outs = refs[:parts_count], refs[parts_count:]
     rows, depth = blocks[0].shape
     columns = high.shape[1]
-    step = math.gcd(depth, 4096)
+    step = math.gcd(depth, 2048)
     all_rows = rows * blocks_count
     total = jnp.zeros((all_rows, columns), jnp.float32)
     for k in range(0, depth, step):
@@ -105,11 +105,11 @@
     chosen = (k_ids[:, None] == c_ids[None, :]).astype(jnp.float32)
     weights = halves(chosen - step_size * covariance_columns)
 
-    half = part_width // 2
-    assert all_rows <= half and half % tile_width == 0
+    cut = part_width // 4 * 3
+    assert all_rows <= cut and cut % tile_width == 0
 
     def products_of(blocks, sources):
-        start = jnp.clip(offset, 0, half - tile_width)
+        start = jnp.clip(offset, 0, cut - tile_width)
         shifts = [
             jnp.where(rep_index == 0, source * block_rows - offset, 1 << 20) for source in sources
         ]
@@ -141,11 +141,11 @@
         held = lax.ppermute(held, "team", backward)
         gathered.append((held, -step))
 
-    last_left = lax.ppermute(last_held[:, :half], "team", onward)
+    last_left = lax.ppermute(last_held[:, :cut], "team", onward)
     sources = [team_index, device_at(place - 1)]
     parts = products_of([own, first], sources)
     last_held, *parts = lax.optimization_barrier((last_held, *parts))
-    last_right = lax.ppermute(last_held[:, half:], "team", onward)
+    last_right = lax.ppermute(last_held[:, cut:], "team", onward)
     for block, step in gathered:
         sources.append(device_at(place - step))
         parts += products_of([block], sources[-1:])
@@ -158,7 +158,7 @@
         for source in sources
     ]
     shares = slot_products(
-        jnp.stack(spots).astype(jnp.int32), [last_right], weights, half, parts, rep_count
+        jnp.stack(spots).astype(jnp.int32), [last_right], weights, cut, parts, rep_count
     )
     terms = [shares[0]]
     for flip in range(rep_count - 1, 0, -1):

time: 46.2 us -> 45.9 us (level)
  transfers between devices with their start and end apart: 7 -> 7, of which waited for: 5 -> 6; matrix products, arithmetic and copies ran while one was open for 18% -> 18% of each run, Pallas kernels for 11% -> 12%
where the time goes in v10:
time: 45.9 us; the launch traced here: 45.6 us
  waiting for transfers between devices  11.4 us (25%)
  starting transfers between devices  9.46 us (21%)
  other arithmetic  8.9 us (19%)
  local copies, waits for them, and re-layouts  8.8 us (19%)
  Pallas kernels  6.35 us (14%)
  between operations  0.72 us (2%)
    unnamed x14, local copies, waits for them, and re-layouts  8.77 us
    convert_element_type x1, other arithmetic, halves(): return (high.astype(jnp.bfloat16), (array - high).astype(jnp.bfloat16))  7.98 us
    pallas_call x4, Pallas kernels, slot_products(): pl.pallas_call(functools.partial(slots_kernel, first_k, len(blocks), len(...  6.35 us
    ppermute x1, starting transfers between devices, per_device(): first = lax.ppermute(omega_rows, 'team', onward)  4.04 us
    ppermute x1, waiting for transfers between devices, per_device(): first = lax.ppermute(omega_rows, 'team', onward)  3.95 us
    ppermute x1, starting transfers between devices, per_device(): last_left = lax.ppermute(last_held[:, :cut], 'team', onward)  3.33 us
    ppermute x1, waiting for transfers between devices, per_device(): held = lax.ppermute(held, 'team', backward)  2.73 us
    ppermute x3, waiting for transfers between devices, per_device(): terms.append(lax.ppermute(shares[flip], 'rep', pairs))  2.69 us
  transfers between devices with their start and end apart: 7, of which 6 were waited for; matrix products, arithmetic and copies ran while one was open for 18% of the time, Pallas kernels for 12%

profile of v10, /device:TPU:0, one launch (start us, length us, event | category | flops | bytes accessed | tf_op | source)
XLA Modules:
  0.0 45.6 jit_solution(16564632685955718951)
XLA Ops:
  0.0 4.0 %collective-permute-start = (f32[16,8192]{1,0:T(8,128)}, f32[16,8192]{1,0:T(8,128)S(1)}, u32[]{:S(2)}, u32[]{:S(2)}) collective-permute-start(f32[16,8192]{1,0:T(8,128)} %refs_0_), channel_id=1, source_target_pairs={{0,8},{8,12},{12,4},{4,0},{1,9},{9,13},{13,5},{5,1},{2,10},{10,14}... | collective-permute-start | bytes 1572872 | tf_op jit(solution)/shard_map/ppermute | solution.py:130
  4.7 0.0 copy-start.6
  4.7 8.0 %subtract_convert_fusion = (bf16[8192,256]{1,0:T(8,128)(2,1)}, bf16[8192,256]{1,0:T(8,128)(2,1)}) fusion(f32[8192,256]{1,0:T(8,128)} %param.4, s32[256]{0:T(256)S(1)} %iota_add_fusion.1, s32[8192]{0:T(1024)S(1)} %iota_add_fusion), kind=kLoop, calls=%fused_computation | loop fusion | flops 18874368 | bytes 16811008 | tf_op jit(solution)/shard_map/convert_element_type | solution.py:18
  12.7 0.0 copy-done.6
  12.7 0.0 collective-permute-start.2
  12.7 4.0 %collective-permute-done.refs_1_ = f32[16,8192]{1,0:T(8,128)S(1)} collective-permute-done((f32[16,8192]{1,0:T(8,128)}, f32[16,8192]{1,0:T(8,128)S(1)}, u32[]{:S(2)}, u32[]{:S(2)}) %collective-permute-start) | collective-permute-done | bytes 524320 | tf_op jit(solution)/shard_map/ppermute | solution.py:130
  16.7 3.3 %collective-permute-start.3 = (f32[16,6144]{1,0:T(8,128)S(1)}, f32[16,6144]{1,0:T(8,128)S(1)}, u32[]{:S(2)}, u32[]{:S(2)}) collective-permute-start(f32[16,6144]{1,0:T(8,128)S(1)} %slice.8), channel_id=1, source_target_pairs={{0,8},{8,12},{12,4},{4,0},{1,9},{9,13},{13,5},{5,1},{2,10},{10,14}... | collective-permute-start | bytes 1179656 | tf_op jit(solution)/shard_map/ppermute | solution.py:144
  20.0 0.1 pad_add_fusion.1.places
  20.1 0.0 copy-start
  20.1 2.2 %copy-done = bf16[8192,256]{1,0:T(8,128)(2,1)S(1)} copy-done((bf16[8192,256]{1,0:T(8,128)(2,1)S(1)}, bf16[8192,256]{1,0:T(8,128)(2,1)}, u32[]{:S(2)}) %copy-start) | copy-done | bytes 4194328
  22.3 0.0 copy-start.3
  22.3 2.2 %copy-done.3 = bf16[8192,256]{1,0:T(8,128)(2,1)S(1)} copy-done((bf16[8192,256]{1,0:T(8,128)(2,1)S(1)}, bf16[8192,256]{1,0:T(8,128)(2,1)}, u32[]{:S(2)}) %copy-start.3) | copy-done | bytes 4194328
  24.5 2.1 %shard_map.37 = (f32[16,256]{1,0:T(8,128)S(1)}, f32[16,256]{1,0:T(8,128)S(1)}) custom-call(s32[3]{0:T(128)S(1)} %pad_add_fusion.1.places, f32[16,8192]{1,0:T(8,128)S(1)} %copy-done.6, f32[16,8192]{1,0:T(8,128)S(1)} %collective-permute-done.refs_1_, bf16[8192,256]{1,0:T(8,128)(2,1)S(1)} %copy-done.3, bf16[8192,256]{1,0:T(8,128)(2,1)S(1)} %copy-done), custom_call_target="tpu_custom_call" | custom-call | bytes 524288 | tf_op jit(solution)/shard_map/pallas_call | solution.py:68
  26.6 0.2 collective-permute-start.1
  26.8 0.1 pad_add_fusion.places
  26.9 0.1 pad_add_fusion.2
  26.9 2.7 %collective-permute-done.2.refs_0_ = f32[16,8192]{1,0:T(8,128)S(1)} collective-permute-done((f32[16,8192]{1,0:T(8,128)S(1)}, f32[16,8192]{1,0:T(8,128)S(1)}, u32[]{:S(2)}, u32[]{:S(2)}) %collective-permute-start.2) | collective-permute-done | bytes 524320 | tf_op jit(solution)/shard_map/ppermute | solution.py:141
  29.7 0.0 copy-start.1
  29.7 2.2 %copy-done.1 = bf16[8192,256]{1,0:T(8,128)(2,1)S(1)} copy-done((bf16[8192,256]{1,0:T(8,128)(2,1)S(1)}, bf16[8192,256]{1,0:T(8,128)(2,1)}, u32[]{:S(2)}) %copy-start.1) | copy-done | bytes 4194328
  31.9 0.0 copy-start.4
  31.9 2.2 %copy-done.4 = bf16[8192,256]{1,0:T(8,128)(2,1)S(1)} copy-done((bf16[8192,256]{1,0:T(8,128)(2,1)S(1)}, bf16[8192,256]{1,0:T(8,128)(2,1)}, u32[]{:S(2)}) %copy-start.4) | copy-done | bytes 4194328
  34.1 0.0 copy-start.2
  34.1 0.0 copy-start.5
  34.1 1.8 %shard_map.38.refs_5_ = f32[16,256]{1,0:T(8,128)S(1)} custom-call(s32[2]{0:T(128)S(1)} %get-tuple-element.31.places, f32[16,8192]{1,0:T(8,128)S(1)} %collective-permute-done.2.refs_0_, bf16[8192,256]{1,0:T(8,128)(2,1)S(1)} %copy-done.4, bf16[8192,256]{1,0:T(8,128)(2,1)S(1)} %copy-done.1), custom_call_target="tpu_custom_call" | custom-call | bytes 524288 | tf_op jit(solution)/shard_map/pallas_call | solution.py:68
  35.9 1.2 %collective-permute-done.3.refs_0_ = f32[16,6144]{1,0:T(8,128)S(1)} collective-permute-done((f32[16,6144]{1,0:T(8,128)S(1)}, f32[16,6144]{1,0:T(8,128)S(1)}, u32[]{:S(2)}, u32[]{:S(2)}) %collective-permute-start.3) | collective-permute-done | bytes 393248 | tf_op jit(solution)/shard_map/ppermute | solution.py:144
  37.1 1.5 %shard_map.39.refs_6_ = f32[16,256]{1,0:T(8,128)S(1)} custom-call(s32[2]{0:T(128)S(1)} %get-tuple-element.32.places, f32[16,6144]{1,0:T(8,128)S(1)} %collective-permute-done.3.refs_0_, bf16[8192,256]{1,0:T(8,128)(2,1)S(1)} %copy-done.4, bf16[8192,256]{1,0:T(8,128)(2,1)S(1)} %copy-done.1), custom_call_target="tpu_custom_call" | custom-call | bytes 393216 | tf_op jit(solution)/shard_map/pallas_call | solution.py:68
  38.5 0.8 %collective-permute-done.1.refs_0_ = f32[16,2048]{1,0:T(8,128)S(1)} collective-permute-done((f32[16,2048]{1,0:T(8,128)S(1)}, f32[16,2048]{1,0:T(8,128)S(1)}, u32[]{:S(2)}, u32[]{:S(2)}) %collective-permute-start.1) | collective-permute-done | bytes 131104 | tf_op jit(solution)/shard_map/ppermute | solution.py:148
  39.4 0.0 copy-done.2
  39.4 0.0 copy-done.5
  39.4 0.9 %shard_map.40 = (f32[16,256]{1,0:T(8,128)S(1)}, f32[16,256]{1,0:T(8,128)S(1)}, f32[16,256]{1,0:T(8,128)S(1)}, f32[16,256]{1,0:T(8,128)S(1)}) custom-call(s32[4]{0:T(128)S(1)} %pad_add_fusion.places, f32[16,2048]{1,0:T(8,128)S(1)} %collective-permute-done.1.refs_0_, bf16[8192,256]{1,0:T(8,128)(2,1)S(1)} %copy-done.5, bf16[8192,256]{1,0:T(8,128)(2,1)S(1)} %copy-done.2, ...), custom_call_target="tpu_custom_call" | custom-call | bytes 131072 | tf_op jit(solution)/shard_map/pallas_call | solution.py:68
  40.3 0.8 %collective-permute-start.4 = (f32[16,256]{1,0:T(8,128)S(1)}, f32[16,256]{1,0:T(8,128)S(1)}, u32[]{:S(2)}, u32[]{:S(2)}) collective-permute-start(f32[16,256]{1,0:T(8,128)S(1)} %get-tuple-element.26), channel_id=1, source_target_pairs={{0,3},{1,2},{2,1},{3,0},{4,7},{5,6},{6,5},{7,4},{8,11},{9,10},{10,... | collective-permute-start | bytes 49160 | tf_op jit(solution)/shard_map/ppermute | solution.py:166
  41.1 0.9 %collective-permute-start.5 = (f32[16,256]{1,0:T(8,128)S(1)}, f32[16,256]{1,0:T(8,128)S(1)}, u32[]{:S(2)}, u32[]{:S(2)}) collective-permute-start(f32[16,256]{1,0:T(8,128)S(1)} %get-tuple-element.27), channel_id=1, source_target_pairs={{0,2},{1,3},{2,0},{3,1},{4,6},{5,7},{6,4},{7,5},{8,10},{9,11},{10,... | collective-permute-start | bytes 49160 | tf_op jit(solution)/shard_map/ppermute | solution.py:166
  41.9 0.3 collective-permute-start.6
  42.2 1.4 %collective-permute-done.4 = f32[16,256]{1,0:T(8,128)S(1)} collective-permute-done((f32[16,256]{1,0:T(8,128)S(1)}, f32[16,256]{1,0:T(8,128)S(1)}, u32[]{:S(2)}, u32[]{:S(2)}) %collective-permute-start.4) | collective-permute-done | bytes 16416 | tf_op jit(solution)/shard_map/ppermute | solution.py:166
  43.7 1.3 %collective-permute-done.5 = f32[16,256]{1,0:T(8,128)S(1)} collective-permute-done((f32[16,256]{1,0:T(8,128)S(1)}, f32[16,256]{1,0:T(8,128)S(1)}, u32[]{:S(2)}, u32[]{:S(2)}) %collective-permute-start.5) | collective-permute-done | bytes 16416 | tf_op jit(solution)/shard_map/ppermute | solution.py:166
  44.9 0.0 collective-permute-done.6
  44.9 0.7 %multiply_select_fusion = f32[16,256]{1,0:T(8,128)} fusion(f32[16,256]{1,0:T(8,128)S(1)} %collective-permute-done.6, f32[16,256]{1,0:T(8,128)S(1)} %collective-permute-done.5, f32[16,256]{1,0:T(8,128)S(1)} %get-tuple-element.25, f32[16,256]{1,0:T(8,128)S(1)} %collective-permute-done.4, s32[256]{0:T(256)S(1)} %iota_add_fusion.1, s32[16]{0:T(128)S(1)} %iota_add_fusion.2), kind=kLoop, calls=%fused_computation.5 | loop fusion | flops 40960 | bytes 83008 | tf_op jit(solution)/shard_map/jit(_where)/select_n | solution.py:173
  (5 shorter events, 0.1 us)
Async XLA Ops:
  0.0 16.7 %collective-permute-start = (f32[16,8192]{1,0:T(8,128)}, f32[16,8192]{1,0:T(8,128)S(1)}, u32[]{:S(2)}, u32[]{:S(2)}) collective-permute-start(f32[16,8192]{1,0:T(8,128)} %refs_0_), channel_id=1, source_target_pairs={{0,8},{8,12},{12,4},{4,0},{1,9},{9,13},{13,5},{5,1},{2,10},{10,14}... | collective-permute-start | bytes 1572872 | tf_op jit(solution)/shard_map/ppermute | solution.py:130
  4.7 8.0 %copy-start.6 = (f32[16,8192]{1,0:T(8,128)S(1)}, f32[16,8192]{1,0:T(8,128)}, u32[]{:S(2)}) copy-start(f32[16,8192]{1,0:T(8,128)} %refs_0_) | copy-start | bytes 1572868
  12.7 17.0 %collective-permute-start.2 = (f32[16,8192]{1,0:T(8,128)S(1)}, f32[16,8192]{1,0:T(8,128)S(1)}, u32[]{:S(2)}, u32[]{:S(2)}) collective-permute-start(f32[16,8192]{1,0:T(8,128)S(1)} %copy-done.6), channel_id=1, source_target_pairs={{8,0},{12,8},{4,12},{0,4},{9,1},{13,9},{5,13},{1,5},{10,2},{14,10}... | collective-permute-start | bytes 1572872 | tf_op jit(solution)/shard_map/ppermute | solution.py:141
  16.7 20.3 %collective-permute-start.3 = (f32[16,6144]{1,0:T(8,128)S(1)}, f32[16,6144]{1,0:T(8,128)S(1)}, u32[]{:S(2)}, u32[]{:S(2)}) collective-permute-start(f32[16,6144]{1,0:T(8,128)S(1)} %slice.8), channel_id=1, source_target_pairs={{0,8},{8,12},{12,4},{4,0},{1,9},{9,13},{13,5},{5,1},{2,10},{10,14}... | collective-permute-start | bytes 1179656 | tf_op jit(solution)/shard_map/ppermute | solution.py:144
  20.1 2.2 %copy-start = (bf16[8192,256]{1,0:T(8,128)(2,1)S(1)}, bf16[8192,256]{1,0:T(8,128)(2,1)}, u32[]{:S(2)}) copy-start(bf16[8192,256]{1,0:T(8,128)(2,1)} %get-tuple-element.19.refs_3_.refs_2_) | copy-start | bytes 12582916
  22.3 2.2 %copy-start.3 = (bf16[8192,256]{1,0:T(8,128)(2,1)S(1)}, bf16[8192,256]{1,0:T(8,128)(2,1)}, u32[]{:S(2)}) copy-start(bf16[8192,256]{1,0:T(8,128)(2,1)} %get-tuple-element.18.refs_2_.refs_1_) | copy-start | bytes 12582916
  26.6 12.7 %collective-permute-start.1 = (f32[16,2048]{1,0:T(8,128)S(1)}, f32[16,2048]{1,0:T(8,128)S(1)}, u32[]{:S(2)}, u32[]{:S(2)}) collective-permute-start(f32[16,2048]{1,0:T(8,128)S(1)} %slice.6), channel_id=1, source_target_pairs={{0,8},{8,12},{12,4},{4,0},{1,9},{9,13},{13,5},{5,1},{2,10},{10,14}... | collective-permute-start | bytes 393224 | tf_op jit(solution)/shard_map/ppermute | solution.py:148
  29.7 2.2 %copy-start.1 = (bf16[8192,256]{1,0:T(8,128)(2,1)S(1)}, bf16[8192,256]{1,0:T(8,128)(2,1)}, u32[]{:S(2)}) copy-start(bf16[8192,256]{1,0:T(8,128)(2,1)} %get-tuple-element.19.refs_3_.refs_2_) | copy-start | bytes 12582916
  31.9 2.2 %copy-start.4 = (bf16[8192,256]{1,0:T(8,128)(2,1)S(1)}, bf16[8192,256]{1,0:T(8,128)(2,1)}, u32[]{:S(2)}) copy-start(bf16[8192,256]{1,0:T(8,128)(2,1)} %get-tuple-element.18.refs_2_.refs_1_) | copy-start | bytes 12582916
  34.1 5.3 %copy-start.2 = (bf16[8192,256]{1,0:T(8,128)(2,1)S(1)}, bf16[8192,256]{1,0:T(8,128)(2,1)}, u32[]{:S(2)}) copy-start(bf16[8192,256]{1,0:T(8,128)(2,1)} %get-tuple-element.19.refs_3_.refs_2_) | copy-start | bytes 12582916
  34.1 5.3 %copy-start.5 = (bf16[8192,256]{1,0:T(8,128)(2,1)S(1)}, bf16[8192,256]{1,0:T(8,128)(2,1)}, u32[]{:S(2)}) copy-start(bf16[8192,256]{1,0:T(8,128)(2,1)} %get-tuple-element.18.refs_2_.refs_1_) | copy-start | bytes 12582916
  40.3 3.4 %collective-permute-start.4 = (f32[16,256]{1,0:T(8,128)S(1)}, f32[16,256]{1,0:T(8,128)S(1)}, u32[]{:S(2)}, u32[]{:S(2)}) collective-permute-start(f32[16,256]{1,0:T(8,128)S(1)} %get-tuple-element.26), channel_id=1, source_target_pairs={{0,3},{1,2},{2,1},{3,0},{4,7},{5,6},{6,5},{7,4},{8,11},{9,10},{10,... | collective-permute-start | bytes 49160 | tf_op jit(solution)/shard_map/ppermute | solution.py:166
  41.1 3.9 %collective-permute-start.5 = (f32[16,256]{1,0:T(8,128)S(1)}, f32[16,256]{1,0:T(8,128)S(1)}, u32[]{:S(2)}, u32[]{:S(2)}) collective-permute-start(f32[16,256]{1,0:T(8,128)S(1)} %get-tuple-element.27), channel_id=1, source_target_pairs={{0,2},{1,3},{2,0},{3,1},{4,6},{5,7},{6,4},{7,5},{8,10},{9,11},{10,... | collective-permute-start | bytes 49160 | tf_op jit(solution)/shard_map/ppermute | solution.py:166
  41.9 3.0 %collective-permute-start.6 = (f32[16,256]{1,0:T(8,128)S(1)}, f32[16,256]{1,0:T(8,128)S(1)}, u32[]{:S(2)}, u32[]{:S(2)}) collective-permute-start(f32[16,256]{1,0:T(8,128)S(1)} %get-tuple-element.28), channel_id=1, source_target_pairs={{0,1},{1,0},{2,3},{3,2},{4,5},{5,4},{6,7},{7,6},{8,9},{9,8},{10,11... | collective-permute-start | bytes 49160 | tf_op jit(solution)/shard_map/ppermute | solution.py:166

commit v11 on v10

v11 whole, which is shorter than its diff:
```python
import functools
import math

import jax
import jax.numpy as jnp
from jax import lax
from jax.experimental import pallas as pl
from jax.experimental.pallas import tpu as pltpu
from jax.sharding import PartitionSpec as P

step_size = 0.5
penalty = 0.1
largest_bf16 = 3.3895313892515355e38


def halves(array):
    high = lax.reduce_precision(jnp.clip(array, -largest_bf16, largest_bf16), 8, 7)
    return high.astype(jnp.bfloat16), (array - high).astype(jnp.bfloat16)


def slots_kernel(firsts, parts_count, shares, places, *refs):
    blocks, refs = refs[: len(firsts)], refs[len(firsts) :]
    high, low, *refs = refs
    parts, outs = refs[:parts_count], refs[parts_count:]
    rows, columns = blocks[0].shape[0], high.shape[1]
    totals = [None] * len(firsts)
    for first_k in sorted(set(firsts)):
        group = [b for b, first in enumerate(firsts) if first == first_k]
        all_rows = rows * len(group)
        depth = blocks[group[0]].shape[1]
        step = math.gcd(depth, 2048)
        total = jnp.zeros((all_rows, columns), jnp.float32)
        for k in range(0, depth, step):
            values = jnp.concatenate([blocks[b][:, k : k + step] for b in group], 0)
            upper = jnp.clip(values, -largest_bf16, largest_bf16).astype(jnp.bfloat16)
            lower = (values - upper.astype(jnp.float32)).astype(jnp.bfloat16)
            both = jnp.concatenate([upper, lower], 0)
            span = slice(first_k + k, first_k + k + step)
            main = jnp.dot(both, high[span], preferred_element_type=jnp.float32)
            cross = jnp.dot(upper, low[span], preferred_element_type=jnp.float32)
            total += main[:all_rows] + main[all_rows:] + cross
        for position, b in enumerate(group):
            totals[b] = total[position * rows : (position + 1) * rows]
    if 0 in firsts:
        start = pl.multiple_of(places[0], columns)
        ahead = lax.broadcasted_iota(jnp.int32, (rows, columns), 1)
        ahead -= lax.broadcasted_iota(jnp.int32, (rows, columns), 0)
        for b, block in enumerate(blocks):
            if firsts[b] == 0:
                current = block[:, pl.ds(start, columns)]
                mask = ahead == places[1 + b]
                inverse = step_size / jnp.where(mask, current, 1.0)
                totals[b] += jnp.where(mask, inverse, 0.0)
    if not shares:
        for out, value in zip(outs, totals):
            out[...] = value
        return
    values = [part[...] for part in parts] + totals
    per_out = outs[0].shape[0] // rows
    for o, out in enumerate(outs):
        for b in range(per_out):
            found = jnp.zeros((rows, columns), jnp.float32)
            for position, value in enumerate(values):
                mine = places[1 + len(firsts) + position] == o * per_out + b
                found += jnp.where(mine, value, 0.0)
            out[b * rows : (b + 1) * rows] = found


def slot_products(places, blocks, firsts, weights, parts=(), shares=0, per_share=1):
    rows, columns = blocks[0].shape[0], weights[0].shape[1]
    outs = shares or len(blocks)
    shape = (rows * per_share if shares else rows, columns)
    return pl.pallas_call(
        functools.partial(slots_kernel, tuple(firsts), len(parts), shares),
        out_shape=[jax.ShapeDtypeStruct(shape, jnp.float32)] * outs,
        in_specs=[pl.BlockSpec(memory_space=pltpu.SMEM)]
        + [pl.BlockSpec(memory_space=pltpu.VMEM)] * (len(blocks) + 2 + len(parts)),
        out_specs=[pl.BlockSpec(memory_space=pltpu.VMEM)] * outs,
        compiler_params=pltpu.CompilerParams(
            vmem_limit_bytes=(4 + len(parts) // 4) * 1024 * 1024
        ),
        cost_estimate=pl.CostEstimate(
            flops=0, bytes_accessed=blocks[0].size * 4, transcendentals=0
        ),
    )(places, *blocks, *weights, *parts)


def sum_of(terms):
    total = terms[0]
    for term in terms[1:]:
        total = total + term
    return total


def per_device(omega_rows, covariance_columns, tile_offsets):
    team_count = lax.axis_size("team")
    rep_count = lax.axis_size("rep")
    team_index = lax.axis_index("team")
    rep_index = lax.axis_index("rep")
    block_rows, part_width = omega_rows.shape
    tile_width = covariance_columns.shape[1]
    all_rows = block_rows * team_count
    rows_share = all_rows // rep_count
    offset = tile_offsets[0]
    assert all_rows <= part_width and part_width % tile_width == 0
    assert rows_share % block_rows == 0 and rep_count & (rep_count - 1) == 0 and rep_count > 1

    k_ids = rep_index * part_width + jnp.arange(part_width, dtype=jnp.int32)
    c_ids = offset + jnp.arange(tile_width, dtype=jnp.int32)
    chosen = (k_ids[:, None] == c_ids[None, :]).astype(jnp.float32)
    weights = halves(chosen - step_size * covariance_columns)

    cut = part_width // 4 * 3
    assert all_rows <= cut and cut % tile_width == 0
    share_blocks = rows_share // block_rows

    def products_of(blocks, sources, firsts=None, spots=(), parts=(), shares=0):
        start = jnp.clip(offset, 0, cut - tile_width)
        shifts = [
            jnp.where(rep_index == 0, source * block_rows - offset, 1 << 20) for source in sources
        ]
        places = jnp.stack([start, *shifts, *spots]).astype(jnp.int32)
        firsts = firsts or [0] * len(blocks)
        return slot_products(places, blocks, firsts, weights, parts, shares, share_blocks)

    def spots_of(sources):
        return [
            ((source // share_blocks) ^ rep_index) * share_blocks + source % share_blocks
            for source in sources
        ]

    def exchanged(share, flip):
        pairs = [(d, d ^ flip) for d in range(rep_count)]
        return lax.ppermute(share, "rep", pairs)

    ring = list(range(0, team_count, 2)) + list(range(1, team_count, 2))[::-1]
    onward = [(ring[k], ring[(k + 1) % team_count]) for k in range(team_count)]
    backward = [(to, source) for source, to in onward]
    rank = team_index // 2
    place = jnp.where(team_index % 2 == 0, rank, team_count - 1 - rank)

    def device_at(spot):
        spot = spot % team_count
        up = 2 * spot
        return jnp.where(up < team_count, up, 2 * team_count - 1 - up)

    if team_count == 4 and rep_count == 4:
        own_left, own_right = omega_rows[:, :cut], omega_rows[:, cut:]
        two_apart = [(0, 2), (1, 3), (2, 0), (3, 1)]
        neighbours = [(0, 1), (1, 0), (2, 3), (3, 2)]
        home = team_index // 2 == rep_index // 2
        left1 = lax.ppermute(own_left, "team", onward)
        own_left, own_right, *weights = lax.optimization_barrier((own_left, own_right, *weights))
        right1 = lax.ppermute(own_right, "team", two_apart)
        left2 = lax.ppermute(own_left, "team", backward)
        left3 = lax.ppermute(left1, "team", onward)
        sources = [team_index, device_at(place - 1), team_index, team_index ^ 2]
        early = jnp.where(home, right1, own_right)
        late = jnp.where(home, own_right, right1)
        right2 = lax.ppermute(early, "team", neighbours)
        parts = products_of([own_left, left1, own_right, right1], sources, [0, 0, cut, cut])
        sources.append(device_at(place + 1))
        parts += products_of([left2], sources[-1:])
        late, *parts = lax.optimization_barrier((late, *parts))
        right3 = lax.ppermute(late, "team", neighbours)
        sources += [device_at(place - 2), jnp.where(home, team_index ^ 3, team_index ^ 1)]
        shares = products_of([left3, right2], sources[-2:], [0, cut], spots_of(sources), parts, 4)
        terms = [exchanged(shares[flip], flip) for flip in (3, 2)]
        source = jnp.where(home, team_index ^ 1, team_index ^ 3)
        kept, for_mate = products_of(
            [right3], [source], [cut], [0, 1] + spots_of([source]), shares[:2], 2
        )
        for_mate, *terms = lax.optimization_barrier((for_mate, *terms))
        moved = sum_of([kept, *terms, exchanged(for_mate, 1)])
    else:
        first = lax.ppermute(omega_rows, "team", onward)
        own, *weights = lax.optimization_barrier((omega_rows, *weights))
        last_step = team_count // 2
        gathered = []
        held = first
        for step in range(2, last_step):
            held = lax.ppermute(held, "team", onward)
            gathered.append((held, step))
        last_held = held
        held = own
        for step in range(1, team_count - last_step):
            held = lax.ppermute(held, "team", backward)
            gathered.append((held, -step))
        last = lax.ppermute(last_held, "team", onward)
        sources = [team_index, device_at(place - 1)]
        parts = products_of([own, first], sources)
        for block, step in gathered:
            sources.append(device_at(place - step))
            parts += products_of([block], sources[-1:])
        sources.append(device_at(place - last_step))
        shares = products_of(
            [last], sources[-1:], None, spots_of(sources), parts, rep_count
        )
        moved = sum_of([shares[0]] + [exchanged(shares[s], s) for s in range(1, rep_count)])

    global_rows = rep_index * rows_share + jnp.arange(rows_share, dtype=jnp.int32)
    global_cols = offset + jnp.arange(tile_width, dtype=jnp.int32)
    diagonal = global_rows[:, None] == global_cols[None, :]
    shrunk = jnp.sign(moved) * jnp.maximum(jnp.abs(moved) - step_size * penalty, 0.0)
    return jnp.where(diagonal, moved, shrunk)


def solution(mesh):
    in_specs = (P(("groups", "team"), "rep"), P("rep", ("groups", "team")), P(("groups", "team")))
    out_specs = P("rep", ("groups", "team"))
    return jax.shard_map(
        per_device, mesh=mesh, in_specs=in_specs, out_specs=out_specs, check_vma=False
    )
```

time: 45.9 us -> 56.7 us (1.24)
  local copies, waits for them, and re-layouts: 8.8 us -> 15.3 us
  starting transfers between devices: 9.46 us -> 11.7 us
  waiting for transfers between devices: 11.4 us -> 13.3 us
    unnamed x14, local copies, waits for them, and re-layouts: 8.77 us -> 13.1 us
    ppermute x7 -> x9, starting transfers between devices: 9.46 us -> 11.7 us  [the longest x1 4.09 us: per_device(): left1 = lax.ppermute(own_left, 'team', onward)]
    ppermute x7 -> x9, waiting for transfers between devices: 11.4 us -> 13.3 us  [the longest x1 9.15 us: per_device(): left2 = lax.ppermute(own_left, 'team', backward)]
    slice x2, local copies, waits for them, and re-layouts: 0.04 us -> 1.94 us  [per_device(): own_left, own_right = (omega_rows[:, :cut], omega_rows[:, cut:])]
  transfers between devices with their start and end apart: 7 -> 9, of which waited for: 6 -> 3; matrix products, arithmetic and copies ran while one was open for 18% -> 16% of each run, Pallas kernels for 12% -> 11%
where the time goes in v11:
time: 56.7 us; the launch traced here: 56.2 us
  local copies, waits for them, and re-layouts  15.3 us (27%)
  waiting for transfers between devices  13.3 us (23%)
  starting transfers between devices  11.7 us (21%)
  other arithmetic  8.76 us (15%)
  Pallas kernels  6.34 us (11%)
  between operations  0.81 us (1%)
    unnamed x14, local copies, waits for them, and re-layouts  13.1 us
    ppermute x1, waiting for transfers between devices, per_device(): left2 = lax.ppermute(own_left, 'team', backward)  9.15 us
    convert_element_type x1, other arithmetic, halves(): return (high.astype(jnp.bfloat16), (array - high).astype(jnp.bfloat16))  7.97 us
    pallas_call x4, Pallas kernels, slot_products(): pl.pallas_call(functools.partial(slots_kernel, tuple(firsts), len(parts),...  6.34 us
    ppermute x1, starting transfers between devices, per_device(): left1 = lax.ppermute(own_left, 'team', onward)  4.09 us
    ppermute x1, waiting for transfers between devices, per_device(): right1 = lax.ppermute(own_right, 'team', two_apart)  3.07 us
    ppermute x1, starting transfers between devices, per_device(): left3 = lax.ppermute(left1, 'team', onward)  2.59 us
    ppermute x3, starting transfers between devices, exchanged(): return lax.ppermute(share, 'rep', pairs)  2.01 us
  transfers between devices with their start and end apart: 9, of which 3 were waited for; matrix products, arithmetic and copies ran while one was open for 16% of the time, Pallas kernels for 11%

profile of v11, /device:TPU:0, one launch (start us, length us, event | category | flops | bytes accessed | tf_op | source)
XLA Modules:
  0.0 56.2 jit_solution(8529541063353409424)
XLA Ops:
  0.0 1.0 %slice.6.refs_0_ = f32[16,6144]{1,0:T(8,128)S(1)} slice(f32[16,8192]{1,0:T(8,128)} %param.3), slice={[0:16], [0:6144]} | slice | bytes 786432 | tf_op jit(solution)/shard_map/slice | solution.py:148
  1.0 4.1 %collective-permute-start.1 = (f32[16,6144]{1,0:T(8,128)S(1)}, f32[16,6144]{1,0:T(8,128)S(1)}, u32[]{:S(2)}, u32[]{:S(2)}) collective-permute-start(f32[16,6144]{1,0:T(8,128)S(1)} %slice.6.refs_0_), channel_id=1, source_target_pairs={{0,8},{8,12},{12,4},{4,0},{1,9},{9,13},{13,5},{5,1},{2,10},{10,14}... | collective-permute-start | bytes 1179656 | tf_op jit(solution)/shard_map/ppermute | solution.py:152
  5.8 8.0 %subtract_convert_fusion = (bf16[8192,256]{1,0:T(8,128)(2,1)}, bf16[8192,256]{1,0:T(8,128)(2,1)}) fusion(f32[8192,256]{1,0:T(8,128)} %param.4, s32[256]{0:T(256)S(1)} %iota_add_fusion.1, s32[8192]{0:T(1024)S(1)} %iota_add_fusion), kind=kLoop, calls=%fused_computation | loop fusion | flops 18874368 | bytes 16811008 | tf_op jit(solution)/shard_map/convert_element_type | solution.py:18
  13.8 0.9 %slice.7.refs_2_ = f32[16,2048]{1,0:T(8,128)S(1)} slice(f32[16,8192]{1,0:T(8,128)} %param.3), slice={[0:16], [6144:8192]} | slice | bytes 262144 | tf_op jit(solution)/shard_map/slice | solution.py:148
  14.7 1.6 %collective-permute-start = (f32[16,2048]{1,0:T(8,128)S(1)}, f32[16,2048]{1,0:T(8,128)S(1)}, u32[]{:S(2)}, u32[]{:S(2)}) collective-permute-start(f32[16,2048]{1,0:T(8,128)S(1)} %slice.7.refs_2_), channel_id=1, source_target_pairs={{0,8},{4,12},{8,0},{12,4},{1,9},{5,13},{9,1},{13,5},{2,10},{6,14},... | collective-permute-start | bytes 393224 | tf_op jit(solution)/shard_map/ppermute | solution.py:154
  16.3 0.3 collective-permute-start.2
  16.7 0.0 collective-permute-done.1.refs_1_
  16.7 2.6 %collective-permute-start.4 = (f32[16,6144]{1,0:T(8,128)S(1)}, f32[16,6144]{1,0:T(8,128)S(1)}, u32[]{:S(2)}, u32[]{:S(2)}) collective-permute-start(f32[16,6144]{1,0:T(8,128)S(1)} %collective-permute-done.1.refs_1_), channel_id=1, source_target_pairs={{0,8},{8,12},{12,4},{4,0},{1,9},{9,13},{13,5},{5,1},{2,10},{10,14}... | collective-permute-start | bytes 1179656 | tf_op jit(solution)/shard_map/ppermute | solution.py:156
  19.3 3.1 %collective-permute-done.refs_3_ = f32[16,2048]{1,0:T(8,128)S(1)} collective-permute-done((f32[16,2048]{1,0:T(8,128)S(1)}, f32[16,2048]{1,0:T(8,128)S(1)}, u32[]{:S(2)}, u32[]{:S(2)}) %collective-permute-start) | collective-permute-done | bytes 131104 | tf_op jit(solution)/shard_map/ppermute | solution.py:154
  22.4 1.0 %collective-permute-start.5 = (f32[16,2048]{1,0:T(8,128)S(1)}, f32[16,2048]{1,0:T(8,128)S(1)}, u32[]{:S(2)}, u32[]{:S(2)}) collective-permute-start(f32[16,2048]{1,0:T(8,128)S(1)} %get-tuple-element.53), channel_id=1, source_target_pairs={{0,4},{4,0},{8,12},{12,8},{1,5},{5,1},{9,13},{13,9},{2,6},{6,2},{1... | collective-permute-start | bytes 393224 | tf_op jit(solution)/shard_map/ppermute | solution.py:160
  23.4 0.1 pad_add_fusion.places
  23.4 0.1 stack.69.places
  23.5 0.0 copy-start
  23.5 2.2 %copy-done = bf16[8192,256]{1,0:T(8,128)(2,1)S(1)} copy-done((bf16[8192,256]{1,0:T(8,128)(2,1)S(1)}, bf16[8192,256]{1,0:T(8,128)(2,1)}, u32[]{:S(2)}) %copy-start) | copy-done | bytes 4194328
  25.7 0.0 copy-start.4
  25.7 2.2 %copy-done.4 = bf16[8192,256]{1,0:T(8,128)(2,1)S(1)} copy-done((bf16[8192,256]{1,0:T(8,128)(2,1)S(1)}, bf16[8192,256]{1,0:T(8,128)(2,1)}, u32[]{:S(2)}) %copy-start.4) | copy-done | bytes 4194328
  27.9 0.0 copy-start.1
  27.9 2.1 %shard_map.37 = (f32[16,256]{1,0:T(8,128)S(1)}, f32[16,256]{1,0:T(8,128)S(1)}, f32[16,256]{1,0:T(8,128)S(1)}, f32[16,256]{1,0:T(8,128)S(1)}) custom-call(s32[5]{0:T(128)S(1)} %stack.69.places, f32[16,6144]{1,0:T(8,128)S(1)} %slice.6.refs_0_, f32[16,6144]{1,0:T(8,128)S(1)} %collective-permute-done.1.refs_1_, f32[16,2048]{1,0:T(8,128)S(1)} %slice.7.refs_2_, ...), custom_call_target="tpu_custom_call" | custom-call | bytes 393216 | tf_op jit(solution)/shard_map/pallas_call | solution.py:73
  30.0 9.1 %collective-permute-done.2.refs_0_ = f32[16,6144]{1,0:T(8,128)S(1)} collective-permute-done((f32[16,6144]{1,0:T(8,128)S(1)}, f32[16,6144]{1,0:T(8,128)S(1)}, u32[]{:S(2)}, u32[]{:S(2)}) %collective-permute-start.2) | collective-permute-done | bytes 393248 | tf_op jit(solution)/shard_map/ppermute | solution.py:155
  39.1 0.0 copy-done.1
  39.1 1.5 %shard_map.38.refs_8_ = f32[16,256]{1,0:T(8,128)S(1)} custom-call(s32[2]{0:T(128)S(1)} %pad_add_fusion.places, f32[16,6144]{1,0:T(8,128)S(1)} %collective-permute-done.2.refs_0_, bf16[8192,256]{1,0:T(8,128)(2,1)S(1)} %copy-done.4, bf16[8192,256]{1,0:T(8,128)(2,1)S(1)} %copy-done.1), custom_call_target="tpu_custom_call" | custom-call | bytes 393216 | tf_op jit(solution)/shard_map/pallas_call | solution.py:73
  40.6 0.1 collective-permute-start.3
  40.7 0.1 stack.80.places
  40.8 0.0 collective-permute-done.5.refs_1_
  40.8 0.0 collective-permute-done.4.refs_0_
  40.8 0.0 copy-start.2
  40.9 2.2 %copy-done.2 = bf16[8192,256]{1,0:T(8,128)(2,1)S(1)} copy-done((bf16[8192,256]{1,0:T(8,128)(2,1)S(1)}, bf16[8192,256]{1,0:T(8,128)(2,1)}, u32[]{:S(2)}) %copy-start.2) | copy-done | bytes 4194328
  43.0 0.0 copy-start.5
  43.0 2.2 %copy-done.5 = bf16[8192,256]{1,0:T(8,128)(2,1)S(1)} copy-done((bf16[8192,256]{1,0:T(8,128)(2,1)S(1)}, bf16[8192,256]{1,0:T(8,128)(2,1)}, u32[]{:S(2)}) %copy-start.5) | copy-done | bytes 4194328
  45.2 1.9 %shard_map.39 = (f32[16,256]{1,0:T(8,128)S(1)}, f32[16,256]{1,0:T(8,128)S(1)}, f32[16,256]{1,0:T(8,128)S(1)}, f32[16,256]{1,0:T(8,128)S(1)}) custom-call(s32[10]{0:T(128)S(1)} %stack.80.places, f32[16,6144]{1,0:T(8,128)S(1)} %collective-permute-done.4.refs_0_, f32[16,2048]{1,0:T(8,128)S(1)} %collective-permute-done.5.refs_1_, ...), custom_call_target="tpu_custom_call" | custom-call | bytes 393216 | tf_op jit(solution)/shard_map/pallas_call | solution.py:73
  47.1 1.2 %collective-permute-start.6 = (f32[16,256]{1,0:T(8,128)S(1)}, f32[16,256]{1,0:T(8,128)S(1)}, u32[]{:S(2)}, u32[]{:S(2)}) collective-permute-start(f32[16,256]{1,0:T(8,128)S(1)} %get-tuple-element.46), channel_id=1, source_target_pairs={{0,3},{1,2},{2,1},{3,0},{4,7},{5,6},{6,5},{7,4},{8,11},{9,10},{10,... | collective-permute-start | bytes 49160 | tf_op jit(solution)/shard_map/ppermute | solution.py:134
  48.3 0.6 collective-permute-start.7
  48.9 0.1 stack.65.places
  49.0 0.0 collective-permute-done.3.refs_0_
  49.0 0.0 copy-start.3
  49.0 2.2 %copy-done.3 = bf16[8192,256]{1,0:T(8,128)(2,1)S(1)} copy-done((bf16[8192,256]{1,0:T(8,128)(2,1)S(1)}, bf16[8192,256]{1,0:T(8,128)(2,1)}, u32[]{:S(2)}) %copy-start.3) | copy-done | bytes 4194328
  51.2 0.0 copy-start.6
  51.2 2.2 %copy-done.6 = bf16[8192,256]{1,0:T(8,128)(2,1)S(1)} copy-done((bf16[8192,256]{1,0:T(8,128)(2,1)S(1)}, bf16[8192,256]{1,0:T(8,128)(2,1)}, u32[]{:S(2)}) %copy-start.6) | copy-done | bytes 4194328
  53.4 0.9 %shard_map.40 = (f32[16,256]{1,0:T(8,128)S(1)}, f32[16,256]{1,0:T(8,128)S(1)}) custom-call(s32[5]{0:T(128)S(1)} %stack.65.places, f32[16,2048]{1,0:T(8,128)S(1)} %collective-permute-done.3.refs_0_, bf16[8192,256]{1,0:T(8,128)(2,1)S(1)} %copy-done.6, bf16[8192,256]{1,0:T(8,128)(2,1)S(1)} %copy-done.3, f32[16,256]{1,0:T(8,128)S(1)} %get-tuple-element.42.refs_3_, ...), custom_call_target="tpu_custom_call" | custom-call | bytes 131072 | tf_op jit(solution)/shard_map/pallas_call | solution.py:73
  54.3 0.0 collective-permute-done.6
  54.3 0.0 collective-permute-done.7
  54.3 0.2 collective-permute-start.8
  54.5 1.0 %collective-permute-done.8 = f32[16,256]{1,0:T(8,128)S(1)} collective-permute-done((f32[16,256]{1,0:T(8,128)S(1)}, f32[16,256]{1,0:T(8,128)S(1)}, u32[]{:S(2)}, u32[]{:S(2)}) %collective-permute-start.8) | collective-permute-done | bytes 16416 | tf_op jit(solution)/shard_map/ppermute | solution.py:134
  55.6 0.7 %multiply_select_fusion = f32[16,256]{1,0:T(8,128)} fusion(f32[16,256]{1,0:T(8,128)S(1)} %collective-permute-done.8, f32[16,256]{1,0:T(8,128)S(1)} %collective-permute-done.7, f32[16,256]{1,0:T(8,128)S(1)} %get-tuple-element.44, f32[16,256]{1,0:T(8,128)S(1)} %collective-permute-done.6, s32[256]{0:T(256)S(1)} %iota_add_fusion.1, s32[16]{0:T(128)S(1)} %iota_add_fusion.2), kind=kLoop, calls=%fused_computation.7 | loop fusion | flops 40960 | bytes 83008 | tf_op jit(solution)/shard_map/jit(_where)/select_n | solution.py:205
  (4 shorter events, 0.0 us)
Async XLA Ops:
  1.0 15.6 %collective-permute-start.1 = (f32[16,6144]{1,0:T(8,128)S(1)}, f32[16,6144]{1,0:T(8,128)S(1)}, u32[]{:S(2)}, u32[]{:S(2)}) collective-permute-start(f32[16,6144]{1,0:T(8,128)S(1)} %slice.6.refs_0_), channel_id=1, source_target_pairs={{0,8},{8,12},{12,4},{4,0},{1,9},{9,13},{13,5},{5,1},{2,10},{10,14}... | collective-permute-start | bytes 1179656 | tf_op jit(solution)/shard_map/ppermute | solution.py:152
  14.7 7.6 %collective-permute-start = (f32[16,2048]{1,0:T(8,128)S(1)}, f32[16,2048]{1,0:T(8,128)S(1)}, u32[]{:S(2)}, u32[]{:S(2)}) collective-permute-start(f32[16,2048]{1,0:T(8,128)S(1)} %slice.7.refs_2_), channel_id=1, source_target_pairs={{0,8},{4,12},{8,0},{12,4},{1,9},{5,13},{9,1},{13,5},{2,10},{6,14},... | collective-permute-start | bytes 393224 | tf_op jit(solution)/shard_map/ppermute | solution.py:154
  16.3 22.8 %collective-permute-start.2 = (f32[16,6144]{1,0:T(8,128)S(1)}, f32[16,6144]{1,0:T(8,128)S(1)}, u32[]{:S(2)}, u32[]{:S(2)}) collective-permute-start(f32[16,6144]{1,0:T(8,128)S(1)} %slice.6.refs_0_), channel_id=1, source_target_pairs={{8,0},{12,8},{4,12},{0,4},{9,1},{13,9},{5,13},{1,5},{10,2},{14,10}... | collective-permute-start | bytes 1179656 | tf_op jit(solution)/shard_map/ppermute | solution.py:155
  16.7 24.2 %collective-permute-start.4 = (f32[16,6144]{1,0:T(8,128)S(1)}, f32[16,6144]{1,0:T(8,128)S(1)}, u32[]{:S(2)}, u32[]{:S(2)}) collective-permute-start(f32[16,6144]{1,0:T(8,128)S(1)} %collective-permute-done.1.refs_1_), channel_id=1, source_target_pairs={{0,8},{8,12},{12,4},{4,0},{1,9},{9,13},{13,5},{5,1},{2,10},{10,14}... | collective-permute-start | bytes 1179656 | tf_op jit(solution)/shard_map/ppermute | solution.py:156
  22.4 18.5 %collective-permute-start.5 = (f32[16,2048]{1,0:T(8,128)S(1)}, f32[16,2048]{1,0:T(8,128)S(1)}, u32[]{:S(2)}, u32[]{:S(2)}) collective-permute-start(f32[16,2048]{1,0:T(8,128)S(1)} %get-tuple-element.53), channel_id=1, source_target_pairs={{0,4},{4,0},{8,12},{12,8},{1,5},{5,1},{9,13},{13,9},{2,6},{6,2},{1... | collective-permute-start | bytes 393224 | tf_op jit(solution)/shard_map/ppermute | solution.py:160
  23.5 2.2 %copy-start = (bf16[8192,256]{1,0:T(8,128)(2,1)S(1)}, bf16[8192,256]{1,0:T(8,128)(2,1)}, u32[]{:S(2)}) copy-start(bf16[8192,256]{1,0:T(8,128)(2,1)} %get-tuple-element.31.refs_5_.refs_2_.refs_3_) | copy-start | bytes 12582916
  25.7 2.2 %copy-start.4 = (bf16[8192,256]{1,0:T(8,128)(2,1)S(1)}, bf16[8192,256]{1,0:T(8,128)(2,1)}, u32[]{:S(2)}) copy-start(bf16[8192,256]{1,0:T(8,128)(2,1)} %get-tuple-element.30.refs_4_.refs_1_.refs_2_) | copy-start | bytes 12582916
  27.9 11.2 %copy-start.1 = (bf16[8192,256]{1,0:T(8,128)(2,1)S(1)}, bf16[8192,256]{1,0:T(8,128)(2,1)}, u32[]{:S(2)}) copy-start(bf16[8192,256]{1,0:T(8,128)(2,1)} %get-tuple-element.31.refs_5_.refs_2_.refs_3_) | copy-start | bytes 12582916
  40.6 8.4 %collective-permute-start.3 = (f32[16,2048]{1,0:T(8,128)S(1)}, f32[16,2048]{1,0:T(8,128)S(1)}, u32[]{:S(2)}, u32[]{:S(2)}) collective-permute-start(f32[16,2048]{1,0:T(8,128)S(1)} %get-tuple-element.36), channel_id=1, source_target_pairs={{0,4},{4,0},{8,12},{12,8},{1,5},{5,1},{9,13},{13,9},{2,6},{6,2},{1... | collective-permute-start | bytes 393224 | tf_op jit(solution)/shard_map/ppermute | solution.py:165
  40.8 2.2 %copy-start.2 = (bf16[8192,256]{1,0:T(8,128)(2,1)S(1)}, bf16[8192,256]{1,0:T(8,128)(2,1)}, u32[]{:S(2)}) copy-start(bf16[8192,256]{1,0:T(8,128)(2,1)} %get-tuple-element.31.refs_5_.refs_2_.refs_3_) | copy-start | bytes 12582916
  43.0 2.2 %copy-start.5 = (bf16[8192,256]{1,0:T(8,128)(2,1)S(1)}, bf16[8192,256]{1,0:T(8,128)(2,1)}, u32[]{:S(2)}) copy-start(bf16[8192,256]{1,0:T(8,128)(2,1)} %get-tuple-element.30.refs_4_.refs_1_.refs_2_) | copy-start | bytes 12582916
  47.1 7.2 %collective-permute-start.6 = (f32[16,256]{1,0:T(8,128)S(1)}, f32[16,256]{1,0:T(8,128)S(1)}, u32[]{:S(2)}, u32[]{:S(2)}) collective-permute-start(f32[16,256]{1,0:T(8,128)S(1)} %get-tuple-element.46), channel_id=1, source_target_pairs={{0,3},{1,2},{2,1},{3,0},{4,7},{5,6},{6,5},{7,4},{8,11},{9,10},{10,... | collective-permute-start | bytes 49160 | tf_op jit(solution)/shard_map/ppermute | solution.py:134
  48.3 6.0 %collective-permute-start.7 = (f32[16,256]{1,0:T(8,128)S(1)}, f32[16,256]{1,0:T(8,128)S(1)}, u32[]{:S(2)}, u32[]{:S(2)}) collective-permute-start(f32[16,256]{1,0:T(8,128)S(1)} %get-tuple-element.47), channel_id=1, source_target_pairs={{0,2},{1,3},{2,0},{3,1},{4,6},{5,7},{6,4},{7,5},{8,10},{9,11},{10,... | collective-permute-start | bytes 49160 | tf_op jit(solution)/shard_map/ppermute | solution.py:134
  49.0 2.2 %copy-start.3 = (bf16[8192,256]{1,0:T(8,128)(2,1)S(1)}, bf16[8192,256]{1,0:T(8,128)(2,1)}, u32[]{:S(2)}) copy-start(bf16[8192,256]{1,0:T(8,128)(2,1)} %get-tuple-element.31.refs_5_.refs_2_.refs_3_) | copy-start | bytes 12582916
  51.2 2.2 %copy-start.6 = (bf16[8192,256]{1,0:T(8,128)(2,1)S(1)}, bf16[8192,256]{1,0:T(8,128)(2,1)}, u32[]{:S(2)}) copy-start(bf16[8192,256]{1,0:T(8,128)(2,1)} %get-tuple-element.30.refs_4_.refs_1_.refs_2_) | copy-start | bytes 12582916
  54.3 1.2 %collective-permute-start.8 = (f32[16,256]{1,0:T(8,128)S(1)}, f32[16,256]{1,0:T(8,128)S(1)}, u32[]{:S(2)}, u32[]{:S(2)}) collective-permute-start(f32[16,256]{1,0:T(8,128)S(1)} %get-tuple-element.50), channel_id=1, source_target_pairs={{0,1},{1,0},{2,3},{3,2},{4,5},{5,4},{6,7},{7,6},{8,9},{9,8},{10,11... | collective-permute-start | bytes 49160 | tf_op jit(solution)/shard_map/ppermute | solution.py:134

commit v12 on v10

--- a/solution.py
+++ b/solution.py
@@ -1,5 +1,4 @@
 import functools
-import math
 
 import jax
 import jax.numpy as jnp
@@ -18,13 +17,15 @@
     return high.astype(jnp.bfloat16), (array - high).astype(jnp.bfloat16)
 
 
-def slots_kernel(first_k, blocks_count, parts_count, places, *refs):
+def slots_kernel(first_k, blocks_count, parts_count, placed, places, *refs):
     blocks, refs = refs[:blocks_count], refs[blocks_count:]
     high, low, *refs = refs
     parts, outs = refs[:parts_count], refs[parts_count:]
     rows, depth = blocks[0].shape
     columns = high.shape[1]
-    step = math.gcd(depth, 2048)
+    pieces = -(-depth // 2048)
+    step = depth // pieces
+    assert depth % pieces == 0 and step % 128 == 0
     all_rows = rows * blocks_count
     total = jnp.zeros((all_rows, columns), jnp.float32)
     for k in range(0, depth, step):
@@ -46,27 +47,30 @@
             mask = ahead == places[1 + b]
             inverse = step_size / jnp.where(mask, current, 1.0)
             totals[b] += jnp.where(mask, inverse, 0.0)
-    if not parts_count:
+    if len(outs) == blocks_count:
         for out, value in zip(outs, totals):
             out[...] = value
         return
-    values = [part[...] for part in parts]
-    values[-1] += totals[0]
     per_out = outs[0].shape[0] // rows
+    values = [totals[0]] if placed else [part[...] for part in parts] + totals
+    spots = 1 if placed else 1 + blocks_count
     for o, out in enumerate(outs):
         for b in range(per_out):
-            found = jnp.zeros((rows, columns), jnp.float32)
-            for part, value in enumerate(values):
-                found = jnp.where(places[part] == o * per_out + b, value, found)
-            out[b * rows : (b + 1) * rows] = found
+            span = slice(b * rows, (b + 1) * rows)
+            found = parts[o][span] if placed else jnp.zeros((rows, columns), jnp.float32)
+            for position, value in enumerate(values):
+                mine = places[spots + position] == o * per_out + b
+                found = found + jnp.where(mine, value, 0.0)
+            out[span] = found
 
 
-def slot_products(places, blocks, weights, first_k=0, parts=(), shares=0):
+def slot_products(places, blocks, weights, first_k=0, parts=(), shares=0, per_share=1):
     rows, columns = blocks[0].shape[0], weights[0].shape[1]
     outs = shares or len(blocks)
-    shape = (rows * len(parts) // shares if shares else rows, columns)
+    placed = first_k > 0
+    shape = (rows * per_share, columns)
     return pl.pallas_call(
-        functools.partial(slots_kernel, first_k, len(blocks), len(parts)),
+        functools.partial(slots_kernel, first_k, len(blocks), len(parts), placed),
         out_shape=[jax.ShapeDtypeStruct(shape, jnp.float32)] * outs,
         in_specs=[pl.BlockSpec(memory_space=pltpu.SMEM)]
         + [pl.BlockSpec(memory_space=pltpu.VMEM)] * (len(blocks) + 2 + len(parts)),
@@ -105,16 +109,20 @@
     chosen = (k_ids[:, None] == c_ids[None, :]).astype(jnp.float32)
     weights = halves(chosen - step_size * covariance_columns)
 
-    cut = part_width // 4 * 3
+    cut = part_width // 16 * 13
     assert all_rows <= cut and cut % tile_width == 0
 
-    def products_of(blocks, sources):
+    share_blocks = rows_share // block_rows
+
+    def products_of(blocks, sources, spots=(), parts=()):
         start = jnp.clip(offset, 0, cut - tile_width)
         shifts = [
             jnp.where(rep_index == 0, source * block_rows - offset, 1 << 20) for source in sources
         ]
-        places = jnp.stack([start, *shifts]).astype(jnp.int32)
-        return slot_products(places, blocks, weights)
+        places = jnp.stack([start, *shifts, *spots]).astype(jnp.int32)
+        if not spots:
+            return slot_products(places, blocks, weights)
+        return slot_products(places, blocks, weights, 0, parts, rep_count, share_blocks)
 
     ring = list(range(0, team_count, 2)) + list(range(1, team_count, 2))[::-1]
     onward = [(ring[k], ring[(k + 1) % team_count]) for k in range(team_count)]
@@ -150,15 +158,15 @@
         sources.append(device_at(place - step))
         parts += products_of([block], sources[-1:])
     sources.append(device_at(place - last_step))
-    parts += products_of([last_left], sources[-1:])
 
-    share_blocks = rows_share // block_rows
     spots = [
         ((source // share_blocks) ^ rep_index) * share_blocks + source % share_blocks
         for source in sources
     ]
+    shares = products_of([last_left], sources[-1:], spots, parts)
+    places = jnp.stack([offset, spots[-1]]).astype(jnp.int32)
     shares = slot_products(
-        jnp.stack(spots).astype(jnp.int32), [last_right], weights, cut, parts, rep_count
+        places, [last_right], weights, cut, shares, rep_count, share_blocks
     )
     terms = [shares[0]]
     for flip in range(rep_count - 1, 0, -1):

time: 45.9 us -> 45.8 us (level)
  local copies, waits for them, and re-layouts: 8.8 us -> 4.51 us
  waiting for transfers between devices: 11.4 us -> 15.5 us
    ppermute x1, waiting for transfers between devices: 1.15 us -> 6.22 us  [per_device(): last_left = lax.ppermute(last_held[:, :cut], 'team', onward)]
    unnamed x14 -> x10, local copies, waits for them, and re-layouts: 8.77 us -> 4.39 us
    ppermute x1, waiting for transfers between devices: 0.84 us -> 0.01 us  [per_device(): last_right = lax.ppermute(last_held[:, cut:], 'team', onward)]
  transfers between devices with their start and end apart: 7 -> 7, of which waited for: 6 -> 5; matrix products, arithmetic and copies ran while one was open for 18% -> 18% of each run, Pallas kernels for 12% -> 12%
where the time goes in v12:
time: 45.8 us; the launch traced here: 45.6 us
  waiting for transfers between devices  15.5 us (34%)
  starting transfers between devices  9.48 us (21%)
  other arithmetic  8.88 us (19%)
  Pallas kernels  6.45 us (14%)
  local copies, waits for them, and re-layouts  4.51 us (10%)
  between operations  0.74 us (2%)
    convert_element_type x1, other arithmetic, halves(): return (high.astype(jnp.bfloat16), (array - high).astype(jnp.bfloat16))  7.96 us
    pallas_call x4, Pallas kernels, slot_products(): pl.pallas_call(functools.partial(slots_kernel, first_k, len(blocks), len(...  6.45 us
    ppermute x1, waiting for transfers between devices, per_device(): last_left = lax.ppermute(last_held[:, :cut], 'team', onward)  6.22 us
    unnamed x10, local copies, waits for them, and re-layouts  4.39 us
    ppermute x1, starting transfers between devices, per_device(): first = lax.ppermute(omega_rows, 'team', onward)  4.04 us
    ppermute x1, waiting for transfers between devices, per_device(): first = lax.ppermute(omega_rows, 'team', onward)  3.98 us
    ppermute x1, starting transfers between devices, per_device(): last_left = lax.ppermute(last_held[:, :cut], 'team', onward)  3.33 us
    ppermute x3, waiting for transfers between devices, per_device(): terms.append(lax.ppermute(shares[flip], 'rep', pairs))  2.69 us
  transfers between devices with their start and end apart: 7, of which 5 were waited for; matrix products, arithmetic and copies ran while one was open for 18% of the time, Pallas kernels for 12%

profile of v12, /device:TPU:0, one launch (start us, length us, event | category | flops | bytes accessed | tf_op | source)
XLA Modules:
  0.0 45.6 jit_solution(12195348288630314104)
XLA Ops:
  0.0 4.0 %collective-permute-start = (f32[16,8192]{1,0:T(8,128)}, f32[16,8192]{1,0:T(8,128)S(1)}, u32[]{:S(2)}, u32[]{:S(2)}) collective-permute-start(f32[16,8192]{1,0:T(8,128)} %refs_0_), channel_id=1, source_target_pairs={{0,8},{8,12},{12,4},{4,0},{1,9},{9,13},{13,5},{5,1},{2,10},{10,14}... | collective-permute-start | bytes 1572872 | tf_op jit(solution)/shard_map/ppermute | solution.py:138
  4.7 0.0 copy-start.4
  4.7 8.0 %subtract_convert_fusion = (bf16[8192,256]{1,0:T(8,128)(2,1)}, bf16[8192,256]{1,0:T(8,128)(2,1)}) fusion(f32[8192,256]{1,0:T(8,128)} %param.4, s32[256]{0:T(256)S(1)} %iota_add_fusion.1, s32[8192]{0:T(1024)S(1)} %iota_add_fusion), kind=kLoop, calls=%fused_computation | loop fusion | flops 18874368 | bytes 16811008 | tf_op jit(solution)/shard_map/convert_element_type | solution.py:17
  12.7 0.0 copy-done.4
  12.7 0.0 collective-permute-start.3
  12.7 4.0 %collective-permute-done.refs_1_ = f32[16,8192]{1,0:T(8,128)S(1)} collective-permute-done((f32[16,8192]{1,0:T(8,128)}, f32[16,8192]{1,0:T(8,128)S(1)}, u32[]{:S(2)}, u32[]{:S(2)}) %collective-permute-start) | collective-permute-done | bytes 524320 | tf_op jit(solution)/shard_map/ppermute | solution.py:138
  16.7 3.3 %collective-permute-start.2 = (f32[16,6656]{1,0:T(8,128)S(1)}, f32[16,6656]{1,0:T(8,128)S(1)}, u32[]{:S(2)}, u32[]{:S(2)}) collective-permute-start(f32[16,6656]{1,0:T(8,128)S(1)} %slice.8), channel_id=1, source_target_pairs={{0,8},{8,12},{12,4},{4,0},{1,9},{9,13},{13,5},{5,1},{2,10},{10,14}... | collective-permute-start | bytes 1277960 | tf_op jit(solution)/shard_map/ppermute | solution.py:152
  20.0 0.1 stack.52.places
  20.1 0.1 pad_add_fusion.places
  20.2 0.1 pad_add_fusion.1.places
  20.3 0.0 copy-start
  20.3 2.2 %copy-done = bf16[8192,256]{1,0:T(8,128)(2,1)S(1)} copy-done((bf16[8192,256]{1,0:T(8,128)(2,1)S(1)}, bf16[8192,256]{1,0:T(8,128)(2,1)}, u32[]{:S(2)}) %copy-start) | copy-done | bytes 4194328
  22.5 0.0 copy-start.2
  22.5 2.2 %copy-done.2 = bf16[8192,256]{1,0:T(8,128)(2,1)S(1)} copy-done((bf16[8192,256]{1,0:T(8,128)(2,1)S(1)}, bf16[8192,256]{1,0:T(8,128)(2,1)}, u32[]{:S(2)}) %copy-start.2) | copy-done | bytes 4194328
  24.7 0.0 copy-start.1
  24.7 0.0 copy-start.3
  24.7 2.1 %shard_map.37 = (f32[16,256]{1,0:T(8,128)S(1)}, f32[16,256]{1,0:T(8,128)S(1)}) custom-call(s32[3]{0:T(128)S(1)} %pad_add_fusion.1.places, f32[16,8192]{1,0:T(8,128)S(1)} %copy-done.4, f32[16,8192]{1,0:T(8,128)S(1)} %collective-permute-done.refs_1_, bf16[8192,256]{1,0:T(8,128)(2,1)S(1)} %copy-done.2, bf16[8192,256]{1,0:T(8,128)(2,1)S(1)} %copy-done), custom_call_target="tpu_custom_call" | custom-call | bytes 524288 | tf_op jit(solution)/shard_map/pallas_call | solution.py:72
  26.8 0.2 collective-permute-start.1
  27.0 0.1 pad_add_fusion.2.places
  27.0 2.6 %collective-permute-done.3.refs_0_ = f32[16,8192]{1,0:T(8,128)S(1)} collective-permute-done((f32[16,8192]{1,0:T(8,128)S(1)}, f32[16,8192]{1,0:T(8,128)S(1)}, u32[]{:S(2)}, u32[]{:S(2)}) %collective-permute-start.3) | collective-permute-done | bytes 524320 | tf_op jit(solution)/shard_map/ppermute | solution.py:149
  29.7 0.0 copy-done.1
  29.7 0.0 copy-done.3
  29.7 1.9 %shard_map.38.refs_5_ = f32[16,256]{1,0:T(8,128)S(1)} custom-call(s32[2]{0:T(128)S(1)} %pad_add_fusion.2.places, f32[16,8192]{1,0:T(8,128)S(1)} %collective-permute-done.3.refs_0_, bf16[8192,256]{1,0:T(8,128)(2,1)S(1)} %copy-done.3, bf16[8192,256]{1,0:T(8,128)(2,1)S(1)} %copy-done.1), custom_call_target="tpu_custom_call" | custom-call | bytes 524288 | tf_op jit(solution)/shard_map/pallas_call | solution.py:72
  31.5 6.2 %collective-permute-done.2.refs_0_ = f32[16,6656]{1,0:T(8,128)S(1)} collective-permute-done((f32[16,6656]{1,0:T(8,128)S(1)}, f32[16,6656]{1,0:T(8,128)S(1)}, u32[]{:S(2)}, u32[]{:S(2)}) %collective-permute-start.2) | collective-permute-done | bytes 426016 | tf_op jit(solution)/shard_map/ppermute | solution.py:152
  37.8 1.6 %shard_map.39 = (f32[16,256]{1,0:T(8,128)S(1)}, f32[16,256]{1,0:T(8,128)S(1)}, f32[16,256]{1,0:T(8,128)S(1)}, f32[16,256]{1,0:T(8,128)S(1)}) custom-call(s32[6]{0:T(128)S(1)} %stack.52.places, f32[16,6656]{1,0:T(8,128)S(1)} %collective-permute-done.2.refs_0_, bf16[8192,256]{1,0:T(8,128)(2,1)S(1)} %copy-done.3, bf16[8192,256]{1,0:T(8,128)(2,1)S(1)} %copy-done.1, ...), custom_call_target="tpu_custom_call" | custom-call | bytes 425984 | tf_op jit(solution)/shard_map/pallas_call | solution.py:72
  39.4 0.0 collective-permute-done.1.refs_0_
  39.4 0.9 %shard_map.40 = (f32[16,256]{1,0:T(8,128)S(1)}, f32[16,256]{1,0:T(8,128)S(1)}, f32[16,256]{1,0:T(8,128)S(1)}, f32[16,256]{1,0:T(8,128)S(1)}) custom-call(s32[2]{0:T(128)S(1)} %pad_add_fusion.places, f32[16,1536]{1,0:T(8,128)S(1)} %collective-permute-done.1.refs_0_, bf16[8192,256]{1,0:T(8,128)(2,1)S(1)} %copy-done.3, bf16[8192,256]{1,0:T(8,128)(2,1)S(1)} %copy-done.1, ...), custom_call_target="tpu_custom_call" | custom-call | bytes 98304 | tf_op jit(solution)/shard_map/pallas_call | solution.py:72
  40.3 0.7 %collective-permute-start.4 = (f32[16,256]{1,0:T(8,128)S(1)}, f32[16,256]{1,0:T(8,128)S(1)}, u32[]{:S(2)}, u32[]{:S(2)}) collective-permute-start(f32[16,256]{1,0:T(8,128)S(1)} %get-tuple-element.34), channel_id=1, source_target_pairs={{0,3},{1,2},{2,1},{3,0},{4,7},{5,6},{6,5},{7,4},{8,11},{9,10},{10,... | collective-permute-start | bytes 49160 | tf_op jit(solution)/shard_map/ppermute | solution.py:174
  41.0 0.9 %collective-permute-start.5 = (f32[16,256]{1,0:T(8,128)S(1)}, f32[16,256]{1,0:T(8,128)S(1)}, u32[]{:S(2)}, u32[]{:S(2)}) collective-permute-start(f32[16,256]{1,0:T(8,128)S(1)} %get-tuple-element.35), channel_id=1, source_target_pairs={{0,2},{1,3},{2,0},{3,1},{4,6},{5,7},{6,4},{7,5},{8,10},{9,11},{10,... | collective-permute-start | bytes 49160 | tf_op jit(solution)/shard_map/ppermute | solution.py:174
  41.9 0.3 collective-permute-start.6
  42.2 1.4 %collective-permute-done.4 = f32[16,256]{1,0:T(8,128)S(1)} collective-permute-done((f32[16,256]{1,0:T(8,128)S(1)}, f32[16,256]{1,0:T(8,128)S(1)}, u32[]{:S(2)}, u32[]{:S(2)}) %collective-permute-start.4) | collective-permute-done | bytes 16416 | tf_op jit(solution)/shard_map/ppermute | solution.py:174
  43.6 1.3 %collective-permute-done.5 = f32[16,256]{1,0:T(8,128)S(1)} collective-permute-done((f32[16,256]{1,0:T(8,128)S(1)}, f32[16,256]{1,0:T(8,128)S(1)}, u32[]{:S(2)}, u32[]{:S(2)}) %collective-permute-start.5) | collective-permute-done | bytes 16416 | tf_op jit(solution)/shard_map/ppermute | solution.py:174
  44.9 0.0 collective-permute-done.6
  44.9 0.7 %multiply_select_fusion = f32[16,256]{1,0:T(8,128)} fusion(f32[16,256]{1,0:T(8,128)S(1)} %collective-permute-done.6, f32[16,256]{1,0:T(8,128)S(1)} %collective-permute-done.5, f32[16,256]{1,0:T(8,128)S(1)} %get-tuple-element.33, f32[16,256]{1,0:T(8,128)S(1)} %collective-permute-done.4, s32[256]{0:T(256)S(1)} %iota_add_fusion.1, s32[16]{0:T(128)S(1)} %iota_add_fusion.2), kind=kLoop, calls=%fused_computation.5 | loop fusion | flops 40960 | bytes 83008 | tf_op jit(solution)/shard_map/jit(_where)/select_n | solution.py:181
  (5 shorter events, 0.1 us)
Async XLA Ops:
  0.0 16.7 %collective-permute-start = (f32[16,8192]{1,0:T(8,128)}, f32[16,8192]{1,0:T(8,128)S(1)}, u32[]{:S(2)}, u32[]{:S(2)}) collective-permute-start(f32[16,8192]{1,0:T(8,128)} %refs_0_), channel_id=1, source_target_pairs={{0,8},{8,12},{12,4},{4,0},{1,9},{9,13},{13,5},{5,1},{2,10},{10,14}... | collective-permute-start | bytes 1572872 | tf_op jit(solution)/shard_map/ppermute | solution.py:138
  4.7 8.0 %copy-start.4 = (f32[16,8192]{1,0:T(8,128)S(1)}, f32[16,8192]{1,0:T(8,128)}, u32[]{:S(2)}) copy-start(f32[16,8192]{1,0:T(8,128)} %refs_0_) | copy-start | bytes 1572868
  12.7 17.0 %collective-permute-start.3 = (f32[16,8192]{1,0:T(8,128)S(1)}, f32[16,8192]{1,0:T(8,128)S(1)}, u32[]{:S(2)}, u32[]{:S(2)}) collective-permute-start(f32[16,8192]{1,0:T(8,128)S(1)} %copy-done.4), channel_id=1, source_target_pairs={{8,0},{12,8},{4,12},{0,4},{9,1},{13,9},{5,13},{1,5},{10,2},{14,10}... | collective-permute-start | bytes 1572872 | tf_op jit(solution)/shard_map/ppermute | solution.py:149
  16.7 21.0 %collective-permute-start.2 = (f32[16,6656]{1,0:T(8,128)S(1)}, f32[16,6656]{1,0:T(8,128)S(1)}, u32[]{:S(2)}, u32[]{:S(2)}) collective-permute-start(f32[16,6656]{1,0:T(8,128)S(1)} %slice.8), channel_id=1, source_target_pairs={{0,8},{8,12},{12,4},{4,0},{1,9},{9,13},{13,5},{5,1},{2,10},{10,14}... | collective-permute-start | bytes 1277960 | tf_op jit(solution)/shard_map/ppermute | solution.py:152
  20.3 2.2 %copy-start = (bf16[8192,256]{1,0:T(8,128)(2,1)S(1)}, bf16[8192,256]{1,0:T(8,128)(2,1)}, u32[]{:S(2)}) copy-start(bf16[8192,256]{1,0:T(8,128)(2,1)} %get-tuple-element.23.refs_3_.refs_2_) | copy-start | bytes 12582916
  22.5 2.2 %copy-start.2 = (bf16[8192,256]{1,0:T(8,128)(2,1)S(1)}, bf16[8192,256]{1,0:T(8,128)(2,1)}, u32[]{:S(2)}) copy-start(bf16[8192,256]{1,0:T(8,128)(2,1)} %get-tuple-element.22.refs_2_.refs_1_) | copy-start | bytes 12582916
  24.7 5.0 %copy-start.1 = (bf16[8192,256]{1,0:T(8,128)(2,1)S(1)}, bf16[8192,256]{1,0:T(8,128)(2,1)}, u32[]{:S(2)}) copy-start(bf16[8192,256]{1,0:T(8,128)(2,1)} %get-tuple-element.23.refs_3_.refs_2_) | copy-start | bytes 12582916
  24.7 5.0 %copy-start.3 = (bf16[8192,256]{1,0:T(8,128)(2,1)S(1)}, bf16[8192,256]{1,0:T(8,128)(2,1)}, u32[]{:S(2)}) copy-start(bf16[8192,256]{1,0:T(8,128)(2,1)} %get-tuple-element.22.refs_2_.refs_1_) | copy-start | bytes 12582916
  26.8 12.6 %collective-permute-start.1 = (f32[16,1536]{1,0:T(8,128)S(1)}, f32[16,1536]{1,0:T(8,128)S(1)}, u32[]{:S(2)}, u32[]{:S(2)}) collective-permute-start(f32[16,1536]{1,0:T(8,128)S(1)} %slice.6), channel_id=1, source_target_pairs={{0,8},{8,12},{12,4},{4,0},{1,9},{9,13},{13,5},{5,1},{2,10},{10,14}... | collective-permute-start | bytes 294920 | tf_op jit(solution)/shard_map/ppermute | solution.py:156
  40.3 3.4 %collective-permute-start.4 = (f32[16,256]{1,0:T(8,128)S(1)}, f32[16,256]{1,0:T(8,128)S(1)}, u32[]{:S(2)}, u32[]{:S(2)}) collective-permute-start(f32[16,256]{1,0:T(8,128)S(1)} %get-tuple-element.34), channel_id=1, source_target_pairs={{0,3},{1,2},{2,1},{3,0},{4,7},{5,6},{6,5},{7,4},{8,11},{9,10},{10,... | collective-permute-start | bytes 49160 | tf_op jit(solution)/shard_map/ppermute | solution.py:174
  41.0 3.9 %collective-permute-start.5 = (f32[16,256]{1,0:T(8,128)S(1)}, f32[16,256]{1,0:T(8,128)S(1)}, u32[]{:S(2)}, u32[]{:S(2)}) collective-permute-start(f32[16,256]{1,0:T(8,128)S(1)} %get-tuple-element.35), channel_id=1, source_target_pairs={{0,2},{1,3},{2,0},{3,1},{4,6},{5,7},{6,4},{7,5},{8,10},{9,11},{10,... | collective-permute-start | bytes 49160 | tf_op jit(solution)/shard_map/ppermute | solution.py:174
  41.9 3.0 %collective-permute-start.6 = (f32[16,256]{1,0:T(8,128)S(1)}, f32[16,256]{1,0:T(8,128)S(1)}, u32[]{:S(2)}, u32[]{:S(2)}) collective-permute-start(f32[16,256]{1,0:T(8,128)S(1)} %get-tuple-element.36), channel_id=1, source_target_pairs={{0,1},{1,0},{2,3},{3,2},{4,5},{5,4},{6,7},{7,6},{8,9},{9,8},{10,11... | collective-permute-start | bytes 49160 | tf_op jit(solution)/shard_map/ppermute | solution.py:174

commit v13 on v12

--- a/solution.py
+++ b/solution.py
@@ -17,17 +17,13 @@
     return high.astype(jnp.bfloat16), (array - high).astype(jnp.bfloat16)
 
 
-def slots_kernel(first_k, blocks_count, parts_count, placed, places, *refs):
-    blocks, refs = refs[:blocks_count], refs[blocks_count:]
-    high, low, *refs = refs
-    parts, outs = refs[:parts_count], refs[parts_count:]
+def products(blocks, high, low, first_k=0):
     rows, depth = blocks[0].shape
-    columns = high.shape[1]
     pieces = -(-depth // 2048)
     step = depth // pieces
     assert depth % pieces == 0 and step % 128 == 0
-    all_rows = rows * blocks_count
-    total = jnp.zeros((all_rows, columns), jnp.float32)
+    all_rows = rows * len(blocks)
+    total = jnp.zeros((all_rows, high.shape[1]), jnp.float32)
     for k in range(0, depth, step):
         values = jnp.concatenate([block[:, k : k + step] for block in blocks], 0)
         upper = jnp.clip(values, -largest_bf16, largest_bf16).astype(jnp.bfloat16)
@@ -37,51 +33,59 @@
         main = jnp.dot(both, high[span], preferred_element_type=jnp.float32)
         cross = jnp.dot(upper, low[span], preferred_element_type=jnp.float32)
         total += main[:all_rows] + main[all_rows:] + cross
-    totals = [total[b * rows : (b + 1) * rows] for b in range(blocks_count)]
-    if first_k == 0:
-        start = pl.multiple_of(places[0], columns)
-        ahead = lax.broadcasted_iota(jnp.int32, (rows, columns), 1)
-        ahead -= lax.broadcasted_iota(jnp.int32, (rows, columns), 0)
-        for b, block in enumerate(blocks):
-            current = block[:, pl.ds(start, columns)]
-            mask = ahead == places[1 + b]
-            inverse = step_size / jnp.where(mask, current, 1.0)
-            totals[b] += jnp.where(mask, inverse, 0.0)
+    return [total[b * rows : (b + 1) * rows] for b in range(len(blocks))]
+
+
+def slots_kernel(blocks_count, parts_count, places, *refs):
+    blocks, refs = refs[:blocks_count], refs[blocks_count:]
+    high, low, *refs = refs
+    parts, outs = refs[:parts_count], refs[parts_count:]
+    rows, columns = blocks[0].shape[0], high.shape[1]
+    totals = products(blocks, high, low)
+    start = pl.multiple_of(places[0], columns)
+    ahead = lax.broadcasted_iota(jnp.int32, (rows, columns), 1)
+    ahead -= lax.broadcasted_iota(jnp.int32, (rows, columns), 0)
+    for b, block in enumerate(blocks):
+        current = block[:, pl.ds(start, columns)]
+        mask = ahead == places[1 + b]
+        inverse = step_size / jnp.where(mask, current, 1.0)
+        totals[b] += jnp.where(mask, inverse, 0.0)
     if len(outs) == blocks_count:
         for out, value in zip(outs, totals):
             out[...] = value
         return
     per_out = outs[0].shape[0] // rows
-    values = [totals[0]] if placed else [part[...] for part in parts] + totals
-    spots = 1 if placed else 1 + blocks_count
     for o, out in enumerate(outs):
         for b in range(per_out):
-            span = slice(b * rows, (b + 1) * rows)
-            found = parts[o][span] if placed else jnp.zeros((rows, columns), jnp.float32)
-            for position, value in enumerate(values):
-                mine = places[spots + position] == o * per_out + b
+            found = jnp.zeros((rows, columns), jnp.float32)
+            for position, value in enumerate([part[...] for part in parts] + totals):
+                mine = places[1 + blocks_count + position] == o * per_out + b
                 found = found + jnp.where(mine, value, 0.0)
-            out[span] = found
+            out[b * rows : (b + 1) * rows] = found
 
 
-def slot_products(places, blocks, weights, first_k=0, parts=(), shares=0, per_share=1):
-    rows, columns = blocks[0].shape[0], weights[0].shape[1]
-    outs = shares or len(blocks)
-    placed = first_k > 0
-    shape = (rows * per_share, columns)
+def last_kernel(first_k, masks, block, high, low, *refs):
+    shares, outs = refs[: len(refs) // 2], refs[len(refs) // 2 :]
+    rows = block.shape[0]
+    (total,) = products([block], high, low, first_k)
+    for o, out in enumerate(outs):
+        for b in range(out.shape[0] // rows):
+            span = slice(b * rows, (b + 1) * rows)
+            out[span] = shares[o][span] + jnp.where(masks[o, span] != 0, total, 0.0)
+
+
+def call(kernel, count, shape, scalars, arrays, limit):
     return pl.pallas_call(
-        functools.partial(slots_kernel, first_k, len(blocks), len(parts), placed),
-        out_shape=[jax.ShapeDtypeStruct(shape, jnp.float32)] * outs,
-        in_specs=[pl.BlockSpec(memory_space=pltpu.SMEM)]
-        + [pl.BlockSpec(memory_space=pltpu.VMEM)] * (len(blocks) + 2 + len(parts)),
-        out_specs=[pl.BlockSpec(memory_space=pltpu.VMEM)] * outs,
-        compiler_params=pltpu.CompilerParams(
-            vmem_limit_bytes=(4 + len(parts) // 4) * 1024 * 1024
+        kernel,
+        out_shape=[jax.ShapeDtypeStruct(shape, jnp.float32)] * count,
+        in_specs=[pl.BlockSpec(memory_space=pltpu.SMEM)] * len(scalars)
+        + [pl.BlockSpec(memory_space=pltpu.VMEM)] * len(arrays),
+        out_specs=[pl.BlockSpec(memory_space=pltpu.VMEM)] * count,
+        compiler_params=pltpu.CompilerParams(vmem_limit_bytes=limit * 1024 * 1024),
+        cost_estimate=pl.CostEstimate(
+            flops=0, bytes_accessed=count * shape[0] * shape[1] * 4, transcendentals=0
         ),
-        cost_estimate=pl.CostEstimate(
-            flops=0, bytes_accessed=blocks[0].size * 4, transcendentals=0
-        ),
-    )(places, *blocks, *weights, *parts)
+    )(*scalars, *arrays)
 
 
 def sum_of(terms):
@@ -109,7 +113,7 @@
     chosen = (k_ids[:, None] == c_ids[None, :]).astype(jnp.float32)
     weights = halves(chosen - step_size * covariance_columns)
 
-    cut = part_width // 16 * 13
+    cut = part_width // 4 * 3
     assert all_rows <= cut and cut % tile_width == 0
 
     share_blocks = rows_share // block_rows
@@ -120,9 +124,10 @@
             jnp.where(rep_index == 0, source * block_rows - offset, 1 << 20) for source in sources
         ]
         places = jnp.stack([start, *shifts, *spots]).astype(jnp.int32)
-        if not spots:
-            return slot_products(places, blocks, weights)
-        return slot_products(places, blocks, weights, 0, parts, rep_count, share_blocks)
+        count, rows = (rep_count, rows_share) if spots else (len(blocks), block_rows)
+        kernel = functools.partial(slots_kernel, len(blocks), len(parts))
+        arrays = [*blocks, *weights, *parts]
+        return call(kernel, count, (rows, tile_width), [places], arrays, 4 + len(parts) // 4)
 
     ring = list(range(0, team_count, 2)) + list(range(1, team_count, 2))[::-1]
     onward = [(ring[k], ring[(k + 1) % team_count]) for k in range(team_count)]
@@ -163,11 +168,16 @@
         ((source // share_blocks) ^ rep_index) * share_blocks + source % share_blocks
         for source in sources
     ]
+    row_spots = jnp.arange(rep_count * rows_share, dtype=jnp.int32) // block_rows
+    masks = jnp.broadcast_to(
+        (row_spots == spots[-1]).astype(jnp.int32).reshape(rep_count, rows_share, 1),
+        (rep_count, rows_share, tile_width),
+    )
+    last_left, masks = lax.optimization_barrier((last_left, masks))
     shares = products_of([last_left], sources[-1:], spots, parts)
-    places = jnp.stack([offset, spots[-1]]).astype(jnp.int32)
-    shares = slot_products(
-        places, [last_right], weights, cut, shares, rep_count, share_blocks
-    )
+    kernel = functools.partial(last_kernel, cut)
+    arrays = [masks, last_right, *weights, *shares]
+    shares = call(kernel, rep_count, (rows_share, tile_width), [], arrays, 4 + rep_count)
     terms = [shares[0]]
     for flip in range(rep_count - 1, 0, -1):
         pairs = [(d, d ^ flip) for d in range(rep_count)]

time: 45.8 us -> 45.4 us (level)
  local copies, waits for them, and re-layouts: 4.51 us -> 9.34 us
  waiting for transfers between devices: 15.5 us -> 10.9 us
  Pallas kernels: 6.45 us -> 5.83 us
    ppermute x1, waiting for transfers between devices: 6.22 us -> 1.15 us  [per_device(): last_left = lax.ppermute(last_held[:, :cut], 'team', onward)]
    unnamed x10 -> x14, local copies, waits for them, and re-layouts: 4.39 us -> 9.15 us
    pallas_call x4, Pallas kernels: 6.45 us -> 5.83 us  [call(): pl.pallas_call(kernel, out_shape=[jax.ShapeDtypeStruct(shape, jnp.float32...]
  transfers between devices with their start and end apart: 7 -> 7, of which waited for: 5 -> 6; matrix products, arithmetic and copies ran while one was open for 18% -> 19% of each run, Pallas kernels for 12% -> 12%
where the time goes in v13:
time: 45.4 us; the launch traced here: 45.1 us
  waiting for transfers between devices  10.9 us (24%)
  starting transfers between devices  9.45 us (21%)
  local copies, waits for them, and re-layouts  9.34 us (21%)
  other arithmetic  8.84 us (19%)
  Pallas kernels  5.83 us (13%)
  between operations  0.73 us (2%)
    unnamed x14, local copies, waits for them, and re-layouts  9.15 us
    convert_element_type x1, other arithmetic, halves(): return (high.astype(jnp.bfloat16), (array - high).astype(jnp.bfloat16))  7.98 us
    pallas_call x4, Pallas kernels, call(): pl.pallas_call(kernel, out_shape=[jax.ShapeDtypeStruct(shape, jnp.float32...  5.83 us
    ppermute x1, starting transfers between devices, per_device(): first = lax.ppermute(omega_rows, 'team', onward)  4.04 us
    ppermute x1, waiting for transfers between devices, per_device(): first = lax.ppermute(omega_rows, 'team', onward)  3.95 us
    ppermute x1, starting transfers between devices, per_device(): last_left = lax.ppermute(last_held[:, :cut], 'team', onward)  3.33 us
    ppermute x1, waiting for transfers between devices, per_device(): held = lax.ppermute(held, 'team', backward)  2.72 us
    ppermute x3, waiting for transfers between devices, per_device(): terms.append(lax.ppermute(shares[flip], 'rep', pairs))  2.69 us
  transfers between devices with their start and end apart: 7, of which 6 were waited for; matrix products, arithmetic and copies ran while one was open for 19% of the time, Pallas kernels for 12%

profile of v13, /device:TPU:0, one launch (start us, length us, event | category | flops | bytes accessed | tf_op | source)
XLA Modules:
  0.0 45.1 jit_solution(13767614367584277029)
XLA Ops:
  0.0 4.0 %collective-permute-start = (f32[16,8192]{1,0:T(8,128)}, f32[16,8192]{1,0:T(8,128)S(1)}, u32[]{:S(2)}, u32[]{:S(2)}) collective-permute-start(f32[16,8192]{1,0:T(8,128)} %refs_0_), channel_id=1, source_target_pairs={{0,8},{8,12},{12,4},{4,0},{1,9},{9,13},{13,5},{5,1},{2,10},{10,14}... | collective-permute-start | bytes 1572872 | tf_op jit(solution)/shard_map/ppermute | solution.py:143
  4.7 0.0 copy-start.6
  4.7 8.0 %subtract_convert_fusion = (bf16[8192,256]{1,0:T(8,128)(2,1)}, bf16[8192,256]{1,0:T(8,128)(2,1)}) fusion(f32[8192,256]{1,0:T(8,128)} %param.4, s32[256]{0:T(256)S(1)} %iota_add_fusion.1, s32[8192]{0:T(1024)S(1)} %iota_add_fusion), kind=kLoop, calls=%fused_computation | loop fusion | flops 18874368 | bytes 16811008 | tf_op jit(solution)/shard_map/convert_element_type | solution.py:17
  12.7 0.0 copy-done.6
  12.7 0.0 collective-permute-start.3
  12.7 4.0 %collective-permute-done.refs_1_ = f32[16,8192]{1,0:T(8,128)S(1)} collective-permute-done((f32[16,8192]{1,0:T(8,128)}, f32[16,8192]{1,0:T(8,128)S(1)}, u32[]{:S(2)}, u32[]{:S(2)}) %collective-permute-start) | collective-permute-done | bytes 524320 | tf_op jit(solution)/shard_map/ppermute | solution.py:143
  16.7 3.3 %collective-permute-start.1 = (f32[16,6144]{1,0:T(8,128)S(1)}, f32[16,6144]{1,0:T(8,128)S(1)}, u32[]{:S(2)}, u32[]{:S(2)}) collective-permute-start(f32[16,6144]{1,0:T(8,128)S(1)} %slice.8), channel_id=1, source_target_pairs={{0,8},{8,12},{12,4},{4,0},{1,9},{9,13},{13,5},{5,1},{2,10},{10,14}... | collective-permute-start | bytes 1179656 | tf_op jit(solution)/shard_map/ppermute | solution.py:157
  20.0 0.1 pad_add_fusion.places
  20.1 0.0 copy-start
  20.1 2.2 %copy-done = bf16[8192,256]{1,0:T(8,128)(2,1)S(1)} copy-done((bf16[8192,256]{1,0:T(8,128)(2,1)S(1)}, bf16[8192,256]{1,0:T(8,128)(2,1)}, u32[]{:S(2)}) %copy-start) | copy-done | bytes 4194328
  22.3 0.0 copy-start.3
  22.3 2.2 %copy-done.3 = bf16[8192,256]{1,0:T(8,128)(2,1)S(1)} copy-done((bf16[8192,256]{1,0:T(8,128)(2,1)S(1)}, bf16[8192,256]{1,0:T(8,128)(2,1)}, u32[]{:S(2)}) %copy-start.3) | copy-done | bytes 4194328
  24.5 2.1 %shard_map.37 = (f32[16,256]{1,0:T(8,128)S(1)}, f32[16,256]{1,0:T(8,128)S(1)}) custom-call(s32[3]{0:T(128)S(1)} %pad_add_fusion.places, f32[16,8192]{1,0:T(8,128)S(1)} %copy-done.6, f32[16,8192]{1,0:T(8,128)S(1)} %collective-permute-done.refs_1_, bf16[8192,256]{1,0:T(8,128)(2,1)S(1)} %copy-done.3, bf16[8192,256]{1,0:T(8,128)(2,1)S(1)} %copy-done), custom_call_target="tpu_custom_call" | custom-call | bytes 32768 | tf_op jit(solution)/shard_map/pallas_call | solution.py:78
  26.6 0.2 collective-permute-start.2
  26.8 0.1 pad_add_fusion.1.places
  26.9 0.1 stack.47.places
  27.0 2.7 %collective-permute-done.3.refs_0_ = f32[16,8192]{1,0:T(8,128)S(1)} collective-permute-done((f32[16,8192]{1,0:T(8,128)S(1)}, f32[16,8192]{1,0:T(8,128)S(1)}, u32[]{:S(2)}, u32[]{:S(2)}) %collective-permute-start.3) | collective-permute-done | bytes 524320 | tf_op jit(solution)/shard_map/ppermute | solution.py:154
  29.7 0.0 copy-start.1
  29.7 2.2 %copy-done.1 = bf16[8192,256]{1,0:T(8,128)(2,1)S(1)} copy-done((bf16[8192,256]{1,0:T(8,128)(2,1)S(1)}, bf16[8192,256]{1,0:T(8,128)(2,1)}, u32[]{:S(2)}) %copy-start.1) | copy-done | bytes 4194328
  31.9 0.0 copy-start.4
  31.9 2.2 %copy-done.4 = bf16[8192,256]{1,0:T(8,128)(2,1)S(1)} copy-done((bf16[8192,256]{1,0:T(8,128)(2,1)S(1)}, bf16[8192,256]{1,0:T(8,128)(2,1)}, u32[]{:S(2)}) %copy-start.4) | copy-done | bytes 4194328
  34.1 0.0 copy-start.2
  34.1 0.0 copy-start.5
  34.1 1.9 %shard_map.38.refs_5_ = f32[16,256]{1,0:T(8,128)S(1)} custom-call(s32[2]{0:T(128)S(1)} %pad_add_fusion.1.places, f32[16,8192]{1,0:T(8,128)S(1)} %collective-permute-done.3.refs_0_, bf16[8192,256]{1,0:T(8,128)(2,1)S(1)} %copy-done.4, bf16[8192,256]{1,0:T(8,128)(2,1)S(1)} %copy-done.1), custom_call_target="tpu_custom_call" | custom-call | bytes 16384 | tf_op jit(solution)/shard_map/pallas_call | solution.py:78
  35.9 1.1 %collective-permute-done.1.refs_0_ = f32[16,6144]{1,0:T(8,128)S(1)} collective-permute-done((f32[16,6144]{1,0:T(8,128)S(1)}, f32[16,6144]{1,0:T(8,128)S(1)}, u32[]{:S(2)}, u32[]{:S(2)}) %collective-permute-start.1) | collective-permute-done | bytes 393248 | tf_op jit(solution)/shard_map/ppermute | solution.py:157
  37.1 0.1 broadcast_in_dim.2.masks
  37.1 0.0 copy-done.2
  37.1 0.4 copy-done.5
  37.5 1.5 %shard_map.39 = (f32[16,256]{1,0:T(8,128)S(1)}, f32[16,256]{1,0:T(8,128)S(1)}, f32[16,256]{1,0:T(8,128)S(1)}, f32[16,256]{1,0:T(8,128)S(1)}) custom-call(s32[6]{0:T(128)S(1)} %stack.47.places, f32[16,6144]{1,0:T(8,128)S(1)} %collective-permute-done.1.refs_0_, bf16[8192,256]{1,0:T(8,128)(2,1)S(1)} %copy-done.5, bf16[8192,256]{1,0:T(8,128)(2,1)S(1)} %copy-done.2, ...), custom_call_target="tpu_custom_call" | custom-call | bytes 65536 | tf_op jit(solution)/shard_map/pallas_call | solution.py:78
  39.0 0.4 collective-permute-done.2.block
  39.4 0.4 shard_map.40
  39.8 0.8 %collective-permute-start.4 = (f32[16,256]{1,0:T(8,128)S(1)}, f32[16,256]{1,0:T(8,128)S(1)}, u32[]{:S(2)}, u32[]{:S(2)}) collective-permute-start(f32[16,256]{1,0:T(8,128)S(1)} %get-tuple-element.38), channel_id=1, source_target_pairs={{0,3},{1,2},{2,1},{3,0},{4,7},{5,6},{6,5},{7,4},{8,11},{9,10},{10,... | collective-permute-start | bytes 49160 | tf_op jit(solution)/shard_map/ppermute | solution.py:184
  40.5 0.9 %collective-permute-start.5 = (f32[16,256]{1,0:T(8,128)S(1)}, f32[16,256]{1,0:T(8,128)S(1)}, u32[]{:S(2)}, u32[]{:S(2)}) collective-permute-start(f32[16,256]{1,0:T(8,128)S(1)} %get-tuple-element.39), channel_id=1, source_target_pairs={{0,2},{1,3},{2,0},{3,1},{4,6},{5,7},{6,4},{7,5},{8,10},{9,11},{10,... | collective-permute-start | bytes 49160 | tf_op jit(solution)/shard_map/ppermute | solution.py:184
  41.4 0.3 collective-permute-start.6
  41.7 1.4 %collective-permute-done.4 = f32[16,256]{1,0:T(8,128)S(1)} collective-permute-done((f32[16,256]{1,0:T(8,128)S(1)}, f32[16,256]{1,0:T(8,128)S(1)}, u32[]{:S(2)}, u32[]{:S(2)}) %collective-permute-start.4) | collective-permute-done | bytes 16416 | tf_op jit(solution)/shard_map/ppermute | solution.py:184
  43.1 1.3 %collective-permute-done.5 = f32[16,256]{1,0:T(8,128)S(1)} collective-permute-done((f32[16,256]{1,0:T(8,128)S(1)}, f32[16,256]{1,0:T(8,128)S(1)}, u32[]{:S(2)}, u32[]{:S(2)}) %collective-permute-start.5) | collective-permute-done | bytes 16416 | tf_op jit(solution)/shard_map/ppermute | solution.py:184
  44.4 0.0 collective-permute-done.6
  44.4 0.7 %multiply_select_fusion = f32[16,256]{1,0:T(8,128)} fusion(f32[16,256]{1,0:T(8,128)S(1)} %collective-permute-done.6, f32[16,256]{1,0:T(8,128)S(1)} %collective-permute-done.5, f32[16,256]{1,0:T(8,128)S(1)} %get-tuple-element.37, f32[16,256]{1,0:T(8,128)S(1)} %collective-permute-done.4, s32[256]{0:T(256)S(1)} %iota_add_fusion.1, s32[16]{0:T(128)S(1)} %iota_add_fusion.2), kind=kLoop, calls=%fused_computation.5 | loop fusion | flops 40960 | bytes 83008 | tf_op jit(solution)/shard_map/jit(_where)/select_n | solution.py:191
  (6 shorter events, 0.1 us)
Async XLA Ops:
  0.0 16.7 %collective-permute-start = (f32[16,8192]{1,0:T(8,128)}, f32[16,8192]{1,0:T(8,128)S(1)}, u32[]{:S(2)}, u32[]{:S(2)}) collective-permute-start(f32[16,8192]{1,0:T(8,128)} %refs_0_), channel_id=1, source_target_pairs={{0,8},{8,12},{12,4},{4,0},{1,9},{9,13},{13,5},{5,1},{2,10},{10,14}... | collective-permute-start | bytes 1572872 | tf_op jit(solution)/shard_map/ppermute | solution.py:143
  4.7 8.0 %copy-start.6 = (f32[16,8192]{1,0:T(8,128)S(1)}, f32[16,8192]{1,0:T(8,128)}, u32[]{:S(2)}) copy-start(f32[16,8192]{1,0:T(8,128)} %refs_0_) | copy-start | bytes 1572868
  12.7 17.0 %collective-permute-start.3 = (f32[16,8192]{1,0:T(8,128)S(1)}, f32[16,8192]{1,0:T(8,128)S(1)}, u32[]{:S(2)}, u32[]{:S(2)}) collective-permute-start(f32[16,8192]{1,0:T(8,128)S(1)} %copy-done.6), channel_id=1, source_target_pairs={{8,0},{12,8},{4,12},{0,4},{9,1},{13,9},{5,13},{1,5},{10,2},{14,10}... | collective-permute-start | bytes 1572872 | tf_op jit(solution)/shard_map/ppermute | solution.py:154
  16.7 20.3 %collective-permute-start.1 = (f32[16,6144]{1,0:T(8,128)S(1)}, f32[16,6144]{1,0:T(8,128)S(1)}, u32[]{:S(2)}, u32[]{:S(2)}) collective-permute-start(f32[16,6144]{1,0:T(8,128)S(1)} %slice.8), channel_id=1, source_target_pairs={{0,8},{8,12},{12,4},{4,0},{1,9},{9,13},{13,5},{5,1},{2,10},{10,14}... | collective-permute-start | bytes 1179656 | tf_op jit(solution)/shard_map/ppermute | solution.py:157
  20.1 2.2 %copy-start = (bf16[8192,256]{1,0:T(8,128)(2,1)S(1)}, bf16[8192,256]{1,0:T(8,128)(2,1)}, u32[]{:S(2)}) copy-start(bf16[8192,256]{1,0:T(8,128)(2,1)} %get-tuple-element.26.refs_3_.refs_2_.low) | copy-start | bytes 12582916
  22.3 2.2 %copy-start.3 = (bf16[8192,256]{1,0:T(8,128)(2,1)S(1)}, bf16[8192,256]{1,0:T(8,128)(2,1)}, u32[]{:S(2)}) copy-start(bf16[8192,256]{1,0:T(8,128)(2,1)} %get-tuple-element.25.refs_2_.refs_1_.high) | copy-start | bytes 12582916
  26.6 12.7 %collective-permute-start.2 = (f32[16,2048]{1,0:T(8,128)S(1)}, f32[16,2048]{1,0:T(8,128)S(1)}, u32[]{:S(2)}, u32[]{:S(2)}) collective-permute-start(f32[16,2048]{1,0:T(8,128)S(1)} %slice.7), channel_id=1, source_target_pairs={{0,8},{8,12},{12,4},{4,0},{1,9},{9,13},{13,5},{5,1},{2,10},{10,14}... | collective-permute-start | bytes 393224 | tf_op jit(solution)/shard_map/ppermute | solution.py:161
  29.7 2.2 %copy-start.1 = (bf16[8192,256]{1,0:T(8,128)(2,1)S(1)}, bf16[8192,256]{1,0:T(8,128)(2,1)}, u32[]{:S(2)}) copy-start(bf16[8192,256]{1,0:T(8,128)(2,1)} %get-tuple-element.26.refs_3_.refs_2_.low) | copy-start | bytes 12582916
  31.9 2.2 %copy-start.4 = (bf16[8192,256]{1,0:T(8,128)(2,1)S(1)}, bf16[8192,256]{1,0:T(8,128)(2,1)}, u32[]{:S(2)}) copy-start(bf16[8192,256]{1,0:T(8,128)(2,1)} %get-tuple-element.25.refs_2_.refs_1_.high) | copy-start | bytes 12582916
  34.1 3.1 %copy-start.2 = (bf16[8192,256]{1,0:T(8,128)(2,1)S(1)}, bf16[8192,256]{1,0:T(8,128)(2,1)}, u32[]{:S(2)}) copy-start(bf16[8192,256]{1,0:T(8,128)(2,1)} %get-tuple-element.26.refs_3_.refs_2_.low) | copy-start | bytes 12582916
  34.1 3.5 %copy-start.5 = (bf16[8192,256]{1,0:T(8,128)(2,1)S(1)}, bf16[8192,256]{1,0:T(8,128)(2,1)}, u32[]{:S(2)}) copy-start(bf16[8192,256]{1,0:T(8,128)(2,1)} %get-tuple-element.25.refs_2_.refs_1_.high) | copy-start | bytes 12582916
  39.8 3.4 %collective-permute-start.4 = (f32[16,256]{1,0:T(8,128)S(1)}, f32[16,256]{1,0:T(8,128)S(1)}, u32[]{:S(2)}, u32[]{:S(2)}) collective-permute-start(f32[16,256]{1,0:T(8,128)S(1)} %get-tuple-element.38), channel_id=1, source_target_pairs={{0,3},{1,2},{2,1},{3,0},{4,7},{5,6},{6,5},{7,4},{8,11},{9,10},{10,... | collective-permute-start | bytes 49160 | tf_op jit(solution)/shard_map/ppermute | solution.py:184
  40.5 3.9 %collective-permute-start.5 = (f32[16,256]{1,0:T(8,128)S(1)}, f32[16,256]{1,0:T(8,128)S(1)}, u32[]{:S(2)}, u32[]{:S(2)}) collective-permute-start(f32[16,256]{1,0:T(8,128)S(1)} %get-tuple-element.39), channel_id=1, source_target_pairs={{0,2},{1,3},{2,0},{3,1},{4,6},{5,7},{6,4},{7,5},{8,10},{9,11},{10,... | collective-permute-start | bytes 49160 | tf_op jit(solution)/shard_map/ppermute | solution.py:184
  41.4 3.0 %collective-permute-start.6 = (f32[16,256]{1,0:T(8,128)S(1)}, f32[16,256]{1,0:T(8,128)S(1)}, u32[]{:S(2)}, u32[]{:S(2)}) collective-permute-start(f32[16,256]{1,0:T(8,128)S(1)} %get-tuple-element.40), channel_id=1, source_target_pairs={{0,1},{1,0},{2,3},{3,2},{4,5},{5,4},{6,7},{7,6},{8,9},{9,8},{10,11... | collective-permute-start | bytes 49160 | tf_op jit(solution)/shard_map/ppermute | solution.py:184

commit v14 on v13

--- a/solution.py
+++ b/solution.py
@@ -129,16 +129,17 @@
         arrays = [*blocks, *weights, *parts]
         return call(kernel, count, (rows, tile_width), [places], arrays, 4 + len(parts) // 4)
 
-    ring = list(range(0, team_count, 2)) + list(range(1, team_count, 2))[::-1]
+    ring = [0] + list(range(1, team_count, 2)) + list(range(2, team_count, 2))[::-1]
     onward = [(ring[k], ring[(k + 1) % team_count]) for k in range(team_count)]
     backward = [(to, source) for source, to in onward]
-    rank = team_index // 2
-    place = jnp.where(team_index % 2 == 0, rank, team_count - 1 - rank)
+    down = (team_count - team_index // 2) % team_count
+    place = jnp.where(team_index % 2 == 1, (team_index + 1) // 2, down)
 
     def device_at(spot):
         spot = spot % team_count
-        up = 2 * spot
-        return jnp.where(up < team_count, up, 2 * team_count - 1 - up)
+        up = 2 * spot - 1
+        down = 2 * (team_count - spot) % (2 * team_count)
+        return jnp.where((up > 0) & (up < team_count), up, down)
 
     first = lax.ppermute(omega_rows, "team", onward)
     own, *weights = lax.optimization_barrier((omega_rows, *weights))

time: 45.4 us -> 54.1 us (1.19)
  starting transfers between devices: 9.45 us -> 22.4 us
  waiting for transfers between devices: 10.9 us -> 5.51 us
  local copies, waits for them, and re-layouts: 9.34 us -> 10.5 us
    ppermute x1, starting transfers between devices: 3.33 us -> 13.1 us  [per_device(): last_left = lax.ppermute(last_held[:, :cut], 'team', onward)]
    ppermute x1, starting transfers between devices: 0.16 us -> 3.33 us  [per_device(): last_right = lax.ppermute(last_held[:, cut:], 'team', onward)]
    ppermute x1, waiting for transfers between devices: 2.72 us -> 0.01 us  [per_device(): held = lax.ppermute(held, 'team', backward)]
    ppermute x1, waiting for transfers between devices: 1.15 us -> 0.01 us  [per_device(): last_left = lax.ppermute(last_held[:, :cut], 'team', onward)]
    unnamed x14, local copies, waits for them, and re-layouts: 9.15 us -> 10.3 us
    ppermute x1, starting transfers between devices: 0.01 us -> 1.02 us  [per_device(): held = lax.ppermute(held, 'team', backward)]
    ppermute x1, starting transfers between devices: 4.04 us -> 3.02 us  [per_device(): first = lax.ppermute(omega_rows, 'team', onward)]
    ppermute x3, waiting for transfers between devices: 2.69 us -> 1.95 us  [per_device(): terms.append(lax.ppermute(shares[flip], 'rep', pairs))]
  transfers between devices with their start and end apart: 7 -> 7, of which waited for: 6 -> 3; matrix products, arithmetic and copies ran while one was open for 19% -> 16% of each run, Pallas kernels for 12% -> 10%
where the time goes in v14:
time: 54.1 us; the launch traced here: 53.8 us
  starting transfers between devices  22.4 us (41%)
  local copies, waits for them, and re-layouts  10.5 us (19%)
  other arithmetic  8.84 us (16%)
  Pallas kernels  5.84 us (11%)
  waiting for transfers between devices  5.51 us (10%)
  between operations  0.76 us (1%)
    ppermute x1, starting transfers between devices, per_device(): last_left = lax.ppermute(last_held[:, :cut], 'team', onward)  13.1 us
    unnamed x14, local copies, waits for them, and re-layouts  10.3 us
    convert_element_type x1, other arithmetic, halves(): return (high.astype(jnp.bfloat16), (array - high).astype(jnp.bfloat16))  7.98 us
    pallas_call x4, Pallas kernels, call(): pl.pallas_call(kernel, out_shape=[jax.ShapeDtypeStruct(shape, jnp.float32...  5.84 us
    ppermute x1, waiting for transfers between devices, per_device(): first = lax.ppermute(omega_rows, 'team', onward)  3.55 us
    ppermute x1, starting transfers between devices, per_device(): last_right = lax.ppermute(last_held[:, cut:], 'team', onward)  3.33 us
    ppermute x1, starting transfers between devices, per_device(): first = lax.ppermute(omega_rows, 'team', onward)  3.02 us
    ppermute x3, waiting for transfers between devices, per_device(): terms.append(lax.ppermute(shares[flip], 'rep', pairs))  1.95 us
  transfers between devices with their start and end apart: 7, of which 3 were waited for; matrix products, arithmetic and copies ran while one was open for 16% of the time, Pallas kernels for 10%

profile of v14, /device:TPU:0, one launch (start us, length us, event | category | flops | bytes accessed | tf_op | source)
XLA Modules:
  0.0 53.8 jit_solution(12070103040907815219)
XLA Ops:
  0.0 3.0 %collective-permute-start = (f32[16,8192]{1,0:T(8,128)}, f32[16,8192]{1,0:T(8,128)S(1)}, u32[]{:S(2)}, u32[]{:S(2)}) collective-permute-start(f32[16,8192]{1,0:T(8,128)} %refs_0_), channel_id=1, source_target_pairs={{0,4},{4,12},{12,8},{8,0},{1,5},{5,13},{13,9},{9,1},{2,6},{6,14},{... | collective-permute-start | bytes 1572872 | tf_op jit(solution)/shard_map/ppermute | solution.py:144
  3.7 0.0 copy-start.6
  3.7 8.0 %subtract_convert_fusion = (bf16[8192,256]{1,0:T(8,128)(2,1)}, bf16[8192,256]{1,0:T(8,128)(2,1)}) fusion(f32[8192,256]{1,0:T(8,128)} %param.4, s32[256]{0:T(256)S(1)} %iota_add_fusion.1, s32[8192]{0:T(1024)S(1)} %iota_add_fusion), kind=kLoop, calls=%fused_computation | loop fusion | flops 18874368 | bytes 16811008 | tf_op jit(solution)/shard_map/convert_element_type | solution.py:17
  11.7 0.0 copy-done.6
  11.7 1.0 %collective-permute-start.3 = (f32[16,8192]{1,0:T(8,128)S(1)}, f32[16,8192]{1,0:T(8,128)S(1)}, u32[]{:S(2)}, u32[]{:S(2)}) collective-permute-start(f32[16,8192]{1,0:T(8,128)S(1)} %copy-done.6), channel_id=1, source_target_pairs={{4,0},{12,4},{8,12},{0,8},{5,1},{13,5},{9,13},{1,9},{6,2},{14,6},{... | collective-permute-start | bytes 1572872 | tf_op jit(solution)/shard_map/ppermute | solution.py:155
  12.7 3.6 %collective-permute-done.refs_1_ = f32[16,8192]{1,0:T(8,128)S(1)} collective-permute-done((f32[16,8192]{1,0:T(8,128)}, f32[16,8192]{1,0:T(8,128)S(1)}, u32[]{:S(2)}, u32[]{:S(2)}) %collective-permute-start) | collective-permute-done | bytes 524320 | tf_op jit(solution)/shard_map/ppermute | solution.py:144
  16.3 13.1 %collective-permute-start.1 = (f32[16,6144]{1,0:T(8,128)S(1)}, f32[16,6144]{1,0:T(8,128)S(1)}, u32[]{:S(2)}, u32[]{:S(2)}) collective-permute-start(f32[16,6144]{1,0:T(8,128)S(1)} %slice.8), channel_id=1, source_target_pairs={{0,4},{4,12},{12,8},{8,0},{1,5},{5,13},{13,9},{9,1},{2,6},{6,14},{... | collective-permute-start | bytes 1179656 | tf_op jit(solution)/shard_map/ppermute | solution.py:158
  29.4 0.1 pad_add_fusion.places
  29.5 0.0 copy-start
  29.5 2.2 %copy-done = bf16[8192,256]{1,0:T(8,128)(2,1)S(1)} copy-done((bf16[8192,256]{1,0:T(8,128)(2,1)S(1)}, bf16[8192,256]{1,0:T(8,128)(2,1)}, u32[]{:S(2)}) %copy-start) | copy-done | bytes 4194328
  31.7 0.0 copy-start.3
  31.7 2.2 %copy-done.3 = bf16[8192,256]{1,0:T(8,128)(2,1)S(1)} copy-done((bf16[8192,256]{1,0:T(8,128)(2,1)S(1)}, bf16[8192,256]{1,0:T(8,128)(2,1)}, u32[]{:S(2)}) %copy-start.3) | copy-done | bytes 4194328
  33.8 2.1 %shard_map.37 = (f32[16,256]{1,0:T(8,128)S(1)}, f32[16,256]{1,0:T(8,128)S(1)}) custom-call(s32[3]{0:T(128)S(1)} %pad_add_fusion.places, f32[16,8192]{1,0:T(8,128)S(1)} %copy-done.6, f32[16,8192]{1,0:T(8,128)S(1)} %collective-permute-done.refs_1_, bf16[8192,256]{1,0:T(8,128)(2,1)S(1)} %copy-done.3, bf16[8192,256]{1,0:T(8,128)(2,1)S(1)} %copy-done), custom_call_target="tpu_custom_call" | custom-call | bytes 32768 | tf_op jit(solution)/shard_map/pallas_call | solution.py:78
  36.0 3.3 %collective-permute-start.2 = (f32[16,2048]{1,0:T(8,128)S(1)}, f32[16,2048]{1,0:T(8,128)S(1)}, u32[]{:S(2)}, u32[]{:S(2)}) collective-permute-start(f32[16,2048]{1,0:T(8,128)S(1)} %slice.7), channel_id=1, source_target_pairs={{0,4},{4,12},{12,8},{8,0},{1,5},{5,13},{13,9},{9,1},{2,6},{6,14},{... | collective-permute-start | bytes 393224 | tf_op jit(solution)/shard_map/ppermute | solution.py:162
  39.3 0.1 pad_add_fusion.1.places
  39.4 0.1 stack.47.places
  39.5 0.0 collective-permute-done.3.refs_0_
  39.5 0.0 copy-start.1
  39.5 2.2 %copy-done.1 = bf16[8192,256]{1,0:T(8,128)(2,1)S(1)} copy-done((bf16[8192,256]{1,0:T(8,128)(2,1)S(1)}, bf16[8192,256]{1,0:T(8,128)(2,1)}, u32[]{:S(2)}) %copy-start.1) | copy-done | bytes 4194328
  41.7 0.0 copy-start.4
  41.7 2.2 %copy-done.4 = bf16[8192,256]{1,0:T(8,128)(2,1)S(1)} copy-done((bf16[8192,256]{1,0:T(8,128)(2,1)S(1)}, bf16[8192,256]{1,0:T(8,128)(2,1)}, u32[]{:S(2)}) %copy-start.4) | copy-done | bytes 4194328
  43.9 0.0 copy-start.2
  43.9 0.0 copy-start.5
  43.9 1.9 %shard_map.38.refs_5_ = f32[16,256]{1,0:T(8,128)S(1)} custom-call(s32[2]{0:T(128)S(1)} %pad_add_fusion.1.places, f32[16,8192]{1,0:T(8,128)S(1)} %collective-permute-done.3.refs_0_, bf16[8192,256]{1,0:T(8,128)(2,1)S(1)} %copy-done.4, bf16[8192,256]{1,0:T(8,128)(2,1)S(1)} %copy-done.1), custom_call_target="tpu_custom_call" | custom-call | bytes 16384 | tf_op jit(solution)/shard_map/pallas_call | solution.py:78
  45.7 0.0 collective-permute-done.1.refs_0_
  45.7 0.1 broadcast_in_dim.2.masks
  45.8 0.2 copy-done.2
  46.0 1.3 %copy-done.5 = bf16[8192,256]{1,0:T(8,128)(2,1)S(1)} copy-done((bf16[8192,256]{1,0:T(8,128)(2,1)S(1)}, bf16[8192,256]{1,0:T(8,128)(2,1)}, u32[]{:S(2)}) %copy-start.5) | copy-done | bytes 4194328
  47.3 1.5 %shard_map.39 = (f32[16,256]{1,0:T(8,128)S(1)}, f32[16,256]{1,0:T(8,128)S(1)}, f32[16,256]{1,0:T(8,128)S(1)}, f32[16,256]{1,0:T(8,128)S(1)}) custom-call(s32[6]{0:T(128)S(1)} %stack.47.places, f32[16,6144]{1,0:T(8,128)S(1)} %collective-permute-done.1.refs_0_, bf16[8192,256]{1,0:T(8,128)(2,1)S(1)} %copy-done.5, bf16[8192,256]{1,0:T(8,128)(2,1)S(1)} %copy-done.2, ...), custom_call_target="tpu_custom_call" | custom-call | bytes 65536 | tf_op jit(solution)/shard_map/pallas_call | solution.py:78
  48.8 0.0 collective-permute-done.2.block
  48.8 0.4 shard_map.40
  49.2 0.1 collective-permute-start.4
  49.3 1.6 %collective-permute-start.5 = (f32[16,256]{1,0:T(8,128)S(1)}, f32[16,256]{1,0:T(8,128)S(1)}, u32[]{:S(2)}, u32[]{:S(2)}) collective-permute-start(f32[16,256]{1,0:T(8,128)S(1)} %get-tuple-element.39), channel_id=1, source_target_pairs={{0,2},{1,3},{2,0},{3,1},{4,6},{5,7},{6,4},{7,5},{8,10},{9,11},{10,... | collective-permute-start | bytes 49160 | tf_op jit(solution)/shard_map/ppermute | solution.py:185
  50.9 0.3 collective-permute-start.6
  51.2 1.4 %collective-permute-done.4 = f32[16,256]{1,0:T(8,128)S(1)} collective-permute-done((f32[16,256]{1,0:T(8,128)S(1)}, f32[16,256]{1,0:T(8,128)S(1)}, u32[]{:S(2)}, u32[]{:S(2)}) %collective-permute-start.4) | collective-permute-done | bytes 16416 | tf_op jit(solution)/shard_map/ppermute | solution.py:185
  52.6 0.5 collective-permute-done.5
  53.1 0.0 collective-permute-done.6
  53.1 0.7 %multiply_select_fusion = f32[16,256]{1,0:T(8,128)} fusion(f32[16,256]{1,0:T(8,128)S(1)} %collective-permute-done.6, f32[16,256]{1,0:T(8,128)S(1)} %collective-permute-done.5, f32[16,256]{1,0:T(8,128)S(1)} %get-tuple-element.37, f32[16,256]{1,0:T(8,128)S(1)} %collective-permute-done.4, s32[256]{0:T(256)S(1)} %iota_add_fusion.1, s32[16]{0:T(128)S(1)} %iota_add_fusion.2), kind=kLoop, calls=%fused_computation.5 | loop fusion | flops 40960 | bytes 83008 | tf_op jit(solution)/shard_map/jit(_where)/select_n | solution.py:192
  (6 shorter events, 0.1 us)
Async XLA Ops:
  0.0 16.3 %collective-permute-start = (f32[16,8192]{1,0:T(8,128)}, f32[16,8192]{1,0:T(8,128)S(1)}, u32[]{:S(2)}, u32[]{:S(2)}) collective-permute-start(f32[16,8192]{1,0:T(8,128)} %refs_0_), channel_id=1, source_target_pairs={{0,4},{4,12},{12,8},{8,0},{1,5},{5,13},{13,9},{9,1},{2,6},{6,14},{... | collective-permute-start | bytes 1572872 | tf_op jit(solution)/shard_map/ppermute | solution.py:144
  3.7 8.0 %copy-start.6 = (f32[16,8192]{1,0:T(8,128)S(1)}, f32[16,8192]{1,0:T(8,128)}, u32[]{:S(2)}) copy-start(f32[16,8192]{1,0:T(8,128)} %refs_0_) | copy-start | bytes 1572868
  11.7 27.8 %collective-permute-start.3 = (f32[16,8192]{1,0:T(8,128)S(1)}, f32[16,8192]{1,0:T(8,128)S(1)}, u32[]{:S(2)}, u32[]{:S(2)}) collective-permute-start(f32[16,8192]{1,0:T(8,128)S(1)} %copy-done.6), channel_id=1, source_target_pairs={{4,0},{12,4},{8,12},{0,8},{5,1},{13,5},{9,13},{1,9},{6,2},{14,6},{... | collective-permute-start | bytes 1572872 | tf_op jit(solution)/shard_map/ppermute | solution.py:155
  16.3 29.4 %collective-permute-start.1 = (f32[16,6144]{1,0:T(8,128)S(1)}, f32[16,6144]{1,0:T(8,128)S(1)}, u32[]{:S(2)}, u32[]{:S(2)}) collective-permute-start(f32[16,6144]{1,0:T(8,128)S(1)} %slice.8), channel_id=1, source_target_pairs={{0,4},{4,12},{12,8},{8,0},{1,5},{5,13},{13,9},{9,1},{2,6},{6,14},{... | collective-permute-start | bytes 1179656 | tf_op jit(solution)/shard_map/ppermute | solution.py:158
  29.5 2.2 %copy-start = (bf16[8192,256]{1,0:T(8,128)(2,1)S(1)}, bf16[8192,256]{1,0:T(8,128)(2,1)}, u32[]{:S(2)}) copy-start(bf16[8192,256]{1,0:T(8,128)(2,1)} %get-tuple-element.26.refs_3_.refs_2_.low) | copy-start | bytes 12582916
  31.7 2.2 %copy-start.3 = (bf16[8192,256]{1,0:T(8,128)(2,1)S(1)}, bf16[8192,256]{1,0:T(8,128)(2,1)}, u32[]{:S(2)}) copy-start(bf16[8192,256]{1,0:T(8,128)(2,1)} %get-tuple-element.25.refs_2_.refs_1_.high) | copy-start | bytes 12582916
  36.0 12.9 %collective-permute-start.2 = (f32[16,2048]{1,0:T(8,128)S(1)}, f32[16,2048]{1,0:T(8,128)S(1)}, u32[]{:S(2)}, u32[]{:S(2)}) collective-permute-start(f32[16,2048]{1,0:T(8,128)S(1)} %slice.7), channel_id=1, source_target_pairs={{0,4},{4,12},{12,8},{8,0},{1,5},{5,13},{13,9},{9,1},{2,6},{6,14},{... | collective-permute-start | bytes 393224 | tf_op jit(solution)/shard_map/ppermute | solution.py:162
  39.5 2.2 %copy-start.1 = (bf16[8192,256]{1,0:T(8,128)(2,1)S(1)}, bf16[8192,256]{1,0:T(8,128)(2,1)}, u32[]{:S(2)}) copy-start(bf16[8192,256]{1,0:T(8,128)(2,1)} %get-tuple-element.26.refs_3_.refs_2_.low) | copy-start | bytes 12582916
  41.7 2.2 %copy-start.4 = (bf16[8192,256]{1,0:T(8,128)(2,1)S(1)}, bf16[8192,256]{1,0:T(8,128)(2,1)}, u32[]{:S(2)}) copy-start(bf16[8192,256]{1,0:T(8,128)(2,1)} %get-tuple-element.25.refs_2_.refs_1_.high) | copy-start | bytes 12582916
  43.9 2.2 %copy-start.2 = (bf16[8192,256]{1,0:T(8,128)(2,1)S(1)}, bf16[8192,256]{1,0:T(8,128)(2,1)}, u32[]{:S(2)}) copy-start(bf16[8192,256]{1,0:T(8,128)(2,1)} %get-tuple-element.26.refs_3_.refs_2_.low) | copy-start | bytes 12582916
  43.9 3.5 %copy-start.5 = (bf16[8192,256]{1,0:T(8,128)(2,1)S(1)}, bf16[8192,256]{1,0:T(8,128)(2,1)}, u32[]{:S(2)}) copy-start(bf16[8192,256]{1,0:T(8,128)(2,1)} %get-tuple-element.25.refs_2_.refs_1_.high) | copy-start | bytes 12582916
  49.2 3.4 %collective-permute-start.4 = (f32[16,256]{1,0:T(8,128)S(1)}, f32[16,256]{1,0:T(8,128)S(1)}, u32[]{:S(2)}, u32[]{:S(2)}) collective-permute-start(f32[16,256]{1,0:T(8,128)S(1)} %get-tuple-element.38), channel_id=1, source_target_pairs={{0,3},{1,2},{2,1},{3,0},{4,7},{5,6},{6,5},{7,4},{8,11},{9,10},{10,... | collective-permute-start | bytes 49160 | tf_op jit(solution)/shard_map/ppermute | solution.py:185
  49.3 3.8 %collective-permute-start.5 = (f32[16,256]{1,0:T(8,128)S(1)}, f32[16,256]{1,0:T(8,128)S(1)}, u32[]{:S(2)}, u32[]{:S(2)}) collective-permute-start(f32[16,256]{1,0:T(8,128)S(1)} %get-tuple-element.39), channel_id=1, source_target_pairs={{0,2},{1,3},{2,0},{3,1},{4,6},{5,7},{6,4},{7,5},{8,10},{9,11},{10,... | collective-permute-start | bytes 49160 | tf_op jit(solution)/shard_map/ppermute | solution.py:185
  50.9 2.3 %collective-permute-start.6 = (f32[16,256]{1,0:T(8,128)S(1)}, f32[16,256]{1,0:T(8,128)S(1)}, u32[]{:S(2)}, u32[]{:S(2)}) collective-permute-start(f32[16,256]{1,0:T(8,128)S(1)} %get-tuple-element.40), channel_id=1, source_target_pairs={{0,1},{1,0},{2,3},{3,2},{4,5},{5,4},{6,7},{7,6},{8,9},{9,8},{10,11... | collective-permute-start | bytes 49160 | tf_op jit(solution)/shard_map/ppermute | solution.py:185

commit v15 on v13

--- a/solution.py
+++ b/solution.py
@@ -1,4 +1,5 @@
 import functools
+import math
 
 import jax
 import jax.numpy as jnp
@@ -12,9 +13,52 @@
 largest_bf16 = 3.3895313892515355e38
 
 
-def halves(array):
-    high = lax.reduce_precision(jnp.clip(array, -largest_bf16, largest_bf16), 8, 7)
-    return high.astype(jnp.bfloat16), (array - high).astype(jnp.bfloat16)
+def weights_kernel(shift, covariance, high, low, held, arrived):
+    depth, columns = covariance.shape
+    step = held.shape[1]
+    pieces = depth // step
+
+    def copy(piece):
+        return pltpu.make_async_copy(
+            covariance.at[pl.ds(piece * step, step)], held.at[piece % 4], arrived.at[piece % 4]
+        )
+
+    for piece in range(min(3, pieces)):
+        copy(piece).start()
+    ahead = lax.broadcasted_iota(jnp.int32, (step, columns), 0)
+    ahead -= lax.broadcasted_iota(jnp.int32, (step, columns), 1)
+    for piece in range(pieces):
+        if piece + 3 < pieces:
+            copy(piece + 3).start()
+        copy(piece).wait()
+        scaled = -step_size * held[piece % 4]
+        values = jnp.where(ahead == shift[0] - piece * step, scaled + 1.0, scaled)
+        upper = values.astype(jnp.bfloat16)
+        rows = slice(piece * step, (piece + 1) * step)
+        high[rows] = upper
+        low[rows] = (values - upper.astype(jnp.float32)).astype(jnp.bfloat16)
+
+
+def weights_of(covariance, shift):
+    depth, columns = covariance.shape
+    step = math.gcd(depth, 512)
+    return pl.pallas_call(
+        weights_kernel,
+        out_shape=[pltpu.VMEM((depth, columns), jnp.bfloat16)] * 2,
+        in_specs=[
+            pl.BlockSpec(memory_space=pltpu.SMEM),
+            pl.BlockSpec(memory_space=pltpu.HBM),
+        ],
+        out_specs=[pl.BlockSpec(memory_space=pltpu.VMEM)] * 2,
+        scratch_shapes=[
+            pltpu.VMEM((4, step, columns), jnp.float32),
+            pltpu.SemaphoreType.DMA((4,)),
+        ],
+        compiler_params=pltpu.CompilerParams(vmem_limit_bytes=8 * 1024 * 1024),
+        cost_estimate=pl.CostEstimate(
+            flops=0, bytes_accessed=covariance.size * 4, transcendentals=0
+        ),
+    )(shift, pltpu.with_memory_space_constraint(covariance, pltpu.HBM))
 
 
 def products(blocks, high, low, first_k=0):
@@ -108,10 +152,8 @@
     assert all_rows <= part_width and part_width % tile_width == 0
     assert rows_share % block_rows == 0 and rep_count & (rep_count - 1) == 0 and rep_count > 1
 
-    k_ids = rep_index * part_width + jnp.arange(part_width, dtype=jnp.int32)
-    c_ids = offset + jnp.arange(tile_width, dtype=jnp.int32)
-    chosen = (k_ids[:, None] == c_ids[None, :]).astype(jnp.float32)
-    weights = halves(chosen - step_size * covariance_columns)
+    shift = jnp.reshape(offset - rep_index * part_width, (1,)).astype(jnp.int32)
+    weights = weights_of(covariance_columns, shift)
 
     cut = part_width // 4 * 3
     assert all_rows <= cut and cut % tile_width == 0

time: 45.4 us -> 45.9 us (1.011)
  other arithmetic: 8.84 us -> 0.85 us
  Pallas kernels: 5.83 us -> 11.1 us
  local copies, waits for them, and re-layouts: 9.34 us -> 13.6 us
  waiting for transfers between devices: 10.9 us -> 9.92 us
    convert_element_type x1 -> x0, other arithmetic: 7.98 us -> none  [halves(): return (high.astype(jnp.bfloat16), (array - high).astype(jnp.bfloat16))]
    pallas_call x0 -> x1, Pallas kernels: none -> 5.34 us  [weights_of(): pl.pallas_call(weights_kernel, out_shape=[pltpu.VMEM((depth, columns), jn...]
    unnamed x14 -> x18, local copies, waits for them, and re-layouts: 9.15 us -> 13.4 us
    ppermute x1, waiting for transfers between devices: 3.95 us -> 2.69 us  [per_device(): first = lax.ppermute(omega_rows, 'team', onward)]
  transfers between devices with their start and end apart: 7 -> 7, of which waited for: 6 -> 6; matrix products, arithmetic and copies ran while one was open for 19% -> 1% of each run, Pallas kernels for 12% -> 24%
where the time goes in v15:
time: 45.9 us; the launch traced here: 45.6 us
  local copies, waits for them, and re-layouts  13.6 us (30%)
  Pallas kernels  11.1 us (24%)
  waiting for transfers between devices  9.92 us (22%)
  starting transfers between devices  9.38 us (20%)
  other arithmetic  0.85 us (2%)
  between operations  0.73 us (2%)
    unnamed x18, local copies, waits for them, and re-layouts  13.4 us
    pallas_call x4, Pallas kernels, call(): pl.pallas_call(kernel, out_shape=[jax.ShapeDtypeStruct(shape, jnp.float32...  5.8 us
    pallas_call x1, Pallas kernels, weights_of(): pl.pallas_call(weights_kernel, out_shape=[pltpu.VMEM((depth, columns), jn...  5.34 us
    ppermute x1, starting transfers between devices, per_device(): first = lax.ppermute(omega_rows, 'team', onward)  4.04 us
    ppermute x1, starting transfers between devices, per_device(): last_left = lax.ppermute(last_held[:, :cut], 'team', onward)  3.33 us
    ppermute x1, waiting for transfers between devices, per_device(): held = lax.ppermute(held, 'team', backward)  3.05 us
    ppermute x3, waiting for transfers between devices, per_device(): terms.append(lax.ppermute(shares[flip], 'rep', pairs))  2.85 us
    ppermute x1, waiting for transfers between devices, per_device(): first = lax.ppermute(omega_rows, 'team', onward)  2.69 us
  transfers between devices with their start and end apart: 7, of which 6 were waited for; matrix products, arithmetic and copies ran while one was open for 1% of the time, Pallas kernels for 24%

profile of v15, /device:TPU:0, one launch (start us, length us, event | category | flops | bytes accessed | tf_op | source)
XLA Modules:
  0.0 45.6 jit_solution(10391784316220682850)
XLA Ops:
  0.0 4.0 %collective-permute-start = (f32[16,8192]{1,0:T(8,128)}, f32[16,8192]{1,0:T(8,128)S(1)}, u32[]{:S(2)}, u32[]{:S(2)}) collective-permute-start(f32[16,8192]{1,0:T(8,128)} %refs_0_), channel_id=1, source_target_pairs={{0,8},{8,12},{12,4},{4,0},{1,9},{9,13},{13,5},{5,1},{2,10},{10,14}... | collective-permute-start | bytes 1572872 | tf_op jit(solution)/shard_map/ppermute | solution.py:185
  4.7 0.0 copy-start.8
  4.7 5.3 %shard_map.37 = (bf16[8192,256]{1,0:T(8,128)(2,1)S(1)}, bf16[8192,256]{1,0:T(8,128)(2,1)S(1)}) custom-call(s32[1]{0:T(128)} %bitcast.4.shift, f32[8192,256]{1,0:T(8,128)} %covariance.1), custom_call_target="tpu_custom_call" | custom-call | bytes 8388608 | tf_op jit(solution)/shard_map/pallas_call | solution.py:45
  10.0 0.0 copy-start
  10.1 1.9 %copy-done = bf16[8192,256]{1,0:T(8,128)(2,1)} copy-done((bf16[8192,256]{1,0:T(8,128)(2,1)}, bf16[8192,256]{1,0:T(8,128)(2,1)S(1)}, u32[]{:S(2)}) %copy-start) | copy-done | bytes 4194328
  12.0 0.0 copy-start.4
  12.0 2.0 %copy-done.4 = bf16[8192,256]{1,0:T(8,128)(2,1)} copy-done((bf16[8192,256]{1,0:T(8,128)(2,1)}, bf16[8192,256]{1,0:T(8,128)(2,1)S(1)}, u32[]{:S(2)}) %copy-start.4) | copy-done | bytes 4194328
  14.0 0.0 copy-done.8
  14.0 0.0 collective-permute-start.3
  14.0 2.7 %collective-permute-done.refs_1_ = f32[16,8192]{1,0:T(8,128)S(1)} collective-permute-done((f32[16,8192]{1,0:T(8,128)}, f32[16,8192]{1,0:T(8,128)S(1)}, u32[]{:S(2)}, u32[]{:S(2)}) %collective-permute-start) | collective-permute-done | bytes 524320 | tf_op jit(solution)/shard_map/ppermute | solution.py:185
  16.7 3.3 %collective-permute-start.1 = (f32[16,6144]{1,0:T(8,128)S(1)}, f32[16,6144]{1,0:T(8,128)S(1)}, u32[]{:S(2)}, u32[]{:S(2)}) collective-permute-start(f32[16,6144]{1,0:T(8,128)S(1)} %slice.8), channel_id=1, source_target_pairs={{0,8},{8,12},{12,4},{4,0},{1,9},{9,13},{13,5},{5,1},{2,10},{10,14}... | collective-permute-start | bytes 1179656 | tf_op jit(solution)/shard_map/ppermute | solution.py:199
  20.0 0.1 pad_add_fusion.places
  20.1 0.0 copy-start.1
  20.1 2.2 %copy-done.1 = bf16[8192,256]{1,0:T(8,128)(2,1)S(1)} copy-done((bf16[8192,256]{1,0:T(8,128)(2,1)S(1)}, bf16[8192,256]{1,0:T(8,128)(2,1)}, u32[]{:S(2)}) %copy-start.1) | copy-done | bytes 4194328
  22.3 0.0 copy-start.5
  22.3 2.2 %copy-done.5 = bf16[8192,256]{1,0:T(8,128)(2,1)S(1)} copy-done((bf16[8192,256]{1,0:T(8,128)(2,1)S(1)}, bf16[8192,256]{1,0:T(8,128)(2,1)}, u32[]{:S(2)}) %copy-start.5) | copy-done | bytes 4194328
  24.5 2.1 %shard_map.38 = (f32[16,256]{1,0:T(8,128)S(1)}, f32[16,256]{1,0:T(8,128)S(1)}) custom-call(s32[3]{0:T(128)S(1)} %pad_add_fusion.places, f32[16,8192]{1,0:T(8,128)S(1)} %copy-done.8, f32[16,8192]{1,0:T(8,128)S(1)} %collective-permute-done.refs_1_, bf16[8192,256]{1,0:T(8,128)(2,1)S(1)} %copy-done.1, bf16[8192,256]{1,0:T(8,128)(2,1)S(1)} %copy-done.5), custom_call_target="tpu_custom_call" | custom-call | bytes 32768 | tf_op jit(solution)/shard_map/pallas_call | solution.py:122
  26.6 0.1 collective-permute-start.2
  26.7 0.1 pad_add_fusion.1.places
  26.8 0.1 stack.47.places
  26.9 3.1 %collective-permute-done.3.refs_0_ = f32[16,8192]{1,0:T(8,128)S(1)} collective-permute-done((f32[16,8192]{1,0:T(8,128)S(1)}, f32[16,8192]{1,0:T(8,128)S(1)}, u32[]{:S(2)}, u32[]{:S(2)}) %collective-permute-start.3) | collective-permute-done | bytes 524320 | tf_op jit(solution)/shard_map/ppermute | solution.py:196
  29.9 0.0 copy-start.2
  29.9 2.2 %copy-done.2 = bf16[8192,256]{1,0:T(8,128)(2,1)S(1)} copy-done((bf16[8192,256]{1,0:T(8,128)(2,1)S(1)}, bf16[8192,256]{1,0:T(8,128)(2,1)}, u32[]{:S(2)}) %copy-start.2) | copy-done | bytes 4194328
  32.1 0.0 copy-start.6
  32.1 2.2 %copy-done.6 = bf16[8192,256]{1,0:T(8,128)(2,1)S(1)} copy-done((bf16[8192,256]{1,0:T(8,128)(2,1)S(1)}, bf16[8192,256]{1,0:T(8,128)(2,1)}, u32[]{:S(2)}) %copy-start.6) | copy-done | bytes 4194328
  34.3 0.0 copy-start.3
  34.3 0.0 copy-start.7
  34.3 1.8 %shard_map.39.refs_5_ = f32[16,256]{1,0:T(8,128)S(1)} custom-call(s32[2]{0:T(128)S(1)} %pad_add_fusion.1.places, f32[16,8192]{1,0:T(8,128)S(1)} %collective-permute-done.3.refs_0_, bf16[8192,256]{1,0:T(8,128)(2,1)S(1)} %copy-done.2, bf16[8192,256]{1,0:T(8,128)(2,1)S(1)} %copy-done.6), custom_call_target="tpu_custom_call" | custom-call | bytes 16384 | tf_op jit(solution)/shard_map/pallas_call | solution.py:122
  36.1 0.9 %collective-permute-done.1.refs_0_ = f32[16,6144]{1,0:T(8,128)S(1)} collective-permute-done((f32[16,6144]{1,0:T(8,128)S(1)}, f32[16,6144]{1,0:T(8,128)S(1)}, u32[]{:S(2)}, u32[]{:S(2)}) %collective-permute-start.1) | collective-permute-done | bytes 393248 | tf_op jit(solution)/shard_map/ppermute | solution.py:199
  37.0 0.1 broadcast_in_dim.2.masks
  37.1 0.0 copy-done.3
  37.1 0.7 %copy-done.7 = bf16[8192,256]{1,0:T(8,128)(2,1)S(1)} copy-done((bf16[8192,256]{1,0:T(8,128)(2,1)S(1)}, bf16[8192,256]{1,0:T(8,128)(2,1)}, u32[]{:S(2)}) %copy-start.7) | copy-done | bytes 4194328
  37.8 1.5 %shard_map.40 = (f32[16,256]{1,0:T(8,128)S(1)}, f32[16,256]{1,0:T(8,128)S(1)}, f32[16,256]{1,0:T(8,128)S(1)}, f32[16,256]{1,0:T(8,128)S(1)}) custom-call(s32[6]{0:T(128)S(1)} %stack.47.places, f32[16,6144]{1,0:T(8,128)S(1)} %collective-permute-done.1.refs_0_, bf16[8192,256]{1,0:T(8,128)(2,1)S(1)} %copy-done.3, bf16[8192,256]{1,0:T(8,128)(2,1)S(1)} %copy-done.7, ...), custom_call_target="tpu_custom_call" | custom-call | bytes 65536 | tf_op jit(solution)/shard_map/pallas_call | solution.py:122
  39.2 0.5 %collective-permute-done.2.block = f32[16,2048]{1,0:T(8,128)S(1)} collective-permute-done((f32[16,2048]{1,0:T(8,128)S(1)}, f32[16,2048]{1,0:T(8,128)S(1)}, u32[]{:S(2)}, u32[]{:S(2)}) %collective-permute-start.2) | collective-permute-done | bytes 131104 | tf_op jit(solution)/shard_map/ppermute | solution.py:203
  39.7 0.4 shard_map.41
  40.1 0.1 collective-permute-start.6
  40.2 1.6 %collective-permute-start.5 = (f32[16,256]{1,0:T(8,128)S(1)}, f32[16,256]{1,0:T(8,128)S(1)}, u32[]{:S(2)}, u32[]{:S(2)}) collective-permute-start(f32[16,256]{1,0:T(8,128)S(1)} %get-tuple-element.43), channel_id=1, source_target_pairs={{0,2},{1,3},{2,0},{3,1},{4,6},{5,7},{6,4},{7,5},{8,10},{9,11},{10,... | collective-permute-start | bytes 49160 | tf_op jit(solution)/shard_map/ppermute | solution.py:226
  41.7 0.3 collective-permute-start.4
  42.0 0.0 collective-permute-done.6
  42.0 1.9 %collective-permute-done.5 = f32[16,256]{1,0:T(8,128)S(1)} collective-permute-done((f32[16,256]{1,0:T(8,128)S(1)}, f32[16,256]{1,0:T(8,128)S(1)}, u32[]{:S(2)}, u32[]{:S(2)}) %collective-permute-start.5) | collective-permute-done | bytes 16416 | tf_op jit(solution)/shard_map/ppermute | solution.py:226
  44.0 0.9 %collective-permute-done.4 = f32[16,256]{1,0:T(8,128)S(1)} collective-permute-done((f32[16,256]{1,0:T(8,128)S(1)}, f32[16,256]{1,0:T(8,128)S(1)}, u32[]{:S(2)}, u32[]{:S(2)}) %collective-permute-start.4) | collective-permute-done | bytes 16416 | tf_op jit(solution)/shard_map/ppermute | solution.py:226
  44.9 0.7 %multiply_select_fusion = f32[16,256]{1,0:T(8,128)} fusion(f32[16,256]{1,0:T(8,128)S(1)} %collective-permute-done.6, f32[16,256]{1,0:T(8,128)S(1)} %collective-permute-done.5, f32[16,256]{1,0:T(8,128)S(1)} %get-tuple-element.41, f32[16,256]{1,0:T(8,128)S(1)} %collective-permute-done.4, s32[256]{0:T(256)S(1)} %iota_add_fusion, s32[16]{0:T(128)S(1)} %iota_add_fusion.1), kind=kLoop, calls=%fused_computation | loop fusion | flops 40960 | bytes 83008 | tf_op jit(solution)/shard_map/jit(_where)/select_n | solution.py:233
  (5 shorter events, 0.1 us)
Async XLA Ops:
  0.0 16.7 %collective-permute-start = (f32[16,8192]{1,0:T(8,128)}, f32[16,8192]{1,0:T(8,128)S(1)}, u32[]{:S(2)}, u32[]{:S(2)}) collective-permute-start(f32[16,8192]{1,0:T(8,128)} %refs_0_), channel_id=1, source_target_pairs={{0,8},{8,12},{12,4},{4,0},{1,9},{9,13},{13,5},{5,1},{2,10},{10,14}... | collective-permute-start | bytes 1572872 | tf_op jit(solution)/shard_map/ppermute | solution.py:185
  4.7 9.3 %copy-start.8 = (f32[16,8192]{1,0:T(8,128)S(1)}, f32[16,8192]{1,0:T(8,128)}, u32[]{:S(2)}) copy-start(f32[16,8192]{1,0:T(8,128)} %refs_0_) | copy-start | bytes 1572868
  10.0 2.0 %copy-start = (bf16[8192,256]{1,0:T(8,128)(2,1)}, bf16[8192,256]{1,0:T(8,128)(2,1)S(1)}, u32[]{:S(2)}) copy-start(bf16[8192,256]{1,0:T(8,128)(2,1)S(1)} %get-tuple-element.29.refs_2_.refs_1_.high) | copy-start | bytes 12582916
  12.0 2.0 %copy-start.4 = (bf16[8192,256]{1,0:T(8,128)(2,1)}, bf16[8192,256]{1,0:T(8,128)(2,1)S(1)}, u32[]{:S(2)}) copy-start(bf16[8192,256]{1,0:T(8,128)(2,1)S(1)} %get-tuple-element.30.refs_3_.refs_2_.low) | copy-start | bytes 12582916
  14.0 15.9 %collective-permute-start.3 = (f32[16,8192]{1,0:T(8,128)S(1)}, f32[16,8192]{1,0:T(8,128)S(1)}, u32[]{:S(2)}, u32[]{:S(2)}) collective-permute-start(f32[16,8192]{1,0:T(8,128)S(1)} %copy-done.8), channel_id=1, source_target_pairs={{8,0},{12,8},{4,12},{0,4},{9,1},{13,9},{5,13},{1,5},{10,2},{14,10}... | collective-permute-start | bytes 1572872 | tf_op jit(solution)/shard_map/ppermute | solution.py:196
  16.7 20.3 %collective-permute-start.1 = (f32[16,6144]{1,0:T(8,128)S(1)}, f32[16,6144]{1,0:T(8,128)S(1)}, u32[]{:S(2)}, u32[]{:S(2)}) collective-permute-start(f32[16,6144]{1,0:T(8,128)S(1)} %slice.8), channel_id=1, source_target_pairs={{0,8},{8,12},{12,4},{4,0},{1,9},{9,13},{13,5},{5,1},{2,10},{10,14}... | collective-permute-start | bytes 1179656 | tf_op jit(solution)/shard_map/ppermute | solution.py:199
  20.1 2.2 %copy-start.1 = (bf16[8192,256]{1,0:T(8,128)(2,1)S(1)}, bf16[8192,256]{1,0:T(8,128)(2,1)}, u32[]{:S(2)}) copy-start(bf16[8192,256]{1,0:T(8,128)(2,1)} %copy-done) | copy-start | bytes 12582916
  22.3 2.2 %copy-start.5 = (bf16[8192,256]{1,0:T(8,128)(2,1)S(1)}, bf16[8192,256]{1,0:T(8,128)(2,1)}, u32[]{:S(2)}) copy-start(bf16[8192,256]{1,0:T(8,128)(2,1)} %copy-done.4) | copy-start | bytes 12582916
  26.6 13.1 %collective-permute-start.2 = (f32[16,2048]{1,0:T(8,128)S(1)}, f32[16,2048]{1,0:T(8,128)S(1)}, u32[]{:S(2)}, u32[]{:S(2)}) collective-permute-start(f32[16,2048]{1,0:T(8,128)S(1)} %slice.7), channel_id=1, source_target_pairs={{0,8},{8,12},{12,4},{4,0},{1,9},{9,13},{13,5},{5,1},{2,10},{10,14}... | collective-permute-start | bytes 393224 | tf_op jit(solution)/shard_map/ppermute | solution.py:203
  29.9 2.2 %copy-start.2 = (bf16[8192,256]{1,0:T(8,128)(2,1)S(1)}, bf16[8192,256]{1,0:T(8,128)(2,1)}, u32[]{:S(2)}) copy-start(bf16[8192,256]{1,0:T(8,128)(2,1)} %copy-done) | copy-start | bytes 12582916
  32.1 2.2 %copy-start.6 = (bf16[8192,256]{1,0:T(8,128)(2,1)S(1)}, bf16[8192,256]{1,0:T(8,128)(2,1)}, u32[]{:S(2)}) copy-start(bf16[8192,256]{1,0:T(8,128)(2,1)} %copy-done.4) | copy-start | bytes 12582916
  34.3 2.8 %copy-start.3 = (bf16[8192,256]{1,0:T(8,128)(2,1)S(1)}, bf16[8192,256]{1,0:T(8,128)(2,1)}, u32[]{:S(2)}) copy-start(bf16[8192,256]{1,0:T(8,128)(2,1)} %copy-done) | copy-start | bytes 12582916
  34.3 3.5 %copy-start.7 = (bf16[8192,256]{1,0:T(8,128)(2,1)S(1)}, bf16[8192,256]{1,0:T(8,128)(2,1)}, u32[]{:S(2)}) copy-start(bf16[8192,256]{1,0:T(8,128)(2,1)} %copy-done.4) | copy-start | bytes 12582916
  40.1 1.9 %collective-permute-start.6 = (f32[16,256]{1,0:T(8,128)S(1)}, f32[16,256]{1,0:T(8,128)S(1)}, u32[]{:S(2)}, u32[]{:S(2)}) collective-permute-start(f32[16,256]{1,0:T(8,128)S(1)} %get-tuple-element.44), channel_id=1, source_target_pairs={{0,1},{1,0},{2,3},{3,2},{4,5},{5,4},{6,7},{7,6},{8,9},{9,8},{10,11... | collective-permute-start | bytes 49160 | tf_op jit(solution)/shard_map/ppermute | solution.py:226
  40.2 3.8 %collective-permute-start.5 = (f32[16,256]{1,0:T(8,128)S(1)}, f32[16,256]{1,0:T(8,128)S(1)}, u32[]{:S(2)}, u32[]{:S(2)}) collective-permute-start(f32[16,256]{1,0:T(8,128)S(1)} %get-tuple-element.43), channel_id=1, source_target_pairs={{0,2},{1,3},{2,0},{3,1},{4,6},{5,7},{6,4},{7,5},{8,10},{9,11},{10,... | collective-permute-start | bytes 49160 | tf_op jit(solution)/shard_map/ppermute | solution.py:226
  41.7 3.2 %collective-permute-start.4 = (f32[16,256]{1,0:T(8,128)S(1)}, f32[16,256]{1,0:T(8,128)S(1)}, u32[]{:S(2)}, u32[]{:S(2)}) collective-permute-start(f32[16,256]{1,0:T(8,128)S(1)} %get-tuple-element.42), channel_id=1, source_target_pairs={{0,3},{1,2},{2,1},{3,0},{4,7},{5,6},{6,5},{7,4},{8,11},{9,10},{10,... | collective-permute-start | bytes 49160 | tf_op jit(solution)/shard_map/ppermute | solution.py:226

commit v16 on v15

--- a/solution.py
+++ b/solution.py
@@ -13,7 +13,7 @@
 largest_bf16 = 3.3895313892515355e38
 
 
-def weights_kernel(shift, covariance, high, low, held, arrived):
+def weights_kernel(shift, covariance, high, low, ticket, held, arrived):
     depth, columns = covariance.shape
     step = held.shape[1]
     pieces = depth // step
@@ -37,6 +37,7 @@
         rows = slice(piece * step, (piece + 1) * step)
         high[rows] = upper
         low[rows] = (values - upper.astype(jnp.float32)).astype(jnp.bfloat16)
+    ticket[...] = jnp.zeros(ticket.shape, jnp.float32)
 
 
 def weights_of(covariance, shift):
@@ -44,12 +45,13 @@
     step = math.gcd(depth, 512)
     return pl.pallas_call(
         weights_kernel,
-        out_shape=[pltpu.VMEM((depth, columns), jnp.bfloat16)] * 2,
+        out_shape=[pltpu.VMEM((depth, columns), jnp.bfloat16)] * 2
+        + [jax.ShapeDtypeStruct((8, 128), jnp.float32)],
         in_specs=[
             pl.BlockSpec(memory_space=pltpu.SMEM),
             pl.BlockSpec(memory_space=pltpu.HBM),
         ],
-        out_specs=[pl.BlockSpec(memory_space=pltpu.VMEM)] * 2,
+        out_specs=[pl.BlockSpec(memory_space=pltpu.VMEM)] * 3,
         scratch_shapes=[
             pltpu.VMEM((4, step, columns), jnp.float32),
             pltpu.SemaphoreType.DMA((4,)),
@@ -153,7 +155,7 @@
     assert rows_share % block_rows == 0 and rep_count & (rep_count - 1) == 0 and rep_count > 1
 
     shift = jnp.reshape(offset - rep_index * part_width, (1,)).astype(jnp.int32)
-    weights = weights_of(covariance_columns, shift)
+    *weights, ticket = weights_of(covariance_columns, shift)
 
     cut = part_width // 4 * 3
     assert all_rows <= cut and cut % tile_width == 0
@@ -183,7 +185,7 @@
         return jnp.where(up < team_count, up, 2 * team_count - 1 - up)
 
     first = lax.ppermute(omega_rows, "team", onward)
-    own, *weights = lax.optimization_barrier((omega_rows, *weights))
+    own, _ = lax.optimization_barrier((omega_rows, ticket))
     last_step = team_count // 2
     gathered = []
     held = first

time: 45.9 us -> 45.5 us (level)
  local copies, waits for them, and re-layouts: 13.6 us -> 6.02 us
  waiting for transfers between devices: 9.92 us -> 16.6 us
  Pallas kernels: 11.1 us -> 11.6 us
    ppermute x1, waiting for transfers between devices: 2.69 us -> 12 us  [per_device(): first = lax.ppermute(omega_rows, 'team', onward)]
    unnamed x18 -> x14, local copies, waits for them, and re-layouts: 13.4 us -> 5.83 us
    ppermute x1, waiting for transfers between devices: 3.05 us -> 0.2 us  [per_device(): held = lax.ppermute(held, 'team', backward)]
    pallas_call x1, Pallas kernels: 5.34 us -> 5.8 us  [weights_of(): pl.pallas_call(weights_kernel, out_shape=[pltpu.VMEM((depth, columns), jn...]
  transfers between devices with their start and end apart: 7 -> 7, of which waited for: 6 -> 6; matrix products, arithmetic and copies ran while one was open for 1% -> 1% of each run, Pallas kernels for 24% -> 25%
where the time goes in v16:
time: 45.5 us; the launch traced here: 45.2 us
  waiting for transfers between devices  16.6 us (36%)
  Pallas kernels  11.6 us (25%)
  starting transfers between devices  9.37 us (21%)
  local copies, waits for them, and re-layouts  6.02 us (13%)
  other arithmetic  0.85 us (2%)
  between operations  0.76 us (2%)
    ppermute x1, waiting for transfers between devices, per_device(): first = lax.ppermute(omega_rows, 'team', onward)  12 us
    unnamed x14, local copies, waits for them, and re-layouts  5.83 us
    pallas_call x4, Pallas kernels, call(): pl.pallas_call(kernel, out_shape=[jax.ShapeDtypeStruct(shape, jnp.float32...  5.82 us
    pallas_call x1, Pallas kernels, weights_of(): pl.pallas_call(weights_kernel, out_shape=[pltpu.VMEM((depth, columns), jn...  5.8 us
    ppermute x1, starting transfers between devices, per_device(): first = lax.ppermute(omega_rows, 'team', onward)  4.04 us
    ppermute x1, starting transfers between devices, per_device(): last_left = lax.ppermute(last_held[:, :cut], 'team', onward)  3.33 us
    ppermute x3, waiting for transfers between devices, per_device(): terms.append(lax.ppermute(shares[flip], 'rep', pairs))  2.85 us
    ppermute x3, starting transfers between devices, per_device(): terms.append(lax.ppermute(shares[flip], 'rep', pairs))  1.93 us
  transfers between devices with their start and end apart: 7, of which 6 were waited for; matrix products, arithmetic and copies ran while one was open for 1% of the time, Pallas kernels for 25%

profile of v16, /device:TPU:0, one launch (start us, length us, event | category | flops | bytes accessed | tf_op | source)
XLA Modules:
  0.0 45.2 jit_solution(1211992381318325815)
XLA Ops:
  0.0 4.0 %collective-permute-start = (f32[16,8192]{1,0:T(8,128)}, f32[16,8192]{1,0:T(8,128)S(1)}, u32[]{:S(2)}, u32[]{:S(2)}) collective-permute-start(f32[16,8192]{1,0:T(8,128)} %refs_0_), channel_id=1, source_target_pairs={{0,8},{8,12},{12,4},{4,0},{1,9},{9,13},{13,5},{5,1},{2,10},{10,14}... | collective-permute-start | bytes 1572872 | tf_op jit(solution)/shard_map/ppermute | solution.py:187
  4.0 0.0 collective-permute-start.3
  4.7 12.0 %collective-permute-done.refs_1_ = f32[16,8192]{1,0:T(8,128)S(1)} collective-permute-done((f32[16,8192]{1,0:T(8,128)}, f32[16,8192]{1,0:T(8,128)S(1)}, u32[]{:S(2)}, u32[]{:S(2)}) %collective-permute-start) | collective-permute-done | bytes 524320 | tf_op jit(solution)/shard_map/ppermute | solution.py:187
  16.8 3.3 %collective-permute-start.1 = (f32[16,6144]{1,0:T(8,128)S(1)}, f32[16,6144]{1,0:T(8,128)S(1)}, u32[]{:S(2)}, u32[]{:S(2)}) collective-permute-start(f32[16,6144]{1,0:T(8,128)S(1)} %slice.8), channel_id=1, source_target_pairs={{0,8},{8,12},{12,4},{4,0},{1,9},{9,13},{13,5},{5,1},{2,10},{10,14}... | collective-permute-start | bytes 1179656 | tf_op jit(solution)/shard_map/ppermute | solution.py:201
  20.1 0.1 pad_add_fusion.places
  20.2 0.0 copy-start.6
  20.2 5.8 %shard_map.37 = (bf16[8192,256]{1,0:T(8,128)(2,1)S(1)}, bf16[8192,256]{1,0:T(8,128)(2,1)S(1)}, f32[8,128]{1,0:T(8,128)}) custom-call(s32[1]{0:T(128)} %bitcast.4.shift, f32[8192,256]{1,0:T(8,128)} %covariance.1), custom_call_target="tpu_custom_call" | custom-call | bytes 8388608 | tf_op jit(solution)/shard_map/pallas_call | solution.py:46
  26.0 0.0 copy-start
  26.0 0.0 copy-start.3
  26.0 0.0 copy-done.6
  26.0 2.1 %shard_map.38 = (f32[16,256]{1,0:T(8,128)S(1)}, f32[16,256]{1,0:T(8,128)S(1)}) custom-call(s32[3]{0:T(128)S(1)} %pad_add_fusion.places, f32[16,8192]{1,0:T(8,128)S(1)} %copy-done.6, f32[16,8192]{1,0:T(8,128)S(1)} %collective-permute-done.refs_1_, bf16[8192,256]{1,0:T(8,128)(2,1)S(1)} %get-tuple-element.23.refs_2_.refs_1_.high, ...), custom_call_target="tpu_custom_call" | custom-call | bytes 32768 | tf_op jit(solution)/shard_map/pallas_call | solution.py:124
  28.1 0.0 copy-done
  28.1 1.1 %copy-done.3 = bf16[8192,256]{1,0:T(8,128)(2,1)} copy-done((bf16[8192,256]{1,0:T(8,128)(2,1)}, bf16[8192,256]{1,0:T(8,128)(2,1)S(1)}, u32[]{:S(2)}) %copy-start.3) | copy-done | bytes 4194328
  29.2 0.1 collective-permute-start.2
  29.3 0.1 pad_add_fusion.1.places
  29.4 0.1 stack.47.places
  29.5 0.2 collective-permute-done.3.refs_0_
  29.7 0.0 copy-start.1
  29.7 2.2 %copy-done.1 = bf16[8192,256]{1,0:T(8,128)(2,1)S(1)} copy-done((bf16[8192,256]{1,0:T(8,128)(2,1)S(1)}, bf16[8192,256]{1,0:T(8,128)(2,1)}, u32[]{:S(2)}) %copy-start.1) | copy-done | bytes 4194328
  31.9 0.0 copy-start.4
  31.9 2.2 %copy-done.4 = bf16[8192,256]{1,0:T(8,128)(2,1)S(1)} copy-done((bf16[8192,256]{1,0:T(8,128)(2,1)S(1)}, bf16[8192,256]{1,0:T(8,128)(2,1)}, u32[]{:S(2)}) %copy-start.4) | copy-done | bytes 4194328
  34.0 0.0 copy-start.2
  34.0 0.0 copy-start.5
  34.0 1.8 %shard_map.39.refs_5_ = f32[16,256]{1,0:T(8,128)S(1)} custom-call(s32[2]{0:T(128)S(1)} %pad_add_fusion.1.places, f32[16,8192]{1,0:T(8,128)S(1)} %collective-permute-done.3.refs_0_, bf16[8192,256]{1,0:T(8,128)(2,1)S(1)} %copy-done.1, bf16[8192,256]{1,0:T(8,128)(2,1)S(1)} %copy-done.4), custom_call_target="tpu_custom_call" | custom-call | bytes 16384 | tf_op jit(solution)/shard_map/pallas_call | solution.py:124
  35.9 1.2 %collective-permute-done.1.refs_0_ = f32[16,6144]{1,0:T(8,128)S(1)} collective-permute-done((f32[16,6144]{1,0:T(8,128)S(1)}, f32[16,6144]{1,0:T(8,128)S(1)}, u32[]{:S(2)}, u32[]{:S(2)}) %collective-permute-start.1) | collective-permute-done | bytes 393248 | tf_op jit(solution)/shard_map/ppermute | solution.py:201
  37.1 0.1 broadcast_in_dim.2.masks
  37.1 0.0 copy-done.2
  37.1 0.4 copy-done.5
  37.5 1.5 %shard_map.40 = (f32[16,256]{1,0:T(8,128)S(1)}, f32[16,256]{1,0:T(8,128)S(1)}, f32[16,256]{1,0:T(8,128)S(1)}, f32[16,256]{1,0:T(8,128)S(1)}) custom-call(s32[6]{0:T(128)S(1)} %stack.47.places, f32[16,6144]{1,0:T(8,128)S(1)} %collective-permute-done.1.refs_0_, bf16[8192,256]{1,0:T(8,128)(2,1)S(1)} %copy-done.2, bf16[8192,256]{1,0:T(8,128)(2,1)S(1)} %copy-done.5, ...), custom_call_target="tpu_custom_call" | custom-call | bytes 65536 | tf_op jit(solution)/shard_map/pallas_call | solution.py:124
  39.0 0.4 collective-permute-done.2.block
  39.4 0.4 shard_map.41
  39.8 0.1 collective-permute-start.6
  39.8 1.6 %collective-permute-start.5 = (f32[16,256]{1,0:T(8,128)S(1)}, f32[16,256]{1,0:T(8,128)S(1)}, u32[]{:S(2)}, u32[]{:S(2)}) collective-permute-start(f32[16,256]{1,0:T(8,128)S(1)} %get-tuple-element.37), channel_id=1, source_target_pairs={{0,2},{1,3},{2,0},{3,1},{4,6},{5,7},{6,4},{7,5},{8,10},{9,11},{10,... | collective-permute-start | bytes 49160 | tf_op jit(solution)/shard_map/ppermute | solution.py:228
  41.4 0.3 collective-permute-start.4
  41.7 0.0 collective-permute-done.6
  41.7 1.9 %collective-permute-done.5 = f32[16,256]{1,0:T(8,128)S(1)} collective-permute-done((f32[16,256]{1,0:T(8,128)S(1)}, f32[16,256]{1,0:T(8,128)S(1)}, u32[]{:S(2)}, u32[]{:S(2)}) %collective-permute-start.5) | collective-permute-done | bytes 16416 | tf_op jit(solution)/shard_map/ppermute | solution.py:228
  43.6 0.9 %collective-permute-done.4 = f32[16,256]{1,0:T(8,128)S(1)} collective-permute-done((f32[16,256]{1,0:T(8,128)S(1)}, f32[16,256]{1,0:T(8,128)S(1)}, u32[]{:S(2)}, u32[]{:S(2)}) %collective-permute-start.4) | collective-permute-done | bytes 16416 | tf_op jit(solution)/shard_map/ppermute | solution.py:228
  44.6 0.7 %multiply_select_fusion = f32[16,256]{1,0:T(8,128)} fusion(f32[16,256]{1,0:T(8,128)S(1)} %collective-permute-done.6, f32[16,256]{1,0:T(8,128)S(1)} %collective-permute-done.5, f32[16,256]{1,0:T(8,128)S(1)} %get-tuple-element.35, f32[16,256]{1,0:T(8,128)S(1)} %collective-permute-done.4, s32[256]{0:T(256)S(1)} %iota_add_fusion, s32[16]{0:T(128)S(1)} %iota_add_fusion.1), kind=kLoop, calls=%fused_computation | loop fusion | flops 40960 | bytes 83008 | tf_op jit(solution)/shard_map/jit(_where)/select_n | solution.py:235
  (5 shorter events, 0.1 us)
Async XLA Ops:
  0.0 16.7 %collective-permute-start = (f32[16,8192]{1,0:T(8,128)}, f32[16,8192]{1,0:T(8,128)S(1)}, u32[]{:S(2)}, u32[]{:S(2)}) collective-permute-start(f32[16,8192]{1,0:T(8,128)} %refs_0_), channel_id=1, source_target_pairs={{0,8},{8,12},{12,4},{4,0},{1,9},{9,13},{13,5},{5,1},{2,10},{10,14}... | collective-permute-start | bytes 1572872 | tf_op jit(solution)/shard_map/ppermute | solution.py:187
  4.0 25.6 %collective-permute-start.3 = (f32[16,8192]{1,0:T(8,128)}, f32[16,8192]{1,0:T(8,128)S(1)}, u32[]{:S(2)}, u32[]{:S(2)}) collective-permute-start(f32[16,8192]{1,0:T(8,128)} %refs_0_), channel_id=1, source_target_pairs={{8,0},{12,8},{4,12},{0,4},{9,1},{13,9},{5,13},{1,5},{10,2},{14,10}... | collective-permute-start | bytes 1572872 | tf_op jit(solution)/shard_map/ppermute | solution.py:198
  16.8 20.3 %collective-permute-start.1 = (f32[16,6144]{1,0:T(8,128)S(1)}, f32[16,6144]{1,0:T(8,128)S(1)}, u32[]{:S(2)}, u32[]{:S(2)}) collective-permute-start(f32[16,6144]{1,0:T(8,128)S(1)} %slice.8), channel_id=1, source_target_pairs={{0,8},{8,12},{12,4},{4,0},{1,9},{9,13},{13,5},{5,1},{2,10},{10,14}... | collective-permute-start | bytes 1179656 | tf_op jit(solution)/shard_map/ppermute | solution.py:201
  20.2 5.8 %copy-start.6 = (f32[16,8192]{1,0:T(8,128)S(1)}, f32[16,8192]{1,0:T(8,128)}, u32[]{:S(2)}) copy-start(f32[16,8192]{1,0:T(8,128)} %refs_0_) | copy-start | bytes 1572868
  26.0 2.2 %copy-start = (bf16[8192,256]{1,0:T(8,128)(2,1)}, bf16[8192,256]{1,0:T(8,128)(2,1)S(1)}, u32[]{:S(2)}) copy-start(bf16[8192,256]{1,0:T(8,128)(2,1)S(1)} %get-tuple-element.23.refs_2_.refs_1_.high) | copy-start | bytes 12582916
  26.0 3.2 %copy-start.3 = (bf16[8192,256]{1,0:T(8,128)(2,1)}, bf16[8192,256]{1,0:T(8,128)(2,1)S(1)}, u32[]{:S(2)}) copy-start(bf16[8192,256]{1,0:T(8,128)(2,1)S(1)} %get-tuple-element.24.refs_3_.refs_2_.low) | copy-start | bytes 12582916
  29.2 10.1 %collective-permute-start.2 = (f32[16,2048]{1,0:T(8,128)S(1)}, f32[16,2048]{1,0:T(8,128)S(1)}, u32[]{:S(2)}, u32[]{:S(2)}) collective-permute-start(f32[16,2048]{1,0:T(8,128)S(1)} %slice.7), channel_id=1, source_target_pairs={{0,8},{8,12},{12,4},{4,0},{1,9},{9,13},{13,5},{5,1},{2,10},{10,14}... | collective-permute-start | bytes 393224 | tf_op jit(solution)/shard_map/ppermute | solution.py:205
  29.7 2.2 %copy-start.1 = (bf16[8192,256]{1,0:T(8,128)(2,1)S(1)}, bf16[8192,256]{1,0:T(8,128)(2,1)}, u32[]{:S(2)}) copy-start(bf16[8192,256]{1,0:T(8,128)(2,1)} %copy-done) | copy-start | bytes 12582916
  31.9 2.2 %copy-start.4 = (bf16[8192,256]{1,0:T(8,128)(2,1)S(1)}, bf16[8192,256]{1,0:T(8,128)(2,1)}, u32[]{:S(2)}) copy-start(bf16[8192,256]{1,0:T(8,128)(2,1)} %copy-done.3) | copy-start | bytes 12582916
  34.0 3.1 %copy-start.2 = (bf16[8192,256]{1,0:T(8,128)(2,1)S(1)}, bf16[8192,256]{1,0:T(8,128)(2,1)}, u32[]{:S(2)}) copy-start(bf16[8192,256]{1,0:T(8,128)(2,1)} %copy-done) | copy-start | bytes 12582916
  34.0 3.5 %copy-start.5 = (bf16[8192,256]{1,0:T(8,128)(2,1)S(1)}, bf16[8192,256]{1,0:T(8,128)(2,1)}, u32[]{:S(2)}) copy-start(bf16[8192,256]{1,0:T(8,128)(2,1)} %copy-done.3) | copy-start | bytes 12582916
  39.8 1.9 %collective-permute-start.6 = (f32[16,256]{1,0:T(8,128)S(1)}, f32[16,256]{1,0:T(8,128)S(1)}, u32[]{:S(2)}, u32[]{:S(2)}) collective-permute-start(f32[16,256]{1,0:T(8,128)S(1)} %get-tuple-element.38), channel_id=1, source_target_pairs={{0,1},{1,0},{2,3},{3,2},{4,5},{5,4},{6,7},{7,6},{8,9},{9,8},{10,11... | collective-permute-start | bytes 49160 | tf_op jit(solution)/shard_map/ppermute | solution.py:228
  39.8 3.8 %collective-permute-start.5 = (f32[16,256]{1,0:T(8,128)S(1)}, f32[16,256]{1,0:T(8,128)S(1)}, u32[]{:S(2)}, u32[]{:S(2)}) collective-permute-start(f32[16,256]{1,0:T(8,128)S(1)} %get-tuple-element.37), channel_id=1, source_target_pairs={{0,2},{1,3},{2,0},{3,1},{4,6},{5,7},{6,4},{7,5},{8,10},{9,11},{10,... | collective-permute-start | bytes 49160 | tf_op jit(solution)/shard_map/ppermute | solution.py:228
  41.4 3.2 %collective-permute-start.4 = (f32[16,256]{1,0:T(8,128)S(1)}, f32[16,256]{1,0:T(8,128)S(1)}, u32[]{:S(2)}, u32[]{:S(2)}) collective-permute-start(f32[16,256]{1,0:T(8,128)S(1)} %get-tuple-element.36), channel_id=1, source_target_pairs={{0,3},{1,2},{2,1},{3,0},{4,7},{5,6},{6,5},{7,4},{8,11},{9,10},{10,... | collective-permute-start | bytes 49160 | tf_op jit(solution)/shard_map/ppermute | solution.py:228

commit v17 on v13

--- a/solution.py
+++ b/solution.py
@@ -141,7 +141,7 @@
         return jnp.where(up < team_count, up, 2 * team_count - 1 - up)
 
     first = lax.ppermute(omega_rows, "team", onward)
-    own, *weights = lax.optimization_barrier((omega_rows, *weights))
+    own = omega_rows
     last_step = team_count // 2
     gathered = []
     held = first

time: 45.4 us -> 50.4 us (1.11)
  waiting for transfers between devices: 10.9 us -> 14.9 us
  local copies, waits for them, and re-layouts: 9.34 us -> 10.5 us
    ppermute x1, waiting for transfers between devices: 3.95 us -> 12 us  [per_device(): first = lax.ppermute(omega_rows, 'team', onward)]
    ppermute x1, waiting for transfers between devices: 2.72 us -> 0.01 us  [per_device(): held = lax.ppermute(held, 'team', backward)]
    ppermute x1, waiting for transfers between devices: 1.15 us -> 0.01 us  [per_device(): last_left = lax.ppermute(last_held[:, :cut], 'team', onward)]
    unnamed x14, local copies, waits for them, and re-layouts: 9.15 us -> 10.3 us
  transfers between devices with their start and end apart: 7 -> 7, of which waited for: 6 -> 3; matrix products, arithmetic and copies ran while one was open for 19% -> 17% of each run, Pallas kernels for 12% -> 11%
where the time goes in v17:
time: 50.4 us; the launch traced here: 50.1 us
  waiting for transfers between devices  14.9 us (30%)
  local copies, waits for them, and re-layouts  10.5 us (21%)
  starting transfers between devices  9.42 us (19%)
  other arithmetic  8.78 us (17%)
  Pallas kernels  5.84 us (12%)
  between operations  0.75 us (1%)
    ppermute x1, waiting for transfers between devices, per_device(): first = lax.ppermute(omega_rows, 'team', onward)  12 us
    unnamed x14, local copies, waits for them, and re-layouts  10.3 us
    convert_element_type x1, other arithmetic, halves(): return (high.astype(jnp.bfloat16), (array - high).astype(jnp.bfloat16))  7.92 us
    pallas_call x4, Pallas kernels, call(): pl.pallas_call(kernel, out_shape=[jax.ShapeDtypeStruct(shape, jnp.float32...  5.84 us
    ppermute x1, starting transfers between devices, per_device(): first = lax.ppermute(omega_rows, 'team', onward)  4.04 us
    ppermute x1, starting transfers between devices, per_device(): last_left = lax.ppermute(last_held[:, :cut], 'team', onward)  3.33 us
    ppermute x3, waiting for transfers between devices, per_device(): terms.append(lax.ppermute(shares[flip], 'rep', pairs))  2.85 us
    ppermute x3, starting transfers between devices, per_device(): terms.append(lax.ppermute(shares[flip], 'rep', pairs))  1.93 us
  transfers between devices with their start and end apart: 7, of which 3 were waited for; matrix products, arithmetic and copies ran while one was open for 17% of the time, Pallas kernels for 11%

profile of v17, /device:TPU:0, one launch (start us, length us, event | category | flops | bytes accessed | tf_op | source)
XLA Modules:
  0.0 50.1 jit_solution(17782585542259380154)
XLA Ops:
  0.0 4.0 %collective-permute-start = (f32[16,8192]{1,0:T(8,128)}, f32[16,8192]{1,0:T(8,128)S(1)}, u32[]{:S(2)}, u32[]{:S(2)}) collective-permute-start(f32[16,8192]{1,0:T(8,128)} %refs_0_.1), channel_id=1, source_target_pairs={{0,8},{8,12},{12,4},{4,0},{1,9},{9,13},{13,5},{5,1},{2,10},{10,14}... | collective-permute-start | bytes 1572872 | tf_op jit(solution)/shard_map/ppermute | solution.py:143
  4.0 0.0 collective-permute-start.3
  4.7 12.0 %collective-permute-done.refs_1_ = f32[16,8192]{1,0:T(8,128)S(1)} collective-permute-done((f32[16,8192]{1,0:T(8,128)}, f32[16,8192]{1,0:T(8,128)S(1)}, u32[]{:S(2)}, u32[]{:S(2)}) %collective-permute-start) | collective-permute-done | bytes 524320 | tf_op jit(solution)/shard_map/ppermute | solution.py:143
  16.8 0.0 copy-start.6
  16.8 3.3 %collective-permute-start.1 = (f32[16,6144]{1,0:T(8,128)S(1)}, f32[16,6144]{1,0:T(8,128)S(1)}, u32[]{:S(2)}, u32[]{:S(2)}) collective-permute-start(f32[16,6144]{1,0:T(8,128)S(1)} %slice.8), channel_id=1, source_target_pairs={{0,8},{8,12},{12,4},{4,0},{1,9},{9,13},{13,5},{5,1},{2,10},{10,14}... | collective-permute-start | bytes 1179656 | tf_op jit(solution)/shard_map/ppermute | solution.py:157
  20.1 7.9 %subtract_convert_fusion = (bf16[8192,256]{1,0:T(8,128)(2,1)}, bf16[8192,256]{1,0:T(8,128)(2,1)}) fusion(f32[8192,256]{1,0:T(8,128)} %param.4, s32[256]{0:T(256)S(1)} %iota_add_fusion.1, s32[8192]{0:T(1024)S(1)} %iota_add_fusion), kind=kLoop, calls=%fused_computation | loop fusion | flops 18874368 | bytes 16811008 | tf_op jit(solution)/shard_map/convert_element_type | solution.py:17
  28.0 0.1 pad_add_fusion.places
  28.1 0.0 copy-done.6
  28.1 0.0 copy-start
  28.1 2.2 %copy-done = bf16[8192,256]{1,0:T(8,128)(2,1)S(1)} copy-done((bf16[8192,256]{1,0:T(8,128)(2,1)S(1)}, bf16[8192,256]{1,0:T(8,128)(2,1)}, u32[]{:S(2)}) %copy-start) | copy-done | bytes 4194328
  30.3 0.0 copy-start.3
  30.3 2.2 %copy-done.3 = bf16[8192,256]{1,0:T(8,128)(2,1)S(1)} copy-done((bf16[8192,256]{1,0:T(8,128)(2,1)S(1)}, bf16[8192,256]{1,0:T(8,128)(2,1)}, u32[]{:S(2)}) %copy-start.3) | copy-done | bytes 4194328
  32.5 2.1 %shard_map.37 = (f32[16,256]{1,0:T(8,128)S(1)}, f32[16,256]{1,0:T(8,128)S(1)}) custom-call(s32[3]{0:T(128)S(1)} %pad_add_fusion.places, f32[16,8192]{1,0:T(8,128)S(1)} %copy-done.6, f32[16,8192]{1,0:T(8,128)S(1)} %collective-permute-done.refs_1_, bf16[8192,256]{1,0:T(8,128)(2,1)S(1)} %copy-done.3, bf16[8192,256]{1,0:T(8,128)(2,1)S(1)} %copy-done), custom_call_target="tpu_custom_call" | custom-call | bytes 32768 | tf_op jit(solution)/shard_map/pallas_call | solution.py:78
  34.6 0.1 collective-permute-start.2
  34.7 0.1 pad_add_fusion.1.places
  34.8 0.1 stack.47.places
  34.9 0.0 collective-permute-done.3.refs_0_
  34.9 0.0 copy-start.1
  34.9 2.2 %copy-done.1 = bf16[8192,256]{1,0:T(8,128)(2,1)S(1)} copy-done((bf16[8192,256]{1,0:T(8,128)(2,1)S(1)}, bf16[8192,256]{1,0:T(8,128)(2,1)}, u32[]{:S(2)}) %copy-start.1) | copy-done | bytes 4194328
  37.1 0.0 copy-start.4
  37.1 2.2 %copy-done.4 = bf16[8192,256]{1,0:T(8,128)(2,1)S(1)} copy-done((bf16[8192,256]{1,0:T(8,128)(2,1)S(1)}, bf16[8192,256]{1,0:T(8,128)(2,1)}, u32[]{:S(2)}) %copy-start.4) | copy-done | bytes 4194328
  39.3 0.0 copy-start.2
  39.3 0.0 copy-start.5
  39.3 1.9 %shard_map.38.refs_5_ = f32[16,256]{1,0:T(8,128)S(1)} custom-call(s32[2]{0:T(128)S(1)} %pad_add_fusion.1.places, f32[16,8192]{1,0:T(8,128)S(1)} %collective-permute-done.3.refs_0_, bf16[8192,256]{1,0:T(8,128)(2,1)S(1)} %copy-done.4, bf16[8192,256]{1,0:T(8,128)(2,1)S(1)} %copy-done.1), custom_call_target="tpu_custom_call" | custom-call | bytes 16384 | tf_op jit(solution)/shard_map/pallas_call | solution.py:78
  41.1 0.0 collective-permute-done.1.refs_0_
  41.1 0.1 broadcast_in_dim.2.masks
  41.2 0.2 copy-done.2
  41.5 1.3 %copy-done.5 = bf16[8192,256]{1,0:T(8,128)(2,1)S(1)} copy-done((bf16[8192,256]{1,0:T(8,128)(2,1)S(1)}, bf16[8192,256]{1,0:T(8,128)(2,1)}, u32[]{:S(2)}) %copy-start.5) | copy-done | bytes 4194328
  42.7 1.5 %shard_map.39 = (f32[16,256]{1,0:T(8,128)S(1)}, f32[16,256]{1,0:T(8,128)S(1)}, f32[16,256]{1,0:T(8,128)S(1)}, f32[16,256]{1,0:T(8,128)S(1)}) custom-call(s32[6]{0:T(128)S(1)} %stack.47.places, f32[16,6144]{1,0:T(8,128)S(1)} %collective-permute-done.1.refs_0_, bf16[8192,256]{1,0:T(8,128)(2,1)S(1)} %copy-done.5, bf16[8192,256]{1,0:T(8,128)(2,1)S(1)} %copy-done.2, ...), custom_call_target="tpu_custom_call" | custom-call | bytes 65536 | tf_op jit(solution)/shard_map/pallas_call | solution.py:78
  44.2 0.0 collective-permute-done.2.block
  44.2 0.4 shard_map.40
  44.7 0.1 collective-permute-start.6
  44.7 1.6 %collective-permute-start.5 = (f32[16,256]{1,0:T(8,128)S(1)}, f32[16,256]{1,0:T(8,128)S(1)}, u32[]{:S(2)}, u32[]{:S(2)}) collective-permute-start(f32[16,256]{1,0:T(8,128)S(1)} %get-tuple-element.33), channel_id=1, source_target_pairs={{0,2},{1,3},{2,0},{3,1},{4,6},{5,7},{6,4},{7,5},{8,10},{9,11},{10,... | collective-permute-start | bytes 49160 | tf_op jit(solution)/shard_map/ppermute | solution.py:184
  46.3 0.3 collective-permute-start.4
  46.6 0.0 collective-permute-done.6
  46.6 1.9 %collective-permute-done.5 = f32[16,256]{1,0:T(8,128)S(1)} collective-permute-done((f32[16,256]{1,0:T(8,128)S(1)}, f32[16,256]{1,0:T(8,128)S(1)}, u32[]{:S(2)}, u32[]{:S(2)}) %collective-permute-start.5) | collective-permute-done | bytes 16416 | tf_op jit(solution)/shard_map/ppermute | solution.py:184
  48.5 0.9 %collective-permute-done.4 = f32[16,256]{1,0:T(8,128)S(1)} collective-permute-done((f32[16,256]{1,0:T(8,128)S(1)}, f32[16,256]{1,0:T(8,128)S(1)}, u32[]{:S(2)}, u32[]{:S(2)}) %collective-permute-start.4) | collective-permute-done | bytes 16416 | tf_op jit(solution)/shard_map/ppermute | solution.py:184
  49.5 0.7 %multiply_select_fusion = f32[16,256]{1,0:T(8,128)} fusion(f32[16,256]{1,0:T(8,128)S(1)} %collective-permute-done.6, f32[16,256]{1,0:T(8,128)S(1)} %collective-permute-done.5, f32[16,256]{1,0:T(8,128)S(1)} %get-tuple-element.31, f32[16,256]{1,0:T(8,128)S(1)} %collective-permute-done.4, s32[256]{0:T(256)S(1)} %iota_add_fusion.1, s32[16]{0:T(128)S(1)} %iota_add_fusion.2), kind=kLoop, calls=%fused_computation.5 | loop fusion | flops 40960 | bytes 83008 | tf_op jit(solution)/shard_map/jit(_where)/select_n | solution.py:191
  (6 shorter events, 0.1 us)
Async XLA Ops:
  0.0 16.7 %collective-permute-start = (f32[16,8192]{1,0:T(8,128)}, f32[16,8192]{1,0:T(8,128)S(1)}, u32[]{:S(2)}, u32[]{:S(2)}) collective-permute-start(f32[16,8192]{1,0:T(8,128)} %refs_0_.1), channel_id=1, source_target_pairs={{0,8},{8,12},{12,4},{4,0},{1,9},{9,13},{13,5},{5,1},{2,10},{10,14}... | collective-permute-start | bytes 1572872 | tf_op jit(solution)/shard_map/ppermute | solution.py:143
  4.0 30.9 %collective-permute-start.3 = (f32[16,8192]{1,0:T(8,128)}, f32[16,8192]{1,0:T(8,128)S(1)}, u32[]{:S(2)}, u32[]{:S(2)}) collective-permute-start(f32[16,8192]{1,0:T(8,128)} %refs_0_.1), channel_id=1, source_target_pairs={{8,0},{12,8},{4,12},{0,4},{9,1},{13,9},{5,13},{1,5},{10,2},{14,10}... | collective-permute-start | bytes 1572872 | tf_op jit(solution)/shard_map/ppermute | solution.py:154
  16.8 11.3 %copy-start.6 = (f32[16,8192]{1,0:T(8,128)S(1)}, f32[16,8192]{1,0:T(8,128)}, u32[]{:S(2)}) copy-start(f32[16,8192]{1,0:T(8,128)} %refs_0_.1) | copy-start | bytes 1572868
  16.8 24.4 %collective-permute-start.1 = (f32[16,6144]{1,0:T(8,128)S(1)}, f32[16,6144]{1,0:T(8,128)S(1)}, u32[]{:S(2)}, u32[]{:S(2)}) collective-permute-start(f32[16,6144]{1,0:T(8,128)S(1)} %slice.8), channel_id=1, source_target_pairs={{0,8},{8,12},{12,4},{4,0},{1,9},{9,13},{13,5},{5,1},{2,10},{10,14}... | collective-permute-start | bytes 1179656 | tf_op jit(solution)/shard_map/ppermute | solution.py:157
  28.1 2.2 %copy-start = (bf16[8192,256]{1,0:T(8,128)(2,1)S(1)}, bf16[8192,256]{1,0:T(8,128)(2,1)}, u32[]{:S(2)}) copy-start(bf16[8192,256]{1,0:T(8,128)(2,1)} %get-tuple-element.35.refs_3_.refs_2_.low) | copy-start | bytes 12582916
  30.3 2.2 %copy-start.3 = (bf16[8192,256]{1,0:T(8,128)(2,1)S(1)}, bf16[8192,256]{1,0:T(8,128)(2,1)}, u32[]{:S(2)}) copy-start(bf16[8192,256]{1,0:T(8,128)(2,1)} %get-tuple-element.36.refs_2_.refs_1_.high) | copy-start | bytes 12582916
  34.6 9.6 %collective-permute-start.2 = (f32[16,2048]{1,0:T(8,128)S(1)}, f32[16,2048]{1,0:T(8,128)S(1)}, u32[]{:S(2)}, u32[]{:S(2)}) collective-permute-start(f32[16,2048]{1,0:T(8,128)S(1)} %slice.7), channel_id=1, source_target_pairs={{0,8},{8,12},{12,4},{4,0},{1,9},{9,13},{13,5},{5,1},{2,10},{10,14}... | collective-permute-start | bytes 393224 | tf_op jit(solution)/shard_map/ppermute | solution.py:161
  34.9 2.2 %copy-start.1 = (bf16[8192,256]{1,0:T(8,128)(2,1)S(1)}, bf16[8192,256]{1,0:T(8,128)(2,1)}, u32[]{:S(2)}) copy-start(bf16[8192,256]{1,0:T(8,128)(2,1)} %get-tuple-element.35.refs_3_.refs_2_.low) | copy-start | bytes 12582916
  37.1 2.2 %copy-start.4 = (bf16[8192,256]{1,0:T(8,128)(2,1)S(1)}, bf16[8192,256]{1,0:T(8,128)(2,1)}, u32[]{:S(2)}) copy-start(bf16[8192,256]{1,0:T(8,128)(2,1)} %get-tuple-element.36.refs_2_.refs_1_.high) | copy-start | bytes 12582916
  39.3 2.2 %copy-start.2 = (bf16[8192,256]{1,0:T(8,128)(2,1)S(1)}, bf16[8192,256]{1,0:T(8,128)(2,1)}, u32[]{:S(2)}) copy-start(bf16[8192,256]{1,0:T(8,128)(2,1)} %get-tuple-element.35.refs_3_.refs_2_.low) | copy-start | bytes 12582916
  39.3 3.5 %copy-start.5 = (bf16[8192,256]{1,0:T(8,128)(2,1)S(1)}, bf16[8192,256]{1,0:T(8,128)(2,1)}, u32[]{:S(2)}) copy-start(bf16[8192,256]{1,0:T(8,128)(2,1)} %get-tuple-element.36.refs_2_.refs_1_.high) | copy-start | bytes 12582916
  44.7 1.9 %collective-permute-start.6 = (f32[16,256]{1,0:T(8,128)S(1)}, f32[16,256]{1,0:T(8,128)S(1)}, u32[]{:S(2)}, u32[]{:S(2)}) collective-permute-start(f32[16,256]{1,0:T(8,128)S(1)} %get-tuple-element.34), channel_id=1, source_target_pairs={{0,1},{1,0},{2,3},{3,2},{4,5},{5,4},{6,7},{7,6},{8,9},{9,8},{10,11... | collective-permute-start | bytes 49160 | tf_op jit(solution)/shard_map/ppermute | solution.py:184
  44.7 3.8 %collective-permute-start.5 = (f32[16,256]{1,0:T(8,128)S(1)}, f32[16,256]{1,0:T(8,128)S(1)}, u32[]{:S(2)}, u32[]{:S(2)}) collective-permute-start(f32[16,256]{1,0:T(8,128)S(1)} %get-tuple-element.33), channel_id=1, source_target_pairs={{0,2},{1,3},{2,0},{3,1},{4,6},{5,7},{6,4},{7,5},{8,10},{9,11},{10,... | collective-permute-start | bytes 49160 | tf_op jit(solution)/shard_map/ppermute | solution.py:184
  46.3 3.2 %collective-permute-start.4 = (f32[16,256]{1,0:T(8,128)S(1)}, f32[16,256]{1,0:T(8,128)S(1)}, u32[]{:S(2)}, u32[]{:S(2)}) collective-permute-start(f32[16,256]{1,0:T(8,128)S(1)} %get-tuple-element.32), channel_id=1, source_target_pairs={{0,3},{1,2},{2,1},{3,0},{4,7},{5,6},{6,5},{7,4},{8,11},{9,10},{10,... | collective-permute-start | bytes 49160 | tf_op jit(solution)/shard_map/ppermute | solution.py:184

commit v18 on v13

--- a/solution.py
+++ b/solution.py
@@ -74,6 +74,14 @@
             out[span] = shares[o][span] + jnp.where(masks[o, span] != 0, total, 0.0)
 
 
+def final_kernel(diagonal, *refs):
+    *terms, out = refs
+    moved = sum_of([term[...] for term in terms])
+    limit = step_size * penalty
+    shrunk = jnp.maximum(moved - limit, 0.0) + jnp.minimum(moved + limit, 0.0)
+    out[...] = jnp.where(diagonal[...] != 0, moved, shrunk)
+
+
 def call(kernel, count, shape, scalars, arrays, limit):
     return pl.pallas_call(
         kernel,
@@ -173,7 +181,9 @@
         (row_spots == spots[-1]).astype(jnp.int32).reshape(rep_count, rows_share, 1),
         (rep_count, rows_share, tile_width),
     )
-    last_left, masks = lax.optimization_barrier((last_left, masks))
+    global_rows = rep_index * rows_share + jnp.arange(rows_share, dtype=jnp.int32)
+    diagonal = (global_rows[:, None] == c_ids[None, :]).astype(jnp.int32)
+    last_left, masks, diagonal = lax.optimization_barrier((last_left, masks, diagonal))
     shares = products_of([last_left], sources[-1:], spots, parts)
     kernel = functools.partial(last_kernel, cut)
     arrays = [masks, last_right, *weights, *shares]
@@ -182,13 +192,8 @@
     for flip in range(rep_count - 1, 0, -1):
         pairs = [(d, d ^ flip) for d in range(rep_count)]
         terms.append(lax.ppermute(shares[flip], "rep", pairs))
-    moved = sum_of(terms)
-
-    global_rows = rep_index * rows_share + jnp.arange(rows_share, dtype=jnp.int32)
-    global_cols = offset + jnp.arange(tile_width, dtype=jnp.int32)
-    diagonal = global_rows[:, None] == global_cols[None, :]
-    shrunk = jnp.sign(moved) * jnp.maximum(jnp.abs(moved) - step_size * penalty, 0.0)
-    return jnp.where(diagonal, moved, shrunk)
+    arrays = [diagonal, *terms]
+    return call(final_kernel, 1, (rows_share, tile_width), [], arrays, 2 + rep_count)[0]
 
 
 def solution(mesh):

time: 45.4 us -> 45.3 us (level)
  Pallas kernels: 5.83 us -> 6.45 us
  other arithmetic: 8.84 us -> 8.23 us
    select_n x1 -> x0, other arithmetic: 0.68 us -> none  [per_device(): return jnp.where(diagonal, moved, shrunk)]
    pallas_call x4 -> x5, Pallas kernels: 5.83 us -> 6.45 us  [call(): pl.pallas_call(kernel, out_shape=[jax.ShapeDtypeStruct(shape, jnp.float32...]
where the time goes in v18:
time: 45.3 us; the launch traced here: 45 us
  waiting for transfers between devices  10.8 us (24%)
  starting transfers between devices  9.39 us (21%)
  local copies, waits for them, and re-layouts  9.34 us (21%)
  other arithmetic  8.23 us (18%)
  Pallas kernels  6.45 us (14%)
  between operations  0.75 us (2%)
    unnamed x14, local copies, waits for them, and re-layouts  9.15 us
    convert_element_type x1, other arithmetic, halves(): return (high.astype(jnp.bfloat16), (array - high).astype(jnp.bfloat16))  7.98 us
    pallas_call x5, Pallas kernels, call(): pl.pallas_call(kernel, out_shape=[jax.ShapeDtypeStruct(shape, jnp.float32...  6.45 us
    ppermute x1, starting transfers between devices, per_device(): first = lax.ppermute(omega_rows, 'team', onward)  4.04 us
    ppermute x1, waiting for transfers between devices, per_device(): first = lax.ppermute(omega_rows, 'team', onward)  3.94 us
    ppermute x1, starting transfers between devices, per_device(): last_left = lax.ppermute(last_held[:, :cut], 'team', onward)  3.33 us
    ppermute x1, waiting for transfers between devices, per_device(): held = lax.ppermute(held, 'team', backward)  2.7 us
    ppermute x3, waiting for transfers between devices, per_device(): terms.append(lax.ppermute(shares[flip], 'rep', pairs))  2.69 us
  transfers between devices with their start and end apart: 7, of which 6 were waited for; matrix products, arithmetic and copies ran while one was open for 19% of the time, Pallas kernels for 12%

profile of v18, /device:TPU:0, one launch (start us, length us, event | category | flops | bytes accessed | tf_op | source)
XLA Modules:
  0.0 45.0 jit_solution(6030591137930947836)
XLA Ops:
  0.0 4.0 %collective-permute-start = (f32[16,8192]{1,0:T(8,128)}, f32[16,8192]{1,0:T(8,128)S(1)}, u32[]{:S(2)}, u32[]{:S(2)}) collective-permute-start(f32[16,8192]{1,0:T(8,128)} %refs_0_), channel_id=1, source_target_pairs={{0,8},{8,12},{12,4},{4,0},{1,9},{9,13},{13,5},{5,1},{2,10},{10,14}... | collective-permute-start | bytes 1572872 | tf_op jit(solution)/shard_map/ppermute | solution.py:151
  4.7 0.0 copy-start.6
  4.7 8.0 %subtract_convert_fusion = (bf16[8192,256]{1,0:T(8,128)(2,1)}, bf16[8192,256]{1,0:T(8,128)(2,1)}) fusion(f32[8192,256]{1,0:T(8,128)} %param.4, s32[256]{0:T(256)S(1)} %iota_add_fusion.1, s32[8192]{0:T(1024)S(1)} %iota_add_fusion), kind=kLoop, calls=%fused_computation | loop fusion | flops 18874368 | bytes 16811008 | tf_op jit(solution)/shard_map/convert_element_type | solution.py:17
  12.7 0.0 copy-done.6
  12.7 0.0 collective-permute-start.3
  12.7 3.9 %collective-permute-done.refs_1_ = f32[16,8192]{1,0:T(8,128)S(1)} collective-permute-done((f32[16,8192]{1,0:T(8,128)}, f32[16,8192]{1,0:T(8,128)S(1)}, u32[]{:S(2)}, u32[]{:S(2)}) %collective-permute-start) | collective-permute-done | bytes 524320 | tf_op jit(solution)/shard_map/ppermute | solution.py:151
  16.7 3.3 %collective-permute-start.1 = (f32[16,6144]{1,0:T(8,128)S(1)}, f32[16,6144]{1,0:T(8,128)S(1)}, u32[]{:S(2)}, u32[]{:S(2)}) collective-permute-start(f32[16,6144]{1,0:T(8,128)S(1)} %slice.8), channel_id=1, source_target_pairs={{0,8},{8,12},{12,4},{4,0},{1,9},{9,13},{13,5},{5,1},{2,10},{10,14}... | collective-permute-start | bytes 1179656 | tf_op jit(solution)/shard_map/ppermute | solution.py:165
  20.0 0.1 compare_convert_fusion.diagonal
  20.1 0.1 pad_add_fusion.places
  20.2 0.0 copy-start
  20.2 2.2 %copy-done = bf16[8192,256]{1,0:T(8,128)(2,1)S(1)} copy-done((bf16[8192,256]{1,0:T(8,128)(2,1)S(1)}, bf16[8192,256]{1,0:T(8,128)(2,1)}, u32[]{:S(2)}) %copy-start) | copy-done | bytes 4194328
  22.4 0.0 copy-start.3
  22.4 2.2 %copy-done.3 = bf16[8192,256]{1,0:T(8,128)(2,1)S(1)} copy-done((bf16[8192,256]{1,0:T(8,128)(2,1)S(1)}, bf16[8192,256]{1,0:T(8,128)(2,1)}, u32[]{:S(2)}) %copy-start.3) | copy-done | bytes 4194328
  24.6 2.1 %shard_map.37 = (f32[16,256]{1,0:T(8,128)S(1)}, f32[16,256]{1,0:T(8,128)S(1)}) custom-call(s32[3]{0:T(128)S(1)} %pad_add_fusion.places, f32[16,8192]{1,0:T(8,128)S(1)} %copy-done.6, f32[16,8192]{1,0:T(8,128)S(1)} %collective-permute-done.refs_1_, bf16[8192,256]{1,0:T(8,128)(2,1)S(1)} %copy-done.3, bf16[8192,256]{1,0:T(8,128)(2,1)S(1)} %copy-done), custom_call_target="tpu_custom_call" | custom-call | bytes 32768 | tf_op jit(solution)/shard_map/pallas_call | solution.py:86
  26.7 0.1 collective-permute-start.2
  26.8 0.1 pad_add_fusion.1.places
  26.9 0.1 stack.47.places
  27.0 2.7 %collective-permute-done.3.refs_0_ = f32[16,8192]{1,0:T(8,128)S(1)} collective-permute-done((f32[16,8192]{1,0:T(8,128)S(1)}, f32[16,8192]{1,0:T(8,128)S(1)}, u32[]{:S(2)}, u32[]{:S(2)}) %collective-permute-start.3) | collective-permute-done | bytes 524320 | tf_op jit(solution)/shard_map/ppermute | solution.py:162
  29.7 0.0 copy-start.1
  29.7 2.2 %copy-done.1 = bf16[8192,256]{1,0:T(8,128)(2,1)S(1)} copy-done((bf16[8192,256]{1,0:T(8,128)(2,1)S(1)}, bf16[8192,256]{1,0:T(8,128)(2,1)}, u32[]{:S(2)}) %copy-start.1) | copy-done | bytes 4194328
  31.9 0.0 copy-start.4
  31.9 2.2 %copy-done.4 = bf16[8192,256]{1,0:T(8,128)(2,1)S(1)} copy-done((bf16[8192,256]{1,0:T(8,128)(2,1)S(1)}, bf16[8192,256]{1,0:T(8,128)(2,1)}, u32[]{:S(2)}) %copy-start.4) | copy-done | bytes 4194328
  34.1 0.0 copy-start.2
  34.1 0.0 copy-start.5
  34.1 1.9 %shard_map.38.refs_5_ = f32[16,256]{1,0:T(8,128)S(1)} custom-call(s32[2]{0:T(128)S(1)} %pad_add_fusion.1.places, f32[16,8192]{1,0:T(8,128)S(1)} %collective-permute-done.3.refs_0_, bf16[8192,256]{1,0:T(8,128)(2,1)S(1)} %copy-done.4, bf16[8192,256]{1,0:T(8,128)(2,1)S(1)} %copy-done.1), custom_call_target="tpu_custom_call" | custom-call | bytes 16384 | tf_op jit(solution)/shard_map/pallas_call | solution.py:86
  35.9 1.1 %collective-permute-done.1.refs_0_ = f32[16,6144]{1,0:T(8,128)S(1)} collective-permute-done((f32[16,6144]{1,0:T(8,128)S(1)}, f32[16,6144]{1,0:T(8,128)S(1)}, u32[]{:S(2)}, u32[]{:S(2)}) %collective-permute-start.1) | collective-permute-done | bytes 393248 | tf_op jit(solution)/shard_map/ppermute | solution.py:165
  37.1 0.1 broadcast_in_dim.2.masks
  37.1 0.0 copy-done.2
  37.1 0.4 copy-done.5
  37.5 1.5 %shard_map.39 = (f32[16,256]{1,0:T(8,128)S(1)}, f32[16,256]{1,0:T(8,128)S(1)}, f32[16,256]{1,0:T(8,128)S(1)}, f32[16,256]{1,0:T(8,128)S(1)}) custom-call(s32[6]{0:T(128)S(1)} %stack.47.places, f32[16,6144]{1,0:T(8,128)S(1)} %collective-permute-done.1.refs_0_, bf16[8192,256]{1,0:T(8,128)(2,1)S(1)} %copy-done.5, bf16[8192,256]{1,0:T(8,128)(2,1)S(1)} %copy-done.2, ...), custom_call_target="tpu_custom_call" | custom-call | bytes 65536 | tf_op jit(solution)/shard_map/pallas_call | solution.py:86
  39.0 0.4 collective-permute-done.2.block
  39.4 0.4 shard_map.40
  39.8 0.8 %collective-permute-start.4 = (f32[16,256]{1,0:T(8,128)S(1)}, f32[16,256]{1,0:T(8,128)S(1)}, u32[]{:S(2)}, u32[]{:S(2)}) collective-permute-start(f32[16,256]{1,0:T(8,128)S(1)} %get-tuple-element.40), channel_id=1, source_target_pairs={{0,3},{1,2},{2,1},{3,0},{4,7},{5,6},{6,5},{7,4},{8,11},{9,10},{10,... | collective-permute-start | bytes 49160 | tf_op jit(solution)/shard_map/ppermute | solution.py:194
  40.5 0.9 %collective-permute-start.5 = (f32[16,256]{1,0:T(8,128)S(1)}, f32[16,256]{1,0:T(8,128)S(1)}, u32[]{:S(2)}, u32[]{:S(2)}) collective-permute-start(f32[16,256]{1,0:T(8,128)S(1)} %get-tuple-element.41), channel_id=1, source_target_pairs={{0,2},{1,3},{2,0},{3,1},{4,6},{5,7},{6,4},{7,5},{8,10},{9,11},{10,... | collective-permute-start | bytes 49160 | tf_op jit(solution)/shard_map/ppermute | solution.py:194
  41.4 0.3 collective-permute-start.6
  41.7 1.4 %collective-permute-done.4.refs_1_ = f32[16,256]{1,0:T(8,128)S(1)} collective-permute-done((f32[16,256]{1,0:T(8,128)S(1)}, f32[16,256]{1,0:T(8,128)S(1)}, u32[]{:S(2)}, u32[]{:S(2)}) %collective-permute-start.4) | collective-permute-done | bytes 16416 | tf_op jit(solution)/shard_map/ppermute | solution.py:194
  43.1 1.3 %collective-permute-done.5.refs_2_ = f32[16,256]{1,0:T(8,128)S(1)} collective-permute-done((f32[16,256]{1,0:T(8,128)S(1)}, f32[16,256]{1,0:T(8,128)S(1)}, u32[]{:S(2)}, u32[]{:S(2)}) %collective-permute-start.5) | collective-permute-done | bytes 16416 | tf_op jit(solution)/shard_map/ppermute | solution.py:194
  44.4 0.0 collective-permute-done.6.refs_3_
  44.4 0.6 %shard_map.41 = f32[16,256]{1,0:T(8,128)} custom-call(s32[16,256]{1,0:T(8,128)S(1)} %compare_convert_fusion.diagonal, f32[16,256]{1,0:T(8,128)S(1)} %get-tuple-element.39.refs_0_, f32[16,256]{1,0:T(8,128)S(1)} %collective-permute-done.4.refs_1_, f32[16,256]{1,0:T(8,128)S(1)} %collective-permute-done.5.refs_2_, f32[16,256]{1,0:T(8,128)S(1)} %collective-permute-done.6.refs_3_), custom_call_target="tpu_custom_call" | custom-call | bytes 16384 | tf_op jit(solution)/shard_map/pallas_call | solution.py:86
  (6 shorter events, 0.1 us)
Async XLA Ops:
  0.0 16.7 %collective-permute-start = (f32[16,8192]{1,0:T(8,128)}, f32[16,8192]{1,0:T(8,128)S(1)}, u32[]{:S(2)}, u32[]{:S(2)}) collective-permute-start(f32[16,8192]{1,0:T(8,128)} %refs_0_), channel_id=1, source_target_pairs={{0,8},{8,12},{12,4},{4,0},{1,9},{9,13},{13,5},{5,1},{2,10},{10,14}... | collective-permute-start | bytes 1572872 | tf_op jit(solution)/shard_map/ppermute | solution.py:151
  4.7 8.0 %copy-start.6 = (f32[16,8192]{1,0:T(8,128)S(1)}, f32[16,8192]{1,0:T(8,128)}, u32[]{:S(2)}) copy-start(f32[16,8192]{1,0:T(8,128)} %refs_0_) | copy-start | bytes 1572868
  12.7 17.0 %collective-permute-start.3 = (f32[16,8192]{1,0:T(8,128)S(1)}, f32[16,8192]{1,0:T(8,128)S(1)}, u32[]{:S(2)}, u32[]{:S(2)}) collective-permute-start(f32[16,8192]{1,0:T(8,128)S(1)} %copy-done.6), channel_id=1, source_target_pairs={{8,0},{12,8},{4,12},{0,4},{9,1},{13,9},{5,13},{1,5},{10,2},{14,10}... | collective-permute-start | bytes 1572872 | tf_op jit(solution)/shard_map/ppermute | solution.py:162
  16.7 20.3 %collective-permute-start.1 = (f32[16,6144]{1,0:T(8,128)S(1)}, f32[16,6144]{1,0:T(8,128)S(1)}, u32[]{:S(2)}, u32[]{:S(2)}) collective-permute-start(f32[16,6144]{1,0:T(8,128)S(1)} %slice.8), channel_id=1, source_target_pairs={{0,8},{8,12},{12,4},{4,0},{1,9},{9,13},{13,5},{5,1},{2,10},{10,14}... | collective-permute-start | bytes 1179656 | tf_op jit(solution)/shard_map/ppermute | solution.py:165
  20.2 2.2 %copy-start = (bf16[8192,256]{1,0:T(8,128)(2,1)S(1)}, bf16[8192,256]{1,0:T(8,128)(2,1)}, u32[]{:S(2)}) copy-start(bf16[8192,256]{1,0:T(8,128)(2,1)} %get-tuple-element.28.refs_3_.refs_2_.low) | copy-start | bytes 12582916
  22.4 2.2 %copy-start.3 = (bf16[8192,256]{1,0:T(8,128)(2,1)S(1)}, bf16[8192,256]{1,0:T(8,128)(2,1)}, u32[]{:S(2)}) copy-start(bf16[8192,256]{1,0:T(8,128)(2,1)} %get-tuple-element.27.refs_2_.refs_1_.high) | copy-start | bytes 12582916
  26.7 12.7 %collective-permute-start.2 = (f32[16,2048]{1,0:T(8,128)S(1)}, f32[16,2048]{1,0:T(8,128)S(1)}, u32[]{:S(2)}, u32[]{:S(2)}) collective-permute-start(f32[16,2048]{1,0:T(8,128)S(1)} %slice.7), channel_id=1, source_target_pairs={{0,8},{8,12},{12,4},{4,0},{1,9},{9,13},{13,5},{5,1},{2,10},{10,14}... | collective-permute-start | bytes 393224 | tf_op jit(solution)/shard_map/ppermute | solution.py:169
  29.7 2.2 %copy-start.1 = (bf16[8192,256]{1,0:T(8,128)(2,1)S(1)}, bf16[8192,256]{1,0:T(8,128)(2,1)}, u32[]{:S(2)}) copy-start(bf16[8192,256]{1,0:T(8,128)(2,1)} %get-tuple-element.28.refs_3_.refs_2_.low) | copy-start | bytes 12582916
  31.9 2.2 %copy-start.4 = (bf16[8192,256]{1,0:T(8,128)(2,1)S(1)}, bf16[8192,256]{1,0:T(8,128)(2,1)}, u32[]{:S(2)}) copy-start(bf16[8192,256]{1,0:T(8,128)(2,1)} %get-tuple-element.27.refs_2_.refs_1_.high) | copy-start | bytes 12582916
  34.1 3.1 %copy-start.2 = (bf16[8192,256]{1,0:T(8,128)(2,1)S(1)}, bf16[8192,256]{1,0:T(8,128)(2,1)}, u32[]{:S(2)}) copy-start(bf16[8192,256]{1,0:T(8,128)(2,1)} %get-tuple-element.28.refs_3_.refs_2_.low) | copy-start | bytes 12582916
  34.1 3.5 %copy-start.5 = (bf16[8192,256]{1,0:T(8,128)(2,1)S(1)}, bf16[8192,256]{1,0:T(8,128)(2,1)}, u32[]{:S(2)}) copy-start(bf16[8192,256]{1,0:T(8,128)(2,1)} %get-tuple-element.27.refs_2_.refs_1_.high) | copy-start | bytes 12582916
  39.8 3.4 %collective-permute-start.4 = (f32[16,256]{1,0:T(8,128)S(1)}, f32[16,256]{1,0:T(8,128)S(1)}, u32[]{:S(2)}, u32[]{:S(2)}) collective-permute-start(f32[16,256]{1,0:T(8,128)S(1)} %get-tuple-element.40), channel_id=1, source_target_pairs={{0,3},{1,2},{2,1},{3,0},{4,7},{5,6},{6,5},{7,4},{8,11},{9,10},{10,... | collective-permute-start | bytes 49160 | tf_op jit(solution)/shard_map/ppermute | solution.py:194
  40.5 3.9 %collective-permute-start.5 = (f32[16,256]{1,0:T(8,128)S(1)}, f32[16,256]{1,0:T(8,128)S(1)}, u32[]{:S(2)}, u32[]{:S(2)}) collective-permute-start(f32[16,256]{1,0:T(8,128)S(1)} %get-tuple-element.41), channel_id=1, source_target_pairs={{0,2},{1,3},{2,0},{3,1},{4,6},{5,7},{6,4},{7,5},{8,10},{9,11},{10,... | collective-permute-start | bytes 49160 | tf_op jit(solution)/shard_map/ppermute | solution.py:194
  41.4 3.0 %collective-permute-start.6 = (f32[16,256]{1,0:T(8,128)S(1)}, f32[16,256]{1,0:T(8,128)S(1)}, u32[]{:S(2)}, u32[]{:S(2)}) collective-permute-start(f32[16,256]{1,0:T(8,128)S(1)} %get-tuple-element.42), channel_id=1, source_target_pairs={{0,1},{1,0},{2,3},{3,2},{4,5},{5,4},{6,7},{7,6},{8,9},{9,8},{10,11... | collective-permute-start | bytes 49160 | tf_op jit(solution)/shard_map/ppermute | solution.py:194

commit v19 on v18

--- a/solution.py
+++ b/solution.py
@@ -149,7 +149,8 @@
         return jnp.where(up < team_count, up, 2 * team_count - 1 - up)
 
     first = lax.ppermute(omega_rows, "team", onward)
-    own, *weights = lax.optimization_barrier((omega_rows, *weights))
+    own = omega_rows
+    first, *weights = lax.optimization_barrier((first, *weights))
     last_step = team_count // 2
     gathered = []
     held = first

time: 45.3 us -> 45.3 us (level)
  no operation moved by 1% of the time
where the time goes in v19:
time: 45.3 us; the launch traced here: 45 us
  waiting for transfers between devices  10.9 us (24%)
  starting transfers between devices  9.39 us (21%)
  local copies, waits for them, and re-layouts  9.33 us (21%)
  other arithmetic  8.23 us (18%)
  Pallas kernels  6.45 us (14%)
  between operations  0.73 us (2%)
    unnamed x14, local copies, waits for them, and re-layouts  9.14 us
    convert_element_type x1, other arithmetic, halves(): return (high.astype(jnp.bfloat16), (array - high).astype(jnp.bfloat16))  7.98 us
    pallas_call x5, Pallas kernels, call(): pl.pallas_call(kernel, out_shape=[jax.ShapeDtypeStruct(shape, jnp.float32...  6.45 us
    ppermute x1, starting transfers between devices, per_device(): first = lax.ppermute(omega_rows, 'team', onward)  4.04 us
    ppermute x1, waiting for transfers between devices, per_device(): first = lax.ppermute(omega_rows, 'team', onward)  4 us
    ppermute x1, starting transfers between devices, per_device(): last_left = lax.ppermute(last_held[:, :cut], 'team', onward)  3.33 us
    ppermute x3, waiting for transfers between devices, per_device(): terms.append(lax.ppermute(shares[flip], 'rep', pairs))  2.69 us
    ppermute x1, waiting for transfers between devices, per_device(): held = lax.ppermute(held, 'team', backward)  2.65 us
  transfers between devices with their start and end apart: 7, of which 6 were waited for; matrix products, arithmetic and copies ran while one was open for 19% of the time, Pallas kernels for 12%

profile of v19, /device:TPU:0, one launch (start us, length us, event | category | flops | bytes accessed | tf_op | source)
XLA Modules:
  0.0 45.0 jit_solution(17372281271740136367)
XLA Ops:
  0.0 4.0 %collective-permute-start = (f32[16,8192]{1,0:T(8,128)}, f32[16,8192]{1,0:T(8,128)S(1)}, u32[]{:S(2)}, u32[]{:S(2)}) collective-permute-start(f32[16,8192]{1,0:T(8,128)} %refs_0_.1), channel_id=1, source_target_pairs={{0,8},{8,12},{12,4},{4,0},{1,9},{9,13},{13,5},{5,1},{2,10},{10,14}... | collective-permute-start | bytes 1572872 | tf_op jit(solution)/shard_map/ppermute | solution.py:151
  4.0 0.0 collective-permute-start.3
  4.7 0.0 copy-start.6
  4.7 8.0 %subtract_convert_fusion = (bf16[8192,256]{1,0:T(8,128)(2,1)}, bf16[8192,256]{1,0:T(8,128)(2,1)}) fusion(f32[8192,256]{1,0:T(8,128)} %param.4, s32[256]{0:T(256)S(1)} %iota_add_fusion.1, s32[8192]{0:T(1024)S(1)} %iota_add_fusion), kind=kLoop, calls=%fused_computation | loop fusion | flops 18874368 | bytes 16811008 | tf_op jit(solution)/shard_map/convert_element_type | solution.py:17
  12.7 4.0 %collective-permute-done.refs_1_ = f32[16,8192]{1,0:T(8,128)S(1)} collective-permute-done((f32[16,8192]{1,0:T(8,128)}, f32[16,8192]{1,0:T(8,128)S(1)}, u32[]{:S(2)}, u32[]{:S(2)}) %collective-permute-start) | collective-permute-done | bytes 524320 | tf_op jit(solution)/shard_map/ppermute | solution.py:151
  16.8 3.3 %collective-permute-start.1 = (f32[16,6144]{1,0:T(8,128)S(1)}, f32[16,6144]{1,0:T(8,128)S(1)}, u32[]{:S(2)}, u32[]{:S(2)}) collective-permute-start(f32[16,6144]{1,0:T(8,128)S(1)} %slice.6), channel_id=1, source_target_pairs={{0,8},{8,12},{12,4},{4,0},{1,9},{9,13},{13,5},{5,1},{2,10},{10,14}... | collective-permute-start | bytes 1179656 | tf_op jit(solution)/shard_map/ppermute | solution.py:166
  20.1 0.1 compare_convert_fusion.diagonal
  20.2 0.1 pad_add_fusion.places
  20.2 0.0 copy-done.6
  20.2 0.0 copy-start
  20.2 2.2 %copy-done = bf16[8192,256]{1,0:T(8,128)(2,1)S(1)} copy-done((bf16[8192,256]{1,0:T(8,128)(2,1)S(1)}, bf16[8192,256]{1,0:T(8,128)(2,1)}, u32[]{:S(2)}) %copy-start) | copy-done | bytes 4194328
  22.4 0.0 copy-start.3
  22.4 2.2 %copy-done.3 = bf16[8192,256]{1,0:T(8,128)(2,1)S(1)} copy-done((bf16[8192,256]{1,0:T(8,128)(2,1)S(1)}, bf16[8192,256]{1,0:T(8,128)(2,1)}, u32[]{:S(2)}) %copy-start.3) | copy-done | bytes 4194328
  24.6 2.1 %shard_map.37 = (f32[16,256]{1,0:T(8,128)S(1)}, f32[16,256]{1,0:T(8,128)S(1)}) custom-call(s32[3]{0:T(128)S(1)} %pad_add_fusion.places, f32[16,8192]{1,0:T(8,128)S(1)} %copy-done.6, f32[16,8192]{1,0:T(8,128)S(1)} %collective-permute-done.refs_1_, bf16[8192,256]{1,0:T(8,128)(2,1)S(1)} %copy-done.3, bf16[8192,256]{1,0:T(8,128)(2,1)S(1)} %copy-done), custom_call_target="tpu_custom_call" | custom-call | bytes 32768 | tf_op jit(solution)/shard_map/pallas_call | solution.py:86
  26.7 0.1 collective-permute-start.2
  26.8 0.1 pad_add_fusion.1.places
  26.9 0.1 stack.47.places
  27.0 2.6 %collective-permute-done.3.refs_0_ = f32[16,8192]{1,0:T(8,128)S(1)} collective-permute-done((f32[16,8192]{1,0:T(8,128)}, f32[16,8192]{1,0:T(8,128)S(1)}, u32[]{:S(2)}, u32[]{:S(2)}) %collective-permute-start.3) | collective-permute-done | bytes 524320 | tf_op jit(solution)/shard_map/ppermute | solution.py:163
  29.7 0.0 copy-start.1
  29.7 2.2 %copy-done.1 = bf16[8192,256]{1,0:T(8,128)(2,1)S(1)} copy-done((bf16[8192,256]{1,0:T(8,128)(2,1)S(1)}, bf16[8192,256]{1,0:T(8,128)(2,1)}, u32[]{:S(2)}) %copy-start.1) | copy-done | bytes 4194328
  31.9 0.0 copy-start.4
  31.9 2.2 %copy-done.4 = bf16[8192,256]{1,0:T(8,128)(2,1)S(1)} copy-done((bf16[8192,256]{1,0:T(8,128)(2,1)S(1)}, bf16[8192,256]{1,0:T(8,128)(2,1)}, u32[]{:S(2)}) %copy-start.4) | copy-done | bytes 4194328
  34.0 0.0 copy-start.2
  34.0 0.0 copy-start.5
  34.0 1.9 %shard_map.38.refs_5_ = f32[16,256]{1,0:T(8,128)S(1)} custom-call(s32[2]{0:T(128)S(1)} %pad_add_fusion.1.places, f32[16,8192]{1,0:T(8,128)S(1)} %collective-permute-done.3.refs_0_, bf16[8192,256]{1,0:T(8,128)(2,1)S(1)} %copy-done.4, bf16[8192,256]{1,0:T(8,128)(2,1)S(1)} %copy-done.1), custom_call_target="tpu_custom_call" | custom-call | bytes 16384 | tf_op jit(solution)/shard_map/pallas_call | solution.py:86
  35.9 1.2 %collective-permute-done.1.refs_0_ = f32[16,6144]{1,0:T(8,128)S(1)} collective-permute-done((f32[16,6144]{1,0:T(8,128)S(1)}, f32[16,6144]{1,0:T(8,128)S(1)}, u32[]{:S(2)}, u32[]{:S(2)}) %collective-permute-start.1) | collective-permute-done | bytes 393248 | tf_op jit(solution)/shard_map/ppermute | solution.py:166
  37.1 0.1 broadcast_in_dim.2.masks
  37.1 0.0 copy-done.2
  37.1 0.4 copy-done.5
  37.5 1.5 %shard_map.39 = (f32[16,256]{1,0:T(8,128)S(1)}, f32[16,256]{1,0:T(8,128)S(1)}, f32[16,256]{1,0:T(8,128)S(1)}, f32[16,256]{1,0:T(8,128)S(1)}) custom-call(s32[6]{0:T(128)S(1)} %stack.47.places, f32[16,6144]{1,0:T(8,128)S(1)} %collective-permute-done.1.refs_0_, bf16[8192,256]{1,0:T(8,128)(2,1)S(1)} %copy-done.5, bf16[8192,256]{1,0:T(8,128)(2,1)S(1)} %copy-done.2, ...), custom_call_target="tpu_custom_call" | custom-call | bytes 65536 | tf_op jit(solution)/shard_map/pallas_call | solution.py:86
  39.0 0.4 collective-permute-done.2.block
  39.4 0.4 shard_map.40
  39.8 0.8 %collective-permute-start.4 = (f32[16,256]{1,0:T(8,128)S(1)}, f32[16,256]{1,0:T(8,128)S(1)}, u32[]{:S(2)}, u32[]{:S(2)}) collective-permute-start(f32[16,256]{1,0:T(8,128)S(1)} %get-tuple-element.40), channel_id=1, source_target_pairs={{0,3},{1,2},{2,1},{3,0},{4,7},{5,6},{6,5},{7,4},{8,11},{9,10},{10,... | collective-permute-start | bytes 49160 | tf_op jit(solution)/shard_map/ppermute | solution.py:195
  40.5 0.9 %collective-permute-start.5 = (f32[16,256]{1,0:T(8,128)S(1)}, f32[16,256]{1,0:T(8,128)S(1)}, u32[]{:S(2)}, u32[]{:S(2)}) collective-permute-start(f32[16,256]{1,0:T(8,128)S(1)} %get-tuple-element.41), channel_id=1, source_target_pairs={{0,2},{1,3},{2,0},{3,1},{4,6},{5,7},{6,4},{7,5},{8,10},{9,11},{10,... | collective-permute-start | bytes 49160 | tf_op jit(solution)/shard_map/ppermute | solution.py:195
  41.4 0.3 collective-permute-start.6
  41.7 1.4 %collective-permute-done.4.refs_1_ = f32[16,256]{1,0:T(8,128)S(1)} collective-permute-done((f32[16,256]{1,0:T(8,128)S(1)}, f32[16,256]{1,0:T(8,128)S(1)}, u32[]{:S(2)}, u32[]{:S(2)}) %collective-permute-start.4) | collective-permute-done | bytes 16416 | tf_op jit(solution)/shard_map/ppermute | solution.py:195
  43.1 1.3 %collective-permute-done.5.refs_2_ = f32[16,256]{1,0:T(8,128)S(1)} collective-permute-done((f32[16,256]{1,0:T(8,128)S(1)}, f32[16,256]{1,0:T(8,128)S(1)}, u32[]{:S(2)}, u32[]{:S(2)}) %collective-permute-start.5) | collective-permute-done | bytes 16416 | tf_op jit(solution)/shard_map/ppermute | solution.py:195
  44.4 0.0 collective-permute-done.6.refs_3_
  44.4 0.6 %shard_map.41 = f32[16,256]{1,0:T(8,128)} custom-call(s32[16,256]{1,0:T(8,128)S(1)} %compare_convert_fusion.diagonal, f32[16,256]{1,0:T(8,128)S(1)} %get-tuple-element.39.refs_0_, f32[16,256]{1,0:T(8,128)S(1)} %collective-permute-done.4.refs_1_, f32[16,256]{1,0:T(8,128)S(1)} %collective-permute-done.5.refs_2_, f32[16,256]{1,0:T(8,128)S(1)} %collective-permute-done.6.refs_3_), custom_call_target="tpu_custom_call" | custom-call | bytes 16384 | tf_op jit(solution)/shard_map/pallas_call | solution.py:86
  (6 shorter events, 0.1 us)
Async XLA Ops:
  0.0 16.7 %collective-permute-start = (f32[16,8192]{1,0:T(8,128)}, f32[16,8192]{1,0:T(8,128)S(1)}, u32[]{:S(2)}, u32[]{:S(2)}) collective-permute-start(f32[16,8192]{1,0:T(8,128)} %refs_0_.1), channel_id=1, source_target_pairs={{0,8},{8,12},{12,4},{4,0},{1,9},{9,13},{13,5},{5,1},{2,10},{10,14}... | collective-permute-start | bytes 1572872 | tf_op jit(solution)/shard_map/ppermute | solution.py:151
  4.0 25.6 %collective-permute-start.3 = (f32[16,8192]{1,0:T(8,128)}, f32[16,8192]{1,0:T(8,128)S(1)}, u32[]{:S(2)}, u32[]{:S(2)}) collective-permute-start(f32[16,8192]{1,0:T(8,128)} %refs_0_.1), channel_id=1, source_target_pairs={{8,0},{12,8},{4,12},{0,4},{9,1},{13,9},{5,13},{1,5},{10,2},{14,10}... | collective-permute-start | bytes 1572872 | tf_op jit(solution)/shard_map/ppermute | solution.py:163
  4.7 15.5 %copy-start.6 = (f32[16,8192]{1,0:T(8,128)S(1)}, f32[16,8192]{1,0:T(8,128)}, u32[]{:S(2)}) copy-start(f32[16,8192]{1,0:T(8,128)} %refs_0_.1) | copy-start | bytes 1572868
  16.8 20.3 %collective-permute-start.1 = (f32[16,6144]{1,0:T(8,128)S(1)}, f32[16,6144]{1,0:T(8,128)S(1)}, u32[]{:S(2)}, u32[]{:S(2)}) collective-permute-start(f32[16,6144]{1,0:T(8,128)S(1)} %slice.6), channel_id=1, source_target_pairs={{0,8},{8,12},{12,4},{4,0},{1,9},{9,13},{13,5},{5,1},{2,10},{10,14}... | collective-permute-start | bytes 1179656 | tf_op jit(solution)/shard_map/ppermute | solution.py:166
  20.2 2.2 %copy-start = (bf16[8192,256]{1,0:T(8,128)(2,1)S(1)}, bf16[8192,256]{1,0:T(8,128)(2,1)}, u32[]{:S(2)}) copy-start(bf16[8192,256]{1,0:T(8,128)(2,1)} %get-tuple-element.28.refs_3_.refs_2_.low) | copy-start | bytes 12582916
  22.4 2.2 %copy-start.3 = (bf16[8192,256]{1,0:T(8,128)(2,1)S(1)}, bf16[8192,256]{1,0:T(8,128)(2,1)}, u32[]{:S(2)}) copy-start(bf16[8192,256]{1,0:T(8,128)(2,1)} %get-tuple-element.27.refs_2_.refs_1_.high) | copy-start | bytes 12582916
  26.7 12.6 %collective-permute-start.2 = (f32[16,2048]{1,0:T(8,128)S(1)}, f32[16,2048]{1,0:T(8,128)S(1)}, u32[]{:S(2)}, u32[]{:S(2)}) collective-permute-start(f32[16,2048]{1,0:T(8,128)S(1)} %slice.7), channel_id=1, source_target_pairs={{0,8},{8,12},{12,4},{4,0},{1,9},{9,13},{13,5},{5,1},{2,10},{10,14}... | collective-permute-start | bytes 393224 | tf_op jit(solution)/shard_map/ppermute | solution.py:170
  29.7 2.2 %copy-start.1 = (bf16[8192,256]{1,0:T(8,128)(2,1)S(1)}, bf16[8192,256]{1,0:T(8,128)(2,1)}, u32[]{:S(2)}) copy-start(bf16[8192,256]{1,0:T(8,128)(2,1)} %get-tuple-element.28.refs_3_.refs_2_.low) | copy-start | bytes 12582916
  31.9 2.2 %copy-start.4 = (bf16[8192,256]{1,0:T(8,128)(2,1)S(1)}, bf16[8192,256]{1,0:T(8,128)(2,1)}, u32[]{:S(2)}) copy-start(bf16[8192,256]{1,0:T(8,128)(2,1)} %get-tuple-element.27.refs_2_.refs_1_.high) | copy-start | bytes 12582916
  34.0 3.1 %copy-start.2 = (bf16[8192,256]{1,0:T(8,128)(2,1)S(1)}, bf16[8192,256]{1,0:T(8,128)(2,1)}, u32[]{:S(2)}) copy-start(bf16[8192,256]{1,0:T(8,128)(2,1)} %get-tuple-element.28.refs_3_.refs_2_.low) | copy-start | bytes 12582916
  34.0 3.5 %copy-start.5 = (bf16[8192,256]{1,0:T(8,128)(2,1)S(1)}, bf16[8192,256]{1,0:T(8,128)(2,1)}, u32[]{:S(2)}) copy-start(bf16[8192,256]{1,0:T(8,128)(2,1)} %get-tuple-element.27.refs_2_.refs_1_.high) | copy-start | bytes 12582916
  39.8 3.4 %collective-permute-start.4 = (f32[16,256]{1,0:T(8,128)S(1)}, f32[16,256]{1,0:T(8,128)S(1)}, u32[]{:S(2)}, u32[]{:S(2)}) collective-permute-start(f32[16,256]{1,0:T(8,128)S(1)} %get-tuple-element.40), channel_id=1, source_target_pairs={{0,3},{1,2},{2,1},{3,0},{4,7},{5,6},{6,5},{7,4},{8,11},{9,10},{10,... | collective-permute-start | bytes 49160 | tf_op jit(solution)/shard_map/ppermute | solution.py:195
  40.5 3.9 %collective-permute-start.5 = (f32[16,256]{1,0:T(8,128)S(1)}, f32[16,256]{1,0:T(8,128)S(1)}, u32[]{:S(2)}, u32[]{:S(2)}) collective-permute-start(f32[16,256]{1,0:T(8,128)S(1)} %get-tuple-element.41), channel_id=1, source_target_pairs={{0,2},{1,3},{2,0},{3,1},{4,6},{5,7},{6,4},{7,5},{8,10},{9,11},{10,... | collective-permute-start | bytes 49160 | tf_op jit(solution)/shard_map/ppermute | solution.py:195
  41.4 3.0 %collective-permute-start.6 = (f32[16,256]{1,0:T(8,128)S(1)}, f32[16,256]{1,0:T(8,128)S(1)}, u32[]{:S(2)}, u32[]{:S(2)}) collective-permute-start(f32[16,256]{1,0:T(8,128)S(1)} %get-tuple-element.42), channel_id=1, source_target_pairs={{0,1},{1,0},{2,3},{3,2},{4,5},{5,4},{6,7},{7,6},{8,9},{9,8},{10,11... | collective-permute-start | bytes 49160 | tf_op jit(solution)/shard_map/ppermute | solution.py:195

commit v20 on v19

--- a/solution.py
+++ b/solution.py
@@ -190,7 +190,8 @@
     arrays = [masks, last_right, *weights, *shares]
     shares = call(kernel, rep_count, (rows_share, tile_width), [], arrays, 4 + rep_count)
     terms = [shares[0]]
-    for flip in range(rep_count - 1, 0, -1):
+    middle = rep_count // 2
+    for flip in [*range(middle, rep_count), *range(middle - 1, 0, -1)]:
         pairs = [(d, d ^ flip) for d in range(rep_count)]
         terms.append(lax.ppermute(shares[flip], "rep", pairs))
     arrays = [diagonal, *terms]

time: 45.3 us -> 45.4 us (level)
  no operation moved by 1% of the time
where the time goes in v20:
time: 45.4 us; the launch traced here: 45.1 us
  waiting for transfers between devices  10.7 us (24%)
  starting transfers between devices  9.67 us (21%)
  local copies, waits for them, and re-layouts  9.33 us (21%)
  other arithmetic  8.23 us (18%)
  Pallas kernels  6.45 us (14%)
  between operations  0.73 us (2%)
    unnamed x14, local copies, waits for them, and re-layouts  9.14 us
    convert_element_type x1, other arithmetic, halves(): return (high.astype(jnp.bfloat16), (array - high).astype(jnp.bfloat16))  7.98 us
    pallas_call x5, Pallas kernels, call(): pl.pallas_call(kernel, out_shape=[jax.ShapeDtypeStruct(shape, jnp.float32...  6.45 us
    ppermute x1, starting transfers between devices, per_device(): first = lax.ppermute(omega_rows, 'team', onward)  4.04 us
    ppermute x1, waiting for transfers between devices, per_device(): first = lax.ppermute(omega_rows, 'team', onward)  4 us
    ppermute x1, starting transfers between devices, per_device(): last_left = lax.ppermute(last_held[:, :cut], 'team', onward)  3.33 us
    ppermute x1, waiting for transfers between devices, per_device(): held = lax.ppermute(held, 'team', backward)  2.65 us
    ppermute x3, waiting for transfers between devices, per_device(): terms.append(lax.ppermute(shares[flip], 'rep', pairs))  2.52 us
  transfers between devices with their start and end apart: 7, of which 6 were waited for; matrix products, arithmetic and copies ran while one was open for 19% of the time, Pallas kernels for 12%

profile of v20, /device:TPU:0, one launch (start us, length us, event | category | flops | bytes accessed | tf_op | source)
XLA Modules:
  0.0 45.1 jit_solution(11924677216956127229)
XLA Ops:
  0.0 4.0 %collective-permute-start = (f32[16,8192]{1,0:T(8,128)}, f32[16,8192]{1,0:T(8,128)S(1)}, u32[]{:S(2)}, u32[]{:S(2)}) collective-permute-start(f32[16,8192]{1,0:T(8,128)} %refs_0_.1), channel_id=1, source_target_pairs={{0,8},{8,12},{12,4},{4,0},{1,9},{9,13},{13,5},{5,1},{2,10},{10,14}... | collective-permute-start | bytes 1572872 | tf_op jit(solution)/shard_map/ppermute | solution.py:151
  4.0 0.0 collective-permute-start.3
  4.7 0.0 copy-start.6
  4.7 8.0 %subtract_convert_fusion = (bf16[8192,256]{1,0:T(8,128)(2,1)}, bf16[8192,256]{1,0:T(8,128)(2,1)}) fusion(f32[8192,256]{1,0:T(8,128)} %param.4, s32[256]{0:T(256)S(1)} %iota_add_fusion.1, s32[8192]{0:T(1024)S(1)} %iota_add_fusion), kind=kLoop, calls=%fused_computation | loop fusion | flops 18874368 | bytes 16811008 | tf_op jit(solution)/shard_map/convert_element_type | solution.py:17
  12.7 4.0 %collective-permute-done.refs_1_ = f32[16,8192]{1,0:T(8,128)S(1)} collective-permute-done((f32[16,8192]{1,0:T(8,128)}, f32[16,8192]{1,0:T(8,128)S(1)}, u32[]{:S(2)}, u32[]{:S(2)}) %collective-permute-start) | collective-permute-done | bytes 524320 | tf_op jit(solution)/shard_map/ppermute | solution.py:151
  16.8 3.3 %collective-permute-start.1 = (f32[16,6144]{1,0:T(8,128)S(1)}, f32[16,6144]{1,0:T(8,128)S(1)}, u32[]{:S(2)}, u32[]{:S(2)}) collective-permute-start(f32[16,6144]{1,0:T(8,128)S(1)} %slice.6), channel_id=1, source_target_pairs={{0,8},{8,12},{12,4},{4,0},{1,9},{9,13},{13,5},{5,1},{2,10},{10,14}... | collective-permute-start | bytes 1179656 | tf_op jit(solution)/shard_map/ppermute | solution.py:166
  20.1 0.1 compare_convert_fusion.diagonal
  20.2 0.1 pad_add_fusion.places
  20.2 0.0 copy-done.6
  20.2 0.0 copy-start
  20.2 2.2 %copy-done = bf16[8192,256]{1,0:T(8,128)(2,1)S(1)} copy-done((bf16[8192,256]{1,0:T(8,128)(2,1)S(1)}, bf16[8192,256]{1,0:T(8,128)(2,1)}, u32[]{:S(2)}) %copy-start) | copy-done | bytes 4194328
  22.4 0.0 copy-start.3
  22.4 2.2 %copy-done.3 = bf16[8192,256]{1,0:T(8,128)(2,1)S(1)} copy-done((bf16[8192,256]{1,0:T(8,128)(2,1)S(1)}, bf16[8192,256]{1,0:T(8,128)(2,1)}, u32[]{:S(2)}) %copy-start.3) | copy-done | bytes 4194328
  24.6 2.1 %shard_map.37 = (f32[16,256]{1,0:T(8,128)S(1)}, f32[16,256]{1,0:T(8,128)S(1)}) custom-call(s32[3]{0:T(128)S(1)} %pad_add_fusion.places, f32[16,8192]{1,0:T(8,128)S(1)} %copy-done.6, f32[16,8192]{1,0:T(8,128)S(1)} %collective-permute-done.refs_1_, bf16[8192,256]{1,0:T(8,128)(2,1)S(1)} %copy-done.3, bf16[8192,256]{1,0:T(8,128)(2,1)S(1)} %copy-done), custom_call_target="tpu_custom_call" | custom-call | bytes 32768 | tf_op jit(solution)/shard_map/pallas_call | solution.py:86
  26.7 0.1 collective-permute-start.2
  26.8 0.1 pad_add_fusion.1.places
  26.9 0.1 stack.47.places
  27.0 2.6 %collective-permute-done.3.refs_0_ = f32[16,8192]{1,0:T(8,128)S(1)} collective-permute-done((f32[16,8192]{1,0:T(8,128)}, f32[16,8192]{1,0:T(8,128)S(1)}, u32[]{:S(2)}, u32[]{:S(2)}) %collective-permute-start.3) | collective-permute-done | bytes 524320 | tf_op jit(solution)/shard_map/ppermute | solution.py:163
  29.7 0.0 copy-start.1
  29.7 2.2 %copy-done.1 = bf16[8192,256]{1,0:T(8,128)(2,1)S(1)} copy-done((bf16[8192,256]{1,0:T(8,128)(2,1)S(1)}, bf16[8192,256]{1,0:T(8,128)(2,1)}, u32[]{:S(2)}) %copy-start.1) | copy-done | bytes 4194328
  31.9 0.0 copy-start.4
  31.9 2.2 %copy-done.4 = bf16[8192,256]{1,0:T(8,128)(2,1)S(1)} copy-done((bf16[8192,256]{1,0:T(8,128)(2,1)S(1)}, bf16[8192,256]{1,0:T(8,128)(2,1)}, u32[]{:S(2)}) %copy-start.4) | copy-done | bytes 4194328
  34.0 0.0 copy-start.2
  34.0 0.0 copy-start.5
  34.0 1.9 %shard_map.38.refs_5_ = f32[16,256]{1,0:T(8,128)S(1)} custom-call(s32[2]{0:T(128)S(1)} %pad_add_fusion.1.places, f32[16,8192]{1,0:T(8,128)S(1)} %collective-permute-done.3.refs_0_, bf16[8192,256]{1,0:T(8,128)(2,1)S(1)} %copy-done.4, bf16[8192,256]{1,0:T(8,128)(2,1)S(1)} %copy-done.1), custom_call_target="tpu_custom_call" | custom-call | bytes 16384 | tf_op jit(solution)/shard_map/pallas_call | solution.py:86
  35.9 1.2 %collective-permute-done.1.refs_0_ = f32[16,6144]{1,0:T(8,128)S(1)} collective-permute-done((f32[16,6144]{1,0:T(8,128)S(1)}, f32[16,6144]{1,0:T(8,128)S(1)}, u32[]{:S(2)}, u32[]{:S(2)}) %collective-permute-start.1) | collective-permute-done | bytes 393248 | tf_op jit(solution)/shard_map/ppermute | solution.py:166
  37.1 0.1 broadcast_in_dim.2.masks
  37.1 0.0 copy-done.2
  37.1 0.4 copy-done.5
  37.5 1.5 %shard_map.39 = (f32[16,256]{1,0:T(8,128)S(1)}, f32[16,256]{1,0:T(8,128)S(1)}, f32[16,256]{1,0:T(8,128)S(1)}, f32[16,256]{1,0:T(8,128)S(1)}) custom-call(s32[6]{0:T(128)S(1)} %stack.47.places, f32[16,6144]{1,0:T(8,128)S(1)} %collective-permute-done.1.refs_0_, bf16[8192,256]{1,0:T(8,128)(2,1)S(1)} %copy-done.5, bf16[8192,256]{1,0:T(8,128)(2,1)S(1)} %copy-done.2, ...), custom_call_target="tpu_custom_call" | custom-call | bytes 65536 | tf_op jit(solution)/shard_map/pallas_call | solution.py:86
  39.0 0.4 collective-permute-done.2.block
  39.4 0.4 shard_map.40
  39.8 1.6 %collective-permute-start.4 = (f32[16,256]{1,0:T(8,128)S(1)}, f32[16,256]{1,0:T(8,128)S(1)}, u32[]{:S(2)}, u32[]{:S(2)}) collective-permute-start(f32[16,256]{1,0:T(8,128)S(1)} %get-tuple-element.40), channel_id=1, source_target_pairs={{0,2},{1,3},{2,0},{3,1},{4,6},{5,7},{6,4},{7,5},{8,10},{9,11},{10,... | collective-permute-start | bytes 49160 | tf_op jit(solution)/shard_map/ppermute | solution.py:196
  41.3 0.0 collective-permute-start.5
  41.3 0.6 %collective-permute-start.6 = (f32[16,256]{1,0:T(8,128)S(1)}, f32[16,256]{1,0:T(8,128)S(1)}, u32[]{:S(2)}, u32[]{:S(2)}) collective-permute-start(f32[16,256]{1,0:T(8,128)S(1)} %get-tuple-element.42), channel_id=1, source_target_pairs={{0,1},{1,0},{2,3},{3,2},{4,5},{5,4},{6,7},{7,6},{8,9},{9,8},{10,11... | collective-permute-start | bytes 49160 | tf_op jit(solution)/shard_map/ppermute | solution.py:196
  42.0 1.6 %collective-permute-done.4.refs_1_ = f32[16,256]{1,0:T(8,128)S(1)} collective-permute-done((f32[16,256]{1,0:T(8,128)S(1)}, f32[16,256]{1,0:T(8,128)S(1)}, u32[]{:S(2)}, u32[]{:S(2)}) %collective-permute-start.4) | collective-permute-done | bytes 16416 | tf_op jit(solution)/shard_map/ppermute | solution.py:196
  43.6 0.9 %collective-permute-done.5.refs_2_ = f32[16,256]{1,0:T(8,128)S(1)} collective-permute-done((f32[16,256]{1,0:T(8,128)S(1)}, f32[16,256]{1,0:T(8,128)S(1)}, u32[]{:S(2)}, u32[]{:S(2)}) %collective-permute-start.5) | collective-permute-done | bytes 16416 | tf_op jit(solution)/shard_map/ppermute | solution.py:196
  44.5 0.0 collective-permute-done.6.refs_3_
  44.5 0.6 %shard_map.41 = f32[16,256]{1,0:T(8,128)} custom-call(s32[16,256]{1,0:T(8,128)S(1)} %compare_convert_fusion.diagonal, f32[16,256]{1,0:T(8,128)S(1)} %get-tuple-element.39.refs_0_, f32[16,256]{1,0:T(8,128)S(1)} %collective-permute-done.4.refs_1_, f32[16,256]{1,0:T(8,128)S(1)} %collective-permute-done.5.refs_2_, f32[16,256]{1,0:T(8,128)S(1)} %collective-permute-done.6.refs_3_), custom_call_target="tpu_custom_call" | custom-call | bytes 16384 | tf_op jit(solution)/shard_map/pallas_call | solution.py:86
  (6 shorter events, 0.1 us)
Async XLA Ops:
  0.0 16.7 %collective-permute-start = (f32[16,8192]{1,0:T(8,128)}, f32[16,8192]{1,0:T(8,128)S(1)}, u32[]{:S(2)}, u32[]{:S(2)}) collective-permute-start(f32[16,8192]{1,0:T(8,128)} %refs_0_.1), channel_id=1, source_target_pairs={{0,8},{8,12},{12,4},{4,0},{1,9},{9,13},{13,5},{5,1},{2,10},{10,14}... | collective-permute-start | bytes 1572872 | tf_op jit(solution)/shard_map/ppermute | solution.py:151
  4.0 25.6 %collective-permute-start.3 = (f32[16,8192]{1,0:T(8,128)}, f32[16,8192]{1,0:T(8,128)S(1)}, u32[]{:S(2)}, u32[]{:S(2)}) collective-permute-start(f32[16,8192]{1,0:T(8,128)} %refs_0_.1), channel_id=1, source_target_pairs={{8,0},{12,8},{4,12},{0,4},{9,1},{13,9},{5,13},{1,5},{10,2},{14,10}... | collective-permute-start | bytes 1572872 | tf_op jit(solution)/shard_map/ppermute | solution.py:163
  4.7 15.5 %copy-start.6 = (f32[16,8192]{1,0:T(8,128)S(1)}, f32[16,8192]{1,0:T(8,128)}, u32[]{:S(2)}) copy-start(f32[16,8192]{1,0:T(8,128)} %refs_0_.1) | copy-start | bytes 1572868
  16.8 20.3 %collective-permute-start.1 = (f32[16,6144]{1,0:T(8,128)S(1)}, f32[16,6144]{1,0:T(8,128)S(1)}, u32[]{:S(2)}, u32[]{:S(2)}) collective-permute-start(f32[16,6144]{1,0:T(8,128)S(1)} %slice.6), channel_id=1, source_target_pairs={{0,8},{8,12},{12,4},{4,0},{1,9},{9,13},{13,5},{5,1},{2,10},{10,14}... | collective-permute-start | bytes 1179656 | tf_op jit(solution)/shard_map/ppermute | solution.py:166
  20.2 2.2 %copy-start = (bf16[8192,256]{1,0:T(8,128)(2,1)S(1)}, bf16[8192,256]{1,0:T(8,128)(2,1)}, u32[]{:S(2)}) copy-start(bf16[8192,256]{1,0:T(8,128)(2,1)} %get-tuple-element.28.refs_3_.refs_2_.low) | copy-start | bytes 12582916
  22.4 2.2 %copy-start.3 = (bf16[8192,256]{1,0:T(8,128)(2,1)S(1)}, bf16[8192,256]{1,0:T(8,128)(2,1)}, u32[]{:S(2)}) copy-start(bf16[8192,256]{1,0:T(8,128)(2,1)} %get-tuple-element.27.refs_2_.refs_1_.high) | copy-start | bytes 12582916
  26.7 12.6 %collective-permute-start.2 = (f32[16,2048]{1,0:T(8,128)S(1)}, f32[16,2048]{1,0:T(8,128)S(1)}, u32[]{:S(2)}, u32[]{:S(2)}) collective-permute-start(f32[16,2048]{1,0:T(8,128)S(1)} %slice.7), channel_id=1, source_target_pairs={{0,8},{8,12},{12,4},{4,0},{1,9},{9,13},{13,5},{5,1},{2,10},{10,14}... | collective-permute-start | bytes 393224 | tf_op jit(solution)/shard_map/ppermute | solution.py:170
  29.7 2.2 %copy-start.1 = (bf16[8192,256]{1,0:T(8,128)(2,1)S(1)}, bf16[8192,256]{1,0:T(8,128)(2,1)}, u32[]{:S(2)}) copy-start(bf16[8192,256]{1,0:T(8,128)(2,1)} %get-tuple-element.28.refs_3_.refs_2_.low) | copy-start | bytes 12582916
  31.9 2.2 %copy-start.4 = (bf16[8192,256]{1,0:T(8,128)(2,1)S(1)}, bf16[8192,256]{1,0:T(8,128)(2,1)}, u32[]{:S(2)}) copy-start(bf16[8192,256]{1,0:T(8,128)(2,1)} %get-tuple-element.27.refs_2_.refs_1_.high) | copy-start | bytes 12582916
  34.0 3.1 %copy-start.2 = (bf16[8192,256]{1,0:T(8,128)(2,1)S(1)}, bf16[8192,256]{1,0:T(8,128)(2,1)}, u32[]{:S(2)}) copy-start(bf16[8192,256]{1,0:T(8,128)(2,1)} %get-tuple-element.28.refs_3_.refs_2_.low) | copy-start | bytes 12582916
  34.0 3.5 %copy-start.5 = (bf16[8192,256]{1,0:T(8,128)(2,1)S(1)}, bf16[8192,256]{1,0:T(8,128)(2,1)}, u32[]{:S(2)}) copy-start(bf16[8192,256]{1,0:T(8,128)(2,1)} %get-tuple-element.27.refs_2_.refs_1_.high) | copy-start | bytes 12582916
  39.8 3.8 %collective-permute-start.4 = (f32[16,256]{1,0:T(8,128)S(1)}, f32[16,256]{1,0:T(8,128)S(1)}, u32[]{:S(2)}, u32[]{:S(2)}) collective-permute-start(f32[16,256]{1,0:T(8,128)S(1)} %get-tuple-element.40), channel_id=1, source_target_pairs={{0,2},{1,3},{2,0},{3,1},{4,6},{5,7},{6,4},{7,5},{8,10},{9,11},{10,... | collective-permute-start | bytes 49160 | tf_op jit(solution)/shard_map/ppermute | solution.py:196
  41.3 3.2 %collective-permute-start.5 = (f32[16,256]{1,0:T(8,128)S(1)}, f32[16,256]{1,0:T(8,128)S(1)}, u32[]{:S(2)}, u32[]{:S(2)}) collective-permute-start(f32[16,256]{1,0:T(8,128)S(1)} %get-tuple-element.41), channel_id=1, source_target_pairs={{0,3},{1,2},{2,1},{3,0},{4,7},{5,6},{6,5},{7,4},{8,11},{9,10},{10,... | collective-permute-start | bytes 49160 | tf_op jit(solution)/shard_map/ppermute | solution.py:196
  41.3 3.2 %collective-permute-start.6 = (f32[16,256]{1,0:T(8,128)S(1)}, f32[16,256]{1,0:T(8,128)S(1)}, u32[]{:S(2)}, u32[]{:S(2)}) collective-permute-start(f32[16,256]{1,0:T(8,128)S(1)} %get-tuple-element.42), channel_id=1, source_target_pairs={{0,1},{1,0},{2,3},{3,2},{4,5},{5,4},{6,7},{7,6},{8,9},{9,8},{10,11... | collective-permute-start | bytes 49160 | tf_op jit(solution)/shard_map/ppermute | solution.py:196

commit v21 on v19

--- a/solution.py
+++ b/solution.py
@@ -164,10 +164,9 @@
         gathered.append((held, -step))
 
     last_left = lax.ppermute(last_held[:, :cut], "team", onward)
+    last_right = lax.ppermute(last_held[:, cut:], "team", onward)
     sources = [team_index, device_at(place - 1)]
     parts = products_of([own, first], sources)
-    last_held, *parts = lax.optimization_barrier((last_held, *parts))
-    last_right = lax.ppermute(last_held[:, cut:], "team", onward)
     for block, step in gathered:
         sources.append(device_at(place - step))
         parts += products_of([block], sources[-1:])

time: 45.3 us -> 45.2 us (level)
  waiting for transfers between devices: 10.9 us -> 15.7 us
  local copies, waits for them, and re-layouts: 9.33 us -> 4.57 us
    unnamed x14 -> x10, local copies, waits for them, and re-layouts: 9.14 us -> 4.38 us
    ppermute x1, waiting for transfers between devices: 1.16 us -> 5.54 us  [per_device(): last_left = lax.ppermute(last_held[:, :cut], 'team', onward)]
where the time goes in v21:
time: 45.2 us; the launch traced here: 45 us
  waiting for transfers between devices  15.7 us (35%)
  starting transfers between devices  9.4 us (21%)
  other arithmetic  8.2 us (18%)
  Pallas kernels  6.44 us (14%)
  local copies, waits for them, and re-layouts  4.57 us (10%)
  between operations  0.74 us (2%)
    convert_element_type x1, other arithmetic, halves(): return (high.astype(jnp.bfloat16), (array - high).astype(jnp.bfloat16))  7.96 us
    pallas_call x5, Pallas kernels, call(): pl.pallas_call(kernel, out_shape=[jax.ShapeDtypeStruct(shape, jnp.float32...  6.44 us
    ppermute x1, waiting for transfers between devices, per_device(): last_left = lax.ppermute(last_held[:, :cut], 'team', onward)  5.54 us
    unnamed x10, local copies, waits for them, and re-layouts  4.38 us
    ppermute x1, starting transfers between devices, per_device(): first = lax.ppermute(omega_rows, 'team', onward)  4.04 us
    ppermute x1, waiting for transfers between devices, per_device(): first = lax.ppermute(omega_rows, 'team', onward)  4.03 us
    ppermute x1, starting transfers between devices, per_device(): last_left = lax.ppermute(last_held[:, :cut], 'team', onward)  3.33 us
    ppermute x3, waiting for transfers between devices, per_device(): terms.append(lax.ppermute(shares[flip], 'rep', pairs))  2.69 us
  transfers between devices with their start and end apart: 7, of which 6 were waited for; matrix products, arithmetic and copies ran while one was open for 19% of the time, Pallas kernels for 12%

profile of v21, /device:TPU:0, one launch (start us, length us, event | category | flops | bytes accessed | tf_op | source)
XLA Modules:
  0.0 45.0 jit_solution(6416310072171458384)
XLA Ops:
  0.0 4.0 %collective-permute-start = (f32[16,8192]{1,0:T(8,128)}, f32[16,8192]{1,0:T(8,128)S(1)}, u32[]{:S(2)}, u32[]{:S(2)}) collective-permute-start(f32[16,8192]{1,0:T(8,128)} %refs_0_.1), channel_id=1, source_target_pairs={{0,8},{8,12},{12,4},{4,0},{1,9},{9,13},{13,5},{5,1},{2,10},{10,14}... | collective-permute-start | bytes 1572872 | tf_op jit(solution)/shard_map/ppermute | solution.py:151
  4.0 0.0 collective-permute-start.3
  4.7 0.0 copy-start.4
  4.7 8.0 %subtract_convert_fusion = (bf16[8192,256]{1,0:T(8,128)(2,1)}, bf16[8192,256]{1,0:T(8,128)(2,1)}) fusion(f32[8192,256]{1,0:T(8,128)} %param.4, s32[256]{0:T(256)S(1)} %iota_add_fusion.1, s32[8192]{0:T(1024)S(1)} %iota_add_fusion), kind=kLoop, calls=%fused_computation | loop fusion | flops 18874368 | bytes 16811008 | tf_op jit(solution)/shard_map/convert_element_type | solution.py:17
  12.7 4.0 %collective-permute-done.refs_1_ = f32[16,8192]{1,0:T(8,128)S(1)} collective-permute-done((f32[16,8192]{1,0:T(8,128)}, f32[16,8192]{1,0:T(8,128)S(1)}, u32[]{:S(2)}, u32[]{:S(2)}) %collective-permute-start) | collective-permute-done | bytes 524320 | tf_op jit(solution)/shard_map/ppermute | solution.py:151
  16.8 3.3 %collective-permute-start.1 = (f32[16,6144]{1,0:T(8,128)S(1)}, f32[16,6144]{1,0:T(8,128)S(1)}, u32[]{:S(2)}, u32[]{:S(2)}) collective-permute-start(f32[16,6144]{1,0:T(8,128)S(1)} %slice.6), channel_id=1, source_target_pairs={{0,8},{8,12},{12,4},{4,0},{1,9},{9,13},{13,5},{5,1},{2,10},{10,14}... | collective-permute-start | bytes 1179656 | tf_op jit(solution)/shard_map/ppermute | solution.py:166
  20.1 0.1 compare_convert_fusion.diagonal
  20.2 0.1 pad_add_fusion.1.places
  20.2 0.1 collective-permute-start.2
  20.3 0.1 pad_add_fusion.places
  20.4 0.1 stack.44.places
  20.5 0.0 copy-done.4
  20.5 0.0 copy-start
  20.5 2.2 %copy-done = bf16[8192,256]{1,0:T(8,128)(2,1)S(1)} copy-done((bf16[8192,256]{1,0:T(8,128)(2,1)S(1)}, bf16[8192,256]{1,0:T(8,128)(2,1)}, u32[]{:S(2)}) %copy-start) | copy-done | bytes 4194328
  22.7 0.0 copy-start.2
  22.7 2.2 %copy-done.2 = bf16[8192,256]{1,0:T(8,128)(2,1)S(1)} copy-done((bf16[8192,256]{1,0:T(8,128)(2,1)S(1)}, bf16[8192,256]{1,0:T(8,128)(2,1)}, u32[]{:S(2)}) %copy-start.2) | copy-done | bytes 4194328
  24.9 0.0 copy-start.1
  24.9 0.0 copy-start.3
  24.9 2.1 %shard_map.37 = (f32[16,256]{1,0:T(8,128)S(1)}, f32[16,256]{1,0:T(8,128)S(1)}) custom-call(s32[3]{0:T(128)S(1)} %pad_add_fusion.places, f32[16,8192]{1,0:T(8,128)S(1)} %copy-done.4, f32[16,8192]{1,0:T(8,128)S(1)} %collective-permute-done.refs_1_, bf16[8192,256]{1,0:T(8,128)(2,1)S(1)} %copy-done.2, bf16[8192,256]{1,0:T(8,128)(2,1)S(1)} %copy-done), custom_call_target="tpu_custom_call" | custom-call | bytes 32768 | tf_op jit(solution)/shard_map/pallas_call | solution.py:86
  27.0 2.7 %collective-permute-done.3.refs_0_ = f32[16,8192]{1,0:T(8,128)S(1)} collective-permute-done((f32[16,8192]{1,0:T(8,128)}, f32[16,8192]{1,0:T(8,128)S(1)}, u32[]{:S(2)}, u32[]{:S(2)}) %collective-permute-start.3) | collective-permute-done | bytes 524320 | tf_op jit(solution)/shard_map/ppermute | solution.py:163
  29.7 0.0 copy-done.1
  29.7 1.9 %shard_map.38.refs_5_ = f32[16,256]{1,0:T(8,128)S(1)} custom-call(s32[2]{0:T(128)S(1)} %pad_add_fusion.1.places, f32[16,8192]{1,0:T(8,128)S(1)} %collective-permute-done.3.refs_0_, bf16[8192,256]{1,0:T(8,128)(2,1)S(1)} %copy-done.2, bf16[8192,256]{1,0:T(8,128)(2,1)S(1)} %copy-done.1), custom_call_target="tpu_custom_call" | custom-call | bytes 16384 | tf_op jit(solution)/shard_map/pallas_call | solution.py:86
  31.5 5.5 %collective-permute-done.1.refs_0_ = f32[16,6144]{1,0:T(8,128)S(1)} collective-permute-done((f32[16,6144]{1,0:T(8,128)S(1)}, f32[16,6144]{1,0:T(8,128)S(1)}, u32[]{:S(2)}, u32[]{:S(2)}) %collective-permute-start.1) | collective-permute-done | bytes 393248 | tf_op jit(solution)/shard_map/ppermute | solution.py:166
  37.1 0.1 broadcast_in_dim.2.masks
  37.1 0.0 copy-done.3
  37.1 1.5 %shard_map.39 = (f32[16,256]{1,0:T(8,128)S(1)}, f32[16,256]{1,0:T(8,128)S(1)}, f32[16,256]{1,0:T(8,128)S(1)}, f32[16,256]{1,0:T(8,128)S(1)}) custom-call(s32[6]{0:T(128)S(1)} %stack.44.places, f32[16,6144]{1,0:T(8,128)S(1)} %collective-permute-done.1.refs_0_, bf16[8192,256]{1,0:T(8,128)(2,1)S(1)} %copy-done.3, bf16[8192,256]{1,0:T(8,128)(2,1)S(1)} %copy-done.1, ...), custom_call_target="tpu_custom_call" | custom-call | bytes 65536 | tf_op jit(solution)/shard_map/pallas_call | solution.py:86
  38.6 0.7 %collective-permute-done.2.block = f32[16,2048]{1,0:T(8,128)S(1)} collective-permute-done((f32[16,2048]{1,0:T(8,128)S(1)}, f32[16,2048]{1,0:T(8,128)S(1)}, u32[]{:S(2)}, u32[]{:S(2)}) %collective-permute-start.2) | collective-permute-done | bytes 131104 | tf_op jit(solution)/shard_map/ppermute | solution.py:167
  39.4 0.4 shard_map.40
  39.8 0.8 %collective-permute-start.4 = (f32[16,256]{1,0:T(8,128)S(1)}, f32[16,256]{1,0:T(8,128)S(1)}, u32[]{:S(2)}, u32[]{:S(2)}) collective-permute-start(f32[16,256]{1,0:T(8,128)S(1)} %get-tuple-element.34), channel_id=1, source_target_pairs={{0,3},{1,2},{2,1},{3,0},{4,7},{5,6},{6,5},{7,4},{8,11},{9,10},{10,... | collective-permute-start | bytes 49160 | tf_op jit(solution)/shard_map/ppermute | solution.py:194
  40.5 0.9 %collective-permute-start.5 = (f32[16,256]{1,0:T(8,128)S(1)}, f32[16,256]{1,0:T(8,128)S(1)}, u32[]{:S(2)}, u32[]{:S(2)}) collective-permute-start(f32[16,256]{1,0:T(8,128)S(1)} %get-tuple-element.35), channel_id=1, source_target_pairs={{0,2},{1,3},{2,0},{3,1},{4,6},{5,7},{6,4},{7,5},{8,10},{9,11},{10,... | collective-permute-start | bytes 49160 | tf_op jit(solution)/shard_map/ppermute | solution.py:194
  41.4 0.3 collective-permute-start.6
  41.7 1.4 %collective-permute-done.4.refs_1_ = f32[16,256]{1,0:T(8,128)S(1)} collective-permute-done((f32[16,256]{1,0:T(8,128)S(1)}, f32[16,256]{1,0:T(8,128)S(1)}, u32[]{:S(2)}, u32[]{:S(2)}) %collective-permute-start.4) | collective-permute-done | bytes 16416 | tf_op jit(solution)/shard_map/ppermute | solution.py:194
  43.1 1.3 %collective-permute-done.5.refs_2_ = f32[16,256]{1,0:T(8,128)S(1)} collective-permute-done((f32[16,256]{1,0:T(8,128)S(1)}, f32[16,256]{1,0:T(8,128)S(1)}, u32[]{:S(2)}, u32[]{:S(2)}) %collective-permute-start.5) | collective-permute-done | bytes 16416 | tf_op jit(solution)/shard_map/ppermute | solution.py:194
  44.4 0.0 collective-permute-done.6.refs_3_
  44.4 0.6 %shard_map.41 = f32[16,256]{1,0:T(8,128)} custom-call(s32[16,256]{1,0:T(8,128)S(1)} %compare_convert_fusion.diagonal, f32[16,256]{1,0:T(8,128)S(1)} %get-tuple-element.33.refs_0_, f32[16,256]{1,0:T(8,128)S(1)} %collective-permute-done.4.refs_1_, f32[16,256]{1,0:T(8,128)S(1)} %collective-permute-done.5.refs_2_, f32[16,256]{1,0:T(8,128)S(1)} %collective-permute-done.6.refs_3_), custom_call_target="tpu_custom_call" | custom-call | bytes 16384 | tf_op jit(solution)/shard_map/pallas_call | solution.py:86
  (6 shorter events, 0.1 us)
Async XLA Ops:
  0.0 16.7 %collective-permute-start = (f32[16,8192]{1,0:T(8,128)}, f32[16,8192]{1,0:T(8,128)S(1)}, u32[]{:S(2)}, u32[]{:S(2)}) collective-permute-start(f32[16,8192]{1,0:T(8,128)} %refs_0_.1), channel_id=1, source_target_pairs={{0,8},{8,12},{12,4},{4,0},{1,9},{9,13},{13,5},{5,1},{2,10},{10,14}... | collective-permute-start | bytes 1572872 | tf_op jit(solution)/shard_map/ppermute | solution.py:151
  4.0 25.6 %collective-permute-start.3 = (f32[16,8192]{1,0:T(8,128)}, f32[16,8192]{1,0:T(8,128)S(1)}, u32[]{:S(2)}, u32[]{:S(2)}) collective-permute-start(f32[16,8192]{1,0:T(8,128)} %refs_0_.1), channel_id=1, source_target_pairs={{8,0},{12,8},{4,12},{0,4},{9,1},{13,9},{5,13},{1,5},{10,2},{14,10}... | collective-permute-start | bytes 1572872 | tf_op jit(solution)/shard_map/ppermute | solution.py:163
  4.7 15.8 %copy-start.4 = (f32[16,8192]{1,0:T(8,128)S(1)}, f32[16,8192]{1,0:T(8,128)}, u32[]{:S(2)}) copy-start(f32[16,8192]{1,0:T(8,128)} %refs_0_.1) | copy-start | bytes 1572868
  16.8 20.3 %collective-permute-start.1 = (f32[16,6144]{1,0:T(8,128)S(1)}, f32[16,6144]{1,0:T(8,128)S(1)}, u32[]{:S(2)}, u32[]{:S(2)}) collective-permute-start(f32[16,6144]{1,0:T(8,128)S(1)} %slice.6), channel_id=1, source_target_pairs={{0,8},{8,12},{12,4},{4,0},{1,9},{9,13},{13,5},{5,1},{2,10},{10,14}... | collective-permute-start | bytes 1179656 | tf_op jit(solution)/shard_map/ppermute | solution.py:166
  20.2 19.1 %collective-permute-start.2 = (f32[16,2048]{1,0:T(8,128)S(1)}, f32[16,2048]{1,0:T(8,128)S(1)}, u32[]{:S(2)}, u32[]{:S(2)}) collective-permute-start(f32[16,2048]{1,0:T(8,128)S(1)} %slice.7), channel_id=1, source_target_pairs={{0,8},{8,12},{12,4},{4,0},{1,9},{9,13},{13,5},{5,1},{2,10},{10,14}... | collective-permute-start | bytes 393224 | tf_op jit(solution)/shard_map/ppermute | solution.py:167
  20.5 2.2 %copy-start = (bf16[8192,256]{1,0:T(8,128)(2,1)S(1)}, bf16[8192,256]{1,0:T(8,128)(2,1)}, u32[]{:S(2)}) copy-start(bf16[8192,256]{1,0:T(8,128)(2,1)} %get-tuple-element.25.refs_3_.refs_2_.low) | copy-start | bytes 12582916
  22.7 2.2 %copy-start.2 = (bf16[8192,256]{1,0:T(8,128)(2,1)S(1)}, bf16[8192,256]{1,0:T(8,128)(2,1)}, u32[]{:S(2)}) copy-start(bf16[8192,256]{1,0:T(8,128)(2,1)} %get-tuple-element.24.refs_2_.refs_1_.high) | copy-start | bytes 12582916
  24.9 4.8 %copy-start.1 = (bf16[8192,256]{1,0:T(8,128)(2,1)S(1)}, bf16[8192,256]{1,0:T(8,128)(2,1)}, u32[]{:S(2)}) copy-start(bf16[8192,256]{1,0:T(8,128)(2,1)} %get-tuple-element.25.refs_3_.refs_2_.low) | copy-start | bytes 12582916
  24.9 12.2 %copy-start.3 = (bf16[8192,256]{1,0:T(8,128)(2,1)S(1)}, bf16[8192,256]{1,0:T(8,128)(2,1)}, u32[]{:S(2)}) copy-start(bf16[8192,256]{1,0:T(8,128)(2,1)} %get-tuple-element.24.refs_2_.refs_1_.high) | copy-start | bytes 12582916
  39.8 3.4 %collective-permute-start.4 = (f32[16,256]{1,0:T(8,128)S(1)}, f32[16,256]{1,0:T(8,128)S(1)}, u32[]{:S(2)}, u32[]{:S(2)}) collective-permute-start(f32[16,256]{1,0:T(8,128)S(1)} %get-tuple-element.34), channel_id=1, source_target_pairs={{0,3},{1,2},{2,1},{3,0},{4,7},{5,6},{6,5},{7,4},{8,11},{9,10},{10,... | collective-permute-start | bytes 49160 | tf_op jit(solution)/shard_map/ppermute | solution.py:194
  40.5 3.9 %collective-permute-start.5 = (f32[16,256]{1,0:T(8,128)S(1)}, f32[16,256]{1,0:T(8,128)S(1)}, u32[]{:S(2)}, u32[]{:S(2)}) collective-permute-start(f32[16,256]{1,0:T(8,128)S(1)} %get-tuple-element.35), channel_id=1, source_target_pairs={{0,2},{1,3},{2,0},{3,1},{4,6},{5,7},{6,4},{7,5},{8,10},{9,11},{10,... | collective-permute-start | bytes 49160 | tf_op jit(solution)/shard_map/ppermute | solution.py:194
  41.4 3.0 %collective-permute-start.6 = (f32[16,256]{1,0:T(8,128)S(1)}, f32[16,256]{1,0:T(8,128)S(1)}, u32[]{:S(2)}, u32[]{:S(2)}) collective-permute-start(f32[16,256]{1,0:T(8,128)S(1)} %get-tuple-element.36), channel_id=1, source_target_pairs={{0,1},{1,0},{2,3},{3,2},{4,5},{5,4},{6,7},{7,6},{8,9},{9,8},{10,11... | collective-permute-start | bytes 49160 | tf_op jit(solution)/shard_map/ppermute | solution.py:194

commit v22 on v21

--- a/solution.py
+++ b/solution.py
@@ -121,7 +121,7 @@
     chosen = (k_ids[:, None] == c_ids[None, :]).astype(jnp.float32)
     weights = halves(chosen - step_size * covariance_columns)
 
-    cut = part_width // 4 * 3
+    cut = part_width // 16 * 13
     assert all_rows <= cut and cut % tile_width == 0
 
     share_blocks = rows_share // block_rows

time: 45.2 us -> 45.2 us (level)
    ppermute x1, waiting for transfers between devices: 0.73 us -> 0.01 us  [per_device(): last_right = lax.ppermute(last_held[:, cut:], 'team', onward)]
    ppermute x1, waiting for transfers between devices: 5.54 us -> 6.24 us  [per_device(): last_left = lax.ppermute(last_held[:, :cut], 'team', onward)]
  transfers between devices with their start and end apart: 7 -> 7, of which waited for: 6 -> 5; matrix products, arithmetic and copies ran while one was open for 19% -> 19% of each run, Pallas kernels for 12% -> 12%
where the time goes in v22:
time: 45.2 us; the launch traced here: 44.9 us
  waiting for transfers between devices  15.5 us (34%)
  starting transfers between devices  9.37 us (21%)
  other arithmetic  8.22 us (18%)
  Pallas kernels  6.51 us (14%)
  local copies, waits for them, and re-layouts  4.58 us (10%)
  between operations  0.73 us (2%)
    convert_element_type x1, other arithmetic, halves(): return (high.astype(jnp.bfloat16), (array - high).astype(jnp.bfloat16))  7.96 us
    pallas_call x5, Pallas kernels, call(): pl.pallas_call(kernel, out_shape=[jax.ShapeDtypeStruct(shape, jnp.float32...  6.51 us
    ppermute x1, waiting for transfers between devices, per_device(): last_left = lax.ppermute(last_held[:, :cut], 'team', onward)  6.24 us
    unnamed x10, local copies, waits for them, and re-layouts  4.39 us
    ppermute x1, starting transfers between devices, per_device(): first = lax.ppermute(omega_rows, 'team', onward)  4.04 us
    ppermute x1, waiting for transfers between devices, per_device(): first = lax.ppermute(omega_rows, 'team', onward)  3.85 us
    ppermute x1, starting transfers between devices, per_device(): last_left = lax.ppermute(last_held[:, :cut], 'team', onward)  3.33 us
    ppermute x1, waiting for transfers between devices, per_device(): held = lax.ppermute(held, 'team', backward)  2.86 us
  transfers between devices with their start and end apart: 7, of which 5 were waited for; matrix products, arithmetic and copies ran while one was open for 19% of the time, Pallas kernels for 12%

profile of v22, /device:TPU:0, one launch (start us, length us, event | category | flops | bytes accessed | tf_op | source)
XLA Modules:
  0.0 44.9 jit_solution(2700538432828653515)
XLA Ops:
  0.0 4.0 %collective-permute-start = (f32[16,8192]{1,0:T(8,128)}, f32[16,8192]{1,0:T(8,128)S(1)}, u32[]{:S(2)}, u32[]{:S(2)}) collective-permute-start(f32[16,8192]{1,0:T(8,128)} %refs_0_.1), channel_id=1, source_target_pairs={{0,8},{8,12},{12,4},{4,0},{1,9},{9,13},{13,5},{5,1},{2,10},{10,14}... | collective-permute-start | bytes 1572872 | tf_op jit(solution)/shard_map/ppermute | solution.py:151
  4.0 0.0 collective-permute-start.3
  4.7 0.0 copy-start.4
  4.7 8.0 %subtract_convert_fusion = (bf16[8192,256]{1,0:T(8,128)(2,1)}, bf16[8192,256]{1,0:T(8,128)(2,1)}) fusion(f32[8192,256]{1,0:T(8,128)} %param.4, s32[256]{0:T(256)S(1)} %iota_add_fusion.1, s32[8192]{0:T(1024)S(1)} %iota_add_fusion), kind=kLoop, calls=%fused_computation | loop fusion | flops 18874368 | bytes 16811008 | tf_op jit(solution)/shard_map/convert_element_type | solution.py:17
  12.7 0.1 stack.44.places
  12.8 0.1 pad_add_fusion.1.places
  12.9 3.8 %collective-permute-done.refs_1_ = f32[16,8192]{1,0:T(8,128)S(1)} collective-permute-done((f32[16,8192]{1,0:T(8,128)}, f32[16,8192]{1,0:T(8,128)S(1)}, u32[]{:S(2)}, u32[]{:S(2)}) %collective-permute-start) | collective-permute-done | bytes 524320 | tf_op jit(solution)/shard_map/ppermute | solution.py:151
  16.8 3.3 %collective-permute-start.1 = (f32[16,6656]{1,0:T(8,128)S(1)}, f32[16,6656]{1,0:T(8,128)S(1)}, u32[]{:S(2)}, u32[]{:S(2)}) collective-permute-start(f32[16,6656]{1,0:T(8,128)S(1)} %slice.6), channel_id=1, source_target_pairs={{0,8},{8,12},{12,4},{4,0},{1,9},{9,13},{13,5},{5,1},{2,10},{10,14}... | collective-permute-start | bytes 1277960 | tf_op jit(solution)/shard_map/ppermute | solution.py:166
  20.1 0.1 compare_convert_fusion.diagonal
  20.2 0.1 collective-permute-start.2
  20.3 0.1 pad_add_fusion.places
  20.3 0.0 copy-done.4
  20.3 0.0 copy-start
  20.3 2.2 %copy-done = bf16[8192,256]{1,0:T(8,128)(2,1)S(1)} copy-done((bf16[8192,256]{1,0:T(8,128)(2,1)S(1)}, bf16[8192,256]{1,0:T(8,128)(2,1)}, u32[]{:S(2)}) %copy-start) | copy-done | bytes 4194328
  22.5 0.0 copy-start.2
  22.5 2.2 %copy-done.2 = bf16[8192,256]{1,0:T(8,128)(2,1)S(1)} copy-done((bf16[8192,256]{1,0:T(8,128)(2,1)S(1)}, bf16[8192,256]{1,0:T(8,128)(2,1)}, u32[]{:S(2)}) %copy-start.2) | copy-done | bytes 4194328
  24.7 0.0 copy-start.1
  24.7 0.0 copy-start.3
  24.7 2.1 %shard_map.37 = (f32[16,256]{1,0:T(8,128)S(1)}, f32[16,256]{1,0:T(8,128)S(1)}) custom-call(s32[3]{0:T(128)S(1)} %pad_add_fusion.places, f32[16,8192]{1,0:T(8,128)S(1)} %copy-done.4, f32[16,8192]{1,0:T(8,128)S(1)} %collective-permute-done.refs_1_, bf16[8192,256]{1,0:T(8,128)(2,1)S(1)} %copy-done.2, bf16[8192,256]{1,0:T(8,128)(2,1)S(1)} %copy-done), custom_call_target="tpu_custom_call" | custom-call | bytes 32768 | tf_op jit(solution)/shard_map/pallas_call | solution.py:86
  26.8 2.9 %collective-permute-done.3.refs_0_ = f32[16,8192]{1,0:T(8,128)S(1)} collective-permute-done((f32[16,8192]{1,0:T(8,128)}, f32[16,8192]{1,0:T(8,128)S(1)}, u32[]{:S(2)}, u32[]{:S(2)}) %collective-permute-start.3) | collective-permute-done | bytes 524320 | tf_op jit(solution)/shard_map/ppermute | solution.py:163
  29.7 0.0 copy-done.1
  29.7 1.9 %shard_map.38.refs_5_ = f32[16,256]{1,0:T(8,128)S(1)} custom-call(s32[2]{0:T(128)S(1)} %pad_add_fusion.1.places, f32[16,8192]{1,0:T(8,128)S(1)} %collective-permute-done.3.refs_0_, bf16[8192,256]{1,0:T(8,128)(2,1)S(1)} %copy-done.2, bf16[8192,256]{1,0:T(8,128)(2,1)S(1)} %copy-done.1), custom_call_target="tpu_custom_call" | custom-call | bytes 16384 | tf_op jit(solution)/shard_map/pallas_call | solution.py:86
  31.5 6.2 %collective-permute-done.1.refs_0_ = f32[16,6656]{1,0:T(8,128)S(1)} collective-permute-done((f32[16,6656]{1,0:T(8,128)S(1)}, f32[16,6656]{1,0:T(8,128)S(1)}, u32[]{:S(2)}, u32[]{:S(2)}) %collective-permute-start.1) | collective-permute-done | bytes 426016 | tf_op jit(solution)/shard_map/ppermute | solution.py:166
  37.8 0.1 broadcast_in_dim.2.masks
  37.8 0.0 copy-done.3
  37.8 1.6 %shard_map.39 = (f32[16,256]{1,0:T(8,128)S(1)}, f32[16,256]{1,0:T(8,128)S(1)}, f32[16,256]{1,0:T(8,128)S(1)}, f32[16,256]{1,0:T(8,128)S(1)}) custom-call(s32[6]{0:T(128)S(1)} %stack.44.places, f32[16,6656]{1,0:T(8,128)S(1)} %collective-permute-done.1.refs_0_, bf16[8192,256]{1,0:T(8,128)(2,1)S(1)} %copy-done.3, bf16[8192,256]{1,0:T(8,128)(2,1)S(1)} %copy-done.1, ...), custom_call_target="tpu_custom_call" | custom-call | bytes 65536 | tf_op jit(solution)/shard_map/pallas_call | solution.py:86
  39.5 0.0 collective-permute-done.2.block
  39.5 0.3 shard_map.40
  39.8 0.6 %collective-permute-start.4 = (f32[16,256]{1,0:T(8,128)S(1)}, f32[16,256]{1,0:T(8,128)S(1)}, u32[]{:S(2)}, u32[]{:S(2)}) collective-permute-start(f32[16,256]{1,0:T(8,128)S(1)} %get-tuple-element.34), channel_id=1, source_target_pairs={{0,3},{1,2},{2,1},{3,0},{4,7},{5,6},{6,5},{7,4},{8,11},{9,10},{10,... | collective-permute-start | bytes 49160 | tf_op jit(solution)/shard_map/ppermute | solution.py:194
  40.5 1.0 %collective-permute-start.5 = (f32[16,256]{1,0:T(8,128)S(1)}, f32[16,256]{1,0:T(8,128)S(1)}, u32[]{:S(2)}, u32[]{:S(2)}) collective-permute-start(f32[16,256]{1,0:T(8,128)S(1)} %get-tuple-element.35), channel_id=1, source_target_pairs={{0,2},{1,3},{2,0},{3,1},{4,6},{5,7},{6,4},{7,5},{8,10},{9,11},{10,... | collective-permute-start | bytes 49160 | tf_op jit(solution)/shard_map/ppermute | solution.py:194
  41.4 0.3 collective-permute-start.6
  41.7 1.4 %collective-permute-done.4.refs_1_ = f32[16,256]{1,0:T(8,128)S(1)} collective-permute-done((f32[16,256]{1,0:T(8,128)S(1)}, f32[16,256]{1,0:T(8,128)S(1)}, u32[]{:S(2)}, u32[]{:S(2)}) %collective-permute-start.4) | collective-permute-done | bytes 16416 | tf_op jit(solution)/shard_map/ppermute | solution.py:194
  43.2 1.2 %collective-permute-done.5.refs_2_ = f32[16,256]{1,0:T(8,128)S(1)} collective-permute-done((f32[16,256]{1,0:T(8,128)S(1)}, f32[16,256]{1,0:T(8,128)S(1)}, u32[]{:S(2)}, u32[]{:S(2)}) %collective-permute-start.5) | collective-permute-done | bytes 16416 | tf_op jit(solution)/shard_map/ppermute | solution.py:194
  44.3 0.0 collective-permute-done.6.refs_3_
  44.3 0.6 %shard_map.41 = f32[16,256]{1,0:T(8,128)} custom-call(s32[16,256]{1,0:T(8,128)S(1)} %compare_convert_fusion.diagonal, f32[16,256]{1,0:T(8,128)S(1)} %get-tuple-element.33.refs_0_, f32[16,256]{1,0:T(8,128)S(1)} %collective-permute-done.4.refs_1_, f32[16,256]{1,0:T(8,128)S(1)} %collective-permute-done.5.refs_2_, f32[16,256]{1,0:T(8,128)S(1)} %collective-permute-done.6.refs_3_), custom_call_target="tpu_custom_call" | custom-call | bytes 16384 | tf_op jit(solution)/shard_map/pallas_call | solution.py:86
  (6 shorter events, 0.1 us)
Async XLA Ops:
  0.0 16.7 %collective-permute-start = (f32[16,8192]{1,0:T(8,128)}, f32[16,8192]{1,0:T(8,128)S(1)}, u32[]{:S(2)}, u32[]{:S(2)}) collective-permute-start(f32[16,8192]{1,0:T(8,128)} %refs_0_.1), channel_id=1, source_target_pairs={{0,8},{8,12},{12,4},{4,0},{1,9},{9,13},{13,5},{5,1},{2,10},{10,14}... | collective-permute-start | bytes 1572872 | tf_op jit(solution)/shard_map/ppermute | solution.py:151
  4.0 25.6 %collective-permute-start.3 = (f32[16,8192]{1,0:T(8,128)}, f32[16,8192]{1,0:T(8,128)S(1)}, u32[]{:S(2)}, u32[]{:S(2)}) collective-permute-start(f32[16,8192]{1,0:T(8,128)} %refs_0_.1), channel_id=1, source_target_pairs={{8,0},{12,8},{4,12},{0,4},{9,1},{13,9},{5,13},{1,5},{10,2},{14,10}... | collective-permute-start | bytes 1572872 | tf_op jit(solution)/shard_map/ppermute | solution.py:163
  4.7 15.6 %copy-start.4 = (f32[16,8192]{1,0:T(8,128)S(1)}, f32[16,8192]{1,0:T(8,128)}, u32[]{:S(2)}) copy-start(f32[16,8192]{1,0:T(8,128)} %refs_0_.1) | copy-start | bytes 1572868
  16.8 21.0 %collective-permute-start.1 = (f32[16,6656]{1,0:T(8,128)S(1)}, f32[16,6656]{1,0:T(8,128)S(1)}, u32[]{:S(2)}, u32[]{:S(2)}) collective-permute-start(f32[16,6656]{1,0:T(8,128)S(1)} %slice.6), channel_id=1, source_target_pairs={{0,8},{8,12},{12,4},{4,0},{1,9},{9,13},{13,5},{5,1},{2,10},{10,14}... | collective-permute-start | bytes 1277960 | tf_op jit(solution)/shard_map/ppermute | solution.py:166
  20.2 19.3 %collective-permute-start.2 = (f32[16,1536]{1,0:T(8,128)S(1)}, f32[16,1536]{1,0:T(8,128)S(1)}, u32[]{:S(2)}, u32[]{:S(2)}) collective-permute-start(f32[16,1536]{1,0:T(8,128)S(1)} %slice.7), channel_id=1, source_target_pairs={{0,8},{8,12},{12,4},{4,0},{1,9},{9,13},{13,5},{5,1},{2,10},{10,14}... | collective-permute-start | bytes 294920 | tf_op jit(solution)/shard_map/ppermute | solution.py:167
  20.3 2.2 %copy-start = (bf16[8192,256]{1,0:T(8,128)(2,1)S(1)}, bf16[8192,256]{1,0:T(8,128)(2,1)}, u32[]{:S(2)}) copy-start(bf16[8192,256]{1,0:T(8,128)(2,1)} %get-tuple-element.25.refs_3_.refs_2_.low) | copy-start | bytes 12582916
  22.5 2.2 %copy-start.2 = (bf16[8192,256]{1,0:T(8,128)(2,1)S(1)}, bf16[8192,256]{1,0:T(8,128)(2,1)}, u32[]{:S(2)}) copy-start(bf16[8192,256]{1,0:T(8,128)(2,1)} %get-tuple-element.24.refs_2_.refs_1_.high) | copy-start | bytes 12582916
  24.7 5.0 %copy-start.1 = (bf16[8192,256]{1,0:T(8,128)(2,1)S(1)}, bf16[8192,256]{1,0:T(8,128)(2,1)}, u32[]{:S(2)}) copy-start(bf16[8192,256]{1,0:T(8,128)(2,1)} %get-tuple-element.25.refs_3_.refs_2_.low) | copy-start | bytes 12582916
  24.7 13.1 %copy-start.3 = (bf16[8192,256]{1,0:T(8,128)(2,1)S(1)}, bf16[8192,256]{1,0:T(8,128)(2,1)}, u32[]{:S(2)}) copy-start(bf16[8192,256]{1,0:T(8,128)(2,1)} %get-tuple-element.24.refs_2_.refs_1_.high) | copy-start | bytes 12582916
  39.8 3.4 %collective-permute-start.4 = (f32[16,256]{1,0:T(8,128)S(1)}, f32[16,256]{1,0:T(8,128)S(1)}, u32[]{:S(2)}, u32[]{:S(2)}) collective-permute-start(f32[16,256]{1,0:T(8,128)S(1)} %get-tuple-element.34), channel_id=1, source_target_pairs={{0,3},{1,2},{2,1},{3,0},{4,7},{5,6},{6,5},{7,4},{8,11},{9,10},{10,... | collective-permute-start | bytes 49160 | tf_op jit(solution)/shard_map/ppermute | solution.py:194
  40.5 3.9 %collective-permute-start.5 = (f32[16,256]{1,0:T(8,128)S(1)}, f32[16,256]{1,0:T(8,128)S(1)}, u32[]{:S(2)}, u32[]{:S(2)}) collective-permute-start(f32[16,256]{1,0:T(8,128)S(1)} %get-tuple-element.35), channel_id=1, source_target_pairs={{0,2},{1,3},{2,0},{3,1},{4,6},{5,7},{6,4},{7,5},{8,10},{9,11},{10,... | collective-permute-start | bytes 49160 | tf_op jit(solution)/shard_map/ppermute | solution.py:194
  41.4 2.9 %collective-permute-start.6 = (f32[16,256]{1,0:T(8,128)S(1)}, f32[16,256]{1,0:T(8,128)S(1)}, u32[]{:S(2)}, u32[]{:S(2)}) collective-permute-start(f32[16,256]{1,0:T(8,128)S(1)} %get-tuple-element.36), channel_id=1, source_target_pairs={{0,1},{1,0},{2,3},{3,2},{4,5},{5,4},{6,7},{7,6},{8,9},{9,8},{10,11... | collective-permute-start | bytes 49160 | tf_op jit(solution)/shard_map/ppermute | solution.py:194

commit v23 on v21

--- a/solution.py
+++ b/solution.py
@@ -189,7 +189,8 @@
     arrays = [masks, last_right, *weights, *shares]
     shares = call(kernel, rep_count, (rows_share, tile_width), [], arrays, 4 + rep_count)
     terms = [shares[0]]
-    for flip in range(rep_count - 1, 0, -1):
+    middle = rep_count // 2
+    for flip in [*range(middle, rep_count), *range(middle - 1, 0, -1)]:
         pairs = [(d, d ^ flip) for d in range(rep_count)]
         terms.append(lax.ppermute(shares[flip], "rep", pairs))
     arrays = [diagonal, *terms]

time: 45.2 us -> 45.3 us (level)
  no operation moved by 1% of the time
where the time goes in v23:
time: 45.3 us; the launch traced here: 45.1 us
  waiting for transfers between devices  15.5 us (34%)
  starting transfers between devices  9.68 us (21%)
  other arithmetic  8.2 us (18%)
  Pallas kernels  6.44 us (14%)
  local copies, waits for them, and re-layouts  4.57 us (10%)
  between operations  0.74 us (2%)
    convert_element_type x1, other arithmetic, halves(): return (high.astype(jnp.bfloat16), (array - high).astype(jnp.bfloat16))  7.96 us
    pallas_call x5, Pallas kernels, call(): pl.pallas_call(kernel, out_shape=[jax.ShapeDtypeStruct(shape, jnp.float32...  6.44 us
    ppermute x1, waiting for transfers between devices, per_device(): last_left = lax.ppermute(last_held[:, :cut], 'team', onward)  5.54 us
    unnamed x10, local copies, waits for them, and re-layouts  4.38 us
    ppermute x1, starting transfers between devices, per_device(): first = lax.ppermute(omega_rows, 'team', onward)  4.04 us
    ppermute x1, waiting for transfers between devices, per_device(): first = lax.ppermute(omega_rows, 'team', onward)  4.03 us
    ppermute x1, starting transfers between devices, per_device(): last_left = lax.ppermute(last_held[:, :cut], 'team', onward)  3.33 us
    ppermute x1, waiting for transfers between devices, per_device(): held = lax.ppermute(held, 'team', backward)  2.66 us
  transfers between devices with their start and end apart: 7, of which 6 were waited for; matrix products, arithmetic and copies ran while one was open for 19% of the time, Pallas kernels for 12%

profile of v23, /device:TPU:0, one launch (start us, length us, event | category | flops | bytes accessed | tf_op | source)
XLA Modules:
  0.0 45.1 jit_solution(14715793959062255640)
XLA Ops:
  0.0 4.0 %collective-permute-start = (f32[16,8192]{1,0:T(8,128)}, f32[16,8192]{1,0:T(8,128)S(1)}, u32[]{:S(2)}, u32[]{:S(2)}) collective-permute-start(f32[16,8192]{1,0:T(8,128)} %refs_0_.1), channel_id=1, source_target_pairs={{0,8},{8,12},{12,4},{4,0},{1,9},{9,13},{13,5},{5,1},{2,10},{10,14}... | collective-permute-start | bytes 1572872 | tf_op jit(solution)/shard_map/ppermute | solution.py:151
  4.0 0.0 collective-permute-start.3
  4.7 0.0 copy-start.4
  4.7 8.0 %subtract_convert_fusion = (bf16[8192,256]{1,0:T(8,128)(2,1)}, bf16[8192,256]{1,0:T(8,128)(2,1)}) fusion(f32[8192,256]{1,0:T(8,128)} %param.4, s32[256]{0:T(256)S(1)} %iota_add_fusion.1, s32[8192]{0:T(1024)S(1)} %iota_add_fusion), kind=kLoop, calls=%fused_computation | loop fusion | flops 18874368 | bytes 16811008 | tf_op jit(solution)/shard_map/convert_element_type | solution.py:17
  12.7 4.0 %collective-permute-done.refs_1_ = f32[16,8192]{1,0:T(8,128)S(1)} collective-permute-done((f32[16,8192]{1,0:T(8,128)}, f32[16,8192]{1,0:T(8,128)S(1)}, u32[]{:S(2)}, u32[]{:S(2)}) %collective-permute-start) | collective-permute-done | bytes 524320 | tf_op jit(solution)/shard_map/ppermute | solution.py:151
  16.8 3.3 %collective-permute-start.1 = (f32[16,6144]{1,0:T(8,128)S(1)}, f32[16,6144]{1,0:T(8,128)S(1)}, u32[]{:S(2)}, u32[]{:S(2)}) collective-permute-start(f32[16,6144]{1,0:T(8,128)S(1)} %slice.6), channel_id=1, source_target_pairs={{0,8},{8,12},{12,4},{4,0},{1,9},{9,13},{13,5},{5,1},{2,10},{10,14}... | collective-permute-start | bytes 1179656 | tf_op jit(solution)/shard_map/ppermute | solution.py:166
  20.1 0.1 compare_convert_fusion.diagonal
  20.2 0.1 pad_add_fusion.1.places
  20.2 0.1 collective-permute-start.2
  20.3 0.1 pad_add_fusion.places
  20.4 0.1 stack.44.places
  20.5 0.0 copy-done.4
  20.5 0.0 copy-start
  20.5 2.2 %copy-done = bf16[8192,256]{1,0:T(8,128)(2,1)S(1)} copy-done((bf16[8192,256]{1,0:T(8,128)(2,1)S(1)}, bf16[8192,256]{1,0:T(8,128)(2,1)}, u32[]{:S(2)}) %copy-start) | copy-done | bytes 4194328
  22.7 0.0 copy-start.2
  22.7 2.2 %copy-done.2 = bf16[8192,256]{1,0:T(8,128)(2,1)S(1)} copy-done((bf16[8192,256]{1,0:T(8,128)(2,1)S(1)}, bf16[8192,256]{1,0:T(8,128)(2,1)}, u32[]{:S(2)}) %copy-start.2) | copy-done | bytes 4194328
  24.9 0.0 copy-start.1
  24.9 0.0 copy-start.3
  24.9 2.1 %shard_map.37 = (f32[16,256]{1,0:T(8,128)S(1)}, f32[16,256]{1,0:T(8,128)S(1)}) custom-call(s32[3]{0:T(128)S(1)} %pad_add_fusion.places, f32[16,8192]{1,0:T(8,128)S(1)} %copy-done.4, f32[16,8192]{1,0:T(8,128)S(1)} %collective-permute-done.refs_1_, bf16[8192,256]{1,0:T(8,128)(2,1)S(1)} %copy-done.2, bf16[8192,256]{1,0:T(8,128)(2,1)S(1)} %copy-done), custom_call_target="tpu_custom_call" | custom-call | bytes 32768 | tf_op jit(solution)/shard_map/pallas_call | solution.py:86
  27.0 2.7 %collective-permute-done.3.refs_0_ = f32[16,8192]{1,0:T(8,128)S(1)} collective-permute-done((f32[16,8192]{1,0:T(8,128)}, f32[16,8192]{1,0:T(8,128)S(1)}, u32[]{:S(2)}, u32[]{:S(2)}) %collective-permute-start.3) | collective-permute-done | bytes 524320 | tf_op jit(solution)/shard_map/ppermute | solution.py:163
  29.7 0.0 copy-done.1
  29.7 1.9 %shard_map.38.refs_5_ = f32[16,256]{1,0:T(8,128)S(1)} custom-call(s32[2]{0:T(128)S(1)} %pad_add_fusion.1.places, f32[16,8192]{1,0:T(8,128)S(1)} %collective-permute-done.3.refs_0_, bf16[8192,256]{1,0:T(8,128)(2,1)S(1)} %copy-done.2, bf16[8192,256]{1,0:T(8,128)(2,1)S(1)} %copy-done.1), custom_call_target="tpu_custom_call" | custom-call | bytes 16384 | tf_op jit(solution)/shard_map/pallas_call | solution.py:86
  31.5 5.5 %collective-permute-done.1.refs_0_ = f32[16,6144]{1,0:T(8,128)S(1)} collective-permute-done((f32[16,6144]{1,0:T(8,128)S(1)}, f32[16,6144]{1,0:T(8,128)S(1)}, u32[]{:S(2)}, u32[]{:S(2)}) %collective-permute-start.1) | collective-permute-done | bytes 393248 | tf_op jit(solution)/shard_map/ppermute | solution.py:166
  37.1 0.1 broadcast_in_dim.2.masks
  37.1 0.0 copy-done.3
  37.1 1.5 %shard_map.39 = (f32[16,256]{1,0:T(8,128)S(1)}, f32[16,256]{1,0:T(8,128)S(1)}, f32[16,256]{1,0:T(8,128)S(1)}, f32[16,256]{1,0:T(8,128)S(1)}) custom-call(s32[6]{0:T(128)S(1)} %stack.44.places, f32[16,6144]{1,0:T(8,128)S(1)} %collective-permute-done.1.refs_0_, bf16[8192,256]{1,0:T(8,128)(2,1)S(1)} %copy-done.3, bf16[8192,256]{1,0:T(8,128)(2,1)S(1)} %copy-done.1, ...), custom_call_target="tpu_custom_call" | custom-call | bytes 65536 | tf_op jit(solution)/shard_map/pallas_call | solution.py:86
  38.6 0.7 %collective-permute-done.2.block = f32[16,2048]{1,0:T(8,128)S(1)} collective-permute-done((f32[16,2048]{1,0:T(8,128)S(1)}, f32[16,2048]{1,0:T(8,128)S(1)}, u32[]{:S(2)}, u32[]{:S(2)}) %collective-permute-start.2) | collective-permute-done | bytes 131104 | tf_op jit(solution)/shard_map/ppermute | solution.py:167
  39.4 0.4 shard_map.40
  39.8 1.6 %collective-permute-start.4 = (f32[16,256]{1,0:T(8,128)S(1)}, f32[16,256]{1,0:T(8,128)S(1)}, u32[]{:S(2)}, u32[]{:S(2)}) collective-permute-start(f32[16,256]{1,0:T(8,128)S(1)} %get-tuple-element.34), channel_id=1, source_target_pairs={{0,2},{1,3},{2,0},{3,1},{4,6},{5,7},{6,4},{7,5},{8,10},{9,11},{10,... | collective-permute-start | bytes 49160 | tf_op jit(solution)/shard_map/ppermute | solution.py:195
  41.3 0.0 collective-permute-start.5
  41.3 0.6 %collective-permute-start.6 = (f32[16,256]{1,0:T(8,128)S(1)}, f32[16,256]{1,0:T(8,128)S(1)}, u32[]{:S(2)}, u32[]{:S(2)}) collective-permute-start(f32[16,256]{1,0:T(8,128)S(1)} %get-tuple-element.36), channel_id=1, source_target_pairs={{0,1},{1,0},{2,3},{3,2},{4,5},{5,4},{6,7},{7,6},{8,9},{9,8},{10,11... | collective-permute-start | bytes 49160 | tf_op jit(solution)/shard_map/ppermute | solution.py:195
  42.0 1.6 %collective-permute-done.4.refs_1_ = f32[16,256]{1,0:T(8,128)S(1)} collective-permute-done((f32[16,256]{1,0:T(8,128)S(1)}, f32[16,256]{1,0:T(8,128)S(1)}, u32[]{:S(2)}, u32[]{:S(2)}) %collective-permute-start.4) | collective-permute-done | bytes 16416 | tf_op jit(solution)/shard_map/ppermute | solution.py:195
  43.6 0.9 %collective-permute-done.5.refs_2_ = f32[16,256]{1,0:T(8,128)S(1)} collective-permute-done((f32[16,256]{1,0:T(8,128)S(1)}, f32[16,256]{1,0:T(8,128)S(1)}, u32[]{:S(2)}, u32[]{:S(2)}) %collective-permute-start.5) | collective-permute-done | bytes 16416 | tf_op jit(solution)/shard_map/ppermute | solution.py:195
  44.5 0.0 collective-permute-done.6.refs_3_
  44.5 0.6 %shard_map.41 = f32[16,256]{1,0:T(8,128)} custom-call(s32[16,256]{1,0:T(8,128)S(1)} %compare_convert_fusion.diagonal, f32[16,256]{1,0:T(8,128)S(1)} %get-tuple-element.33.refs_0_, f32[16,256]{1,0:T(8,128)S(1)} %collective-permute-done.4.refs_1_, f32[16,256]{1,0:T(8,128)S(1)} %collective-permute-done.5.refs_2_, f32[16,256]{1,0:T(8,128)S(1)} %collective-permute-done.6.refs_3_), custom_call_target="tpu_custom_call" | custom-call | bytes 16384 | tf_op jit(solution)/shard_map/pallas_call | solution.py:86
  (6 shorter events, 0.1 us)
Async XLA Ops:
  0.0 16.7 %collective-permute-start = (f32[16,8192]{1,0:T(8,128)}, f32[16,8192]{1,0:T(8,128)S(1)}, u32[]{:S(2)}, u32[]{:S(2)}) collective-permute-start(f32[16,8192]{1,0:T(8,128)} %refs_0_.1), channel_id=1, source_target_pairs={{0,8},{8,12},{12,4},{4,0},{1,9},{9,13},{13,5},{5,1},{2,10},{10,14}... | collective-permute-start | bytes 1572872 | tf_op jit(solution)/shard_map/ppermute | solution.py:151
  4.0 25.6 %collective-permute-start.3 = (f32[16,8192]{1,0:T(8,128)}, f32[16,8192]{1,0:T(8,128)S(1)}, u32[]{:S(2)}, u32[]{:S(2)}) collective-permute-start(f32[16,8192]{1,0:T(8,128)} %refs_0_.1), channel_id=1, source_target_pairs={{8,0},{12,8},{4,12},{0,4},{9,1},{13,9},{5,13},{1,5},{10,2},{14,10}... | collective-permute-start | bytes 1572872 | tf_op jit(solution)/shard_map/ppermute | solution.py:163
  4.7 15.8 %copy-start.4 = (f32[16,8192]{1,0:T(8,128)S(1)}, f32[16,8192]{1,0:T(8,128)}, u32[]{:S(2)}) copy-start(f32[16,8192]{1,0:T(8,128)} %refs_0_.1) | copy-start | bytes 1572868
  16.8 20.3 %collective-permute-start.1 = (f32[16,6144]{1,0:T(8,128)S(1)}, f32[16,6144]{1,0:T(8,128)S(1)}, u32[]{:S(2)}, u32[]{:S(2)}) collective-permute-start(f32[16,6144]{1,0:T(8,128)S(1)} %slice.6), channel_id=1, source_target_pairs={{0,8},{8,12},{12,4},{4,0},{1,9},{9,13},{13,5},{5,1},{2,10},{10,14}... | collective-permute-start | bytes 1179656 | tf_op jit(solution)/shard_map/ppermute | solution.py:166
  20.2 19.1 %collective-permute-start.2 = (f32[16,2048]{1,0:T(8,128)S(1)}, f32[16,2048]{1,0:T(8,128)S(1)}, u32[]{:S(2)}, u32[]{:S(2)}) collective-permute-start(f32[16,2048]{1,0:T(8,128)S(1)} %slice.7), channel_id=1, source_target_pairs={{0,8},{8,12},{12,4},{4,0},{1,9},{9,13},{13,5},{5,1},{2,10},{10,14}... | collective-permute-start | bytes 393224 | tf_op jit(solution)/shard_map/ppermute | solution.py:167
  20.5 2.2 %copy-start = (bf16[8192,256]{1,0:T(8,128)(2,1)S(1)}, bf16[8192,256]{1,0:T(8,128)(2,1)}, u32[]{:S(2)}) copy-start(bf16[8192,256]{1,0:T(8,128)(2,1)} %get-tuple-element.25.refs_3_.refs_2_.low) | copy-start | bytes 12582916
  22.7 2.2 %copy-start.2 = (bf16[8192,256]{1,0:T(8,128)(2,1)S(1)}, bf16[8192,256]{1,0:T(8,128)(2,1)}, u32[]{:S(2)}) copy-start(bf16[8192,256]{1,0:T(8,128)(2,1)} %get-tuple-element.24.refs_2_.refs_1_.high) | copy-start | bytes 12582916
  24.9 4.8 %copy-start.1 = (bf16[8192,256]{1,0:T(8,128)(2,1)S(1)}, bf16[8192,256]{1,0:T(8,128)(2,1)}, u32[]{:S(2)}) copy-start(bf16[8192,256]{1,0:T(8,128)(2,1)} %get-tuple-element.25.refs_3_.refs_2_.low) | copy-start | bytes 12582916
  24.9 12.2 %copy-start.3 = (bf16[8192,256]{1,0:T(8,128)(2,1)S(1)}, bf16[8192,256]{1,0:T(8,128)(2,1)}, u32[]{:S(2)}) copy-start(bf16[8192,256]{1,0:T(8,128)(2,1)} %get-tuple-element.24.refs_2_.refs_1_.high) | copy-start | bytes 12582916
  39.8 3.8 %collective-permute-start.4 = (f32[16,256]{1,0:T(8,128)S(1)}, f32[16,256]{1,0:T(8,128)S(1)}, u32[]{:S(2)}, u32[]{:S(2)}) collective-permute-start(f32[16,256]{1,0:T(8,128)S(1)} %get-tuple-element.34), channel_id=1, source_target_pairs={{0,2},{1,3},{2,0},{3,1},{4,6},{5,7},{6,4},{7,5},{8,10},{9,11},{10,... | collective-permute-start | bytes 49160 | tf_op jit(solution)/shard_map/ppermute | solution.py:195
  41.3 3.2 %collective-permute-start.5 = (f32[16,256]{1,0:T(8,128)S(1)}, f32[16,256]{1,0:T(8,128)S(1)}, u32[]{:S(2)}, u32[]{:S(2)}) collective-permute-start(f32[16,256]{1,0:T(8,128)S(1)} %get-tuple-element.35), channel_id=1, source_target_pairs={{0,3},{1,2},{2,1},{3,0},{4,7},{5,6},{6,5},{7,4},{8,11},{9,10},{10,... | collective-permute-start | bytes 49160 | tf_op jit(solution)/shard_map/ppermute | solution.py:195
  41.3 3.2 %collective-permute-start.6 = (f32[16,256]{1,0:T(8,128)S(1)}, f32[16,256]{1,0:T(8,128)S(1)}, u32[]{:S(2)}, u32[]{:S(2)}) collective-permute-start(f32[16,256]{1,0:T(8,128)S(1)} %get-tuple-element.36), channel_id=1, source_target_pairs={{0,1},{1,0},{2,3},{3,2},{4,5},{5,4},{6,7},{7,6},{8,9},{9,8},{10,11... | collective-permute-start | bytes 49160 | tf_op jit(solution)/shard_map/ppermute | solution.py:195

commit v24 on v21

--- a/solution.py
+++ b/solution.py
@@ -189,7 +189,8 @@
     arrays = [masks, last_right, *weights, *shares]
     shares = call(kernel, rep_count, (rows_share, tile_width), [], arrays, 4 + rep_count)
     terms = [shares[0]]
-    for flip in range(rep_count - 1, 0, -1):
+    flips = list(range(rep_count - 1, 0, -1))
+    for flip in [flips[0], *flips[:0:-1]]:
         pairs = [(d, d ^ flip) for d in range(rep_count)]
         terms.append(lax.ppermute(shares[flip], "rep", pairs))
     arrays = [diagonal, *terms]

time: 45.2 us -> 46 us (1.018)
  waiting for transfers between devices: 15.7 us -> 16.2 us
    ppermute x3, waiting for transfers between devices: 2.69 us -> 3.2 us  [per_device(): terms.append(lax.ppermute(shares[flip], 'rep', pairs))]
  transfers between devices with their start and end apart: 7 -> 7, of which waited for: 6 -> 6; matrix products, arithmetic and copies ran while one was open for 19% -> 18% of each run, Pallas kernels for 12% -> 12%
where the time goes in v24:
time: 46 us; the launch traced here: 45.8 us
  waiting for transfers between devices  16.2 us (35%)
  starting transfers between devices  9.68 us (21%)
  other arithmetic  8.2 us (18%)
  Pallas kernels  6.43 us (14%)
  local copies, waits for them, and re-layouts  4.57 us (10%)
  between operations  0.74 us (2%)
    convert_element_type x1, other arithmetic, halves(): return (high.astype(jnp.bfloat16), (array - high).astype(jnp.bfloat16))  7.96 us
    pallas_call x5, Pallas kernels, call(): pl.pallas_call(kernel, out_shape=[jax.ShapeDtypeStruct(shape, jnp.float32...  6.43 us
    ppermute x1, waiting for transfers between devices, per_device(): last_left = lax.ppermute(last_held[:, :cut], 'team', onward)  5.54 us
    unnamed x10, local copies, waits for them, and re-layouts  4.38 us
    ppermute x1, starting transfers between devices, per_device(): first = lax.ppermute(omega_rows, 'team', onward)  4.04 us
    ppermute x1, waiting for transfers between devices, per_device(): first = lax.ppermute(omega_rows, 'team', onward)  4.03 us
    ppermute x1, starting transfers between devices, per_device(): last_left = lax.ppermute(last_held[:, :cut], 'team', onward)  3.33 us
    ppermute x3, waiting for transfers between devices, per_device(): terms.append(lax.ppermute(shares[flip], 'rep', pairs))  3.2 us
  transfers between devices with their start and end apart: 7, of which 6 were waited for; matrix products, arithmetic and copies ran while one was open for 18% of the time, Pallas kernels for 12%

profile of v24, /device:TPU:0, one launch (start us, length us, event | category | flops | bytes accessed | tf_op | source)
XLA Modules:
  0.0 45.8 jit_solution(8474446212904341799)
XLA Ops:
  0.0 4.0 %collective-permute-start = (f32[16,8192]{1,0:T(8,128)}, f32[16,8192]{1,0:T(8,128)S(1)}, u32[]{:S(2)}, u32[]{:S(2)}) collective-permute-start(f32[16,8192]{1,0:T(8,128)} %refs_0_.1), channel_id=1, source_target_pairs={{0,8},{8,12},{12,4},{4,0},{1,9},{9,13},{13,5},{5,1},{2,10},{10,14}... | collective-permute-start | bytes 1572872 | tf_op jit(solution)/shard_map/ppermute | solution.py:151
  4.0 0.0 collective-permute-start.3
  4.7 0.0 copy-start.4
  4.7 8.0 %subtract_convert_fusion = (bf16[8192,256]{1,0:T(8,128)(2,1)}, bf16[8192,256]{1,0:T(8,128)(2,1)}) fusion(f32[8192,256]{1,0:T(8,128)} %param.4, s32[256]{0:T(256)S(1)} %iota_add_fusion.1, s32[8192]{0:T(1024)S(1)} %iota_add_fusion), kind=kLoop, calls=%fused_computation | loop fusion | flops 18874368 | bytes 16811008 | tf_op jit(solution)/shard_map/convert_element_type | solution.py:17
  12.7 4.0 %collective-permute-done.refs_1_ = f32[16,8192]{1,0:T(8,128)S(1)} collective-permute-done((f32[16,8192]{1,0:T(8,128)}, f32[16,8192]{1,0:T(8,128)S(1)}, u32[]{:S(2)}, u32[]{:S(2)}) %collective-permute-start) | collective-permute-done | bytes 524320 | tf_op jit(solution)/shard_map/ppermute | solution.py:151
  16.8 3.3 %collective-permute-start.1 = (f32[16,6144]{1,0:T(8,128)S(1)}, f32[16,6144]{1,0:T(8,128)S(1)}, u32[]{:S(2)}, u32[]{:S(2)}) collective-permute-start(f32[16,6144]{1,0:T(8,128)S(1)} %slice.6), channel_id=1, source_target_pairs={{0,8},{8,12},{12,4},{4,0},{1,9},{9,13},{13,5},{5,1},{2,10},{10,14}... | collective-permute-start | bytes 1179656 | tf_op jit(solution)/shard_map/ppermute | solution.py:166
  20.1 0.1 compare_convert_fusion.diagonal
  20.2 0.1 pad_add_fusion.1.places
  20.2 0.1 collective-permute-start.2
  20.3 0.1 pad_add_fusion.places
  20.4 0.1 stack.44.places
  20.5 0.0 copy-done.4
  20.5 0.0 copy-start
  20.5 2.2 %copy-done = bf16[8192,256]{1,0:T(8,128)(2,1)S(1)} copy-done((bf16[8192,256]{1,0:T(8,128)(2,1)S(1)}, bf16[8192,256]{1,0:T(8,128)(2,1)}, u32[]{:S(2)}) %copy-start) | copy-done | bytes 4194328
  22.7 0.0 copy-start.2
  22.7 2.2 %copy-done.2 = bf16[8192,256]{1,0:T(8,128)(2,1)S(1)} copy-done((bf16[8192,256]{1,0:T(8,128)(2,1)S(1)}, bf16[8192,256]{1,0:T(8,128)(2,1)}, u32[]{:S(2)}) %copy-start.2) | copy-done | bytes 4194328
  24.9 0.0 copy-start.1
  24.9 0.0 copy-start.3
  24.9 2.1 %shard_map.37 = (f32[16,256]{1,0:T(8,128)S(1)}, f32[16,256]{1,0:T(8,128)S(1)}) custom-call(s32[3]{0:T(128)S(1)} %pad_add_fusion.places, f32[16,8192]{1,0:T(8,128)S(1)} %copy-done.4, f32[16,8192]{1,0:T(8,128)S(1)} %collective-permute-done.refs_1_, bf16[8192,256]{1,0:T(8,128)(2,1)S(1)} %copy-done.2, bf16[8192,256]{1,0:T(8,128)(2,1)S(1)} %copy-done), custom_call_target="tpu_custom_call" | custom-call | bytes 32768 | tf_op jit(solution)/shard_map/pallas_call | solution.py:86
  27.0 2.7 %collective-permute-done.3.refs_0_ = f32[16,8192]{1,0:T(8,128)S(1)} collective-permute-done((f32[16,8192]{1,0:T(8,128)}, f32[16,8192]{1,0:T(8,128)S(1)}, u32[]{:S(2)}, u32[]{:S(2)}) %collective-permute-start.3) | collective-permute-done | bytes 524320 | tf_op jit(solution)/shard_map/ppermute | solution.py:163
  29.7 0.0 copy-done.1
  29.7 1.9 %shard_map.38.refs_5_ = f32[16,256]{1,0:T(8,128)S(1)} custom-call(s32[2]{0:T(128)S(1)} %pad_add_fusion.1.places, f32[16,8192]{1,0:T(8,128)S(1)} %collective-permute-done.3.refs_0_, bf16[8192,256]{1,0:T(8,128)(2,1)S(1)} %copy-done.2, bf16[8192,256]{1,0:T(8,128)(2,1)S(1)} %copy-done.1), custom_call_target="tpu_custom_call" | custom-call | bytes 16384 | tf_op jit(solution)/shard_map/pallas_call | solution.py:86
  31.5 5.5 %collective-permute-done.1.refs_0_ = f32[16,6144]{1,0:T(8,128)S(1)} collective-permute-done((f32[16,6144]{1,0:T(8,128)S(1)}, f32[16,6144]{1,0:T(8,128)S(1)}, u32[]{:S(2)}, u32[]{:S(2)}) %collective-permute-start.1) | collective-permute-done | bytes 393248 | tf_op jit(solution)/shard_map/ppermute | solution.py:166
  37.1 0.1 broadcast_in_dim.2.masks
  37.1 0.0 copy-done.3
  37.1 1.5 %shard_map.39 = (f32[16,256]{1,0:T(8,128)S(1)}, f32[16,256]{1,0:T(8,128)S(1)}, f32[16,256]{1,0:T(8,128)S(1)}, f32[16,256]{1,0:T(8,128)S(1)}) custom-call(s32[6]{0:T(128)S(1)} %stack.44.places, f32[16,6144]{1,0:T(8,128)S(1)} %collective-permute-done.1.refs_0_, bf16[8192,256]{1,0:T(8,128)(2,1)S(1)} %copy-done.3, bf16[8192,256]{1,0:T(8,128)(2,1)S(1)} %copy-done.1, ...), custom_call_target="tpu_custom_call" | custom-call | bytes 65536 | tf_op jit(solution)/shard_map/pallas_call | solution.py:86
  38.6 0.7 %collective-permute-done.2.block = f32[16,2048]{1,0:T(8,128)S(1)} collective-permute-done((f32[16,2048]{1,0:T(8,128)S(1)}, f32[16,2048]{1,0:T(8,128)S(1)}, u32[]{:S(2)}, u32[]{:S(2)}) %collective-permute-start.2) | collective-permute-done | bytes 131104 | tf_op jit(solution)/shard_map/ppermute | solution.py:167
  39.4 0.4 shard_map.40
  39.8 0.8 %collective-permute-start.4 = (f32[16,256]{1,0:T(8,128)S(1)}, f32[16,256]{1,0:T(8,128)S(1)}, u32[]{:S(2)}, u32[]{:S(2)}) collective-permute-start(f32[16,256]{1,0:T(8,128)S(1)} %get-tuple-element.34), channel_id=1, source_target_pairs={{0,3},{1,2},{2,1},{3,0},{4,7},{5,6},{6,5},{7,4},{8,11},{9,10},{10,... | collective-permute-start | bytes 49160 | tf_op jit(solution)/shard_map/ppermute | solution.py:195
  40.5 0.9 %collective-permute-start.5 = (f32[16,256]{1,0:T(8,128)S(1)}, f32[16,256]{1,0:T(8,128)S(1)}, u32[]{:S(2)}, u32[]{:S(2)}) collective-permute-start(f32[16,256]{1,0:T(8,128)S(1)} %get-tuple-element.35), channel_id=1, source_target_pairs={{0,1},{1,0},{2,3},{3,2},{4,5},{5,4},{6,7},{7,6},{8,9},{9,8},{10,11... | collective-permute-start | bytes 49160 | tf_op jit(solution)/shard_map/ppermute | solution.py:195
  41.4 0.5 %collective-permute-start.6 = (f32[16,256]{1,0:T(8,128)S(1)}, f32[16,256]{1,0:T(8,128)S(1)}, u32[]{:S(2)}, u32[]{:S(2)}) collective-permute-start(f32[16,256]{1,0:T(8,128)S(1)} %get-tuple-element.36), channel_id=1, source_target_pairs={{0,2},{1,3},{2,0},{3,1},{4,6},{5,7},{6,4},{7,5},{8,10},{9,11},{10,... | collective-permute-start | bytes 49160 | tf_op jit(solution)/shard_map/ppermute | solution.py:195
  42.0 1.1 %collective-permute-done.4.refs_1_ = f32[16,256]{1,0:T(8,128)S(1)} collective-permute-done((f32[16,256]{1,0:T(8,128)S(1)}, f32[16,256]{1,0:T(8,128)S(1)}, u32[]{:S(2)}, u32[]{:S(2)}) %collective-permute-start.4) | collective-permute-done | bytes 16416 | tf_op jit(solution)/shard_map/ppermute | solution.py:195
  43.1 0.0 collective-permute-done.5.refs_2_
  43.1 2.1 %collective-permute-done.6.refs_3_ = f32[16,256]{1,0:T(8,128)S(1)} collective-permute-done((f32[16,256]{1,0:T(8,128)S(1)}, f32[16,256]{1,0:T(8,128)S(1)}, u32[]{:S(2)}, u32[]{:S(2)}) %collective-permute-start.6) | collective-permute-done | bytes 16416 | tf_op jit(solution)/shard_map/ppermute | solution.py:195
  45.2 0.6 %shard_map.41 = f32[16,256]{1,0:T(8,128)} custom-call(s32[16,256]{1,0:T(8,128)S(1)} %compare_convert_fusion.diagonal, f32[16,256]{1,0:T(8,128)S(1)} %get-tuple-element.33.refs_0_, f32[16,256]{1,0:T(8,128)S(1)} %collective-permute-done.4.refs_1_, f32[16,256]{1,0:T(8,128)S(1)} %collective-permute-done.5.refs_2_, f32[16,256]{1,0:T(8,128)S(1)} %collective-permute-done.6.refs_3_), custom_call_target="tpu_custom_call" | custom-call | bytes 16384 | tf_op jit(solution)/shard_map/pallas_call | solution.py:86
  (6 shorter events, 0.1 us)
Async XLA Ops:
  0.0 16.7 %collective-permute-start = (f32[16,8192]{1,0:T(8,128)}, f32[16,8192]{1,0:T(8,128)S(1)}, u32[]{:S(2)}, u32[]{:S(2)}) collective-permute-start(f32[16,8192]{1,0:T(8,128)} %refs_0_.1), channel_id=1, source_target_pairs={{0,8},{8,12},{12,4},{4,0},{1,9},{9,13},{13,5},{5,1},{2,10},{10,14}... | collective-permute-start | bytes 1572872 | tf_op jit(solution)/shard_map/ppermute | solution.py:151
  4.0 25.6 %collective-permute-start.3 = (f32[16,8192]{1,0:T(8,128)}, f32[16,8192]{1,0:T(8,128)S(1)}, u32[]{:S(2)}, u32[]{:S(2)}) collective-permute-start(f32[16,8192]{1,0:T(8,128)} %refs_0_.1), channel_id=1, source_target_pairs={{8,0},{12,8},{4,12},{0,4},{9,1},{13,9},{5,13},{1,5},{10,2},{14,10}... | collective-permute-start | bytes 1572872 | tf_op jit(solution)/shard_map/ppermute | solution.py:163
  4.7 15.8 %copy-start.4 = (f32[16,8192]{1,0:T(8,128)S(1)}, f32[16,8192]{1,0:T(8,128)}, u32[]{:S(2)}) copy-start(f32[16,8192]{1,0:T(8,128)} %refs_0_.1) | copy-start | bytes 1572868
  16.8 20.3 %collective-permute-start.1 = (f32[16,6144]{1,0:T(8,128)S(1)}, f32[16,6144]{1,0:T(8,128)S(1)}, u32[]{:S(2)}, u32[]{:S(2)}) collective-permute-start(f32[16,6144]{1,0:T(8,128)S(1)} %slice.6), channel_id=1, source_target_pairs={{0,8},{8,12},{12,4},{4,0},{1,9},{9,13},{13,5},{5,1},{2,10},{10,14}... | collective-permute-start | bytes 1179656 | tf_op jit(solution)/shard_map/ppermute | solution.py:166
  20.2 19.1 %collective-permute-start.2 = (f32[16,2048]{1,0:T(8,128)S(1)}, f32[16,2048]{1,0:T(8,128)S(1)}, u32[]{:S(2)}, u32[]{:S(2)}) collective-permute-start(f32[16,2048]{1,0:T(8,128)S(1)} %slice.7), channel_id=1, source_target_pairs={{0,8},{8,12},{12,4},{4,0},{1,9},{9,13},{13,5},{5,1},{2,10},{10,14}... | collective-permute-start | bytes 393224 | tf_op jit(solution)/shard_map/ppermute | solution.py:167
  20.5 2.2 %copy-start = (bf16[8192,256]{1,0:T(8,128)(2,1)S(1)}, bf16[8192,256]{1,0:T(8,128)(2,1)}, u32[]{:S(2)}) copy-start(bf16[8192,256]{1,0:T(8,128)(2,1)} %get-tuple-element.25.refs_3_.refs_2_.low) | copy-start | bytes 12582916
  22.7 2.2 %copy-start.2 = (bf16[8192,256]{1,0:T(8,128)(2,1)S(1)}, bf16[8192,256]{1,0:T(8,128)(2,1)}, u32[]{:S(2)}) copy-start(bf16[8192,256]{1,0:T(8,128)(2,1)} %get-tuple-element.24.refs_2_.refs_1_.high) | copy-start | bytes 12582916
  24.9 4.8 %copy-start.1 = (bf16[8192,256]{1,0:T(8,128)(2,1)S(1)}, bf16[8192,256]{1,0:T(8,128)(2,1)}, u32[]{:S(2)}) copy-start(bf16[8192,256]{1,0:T(8,128)(2,1)} %get-tuple-element.25.refs_3_.refs_2_.low) | copy-start | bytes 12582916
  24.9 12.2 %copy-start.3 = (bf16[8192,256]{1,0:T(8,128)(2,1)S(1)}, bf16[8192,256]{1,0:T(8,128)(2,1)}, u32[]{:S(2)}) copy-start(bf16[8192,256]{1,0:T(8,128)(2,1)} %get-tuple-element.24.refs_2_.refs_1_.high) | copy-start | bytes 12582916
  39.8 3.4 %collective-permute-start.4 = (f32[16,256]{1,0:T(8,128)S(1)}, f32[16,256]{1,0:T(8,128)S(1)}, u32[]{:S(2)}, u32[]{:S(2)}) collective-permute-start(f32[16,256]{1,0:T(8,128)S(1)} %get-tuple-element.34), channel_id=1, source_target_pairs={{0,3},{1,2},{2,1},{3,0},{4,7},{5,6},{6,5},{7,4},{8,11},{9,10},{10,... | collective-permute-start | bytes 49160 | tf_op jit(solution)/shard_map/ppermute | solution.py:195
  40.5 2.6 %collective-permute-start.5 = (f32[16,256]{1,0:T(8,128)S(1)}, f32[16,256]{1,0:T(8,128)S(1)}, u32[]{:S(2)}, u32[]{:S(2)}) collective-permute-start(f32[16,256]{1,0:T(8,128)S(1)} %get-tuple-element.35), channel_id=1, source_target_pairs={{0,1},{1,0},{2,3},{3,2},{4,5},{5,4},{6,7},{7,6},{8,9},{9,8},{10,11... | collective-permute-start | bytes 49160 | tf_op jit(solution)/shard_map/ppermute | solution.py:195
  41.4 3.7 %collective-permute-start.6 = (f32[16,256]{1,0:T(8,128)S(1)}, f32[16,256]{1,0:T(8,128)S(1)}, u32[]{:S(2)}, u32[]{:S(2)}) collective-permute-start(f32[16,256]{1,0:T(8,128)S(1)} %get-tuple-element.36), channel_id=1, source_target_pairs={{0,2},{1,3},{2,0},{3,1},{4,6},{5,7},{6,4},{7,5},{8,10},{9,11},{10,... | collective-permute-start | bytes 49160 | tf_op jit(solution)/shard_map/ppermute | solution.py:195
